TPU v7x, 32 devices: a whole 2x2x4 slice. The times are simulated.
32 devices in a mesh: pipe: 2 (over core), expert: 16 (over z, y, x).
Axes of the slice: x: 2, y: 2, z: 4, core: 2. Of those that a mesh axis runs over, the one named last changes fastest.
Arguments:
- a_input: bfloat16 [2, 2048, 3584], P('pipe', 'expert'), may hold values from -6 to 6
- a_route: int32 [2, 2048, 1], P('pipe', 'expert'), may hold values from 0 to 3; in each aligned block of 128 rows (0 to 127, 128 to 255, ..., all dimensions but the last counted through in order) at most 34 rows name the same one
- b_saved: bfloat16 [2, 2048, 3584], P('pipe', 'expert'), may hold values from -6 to 6
- b_grad: bfloat16 [2, 2048, 3584], P('pipe', 'expert'), may hold values from -6 to 6
- b_route: int32 [2, 2048, 1], P('pipe', 'expert'), may hold values from 0 to 3; in each aligned block of 128 rows (0 to 127, 128 to 255, ..., all dimensions but the last counted through in order) at most 34 rows name the same one
- up_weight: bfloat16 [2, 3584, 4096], P('pipe', None, 'expert'), may hold values from -0.09375 to 0.09375
- down_weight: bfloat16 [2, 4096, 3584], P('pipe', 'expert'), may hold values from -0.1875 to 0.1875
- router: bfloat16 [2, 3584, 4], P('pipe'), may hold values from -0.09375 to 0.09375
Outputs:
- a_next: bfloat16 [2, 2048, 3584], P('pipe', 'expert')
- b_next: bfloat16 [2, 2048, 3584], P('pipe', 'expert')
- up_grad: bfloat16 [2, 3584, 4096], P('pipe', None, 'expert')
- down_grad: bfloat16 [2, 4096, 3584], P('pipe', 'expert')
Inputs may be any that keep to these rules, and one draw needn't show every extreme that they name: `a_route`: within each device's 128 rows, no expert is named by more than 34 of the (token, choice) pairs, a bound that some block reaches. `b_route`: within each device's 128 rows, no expert is named by more than 34 of the (token, choice) pairs, a bound that some block reaches.
All inputs are finite; a program needn't handle non-finite values.
Results may differ from a plain program's by a relative error of at most 0.0067.
Values may be sent and summed in bfloat16 or wider, within the bound.
No kernel may reach another device: no remote copies, remote signals or barrier semaphores. Data moves between devices by JAX's collectives and lax.ppermute only.
A program may use at most 128 MiB of HBM per device.

v0:
```python
import jax
import jax.numpy as jnp
from jax import lax
from jax.sharding import PartitionSpec as P

EPS = 1e-06


def partner(block, axis, bit):
    count = lax.axis_size(axis)
    route = []
    for low in range(count):
        high = low | 1 << bit
        if high != low and high < count:
            route += [(low, high), (high, low)]
    return lax.ppermute(block, axis, route)


def from_behind(array, axis, by):
    devices = lax.axis_size(axis)
    return lax.ppermute(array, axis, [(i, (i + by) % devices) for i in range(devices)])


def rounded(values):
    return lax.optimization_barrier(values.astype(jnp.bfloat16)).astype(jnp.float32)


def route_plan(features, route_ids, router_cols, capacity):
    feat_float = features.astype(jnp.float32)
    inv_scale = lax.rsqrt(jnp.mean(feat_float * feat_float, axis=-1, keepdims=True) + EPS)
    normed = (feat_float * inv_scale).astype(jnp.bfloat16)
    scores = jnp.dot(normed, router_cols, preferred_element_type=jnp.float32)
    gate_value = jax.nn.sigmoid(jnp.take_along_axis(scores, route_ids, axis=1))
    flat_ids = route_ids.reshape(-1)
    onehot = (flat_ids[:, None] == jnp.arange(router_cols.shape[1], dtype=jnp.int32)).astype(
        jnp.int32
    )
    slot_pos = jnp.sum(onehot * (jnp.cumsum(onehot, axis=0) - 1), axis=1)
    flat_index = flat_ids * capacity + slot_pos
    return (feat_float, inv_scale, normed, gate_value, flat_index)


def fill_slots(row_block, flat_index, experts, capacity, group_size):
    model_width = row_block.shape[1]
    buffer = (
        jnp.zeros((experts * capacity, model_width), row_block.dtype).at[flat_index].set(row_block)
    )
    return jnp.repeat(buffer.reshape(experts, capacity, model_width), group_size, axis=0)


def expert_rows(received, up_slice, down_slice):
    row_block = received.reshape(-1, received.shape[2])
    hidden = jnp.dot(row_block, up_slice, preferred_element_type=jnp.float32)
    sigma_vals = jax.nn.sigmoid(hidden)
    activated = (hidden * sigma_vals).astype(jnp.bfloat16)
    partial_value = jnp.dot(activated, down_slice, preferred_element_type=jnp.float32).astype(
        jnp.bfloat16
    )
    return (row_block, hidden, sigma_vals, activated, partial_value)


def expert_back(received, received_cot, up_slice, down_slice):
    row_block, hidden, sigma_vals, activated, partial_value = expert_rows(
        received, up_slice, down_slice
    )
    cot_block = received_cot.reshape(-1, received_cot.shape[2])
    gate_terms = jnp.sum(cot_block.astype(jnp.float32) * partial_value.astype(jnp.float32), axis=1)
    gate_terms = gate_terms.astype(jnp.bfloat16).reshape(received.shape[0], received.shape[1])
    act_grad = lax.dot_general(
        cot_block, down_slice, (((1,), (1,)), ((), ())), preferred_element_type=jnp.float32
    )
    hid_grad = (act_grad * sigma_vals * (1.0 + hidden * (1.0 - sigma_vals))).astype(jnp.bfloat16)
    grad_down = lax.dot_general(
        activated, cot_block, (((0,), (0,)), ((), ())), preferred_element_type=jnp.float32
    ).astype(jnp.bfloat16)
    grad_up = lax.dot_general(
        row_block, hid_grad, (((0,), (0,)), ((), ())), preferred_element_type=jnp.float32
    ).astype(jnp.bfloat16)
    input_part = lax.dot_general(
        hid_grad, up_slice, (((1,), (1,)), ((), ())), preferred_element_type=jnp.float32
    )
    input_part = input_part.astype(jnp.bfloat16).reshape(received.shape)
    return (input_part, gate_terms, grad_up, grad_down)


def group_total(returned, experts, group_size):
    shape_in = returned.shape
    summed = returned.reshape((experts, group_size) + shape_in[1:]).astype(jnp.float32).sum(axis=1)
    return summed.reshape((experts * shape_in[1],) + shape_in[2:])


def body(a_input, a_route, b_saved, b_grad, b_route, up_weight, down_weight, router):
    n_expert = lax.axis_size("expert")
    bit_count = lax.axis_size("pipe").bit_length() - 1
    experts = router.shape[2]
    group_size = n_expert // experts
    tokens = a_input.shape[1]
    top_count = a_route.shape[2]
    model_width = a_input.shape[2]
    capacity = tokens * top_count // experts + 2
    up_home = up_weight[0]
    down_home = down_weight[0]
    router_home = router[0]
    partner_pack = (b_saved[0], b_grad[0], b_route[0].astype(jnp.bfloat16))
    for bit_number in range(bit_count):
        partner_pack = partner(
            (partner_pack[0], partner_pack[1], partner_pack[2]), "pipe", bit_number
        )
    up_other, down_other, router_other = (up_home, down_home, router_home)
    b_features, b_cot, b_ids = partner_pack
    b_ids = b_ids.astype(jnp.int32)
    a_float, a_scale, a_normed, a_gate, a_index = route_plan(
        a_input[0], a_route[0], router_home, capacity
    )
    a_send = fill_slots(
        jnp.repeat(a_normed, top_count, axis=0), a_index, experts, capacity, group_size
    )
    b_float, b_scale, b_normed, b_gate, b_index = route_plan(
        b_features, b_ids, router_other, capacity
    )
    cot_rows = (
        (b_gate[:, :, None] * b_cot.astype(jnp.float32)[:, None, :])
        .astype(jnp.bfloat16)
        .reshape(-1, model_width)
    )
    b_send = fill_slots(
        jnp.repeat(b_normed, top_count, axis=0), b_index, experts, capacity, group_size
    )
    cot_send = fill_slots(cot_rows, b_index, experts, capacity, group_size)
    a_recv = lax.all_to_all(a_send, "expert", split_axis=0, concat_axis=0, tiled=True)
    a_part = expert_rows(a_recv, up_home, down_home)[4].reshape(a_recv.shape)
    a_back = lax.all_to_all(a_part, "expert", split_axis=0, concat_axis=0, tiled=True)
    b_recv, cot_recv = (
        lax.all_to_all(b_send, "expert", split_axis=0, concat_axis=0, tiled=True),
        lax.all_to_all(cot_send, "expert", split_axis=0, concat_axis=0, tiled=True),
    )
    input_part, gate_terms, up_grad, down_grad = expert_back(b_recv, cot_recv, up_other, down_other)
    back_input, back_terms = (
        lax.all_to_all(input_part, "expert", split_axis=0, concat_axis=0, tiled=True),
        lax.all_to_all(gate_terms, "expert", split_axis=0, concat_axis=0, tiled=True),
    )
    a_total = rounded(group_total(a_back, experts, group_size))
    input_total = rounded(group_total(back_input, experts, group_size))
    term_total = rounded(group_total(back_terms, experts, group_size))
    a_tok = a_total[a_index].reshape(tokens, top_count, model_width)
    a_out = (a_float + jnp.sum(a_gate[:, :, None] * a_tok, axis=1)).astype(jnp.bfloat16)
    input_tok = jnp.sum(input_total[b_index].reshape(tokens, top_count, model_width), axis=1)
    score_grad = term_total[b_index].reshape(tokens, top_count) * (1.0 - b_gate)
    onehot_b = (b_ids[:, :, None] == jnp.arange(experts, dtype=jnp.int32)).astype(jnp.float32)
    full_grad = jnp.sum(onehot_b * score_grad[:, :, None], axis=1)
    normed_grad = input_tok + jnp.dot(
        full_grad, router_other.astype(jnp.float32).T, precision=lax.Precision.HIGHEST
    )
    cubed = b_scale * b_scale * b_scale
    feature_grad = (
        b_scale * normed_grad
        - b_float * cubed * jnp.sum(normed_grad * b_float, axis=-1, keepdims=True) / model_width
    )
    b_out = (b_cot.astype(jnp.float32) + feature_grad).astype(jnp.bfloat16)
    for bit_number in range(bit_count):
        b_out = partner(b_out, "pipe", bit_number)
    a_next, b_next = from_behind((a_out, b_out), "pipe", 1)
    return (a_next[None], b_next[None], up_grad[None], down_grad[None])


def solution(mesh):
    return jax.shard_map(
        body,
        mesh=mesh,
        in_specs=(
            P("pipe", "expert", None),
            P("pipe", "expert", None),
            P("pipe", "expert", None),
            P("pipe", "expert", None),
            P("pipe", "expert", None),
            P("pipe", None, "expert"),
            P("pipe", "expert", None),
            P("pipe", None, None),
        ),
        out_specs=(
            P("pipe", "expert", None),
            P("pipe", "expert", None),
            P("pipe", None, "expert"),
            P("pipe", "expert", None),
        ),
        check_vma=False,
    )
```

profile of v0, /device:TPU:15, one launch (start us, length us, event | category | flops | bytes accessed | tf_op | source)
XLA Modules:
  0.0 610.3 jit_solution(17211328158430504446)
XLA Ops:
  4.7 3.6 scatter_custom_fusion
  12.2 6.7 %all-to-all-start = ((bf16[16,34,3584]{2,1,0:T(8,128)(2,1)}), bf16[16,34,3584]{2,1,0:T(8,128)(2,1)}, u32[]{:S(2)}, u32[]{:S(2)}) async-start(bf16[16,34,3584]{2,1,0:T(8,128)(2,1)} %bitcast.134), calls=%async_computation | async-start | bytes 9175040 | tf_op jit(solution)/shard_map/all_to_all | solution.py:130
  28.2 94.1 %all-to-all-done = bf16[16,34,3584]{2,1,0:T(8,128)(2,1)} async-done(((bf16[16,34,3584]{2,1,0:T(8,128)(2,1)}), bf16[16,34,3584]{2,1,0:T(8,128)(2,1)}, u32[]{:S(2)}, u32[]{:S(2)}) %all-to-all-start) | async-done | bytes 3899424 | tf_op jit(solution)/shard_map/all_to_all | solution.py:130
  122.2 3.8 broadcast_in_dim.20
  126.0 4.7 all-to-all-start.3
  135.1 3.6 scatter_custom_fusion.1
  141.2 91.5 %all-to-all-done.3 = bf16[16,34,3584]{2,1,0:T(8,128)(2,1)} async-done(((bf16[16,34,3584]{2,1,0:T(8,128)(2,1)}), bf16[16,34,3584]{2,1,0:T(8,128)(2,1)}, u32[]{:S(2)}, u32[]{:S(2)}) %all-to-all-start.3) | async-done | bytes 3899424 | tf_op jit(solution)/shard_map/all_to_all | solution.py:134
  232.6 3.7 broadcast_in_dim.19
  236.4 4.6 all-to-all-start.2
  241.0 5.2 reshape.272
  246.2 5.2 reshape.279
  251.4 4.1 fusion.22
  255.5 87.4 %all-to-all-done.2 = bf16[16,34,3584]{2,1,0:T(8,128)(2,1)} async-done(((bf16[16,34,3584]{2,1,0:T(8,128)(2,1)}), bf16[16,34,3584]{2,1,0:T(8,128)(2,1)}, u32[]{:S(2)}, u32[]{:S(2)}) %all-to-all-start.2) | async-done | bytes 3899424 | tf_op jit(solution)/shard_map/all_to_all | solution.py:135
  342.8 5.2 reshape.276
  348.1 4.2 multiply_reduce_fusion
  352.9 4.6 all-to-all-start.5
  357.5 8.7 %convolution_convert_fusion.2 = bf16[544,3584]{1,0:T(8,128)(2,1)} fusion(bf16[1,256,3584]{2,1,0:T(8,128)(2,1)} %param.16, bf16[544,3584]{1,0:T(8,128)(2,1)} %reshape.272, bf16[1,3584,256]{2,1,0:T(8,128)(2,1)S(1)} %copy-done), kind=kOutput, calls=%fused_computation.11 | convolution fusion | flops 1999134720 | bytes 11468800 | tf_op jit(solution)/shard_map/dot_general | solution.py:56
  366.2 5.2 reshape.273
  371.4 6.4 %all-to-all-start.1 = ((bf16[16,34,3584]{2,1,0:T(8,128)(2,1)}), bf16[16,34,3584]{2,1,0:T(8,128)(2,1)}, u32[]{:S(2)}, u32[]{:S(2)}) async-start(bf16[16,34,3584]{2,1,0:T(8,128)(2,1)} %reshape.273), calls=%async_computation.1 | async-start | bytes 9175040 | tf_op jit(solution)/shard_map/all_to_all | solution.py:132
  377.7 3.9 fusion.32
  384.8 5.2 reshape.280
  390.0 89.3 %all-to-all-done.1 = bf16[16,34,3584]{2,1,0:T(8,128)(2,1)} async-done(((bf16[16,34,3584]{2,1,0:T(8,128)(2,1)}), bf16[16,34,3584]{2,1,0:T(8,128)(2,1)}, u32[]{:S(2)}, u32[]{:S(2)}) %all-to-all-start.1) | async-done | bytes 3899424 | tf_op jit(solution)/shard_map/all_to_all | solution.py:132
  479.3 4.7 all-to-all-start.4
  495.9 89.9 %all-to-all-done.4 = bf16[16,34,3584]{2,1,0:T(8,128)(2,1)} async-done(((bf16[16,34,3584]{2,1,0:T(8,128)(2,1)}), bf16[16,34,3584]{2,1,0:T(8,128)(2,1)}, u32[]{:S(2)}, u32[]{:S(2)}) %all-to-all-start.4) | async-done | bytes 3899424 | tf_op jit(solution)/shard_map/all_to_all | solution.py:139
  (90 shorter events, 64.1 us)
Async XLA Ops:
  0.6 250.7 %copy-start = (bf16[1,3584,256]{2,1,0:T(8,128)(2,1)S(1)}, bf16[1,3584,256]{2,1,0:T(8,128)(2,1)}, u32[]{:S(2)}) copy-start(bf16[1,3584,256]{2,1,0:T(8,128)(2,1)} %param.15) | copy-start | bytes 5505028
  12.1 8.0 %copy-start.9 = (s32[1,128,1]{1,2,0:T(1,128)S(1)}, s32[1,128,1]{1,2,0:T(1,128)}, u32[]{:S(2)}) copy-start(s32[1,128,1]{1,2,0:T(1,128)} %param.14) | copy-start | bytes 1540
  12.2 110.1 %all-to-all-start = ((bf16[16,34,3584]{2,1,0:T(8,128)(2,1)}), bf16[16,34,3584]{2,1,0:T(8,128)(2,1)}, u32[]{:S(2)}, u32[]{:S(2)}) async-start(bf16[16,34,3584]{2,1,0:T(8,128)(2,1)} %bitcast.134), calls=%async_computation | async-start | bytes 9175040 | tf_op jit(solution)/shard_map/all_to_all | solution.py:130
  18.9 3.6 collective-permute-start.2
  20.1 1.9 collective-permute-start.3
  126.0 6.7 %copy-start.7 = (bf16[1,3584,4]{1,2,0:T(4,128)(2,1)S(1)}, bf16[1,3584,4]{1,2,0:T(4,128)(2,1)}, u32[]{:S(2)}) copy-start(bf16[1,3584,4]{1,2,0:T(4,128)(2,1)} %param.17) | copy-start | bytes 86020
  126.0 106.6 %all-to-all-start.3 = ((bf16[16,34,3584]{2,1,0:T(8,128)(2,1)}), bf16[16,34,3584]{2,1,0:T(8,128)(2,1)}, u32[]{:S(2)}, u32[]{:S(2)}) async-start(bf16[16,34,3584]{2,1,0:T(8,128)(2,1)} %bitcast.135), calls=%async_computation.3 | async-start | bytes 9175040 | tf_op jit(solution)/shard_map/all_to_all | solution.py:134
  130.7 4.5 collective-permute-start.1
  236.4 106.5 %all-to-all-start.2 = ((bf16[16,34,3584]{2,1,0:T(8,128)(2,1)}), bf16[16,34,3584]{2,1,0:T(8,128)(2,1)}, u32[]{:S(2)}, u32[]{:S(2)}) async-start(bf16[16,34,3584]{2,1,0:T(8,128)(2,1)} %bitcast.136), calls=%async_computation.2 | async-start | bytes 9175040 | tf_op jit(solution)/shard_map/all_to_all | solution.py:135
  352.9 18.4 %all-to-all-start.5 = ((bf16[16,1,34]{2,1,0:T(2,128)(2,1)}), bf16[16,1,34]{2,1,0:T(2,128)(2,1)S(1)}, u32[]{:S(2)}, u32[]{:S(2)}) async-start(bf16[16,1,34]{2,1,0:T(2,128)(2,1)} %convert_element_type.199), calls=%async_computation.5 | async-start | bytes 16384 | tf_op jit(solution)/shard_map/all_to_all | solution.py:140
  371.4 107.9 %all-to-all-start.1 = ((bf16[16,34,3584]{2,1,0:T(8,128)(2,1)}), bf16[16,34,3584]{2,1,0:T(8,128)(2,1)}, u32[]{:S(2)}, u32[]{:S(2)}) async-start(bf16[16,34,3584]{2,1,0:T(8,128)(2,1)} %reshape.273), calls=%async_computation.1 | async-start | bytes 9175040 | tf_op jit(solution)/shard_map/all_to_all | solution.py:132
  390.0 94.0 %copy-start.2 = (bf16[1,128,3584]{2,1,0:T(8,128)(2,1)S(1)}, bf16[1,128,3584]{2,1,0:T(8,128)(2,1)}, u32[]{:S(2)}) copy-start(bf16[1,128,3584]{2,1,0:T(8,128)(2,1)} %param.10) | copy-start | bytes 2752516
  390.0 96.0 %copy-start.8 = (s32[1,128,1]{1,2,0:T(1,128)S(1)}, s32[1,128,1]{1,2,0:T(1,128)}, u32[]{:S(2)}) copy-start(s32[1,128,1]{1,2,0:T(1,128)} %param.11) | copy-start | bytes 1540
  479.3 106.5 %all-to-all-start.4 = ((bf16[16,34,3584]{2,1,0:T(8,128)(2,1)}), bf16[16,34,3584]{2,1,0:T(8,128)(2,1)}, u32[]{:S(2)}, u32[]{:S(2)}) async-start(bf16[16,34,3584]{2,1,0:T(8,128)(2,1)} %reshape.280), calls=%async_computation.4 | async-start | bytes 9175040 | tf_op jit(solution)/shard_map/all_to_all | solution.py:139
  596.5 3.6 copy-start.3
  596.6 3.6 copy-start.4
  596.6 6.0 copy-start.6
  598.6 4.0 copy-start.10
  598.6 3.6 collective-permute-start.4
  600.4 5.1 copy-start.5
  600.4 7.9 %collective-permute-start = (bf16[128,3584]{1,0:T(8,128)(2,1)S(1)}, bf16[128,3584]{1,0:T(8,128)(2,1)S(1)}, u32[]{:S(2)}, u32[]{:S(2)}) collective-permute-start(bf16[128,3584]{1,0:T(8,128)(2,1)S(1)} %fusion.9), channel_id=1, source_target_pairs={{0,16},{16,0},{1,17},{17,1},{2,18},{18,2},{3,19},{19,3},{4,20},{20... | collective-permute-start | bytes 2752520 | tf_op jit(solution)/shard_map/ppermute | solution.py:21
  602.2 6.2 %collective-permute-start.5 = (bf16[128,3584]{1,0:T(8,128)(2,1)S(1)}, bf16[128,3584]{1,0:T(8,128)(2,1)S(1)}, u32[]{:S(2)}, u32[]{:S(2)}) collective-permute-start(bf16[128,3584]{1,0:T(8,128)(2,1)S(1)} %collective-permute-done.4), channel_id=1, source_target_pairs={{0,16},{16,0},{1,17},{17,1},{2,18},{18,2},{3,19},{19,3},{4,20},{20... | collective-permute-start | bytes 2752520 | tf_op jit(solution)/shard_map/ppermute | solution.py:21
  608.4 1.9 copy-start.1
where the time goes:
time: 612 us; the launch traced here: 610 us
  waiting for transfers between devices  456 us (75%)
  local copies, waits for them, and re-layouts  56.6 us (9%)
  starting transfers between devices  37 us (6%)
  matrix products  33.2 us (5%)
  other arithmetic  26.5 us (4%)
    all_to_all x1, waiting for transfers between devices, body(): lax.all_to_all(a_send, 'expert', split_axis=0, concat_axis=0, tiled=True)  94.1 us
    all_to_all x1, waiting for transfers between devices, body(): lax.all_to_all(b_send, 'expert', split_axis=0, concat_axis=0, tiled=True)  91.5 us
    all_to_all x1, waiting for transfers between devices, body(): lax.all_to_all(input_part, 'expert', split_axis=0, concat_axis=0, tiled=T...  89.9 us
    all_to_all x1, waiting for transfers between devices, body(): lax.all_to_all(a_part, 'expert', split_axis=0, concat_axis=0, tiled=True)  89.3 us
    all_to_all x1, waiting for transfers between devices, body(): lax.all_to_all(cot_send, 'expert', split_axis=0, concat_axis=0, tiled=True)  87.4 us
    dot_general x2, matrix products, expert_rows(): jnp.dot(activated, down_slice, preferred_element_type=jnp.float32)  12.9 us
  transfers between devices with their start and end apart: 12, of which 8 were waited for; matrix products, arithmetic and copies ran while one was open for 12% of the time, Pallas kernels for 0%

commit v1 on v0

v1 whole, which is shorter than its diff:
```python
import jax
import jax.numpy as jnp
from jax import lax
from jax.sharding import PartitionSpec as P

EPS = 1e-06
F32 = jnp.float32
BF16 = jnp.bfloat16


def dot(a, b, dims=((1,), (0,))):
    return lax.dot_general(a, b, (dims, ((), ())), preferred_element_type=F32)


def pipe_move(array, target):
    count = lax.axis_size("pipe")
    pairs = [(i, target(i, count) % count) for i in range(count)]
    if all(a == b for a, b in pairs):
        return array
    return lax.ppermute(array, "pipe", pairs)


def plane_move(array, experts, bit):
    devices = lax.axis_size("expert")
    return lax.ppermute(array, "expert", [(i, i ^ bit) for i in range(devices)])


def depth_move(array, experts, k):
    devices = lax.axis_size("expert")
    group = devices // experts
    pairs = [(i, ((i // group) ^ k) * group + i % group) for i in range(devices)]
    return lax.ppermute(array, "expert", pairs)


class Layout:
    def __init__(self, experts, capacity):
        self.experts = experts
        self.main = capacity // 8 * 8
        self.rest = capacity - self.main
        self.tail = -(-experts * self.rest // 8) * 8
        self.rows = self.main + self.tail
        self.packed = experts * self.main + self.tail


def selectors(ids, layout, here):
    tokens = ids.shape[0]
    onehot = (ids[:, None] == jnp.arange(layout.experts, dtype=jnp.int32)).astype(jnp.int32)
    slot = jnp.sum(onehot * (jnp.cumsum(onehot, axis=0) - 1), axis=1)
    row = jnp.arange(layout.rows, dtype=jnp.int32)[:, None]
    picks = []
    for k in range(layout.experts):
        place = jnp.where(slot < layout.main, slot, slot + k * layout.rest)
        picks.append(((ids[None, :] == (here ^ k)) & (place[None, :] == row)).astype(BF16))
    return picks


def statistics(features):
    feat = features.astype(F32)
    scale = lax.rsqrt(jnp.mean(feat * feat, axis=-1, keepdims=True) + EPS)
    return feat, scale, (feat * scale).astype(BF16)


def gate_of(normed, ids, router):
    scores = dot(normed, router)
    onehot = ids[:, None] == jnp.arange(router.shape[1], dtype=jnp.int32)
    return jax.nn.sigmoid(jnp.sum(jnp.where(onehot, scores, 0.0), axis=1, keepdims=True))


def to_planes(rows, picks, layout):
    blocks = []
    for k, pick in enumerate(picks):
        block = dot(pick, rows).astype(BF16)
        blocks.append(depth_move(block, layout.experts, k) if k else block)
    return blocks


def pack(blocks, layout, cols):
    tail = blocks[0][layout.main :, cols]
    for block in blocks[1:]:
        tail = tail + block[layout.main :, cols]
    return jnp.concatenate([b[: layout.main, cols] for b in blocks] + [tail], axis=0)


def spread(blocks, layout, halves):
    e = layout.experts
    lo, hi = [pack(blocks, layout, cols) for cols in halves]
    x_lo, y_hi = plane_move(lo, e, 1), plane_move(hi, e, 2)
    x_hi, y_lo = plane_move(hi, e, 1), plane_move(lo, e, 2)
    d_lo, d_hi = plane_move(x_lo, e, 2), plane_move(y_hi, e, 1)
    return [(lo, hi), (x_lo, x_hi), (y_lo, y_hi), (d_lo, d_hi)]


def gather_back(part, layout):
    e = layout.experts
    s_lo = plane_move(part(3, 0).astype(BF16), e, 1)
    s_hi = plane_move(part(3, 1).astype(BF16), e, 2)
    x_lo = plane_move(part(1, 0).astype(BF16), e, 1)
    y_hi = plane_move(part(2, 1).astype(BF16), e, 2)
    x_hi = plane_move((part(1, 1) + s_hi.astype(F32)).astype(BF16), e, 1)
    y_lo = plane_move((part(2, 0) + s_lo.astype(F32)).astype(BF16), e, 2)
    lo = (part(0, 0) + x_lo.astype(F32) + y_lo.astype(F32)).astype(BF16)
    hi = (part(0, 1) + x_hi.astype(F32) + y_hi.astype(F32)).astype(BF16)
    return lo, hi


def to_tokens(total, picks, layout):
    lo, hi = total
    token_rows = 0.0
    for k, pick in enumerate(picks):
        rows = slice(k * layout.main, (k + 1) * layout.main)
        tail = slice(layout.experts * layout.main, layout.packed)
        block = jnp.concatenate(
            [
                jnp.concatenate([lo[rows], hi[rows]], axis=1),
                jnp.concatenate([lo[tail], hi[tail]], axis=1),
            ],
            axis=0,
        )
        if k:
            block = depth_move(block, layout.experts, k)
        token_rows = token_rows + dot(pick, block, ((0,), (0,)))
    return token_rows


def body(a_input, a_route, b_saved, b_grad, b_route, up_weight, down_weight, router):
    devices = lax.axis_size("expert")
    experts = router.shape[2]
    group = devices // experts
    tokens, width = a_input.shape[1], a_input.shape[2]
    layout = Layout(experts, tokens * a_route.shape[2] // experts + 2)
    here = lax.axis_index("expert") // group
    up, down, cols_r = up_weight[0], down_weight[0], router[0]
    half = width // 2
    halves = (slice(0, half), slice(half, width))

    b_ids = pipe_move(b_route[0].astype(BF16), lambda i, n: n - 1 - i).astype(jnp.int32)[:, 0]
    b_x = pipe_move(b_saved[0], lambda i, n: n - 1 - i)
    b_c = pipe_move(b_grad[0], lambda i, n: n - 1 - i)
    a_ids = a_route[0][:, 0]

    a_float, _, a_normed = statistics(a_input[0])
    a_picks = selectors(a_ids, layout, here)
    a_rows = spread(to_planes(a_normed, a_picks, layout), layout, halves)
    a_gate = gate_of(a_normed, a_ids, cols_r)

    b_float, b_scale, b_normed = statistics(b_x)
    b_picks = selectors(b_ids, layout, here)
    b_rows = spread(to_planes(b_normed, b_picks, layout), layout, halves)
    b_gate = gate_of(b_normed, b_ids, cols_r)
    cot = (b_gate * b_c.astype(F32)).astype(BF16)
    c_rows = spread(to_planes(cot, b_picks, layout), layout, halves)

    own_col = jnp.sum(
        jnp.where(jnp.arange(experts) == here, cols_r.astype(F32), 0.0), axis=1, keepdims=True
    ).astype(BF16)

    a_act = []
    for lo, hi in a_rows:
        hidden = dot(lo, up[:half]) + dot(hi, up[half:])
        a_act.append((hidden * jax.nn.sigmoid(hidden)).astype(BF16))
    a_total = gather_back(lambda j, h: dot(a_act[j], down[:, halves[h]]), layout)
    a_out = (a_float + a_gate * to_tokens(a_total, a_picks, layout)).astype(BF16)
    a_next = pipe_move(a_out, lambda i, n: i + 1)

    act, hid_grad, score_grad = [], [], []
    for (lo, hi), (c_lo, c_hi) in zip(b_rows, c_rows):
        hidden = dot(lo, up[:half]) + dot(hi, up[half:])
        score = dot(lo, own_col[:half]) + dot(hi, own_col[half:])
        sigma = jax.nn.sigmoid(hidden)
        active = hidden * sigma
        act_grad = dot(c_lo, down[:, :half], ((1,), (1,))) + dot(c_hi, down[:, half:], ((1,), (1,)))
        act.append(active.astype(BF16))
        hid_grad.append((act_grad * sigma * (1.0 + hidden * (1.0 - sigma))).astype(BF16))
        term = jnp.sum(active * act_grad, axis=1, keepdims=True)
        score_grad.append(term * jax.nn.sigmoid(-score))
    col_row = own_col.astype(F32).reshape(1, width)

    def input_part(j, h):
        return dot(hid_grad[j], up[halves[h]], ((1,), (1,))) + score_grad[j] * col_row[:, halves[h]]

    b_total = gather_back(input_part, layout)
    normed_grad = to_tokens(b_total, b_picks, layout)
    along = jnp.sum(normed_grad * b_float, axis=-1, keepdims=True) / width
    feature_grad = b_scale * normed_grad - b_float * (b_scale * b_scale * b_scale) * along
    b_out = (b_c.astype(F32) + feature_grad).astype(BF16)
    b_next = pipe_move(b_out, lambda i, n: n - i)

    acts, hids = jnp.concatenate(act, axis=0), jnp.concatenate(hid_grad, axis=0)
    down_parts, up_parts = [], []
    for h in range(2):
        b_all = jnp.concatenate([r[h] for r in b_rows], axis=0)
        c_all = jnp.concatenate([r[h] for r in c_rows], axis=0)
        up_parts.append(dot(b_all, hids, ((0,), (0,))).astype(BF16))
        down_parts.append(dot(acts, c_all, ((0,), (0,))).astype(BF16))
    up_grad = jnp.concatenate(up_parts, axis=0)
    down_grad = jnp.concatenate(down_parts, axis=1)
    return (a_next[None], b_next[None], up_grad[None], down_grad[None])


def solution(mesh):
    return jax.shard_map(
        body,
        mesh=mesh,
        in_specs=(
            P("pipe", "expert", None),
            P("pipe", "expert", None),
            P("pipe", "expert", None),
            P("pipe", "expert", None),
            P("pipe", "expert", None),
            P("pipe", None, "expert"),
            P("pipe", "expert", None),
            P("pipe", None, None),
        ),
        out_specs=(
            P("pipe", "expert", None),
            P("pipe", "expert", None),
            P("pipe", None, "expert"),
            P("pipe", "expert", None),
        ),
        check_vma=False,
    )
```

time: 612 us -> 341 us (0.56)
  the two profiles are of different devices: /device:TPU:15 before, /device:TPU:0 now
where the time goes in v1:
time: 341 us
  waiting for transfers between devices  212 us (62%)
  starting transfers between devices  71.1 us (21%)
  matrix products  35.2 us (10%)
  other arithmetic  13 us (4%)
  local copies, waits for them, and re-layouts  8.29 us (2%)
    ppermute x30, waiting for transfers between devices, plane_move(): return lax.ppermute(array, 'expert', [(i, i ^ bit) for i in range(devices)])  116 us
    ppermute x15, waiting for transfers between devices, depth_move(): return lax.ppermute(array, 'expert', pairs)  96 us
    ppermute x15, starting transfers between devices, depth_move(): return lax.ppermute(array, 'expert', pairs)  36.4 us
    dot_general x74, matrix products, dot(): return lax.dot_general(a, b, (dims, ((), ())), preferred_element_type=F32)  35.2 us
    ppermute x30, starting transfers between devices, plane_move(): return lax.ppermute(array, 'expert', [(i, i ^ bit) for i in range(devices)])  33.7 us
    unnamed x37, local copies, waits for them, and re-layouts  7.56 us
  transfers between devices with their start and end apart: 49, of which 29 were waited for; matrix products, arithmetic and copies ran while one was open for 15% of the time, Pallas kernels for 0%

profile of v1, /device:TPU:0, one launch (start us, length us, event | category | flops | bytes accessed | tf_op | source)
XLA Modules:
  0.0 340.8 jit_solution(11607287582359683158)
XLA Ops:
  19.1 5.3 %collective-permute-done = bf16[40,3584]{1,0:T(8,128)(2,1)} collective-permute-done((bf16[40,3584]{1,0:T(8,128)(2,1)}, bf16[40,3584]{1,0:T(8,128)(2,1)}, u32[]{:S(2)}, u32[]{:S(2)}) %collective-permute-start) | collective-permute-done | bytes 286752 | tf_op jit(solution)/shard_map/ppermute | solution.py:32
  26.1 8.3 %collective-permute-done.1 = bf16[40,3584]{1,0:T(8,128)(2,1)} collective-permute-done((bf16[40,3584]{1,0:T(8,128)(2,1)S(1)}, bf16[40,3584]{1,0:T(8,128)(2,1)}, u32[]{:S(2)}, u32[]{:S(2)}) %collective-permute-start.1) | collective-permute-done | bytes 286752 | tf_op jit(solution)/shard_map/ppermute | solution.py:32
  46.5 8.6 %collective-permute-done.4 = bf16[136,1792]{1,0:T(8,128)(2,1)S(1)} collective-permute-done((bf16[136,1792]{1,0:T(8,128)(2,1)}, bf16[136,1792]{1,0:T(8,128)(2,1)S(1)}, u32[]{:S(2)}, u32[]{:S(2)}) %collective-permute-start.4) | collective-permute-done | bytes 487456 | tf_op jit(solution)/shard_map/ppermute | solution.py:25
  55.9 6.1 %collective-permute-done.3 = bf16[136,1792]{1,0:T(8,128)(2,1)S(1)} collective-permute-done((bf16[136,1792]{1,0:T(8,128)(2,1)}, bf16[136,1792]{1,0:T(8,128)(2,1)S(1)}, u32[]{:S(2)}, u32[]{:S(2)}) %collective-permute-start.3) | collective-permute-done | bytes 487456 | tf_op jit(solution)/shard_map/ppermute | solution.py:25
  84.2 13.4 %collective-permute-done.23 = bf16[40,3584]{1,0:T(8,128)(2,1)S(1)} collective-permute-done((bf16[40,3584]{1,0:T(8,128)(2,1)S(1)}, bf16[40,3584]{1,0:T(8,128)(2,1)S(1)}, u32[]{:S(2)}, u32[]{:S(2)}) %collective-permute-start.23) | collective-permute-done | bytes 286752 | tf_op jit(solution)/shard_map/ppermute | solution.py:32
  99.7 8.5 %collective-permute-done.24 = bf16[40,3584]{1,0:T(8,128)(2,1)S(1)} collective-permute-done((bf16[40,3584]{1,0:T(8,128)(2,1)S(1)}, bf16[40,3584]{1,0:T(8,128)(2,1)S(1)}, u32[]{:S(2)}, u32[]{:S(2)}) %collective-permute-start.24) | collective-permute-done | bytes 286752 | tf_op jit(solution)/shard_map/ppermute | solution.py:32
  108.3 9.2 %collective-permute-done.25 = bf16[40,3584]{1,0:T(8,128)(2,1)S(1)} collective-permute-done((bf16[40,3584]{1,0:T(8,128)(2,1)S(1)}, bf16[40,3584]{1,0:T(8,128)(2,1)S(1)}, u32[]{:S(2)}, u32[]{:S(2)}) %collective-permute-start.25) | collective-permute-done | bytes 286752 | tf_op jit(solution)/shard_map/ppermute | solution.py:32
  117.5 11.3 %collective-permute-done.26 = bf16[40,3584]{1,0:T(8,128)(2,1)S(1)} collective-permute-done((bf16[40,3584]{1,0:T(8,128)(2,1)S(1)}, bf16[40,3584]{1,0:T(8,128)(2,1)S(1)}, u32[]{:S(2)}, u32[]{:S(2)}) %collective-permute-start.26) | collective-permute-done | bytes 286752 | tf_op jit(solution)/shard_map/ppermute | solution.py:32
  131.6 5.8 %collective-permute-done.27 = bf16[40,3584]{1,0:T(8,128)(2,1)S(1)} collective-permute-done((bf16[40,3584]{1,0:T(8,128)(2,1)S(1)}, bf16[40,3584]{1,0:T(8,128)(2,1)S(1)}, u32[]{:S(2)}, u32[]{:S(2)}) %collective-permute-start.27) | collective-permute-done | bytes 286752 | tf_op jit(solution)/shard_map/ppermute | solution.py:32
  145.8 16.4 %collective-permute-done.31 = bf16[136,1792]{1,0:T(8,128)(2,1)S(1)} collective-permute-done((bf16[136,1792]{1,0:T(8,128)(2,1)S(1)}, bf16[136,1792]{1,0:T(8,128)(2,1)S(1)}, u32[]{:S(2)}, u32[]{:S(2)}) %collective-permute-start.31) | collective-permute-done | bytes 487456 | tf_op jit(solution)/shard_map/ppermute | solution.py:25
  164.2 6.8 %collective-permute-done.29 = bf16[136,1792]{1,0:T(8,128)(2,1)S(1)} collective-permute-done((bf16[136,1792]{1,0:T(8,128)(2,1)S(1)}, bf16[136,1792]{1,0:T(8,128)(2,1)S(1)}, u32[]{:S(2)}, u32[]{:S(2)}) %collective-permute-start.29) | collective-permute-done | bytes 487456 | tf_op jit(solution)/shard_map/ppermute | solution.py:25
  175.3 17.4 %collective-permute-done.36 = bf16[136,1792]{1,0:T(8,128)(2,1)S(1)} collective-permute-done((bf16[136,1792]{1,0:T(8,128)(2,1)S(1)}, bf16[136,1792]{1,0:T(8,128)(2,1)S(1)}, u32[]{:S(2)}, u32[]{:S(2)}) %collective-permute-start.36) | collective-permute-done | bytes 487456 | tf_op jit(solution)/shard_map/ppermute | solution.py:25
  194.2 6.2 %collective-permute-done.34 = bf16[136,1792]{1,0:T(8,128)(2,1)S(1)} collective-permute-done((bf16[136,1792]{1,0:T(8,128)(2,1)S(1)}, bf16[136,1792]{1,0:T(8,128)(2,1)S(1)}, u32[]{:S(2)}, u32[]{:S(2)}) %collective-permute-start.34) | collective-permute-done | bytes 487456 | tf_op jit(solution)/shard_map/ppermute | solution.py:25
  202.3 8.5 %collective-permute-done.35 = bf16[136,1792]{1,0:T(8,128)(2,1)S(1)} collective-permute-done((bf16[136,1792]{1,0:T(8,128)(2,1)S(1)}, bf16[136,1792]{1,0:T(8,128)(2,1)S(1)}, u32[]{:S(2)}, u32[]{:S(2)}) %collective-permute-start.35) | collective-permute-done | bytes 487456 | tf_op jit(solution)/shard_map/ppermute | solution.py:25
  215.5 9.4 %collective-permute-done.12 = bf16[136,1792]{1,0:T(8,128)(2,1)S(1)} collective-permute-done((bf16[136,1792]{1,0:T(8,128)(2,1)S(1)}, bf16[136,1792]{1,0:T(8,128)(2,1)S(1)}, u32[]{:S(2)}, u32[]{:S(2)}) %collective-permute-start.12) | collective-permute-done | bytes 487456 | tf_op jit(solution)/shard_map/ppermute | solution.py:25
  227.6 6.9 %collective-permute-done.38 = bf16[136,1792]{1,0:T(8,128)(2,1)S(1)} collective-permute-done((bf16[136,1792]{1,0:T(8,128)(2,1)S(1)}, bf16[136,1792]{1,0:T(8,128)(2,1)S(1)}, u32[]{:S(2)}, u32[]{:S(2)}) %collective-permute-start.38) | collective-permute-done | bytes 487456 | tf_op jit(solution)/shard_map/ppermute | solution.py:25
  239.6 14.6 %collective-permute-done.37 = bf16[136,1792]{1,0:T(8,128)(2,1)S(1)} collective-permute-done((bf16[136,1792]{1,0:T(8,128)(2,1)S(1)}, bf16[136,1792]{1,0:T(8,128)(2,1)S(1)}, u32[]{:S(2)}, u32[]{:S(2)}) %collective-permute-start.37) | collective-permute-done | bytes 487456 | tf_op jit(solution)/shard_map/ppermute | solution.py:25
  266.1 5.0 %collective-permute-done.13 = bf16[136,1792]{1,0:T(8,128)(2,1)S(1)} collective-permute-done((bf16[136,1792]{1,0:T(8,128)(2,1)S(1)}, bf16[136,1792]{1,0:T(8,128)(2,1)S(1)}, u32[]{:S(2)}, u32[]{:S(2)}) %collective-permute-start.13) | collective-permute-done | bytes 487456 | tf_op jit(solution)/shard_map/ppermute | solution.py:25
  271.4 5.0 %collective-permute-start.15 = (bf16[40,3584]{1,0:T(8,128)(2,1)S(1)}, bf16[40,3584]{1,0:T(8,128)(2,1)S(1)}, u32[]{:S(2)}, u32[]{:S(2)}) collective-permute-start(bf16[40,3584]{1,0:T(8,128)(2,1)S(1)} %get-tuple-element.92), channel_id=1, source_target_pairs={{0,4},{1,5},{2,6},{3,7},{4,0},{5,1},{6,2},{7,3},{8,12},{9,13},{10,... | collective-permute-start | bytes 860168 | tf_op jit(solution)/shard_map/ppermute | solution.py:32
  282.4 4.4 %collective-permute-start.17 = (bf16[40,3584]{1,0:T(8,128)(2,1)S(1)}, bf16[40,3584]{1,0:T(8,128)(2,1)S(1)}, u32[]{:S(2)}, u32[]{:S(2)}) collective-permute-start(bf16[40,3584]{1,0:T(8,128)(2,1)S(1)} %get-tuple-element.93), channel_id=1, source_target_pairs={{0,12},{1,13},{2,14},{3,15},{4,8},{5,9},{6,10},{7,11},{8,4},{9,5},... | collective-permute-start | bytes 860168 | tf_op jit(solution)/shard_map/ppermute | solution.py:32
  296.5 5.3 %collective-permute-done.42 = bf16[136,1792]{1,0:T(8,128)(2,1)S(1)} collective-permute-done((bf16[136,1792]{1,0:T(8,128)(2,1)S(1)}, bf16[136,1792]{1,0:T(8,128)(2,1)S(1)}, u32[]{:S(2)}, u32[]{:S(2)}) %collective-permute-start.42) | collective-permute-done | bytes 487456 | tf_op jit(solution)/shard_map/ppermute | solution.py:25
  304.2 4.6 %collective-permute-start.46 = (bf16[40,3584]{1,0:T(8,128)(2,1)S(1)}, bf16[40,3584]{1,0:T(8,128)(2,1)S(1)}, u32[]{:S(2)}, u32[]{:S(2)}) collective-permute-start(bf16[40,3584]{1,0:T(8,128)(2,1)S(1)} %get-tuple-element.89), channel_id=1, source_target_pairs={{0,4},{1,5},{2,6},{3,7},{4,0},{5,1},{6,2},{7,3},{8,12},{9,13},{10,... | collective-permute-start | bytes 860168 | tf_op jit(solution)/shard_map/ppermute | solution.py:32
  313.9 11.0 %collective-permute-done.48 = bf16[40,3584]{1,0:T(8,128)(2,1)S(1)} collective-permute-done((bf16[40,3584]{1,0:T(8,128)(2,1)S(1)}, bf16[40,3584]{1,0:T(8,128)(2,1)S(1)}, u32[]{:S(2)}, u32[]{:S(2)}) %collective-permute-start.48) | collective-permute-done | bytes 286752 | tf_op jit(solution)/shard_map/ppermute | solution.py:32
  325.4 12.3 %collective-permute-done.47 = bf16[40,3584]{1,0:T(8,128)(2,1)S(1)} collective-permute-done((bf16[40,3584]{1,0:T(8,128)(2,1)S(1)}, bf16[40,3584]{1,0:T(8,128)(2,1)S(1)}, u32[]{:S(2)}, u32[]{:S(2)}) %collective-permute-start.47) | collective-permute-done | bytes 286752 | tf_op jit(solution)/shard_map/ppermute | solution.py:32
  (247 shorter events, 128.8 us)
Async XLA Ops:
  1.8 66.9 %collective-permute-start.20 = (bf16[128,3584]{1,0:T(8,128)(2,1)}, bf16[128,3584]{1,0:T(8,128)(2,1)S(1)}, u32[]{:S(2)}, u32[]{:S(2)}) collective-permute-start(bf16[128,3584]{1,0:T(8,128)(2,1)} %bitcast.213), channel_id=1, source_target_pairs={{0,16},{16,0},{1,17},{17,1},{2,18},{18,2},{3,19},{19,3},{4,20},{20... | collective-permute-start | bytes 2752520 | tf_op jit(solution)/shard_map/ppermute | solution.py:20
  1.9 69.1 %collective-permute-start.19 = (bf16[128,3584]{1,0:T(8,128)(2,1)}, bf16[128,3584]{1,0:T(8,128)(2,1)S(1)}, u32[]{:S(2)}, u32[]{:S(2)}) collective-permute-start(bf16[128,3584]{1,0:T(8,128)(2,1)} %bitcast.214), channel_id=1, source_target_pairs={{0,16},{16,0},{1,17},{17,1},{2,18},{18,2},{3,19},{19,3},{4,20},{20... | collective-permute-start | bytes 2752520 | tf_op jit(solution)/shard_map/ppermute | solution.py:20
  11.4 23.1 %collective-permute-start.1 = (bf16[40,3584]{1,0:T(8,128)(2,1)S(1)}, bf16[40,3584]{1,0:T(8,128)(2,1)}, u32[]{:S(2)}, u32[]{:S(2)}) collective-permute-start(bf16[40,3584]{1,0:T(8,128)(2,1)S(1)} %convolution_convert_fusion.9), channel_id=1, source_target_pairs={{0,8},{1,9},{2,10},{3,11},{4,12},{5,13},{6,14},{7,15},{8,0},{9,1},... | collective-permute-start | bytes 860168 | tf_op jit(solution)/shard_map/ppermute | solution.py:32
  17.4 18.7 %collective-permute-start.2 = (bf16[40,3584]{1,0:T(8,128)(2,1)}, bf16[40,3584]{1,0:T(8,128)(2,1)}, u32[]{:S(2)}, u32[]{:S(2)}) collective-permute-start(bf16[40,3584]{1,0:T(8,128)(2,1)} %convolution_convert_fusion.8), channel_id=1, source_target_pairs={{0,12},{1,13},{2,14},{3,15},{4,8},{5,9},{6,10},{7,11},{8,4},{9,5},... | collective-permute-start | bytes 860168 | tf_op jit(solution)/shard_map/ppermute | solution.py:32
  39.2 25.0 %collective-permute-start.7 = (bf16[136,1792]{1,0:T(8,128)(2,1)}, bf16[136,1792]{1,0:T(8,128)(2,1)S(1)}, u32[]{:S(2)}, u32[]{:S(2)}) collective-permute-start(bf16[136,1792]{1,0:T(8,128)(2,1)} %get-tuple-element.19), channel_id=1, source_target_pairs={{0,2},{1,3},{2,0},{3,1},{4,6},{5,7},{6,4},{7,5},{8,10},{9,11},{10,... | collective-permute-start | bytes 1462280 | tf_op jit(solution)/shard_map/ppermute | solution.py:25
  42.2 19.7 %collective-permute-start.3 = (bf16[136,1792]{1,0:T(8,128)(2,1)}, bf16[136,1792]{1,0:T(8,128)(2,1)S(1)}, u32[]{:S(2)}, u32[]{:S(2)}) collective-permute-start(bf16[136,1792]{1,0:T(8,128)(2,1)} %get-tuple-element.18), channel_id=1, source_target_pairs={{0,1},{1,0},{2,3},{3,2},{4,5},{5,4},{6,7},{7,6},{8,9},{9,8},{10,11... | collective-permute-start | bytes 1462280 | tf_op jit(solution)/shard_map/ppermute | solution.py:25
  62.6 199.7 %collective-permute-start.5 = (bf16[136,1792]{1,0:T(8,128)(2,1)S(1)}, bf16[136,1792]{1,0:T(8,128)(2,1)S(1)}, u32[]{:S(2)}, u32[]{:S(2)}) collective-permute-start(bf16[136,1792]{1,0:T(8,128)(2,1)S(1)} %convolution_convert_fusion.19), channel_id=1, source_target_pairs={{0,1},{1,0},{2,3},{3,2},{4,5},{5,4},{6,7},{7,6},{8,9},{9,8},{10,11... | collective-permute-start | bytes 1462280 | tf_op jit(solution)/shard_map/ppermute | solution.py:25
  65.7 198.9 %collective-permute-start.14 = (bf16[136,1792]{1,0:T(8,128)(2,1)S(1)}, bf16[136,1792]{1,0:T(8,128)(2,1)S(1)}, u32[]{:S(2)}, u32[]{:S(2)}) collective-permute-start(bf16[136,1792]{1,0:T(8,128)(2,1)S(1)} %convolution_convert_fusion.16), channel_id=1, source_target_pairs={{0,2},{1,3},{2,0},{3,1},{4,6},{5,7},{6,4},{7,5},{8,10},{9,11},{10,... | collective-permute-start | bytes 1462280 | tf_op jit(solution)/shard_map/ppermute | solution.py:25
  66.3 75.8 %collective-permute-start.9 = (bf16[136,1792]{1,0:T(8,128)(2,1)S(1)}, bf16[136,1792]{1,0:T(8,128)(2,1)S(1)}, u32[]{:S(2)}, u32[]{:S(2)}) collective-permute-start(bf16[136,1792]{1,0:T(8,128)(2,1)S(1)} %collective-permute-done.7), channel_id=1, source_target_pairs={{0,1},{1,0},{2,3},{3,2},{4,5},{5,4},{6,7},{7,6},{8,9},{9,8},{10,11... | collective-permute-start | bytes 1462280 | tf_op jit(solution)/shard_map/ppermute | solution.py:25
  68.8 74.3 %collective-permute-start.8 = (bf16[136,1792]{1,0:T(8,128)(2,1)S(1)}, bf16[136,1792]{1,0:T(8,128)(2,1)S(1)}, u32[]{:S(2)}, u32[]{:S(2)}) collective-permute-start(bf16[136,1792]{1,0:T(8,128)(2,1)S(1)} %collective-permute-done.3), channel_id=1, source_target_pairs={{0,2},{1,3},{2,0},{3,1},{4,6},{5,7},{6,4},{7,5},{8,10},{9,11},{10,... | collective-permute-start | bytes 1462280 | tf_op jit(solution)/shard_map/ppermute | solution.py:25
  137.4 36.7 %collective-permute-start.28 = (bf16[136,1792]{1,0:T(8,128)(2,1)S(1)}, bf16[136,1792]{1,0:T(8,128)(2,1)S(1)}, u32[]{:S(2)}, u32[]{:S(2)}) collective-permute-start(bf16[136,1792]{1,0:T(8,128)(2,1)S(1)} %constant_dynamic-update-slice_fusion.10), channel_id=1, source_target_pairs={{0,1},{1,0},{2,3},{3,2},{4,5},{5,4},{6,7},{7,6},{8,9},{9,8},{10,11... | collective-permute-start | bytes 1462280 | tf_op jit(solution)/shard_map/ppermute | solution.py:25
  142.2 29.8 %collective-permute-start.30 = (bf16[136,1792]{1,0:T(8,128)(2,1)S(1)}, bf16[136,1792]{1,0:T(8,128)(2,1)S(1)}, u32[]{:S(2)}, u32[]{:S(2)}) collective-permute-start(bf16[136,1792]{1,0:T(8,128)(2,1)S(1)} %constant_dynamic-update-slice_fusion.20), channel_id=1, source_target_pairs={{0,1},{1,0},{2,3},{3,2},{4,5},{5,4},{6,7},{7,6},{8,9},{9,8},{10,11... | collective-permute-start | bytes 1462280 | tf_op jit(solution)/shard_map/ppermute | solution.py:25
  143.1 19.1 %collective-permute-start.31 = (bf16[136,1792]{1,0:T(8,128)(2,1)S(1)}, bf16[136,1792]{1,0:T(8,128)(2,1)S(1)}, u32[]{:S(2)}, u32[]{:S(2)}) collective-permute-start(bf16[136,1792]{1,0:T(8,128)(2,1)S(1)} %constant_dynamic-update-slice_fusion.25), channel_id=1, source_target_pairs={{0,1},{1,0},{2,3},{3,2},{4,5},{5,4},{6,7},{7,6},{8,9},{9,8},{10,11... | collective-permute-start | bytes 1462280 | tf_op jit(solution)/shard_map/ppermute | solution.py:25
  170.9 40.7 %collective-permute-start.33 = (bf16[136,1792]{1,0:T(8,128)(2,1)S(1)}, bf16[136,1792]{1,0:T(8,128)(2,1)S(1)}, u32[]{:S(2)}, u32[]{:S(2)}) collective-permute-start(bf16[136,1792]{1,0:T(8,128)(2,1)S(1)} %constant_dynamic-update-slice_fusion.10), channel_id=1, source_target_pairs={{0,2},{1,3},{2,0},{3,1},{4,6},{5,7},{6,4},{7,5},{8,10},{9,11},{10,... | collective-permute-start | bytes 1462280 | tf_op jit(solution)/shard_map/ppermute | solution.py:25
  171.9 20.8 %collective-permute-start.36 = (bf16[136,1792]{1,0:T(8,128)(2,1)S(1)}, bf16[136,1792]{1,0:T(8,128)(2,1)S(1)}, u32[]{:S(2)}, u32[]{:S(2)}) collective-permute-start(bf16[136,1792]{1,0:T(8,128)(2,1)S(1)} %constant_dynamic-update-slice_fusion.25), channel_id=1, source_target_pairs={{0,2},{1,3},{2,0},{3,1},{4,6},{5,7},{6,4},{7,5},{8,10},{9,11},{10,... | collective-permute-start | bytes 1462280 | tf_op jit(solution)/shard_map/ppermute | solution.py:25
  174.1 26.3 %collective-permute-start.34 = (bf16[136,1792]{1,0:T(8,128)(2,1)S(1)}, bf16[136,1792]{1,0:T(8,128)(2,1)S(1)}, u32[]{:S(2)}, u32[]{:S(2)}) collective-permute-start(bf16[136,1792]{1,0:T(8,128)(2,1)S(1)} %constant_dynamic-update-slice_fusion.15), channel_id=1, source_target_pairs={{0,2},{1,3},{2,0},{3,1},{4,6},{5,7},{6,4},{7,5},{8,10},{9,11},{10,... | collective-permute-start | bytes 1462280 | tf_op jit(solution)/shard_map/ppermute | solution.py:25
  192.7 18.1 %collective-permute-start.35 = (bf16[136,1792]{1,0:T(8,128)(2,1)S(1)}, bf16[136,1792]{1,0:T(8,128)(2,1)S(1)}, u32[]{:S(2)}, u32[]{:S(2)}) collective-permute-start(bf16[136,1792]{1,0:T(8,128)(2,1)S(1)} %constant_dynamic-update-slice_fusion.20), channel_id=1, source_target_pairs={{0,2},{1,3},{2,0},{3,1},{4,6},{5,7},{6,4},{7,5},{8,10},{9,11},{10,... | collective-permute-start | bytes 1462280 | tf_op jit(solution)/shard_map/ppermute | solution.py:25
  211.6 84.9 %collective-permute-start.32 = (bf16[136,1792]{1,0:T(8,128)(2,1)S(1)}, bf16[136,1792]{1,0:T(8,128)(2,1)S(1)}, u32[]{:S(2)}, u32[]{:S(2)}) collective-permute-start(bf16[136,1792]{1,0:T(8,128)(2,1)S(1)} %fusion.5), channel_id=1, source_target_pairs={{0,1},{1,0},{2,3},{3,2},{4,5},{5,4},{6,7},{7,6},{8,9},{9,8},{10,11... | collective-permute-start | bytes 1462280 | tf_op jit(solution)/shard_map/ppermute | solution.py:25
  234.5 67.6 %collective-permute-start.45 = (bf16[136,1792]{1,0:T(8,128)(2,1)S(1)}, bf16[136,1792]{1,0:T(8,128)(2,1)S(1)}, u32[]{:S(2)}, u32[]{:S(2)}) collective-permute-start(bf16[136,1792]{1,0:T(8,128)(2,1)S(1)} %fusion.8), channel_id=1, source_target_pairs={{0,2},{1,3},{2,0},{3,1},{4,6},{5,7},{6,4},{7,5},{8,10},{9,11},{10,... | collective-permute-start | bytes 1462280 | tf_op jit(solution)/shard_map/ppermute | solution.py:25
  263.8 23.4 %collective-permute-start.41 = (bf16[136,1792]{1,0:T(8,128)(2,1)S(1)}, bf16[136,1792]{1,0:T(8,128)(2,1)S(1)}, u32[]{:S(2)}, u32[]{:S(2)}) collective-permute-start(bf16[136,1792]{1,0:T(8,128)(2,1)S(1)} %fusion.6), channel_id=1, source_target_pairs={{0,1},{1,0},{2,3},{3,2},{4,5},{5,4},{6,7},{7,6},{8,9},{9,8},{10,11... | collective-permute-start | bytes 1462280 | tf_op jit(solution)/shard_map/ppermute | solution.py:25
  264.7 29.9 %collective-permute-start.43 = (bf16[136,1792]{1,0:T(8,128)(2,1)S(1)}, bf16[136,1792]{1,0:T(8,128)(2,1)S(1)}, u32[]{:S(2)}, u32[]{:S(2)}) collective-permute-start(bf16[136,1792]{1,0:T(8,128)(2,1)S(1)} %fusion.7), channel_id=1, source_target_pairs={{0,2},{1,3},{2,0},{3,1},{4,6},{5,7},{6,4},{7,5},{8,10},{9,11},{10,... | collective-permute-start | bytes 1462280 | tf_op jit(solution)/shard_map/ppermute | solution.py:25
  287.3 21.6 %collective-permute-start.16 = (bf16[40,3584]{1,0:T(8,128)(2,1)S(1)}, bf16[40,3584]{1,0:T(8,128)(2,1)S(1)}, u32[]{:S(2)}, u32[]{:S(2)}) collective-permute-start(bf16[40,3584]{1,0:T(8,128)(2,1)S(1)} %get-tuple-element.91), channel_id=1, source_target_pairs={{0,8},{1,9},{2,10},{3,11},{4,12},{5,13},{6,14},{7,15},{8,0},{9,1},... | collective-permute-start | bytes 860168 | tf_op jit(solution)/shard_map/ppermute | solution.py:32
  309.5 28.8 %collective-permute-start.18 = (bf16[128,3584]{1,0:T(8,128)(2,1)S(1)}, bf16[128,3584]{1,0:T(8,128)(2,1)S(1)}, u32[]{:S(2)}, u32[]{:S(2)}) collective-permute-start(bf16[128,3584]{1,0:T(8,128)(2,1)S(1)} %fusion.4), channel_id=1, source_target_pairs={{0,16},{16,0},{1,17},{17,1},{2,18},{18,2},{3,19},{19,3},{4,20},{20... | collective-permute-start | bytes 2752520 | tf_op jit(solution)/shard_map/ppermute | solution.py:20
  312.7 24.9 %collective-permute-start.47 = (bf16[40,3584]{1,0:T(8,128)(2,1)S(1)}, bf16[40,3584]{1,0:T(8,128)(2,1)S(1)}, u32[]{:S(2)}, u32[]{:S(2)}) collective-permute-start(bf16[40,3584]{1,0:T(8,128)(2,1)S(1)} %get-tuple-element.88), channel_id=1, source_target_pairs={{0,8},{1,9},{2,10},{3,11},{4,12},{5,13},{6,14},{7,15},{8,0},{9,1},... | collective-permute-start | bytes 860168 | tf_op jit(solution)/shard_map/ppermute | solution.py:32
  (33 other events, 369.7 us)

commit v2 on v1

--- a/solution.py
+++ b/solution.py
@@ -25,11 +25,13 @@
     return lax.ppermute(array, "expert", [(i, i ^ bit) for i in range(devices)])
 
 
-def depth_move(array, experts, k):
+def depth_exchange(blocks, experts):
     devices = lax.axis_size("expert")
     group = devices // experts
-    pairs = [(i, ((i // group) ^ k) * group + i % group) for i in range(devices)]
-    return lax.ppermute(array, "expert", pairs)
+    columns = [[e * group + m for e in range(experts)] for m in range(group)]
+    return lax.all_to_all(
+        blocks, "expert", split_axis=0, concat_axis=0, tiled=True, axis_index_groups=columns
+    )
 
 
 class Layout:
@@ -42,16 +44,24 @@
         self.packed = experts * self.main + self.tail
 
 
-def selectors(ids, layout, here):
-    tokens = ids.shape[0]
+def selector(ids, layout, here):
     onehot = (ids[:, None] == jnp.arange(layout.experts, dtype=jnp.int32)).astype(jnp.int32)
     slot = jnp.sum(onehot * (jnp.cumsum(onehot, axis=0) - 1), axis=1)
-    row = jnp.arange(layout.rows, dtype=jnp.int32)[:, None]
-    picks = []
-    for k in range(layout.experts):
-        place = jnp.where(slot < layout.main, slot, slot + k * layout.rest)
-        picks.append(((ids[None, :] == (here ^ k)) & (place[None, :] == row)).astype(BF16))
-    return picks
+    place = jnp.where(slot < layout.main, slot, slot + here * layout.rest)
+    row = jnp.arange(layout.experts * layout.rows, dtype=jnp.int32)[:, None]
+    return ((ids * layout.rows + place)[None, :] == row).astype(BF16)
+
+
+def packer(layout):
+    packed = jnp.arange(layout.packed, dtype=jnp.int32)[:, None]
+    row = jnp.arange(layout.experts * layout.rows, dtype=jnp.int32)[None, :]
+    block, place = row // layout.rows, row % layout.rows
+    target = jnp.where(
+        place < layout.main,
+        block * layout.main + place,
+        layout.experts * layout.main + place - layout.main,
+    )
+    return (target == packed).astype(BF16)
 
 
 def statistics(features):
@@ -66,28 +76,22 @@
     return jax.nn.sigmoid(jnp.sum(jnp.where(onehot, scores, 0.0), axis=1, keepdims=True))
 
 
-def to_planes(rows, picks, layout):
-    blocks = []
-    for k, pick in enumerate(picks):
-        block = dot(pick, rows).astype(BF16)
-        blocks.append(depth_move(block, layout.experts, k) if k else block)
-    return blocks
-
-
-def pack(blocks, layout, cols):
-    tail = blocks[0][layout.main :, cols]
-    for block in blocks[1:]:
-        tail = tail + block[layout.main :, cols]
-    return jnp.concatenate([b[: layout.main, cols] for b in blocks] + [tail], axis=0)
-
-
-def spread(blocks, layout, halves):
-    e = layout.experts
-    lo, hi = [pack(blocks, layout, cols) for cols in halves]
-    x_lo, y_hi = plane_move(lo, e, 1), plane_move(hi, e, 2)
-    x_hi, y_lo = plane_move(hi, e, 1), plane_move(lo, e, 2)
-    d_lo, d_hi = plane_move(x_lo, e, 2), plane_move(y_hi, e, 1)
-    return [(lo, hi), (x_lo, x_hi), (y_lo, y_hi), (d_lo, d_hi)]
+def to_planes(rows, pick, layout):
+    blocks = dot(pick, rows).astype(BF16).reshape(layout.experts, layout.rows, rows.shape[1])
+    blocks = depth_exchange(blocks, layout.experts)
+    blocks = blocks.reshape(layout.experts * layout.rows, rows.shape[1])
+    return dot(packer(layout), blocks).astype(BF16)
+
+
+def to_neighbours(mine, experts):
+    return plane_move(mine, experts, 1), plane_move(mine, experts, 2)
+
+
+def to_diagonal(from_x, from_y, experts, halves):
+    return (
+        plane_move(from_x[:, halves[0]], experts, 2),
+        plane_move(from_y[:, halves[1]], experts, 1),
+    )
 
 
 def gather_back(part, layout):
@@ -103,23 +107,13 @@
     return lo, hi
 
 
-def to_tokens(total, picks, layout):
-    lo, hi = total
-    token_rows = 0.0
-    for k, pick in enumerate(picks):
-        rows = slice(k * layout.main, (k + 1) * layout.main)
-        tail = slice(layout.experts * layout.main, layout.packed)
-        block = jnp.concatenate(
-            [
-                jnp.concatenate([lo[rows], hi[rows]], axis=1),
-                jnp.concatenate([lo[tail], hi[tail]], axis=1),
-            ],
-            axis=0,
-        )
-        if k:
-            block = depth_move(block, layout.experts, k)
-        token_rows = token_rows + dot(pick, block, ((0,), (0,)))
-    return token_rows
+def to_tokens(total, pick, layout):
+    blocks = [dot(packer(layout), t, ((0,), (0,))).astype(BF16) for t in total]
+    blocks = jnp.concatenate(blocks, axis=1)
+    blocks = blocks.reshape(layout.experts, layout.rows, blocks.shape[1])
+    blocks = depth_exchange(blocks, layout.experts)
+    blocks = blocks.reshape(layout.experts * layout.rows, blocks.shape[2])
+    return dot(pick, blocks, ((0,), (0,)))
 
 
 def body(a_input, a_route, b_saved, b_grad, b_route, up_weight, down_weight, router):
@@ -139,16 +133,25 @@
     a_ids = a_route[0][:, 0]
 
     a_float, _, a_normed = statistics(a_input[0])
-    a_picks = selectors(a_ids, layout, here)
-    a_rows = spread(to_planes(a_normed, a_picks, layout), layout, halves)
+    a_pick = selector(a_ids, layout, here)
+    a_mine = to_planes(a_normed, a_pick, layout)
     a_gate = gate_of(a_normed, a_ids, cols_r)
 
     b_float, b_scale, b_normed = statistics(b_x)
-    b_picks = selectors(b_ids, layout, here)
-    b_rows = spread(to_planes(b_normed, b_picks, layout), layout, halves)
+    b_pick = selector(b_ids, layout, here)
+    b_mine = to_planes(b_normed, b_pick, layout)
     b_gate = gate_of(b_normed, b_ids, cols_r)
     cot = (b_gate * b_c.astype(F32)).astype(BF16)
-    c_rows = spread(to_planes(cot, b_picks, layout), layout, halves)
+    c_mine = to_planes(cot, b_pick, layout)
+
+    a_x, a_y = to_neighbours(a_mine, experts)
+    b_mine, a_x, a_y = lax.optimization_barrier((b_mine, a_x, a_y))
+    a_d = to_diagonal(a_x, a_y, experts, halves)
+    b_nx, b_ny = to_neighbours(b_mine, experts)
+    c_mine, b_nx, b_ny, a_d = lax.optimization_barrier((c_mine, b_nx, b_ny, a_d))
+    b_d = to_diagonal(b_nx, b_ny, experts, halves)
+    c_nx, c_ny = to_neighbours(c_mine, experts)
+    a_rows = [(v[:, halves[0]], v[:, halves[1]]) for v in (a_mine, a_x, a_y)] + [a_d]
 
     own_col = jnp.sum(
         jnp.where(jnp.arange(experts) == here, cols_r.astype(F32), 0.0), axis=1, keepdims=True
@@ -158,10 +161,14 @@
     for lo, hi in a_rows:
         hidden = dot(lo, up[:half]) + dot(hi, up[half:])
         a_act.append((hidden * jax.nn.sigmoid(hidden)).astype(BF16))
+    a_act, c_nx, c_ny, b_d = lax.optimization_barrier((a_act, c_nx, c_ny, b_d))
+    c_d = to_diagonal(c_nx, c_ny, experts, halves)
     a_total = gather_back(lambda j, h: dot(a_act[j], down[:, halves[h]]), layout)
-    a_out = (a_float + a_gate * to_tokens(a_total, a_picks, layout)).astype(BF16)
+    a_out = (a_float + a_gate * to_tokens(a_total, a_pick, layout)).astype(BF16)
     a_next = pipe_move(a_out, lambda i, n: i + 1)
 
+    b_rows = [(v[:, halves[0]], v[:, halves[1]]) for v in (b_mine, b_nx, b_ny)] + [b_d]
+    c_rows = [(v[:, halves[0]], v[:, halves[1]]) for v in (c_mine, c_nx, c_ny)] + [c_d]
     act, hid_grad, score_grad = [], [], []
     for (lo, hi), (c_lo, c_hi) in zip(b_rows, c_rows):
         hidden = dot(lo, up[:half]) + dot(hi, up[half:])
@@ -179,7 +186,7 @@
         return dot(hid_grad[j], up[halves[h]], ((1,), (1,))) + score_grad[j] * col_row[:, halves[h]]
 
     b_total = gather_back(input_part, layout)
-    normed_grad = to_tokens(b_total, b_picks, layout)
+    normed_grad = to_tokens(b_total, b_pick, layout)
     along = jnp.sum(normed_grad * b_float, axis=-1, keepdims=True) / width
     feature_grad = b_scale * normed_grad - b_float * (b_scale * b_scale * b_scale) * along
     b_out = (b_c.astype(F32) + feature_grad).astype(BF16)

time: 341 us -> 312 us (0.915)
  waiting for transfers between devices: 212 us -> 170 us
  matrix products: 35.2 us -> 62.5 us
  starting transfers between devices: 71.1 us -> 53 us
    ppermute x15 -> x0, waiting for transfers between devices: 96 us -> none  [depth_move(): return lax.ppermute(array, 'expert', pairs)]
    all_to_all x0 -> x5, waiting for transfers between devices: none -> 83.4 us  [depth_exchange(): lax.all_to_all(blocks, 'expert', split_axis=0, concat_axis=0, tiled=True,...]
    ppermute x15 -> x0, starting transfers between devices: 36.4 us -> none  [depth_move(): return lax.ppermute(array, 'expert', pairs)]
    ppermute x30 -> x24, waiting for transfers between devices: 116 us -> 86.7 us  [plane_move(): return lax.ppermute(array, 'expert', [(i, i ^ bit) for i in range(devices)])]
    dot_general x74 -> x62, matrix products: 35.2 us -> 62.5 us  [dot(): return lax.dot_general(a, b, (dims, ((), ())), preferred_element_type=F32)]
    all_to_all x0 -> x5, starting transfers between devices: none -> 21.9 us  [depth_exchange(): lax.all_to_all(blocks, 'expert', split_axis=0, concat_axis=0, tiled=True,...]
    slice x8, local copies, waits for them, and re-layouts: 0.15 us -> 6.66 us  [the longest x5 4.67 us: body(): v[:, halves[0]]]
    unnamed x37 -> x77, local copies, waits for them, and re-layouts: 7.56 us -> 2.66 us
  transfers between devices with their start and end apart: 49 -> 33, of which waited for: 29 -> 13; matrix products, arithmetic and copies ran while one was open for 15% -> 22% of each run, Pallas kernels for 0% -> 0%
where the time goes in v2:
time: 312 us; the launch traced here: 310 us
  waiting for transfers between devices  170 us (54%)
  matrix products  62.5 us (20%)
  starting transfers between devices  53 us (17%)
  other arithmetic  13.8 us (4%)
  local copies, waits for them, and re-layouts  9.73 us (3%)
    ppermute x24, waiting for transfers between devices, plane_move(): return lax.ppermute(array, 'expert', [(i, i ^ bit) for i in range(devices)])  86.7 us
    all_to_all x5, waiting for transfers between devices, depth_exchange(): lax.all_to_all(blocks, 'expert', split_axis=0, concat_axis=0, tiled=True,...  83.4 us
    dot_general x62, matrix products, dot(): return lax.dot_general(a, b, (dims, ((), ())), preferred_element_type=F32)  62.5 us
    ppermute x24, starting transfers between devices, plane_move(): return lax.ppermute(array, 'expert', [(i, i ^ bit) for i in range(devices)])  30.2 us
    all_to_all x5, starting transfers between devices, depth_exchange(): lax.all_to_all(blocks, 'expert', split_axis=0, concat_axis=0, tiled=True,...  21.9 us
  transfers between devices with their start and end apart: 33, of which 13 were waited for; matrix products, arithmetic and copies ran while one was open for 22% of the time, Pallas kernels for 0%

profile of v2, /device:TPU:0, one launch (start us, length us, event | category | flops | bytes accessed | tf_op | source)
XLA Modules:
  0.0 310.5 jit_solution(6410775884508468841)
XLA Ops:
  7.7 6.0 %all-to-all-start = ((bf16[4,40,3584]{2,1,0:T(8,128)(2,1)}), bf16[4,40,3584]{2,1,0:T(8,128)(2,1)S(1)}, u32[]{:S(2)}, u32[]{:S(2)}) async-start(bf16[4,40,3584]{2,1,0:T(8,128)(2,1)} %bitcast.4), calls=%async_computation | async-start | bytes 2293760 | tf_op jit(solution)/shard_map/all_to_all | solution.py:32
  14.9 2.7 convolution_convert_fusion
  17.6 24.6 %all-to-all-done = bf16[4,40,3584]{2,1,0:T(8,128)(2,1)S(1)} async-done(((bf16[4,40,3584]{2,1,0:T(8,128)(2,1)}), bf16[4,40,3584]{2,1,0:T(8,128)(2,1)S(1)}, u32[]{:S(2)}, u32[]{:S(2)}) %all-to-all-start) | async-done | bytes 1146912 | tf_op jit(solution)/shard_map/all_to_all | solution.py:32
  42.2 4.3 %all-to-all-start.2 = ((bf16[4,40,3584]{2,1,0:T(8,128)(2,1)}), bf16[4,40,3584]{2,1,0:T(8,128)(2,1)}, u32[]{:S(2)}, u32[]{:S(2)}) async-start(bf16[4,40,3584]{2,1,0:T(8,128)(2,1)} %bitcast.15), calls=%async_computation.2 | async-start | bytes 2293760 | tf_op jit(solution)/shard_map/all_to_all | solution.py:32
  48.2 26.1 %all-to-all-done.2 = bf16[4,40,3584]{2,1,0:T(8,128)(2,1)} async-done(((bf16[4,40,3584]{2,1,0:T(8,128)(2,1)}), bf16[4,40,3584]{2,1,0:T(8,128)(2,1)}, u32[]{:S(2)}, u32[]{:S(2)}) %all-to-all-start.2) | async-done | bytes 1146912 | tf_op jit(solution)/shard_map/all_to_all | solution.py:32
  74.3 4.4 %all-to-all-start.1 = ((bf16[4,40,3584]{2,1,0:T(8,128)(2,1)}), bf16[4,40,3584]{2,1,0:T(8,128)(2,1)}, u32[]{:S(2)}, u32[]{:S(2)}) async-start(bf16[4,40,3584]{2,1,0:T(8,128)(2,1)} %bitcast.12), calls=%async_computation.1 | async-start | bytes 2293760 | tf_op jit(solution)/shard_map/all_to_all | solution.py:32
  86.4 2.8 convolution_convert_fusion.3
  89.2 16.7 %all-to-all-done.1 = bf16[4,40,3584]{2,1,0:T(8,128)(2,1)} async-done(((bf16[4,40,3584]{2,1,0:T(8,128)(2,1)}), bf16[4,40,3584]{2,1,0:T(8,128)(2,1)}, u32[]{:S(2)}, u32[]{:S(2)}) %all-to-all-start.1) | async-done | bytes 1146912 | tf_op jit(solution)/shard_map/all_to_all | solution.py:32
  121.4 25.7 %collective-permute-done.8 = bf16[136,1792]{1,0:T(8,128)(2,1)S(1)} collective-permute-done((bf16[136,1792]{1,0:T(8,128)(2,1)S(1)}, bf16[136,1792]{1,0:T(8,128)(2,1)S(1)}, u32[]{:S(2)}, u32[]{:S(2)}) %collective-permute-start.8) | collective-permute-done | bytes 487456 | tf_op jit(solution)/shard_map/ppermute | solution.py:25
  157.9 24.1 %collective-permute-done.12 = bf16[136,1792]{1,0:T(8,128)(2,1)S(1)} collective-permute-done((bf16[136,1792]{1,0:T(8,128)(2,1)S(1)}, bf16[136,1792]{1,0:T(8,128)(2,1)S(1)}, u32[]{:S(2)}, u32[]{:S(2)}) %collective-permute-start.12) | collective-permute-done | bytes 487456 | tf_op jit(solution)/shard_map/ppermute | solution.py:25
  198.0 3.4 %collective-permute-done.14 = bf16[136,1792]{1,0:T(8,128)(2,1)S(1)} collective-permute-done((bf16[136,1792]{1,0:T(8,128)(2,1)S(1)}, bf16[136,1792]{1,0:T(8,128)(2,1)S(1)}, u32[]{:S(2)}, u32[]{:S(2)}) %collective-permute-start.14) | collective-permute-done | bytes 487456 | tf_op jit(solution)/shard_map/ppermute | solution.py:25
  203.9 18.4 %collective-permute-done.22 = bf16[136,1792]{1,0:T(8,128)(2,1)S(1)} collective-permute-done((bf16[136,1792]{1,0:T(8,128)(2,1)S(1)}, bf16[136,1792]{1,0:T(8,128)(2,1)S(1)}, u32[]{:S(2)}, u32[]{:S(2)}) %collective-permute-start.22) | collective-permute-done | bytes 487456 | tf_op jit(solution)/shard_map/ppermute | solution.py:25
  225.1 7.4 %collective-permute-done.21 = bf16[136,1792]{1,0:T(8,128)(2,1)S(1)} collective-permute-done((bf16[136,1792]{1,0:T(8,128)(2,1)S(1)}, bf16[136,1792]{1,0:T(8,128)(2,1)S(1)}, u32[]{:S(2)}, u32[]{:S(2)}) %collective-permute-start.21) | collective-permute-done | bytes 487456 | tf_op jit(solution)/shard_map/ppermute | solution.py:25
  232.5 2.3 collective-permute-start.17
  242.0 4.0 %collective-permute-done.17 = bf16[136,1792]{1,0:T(8,128)(2,1)S(1)} collective-permute-done((bf16[136,1792]{1,0:T(8,128)(2,1)S(1)}, bf16[136,1792]{1,0:T(8,128)(2,1)S(1)}, u32[]{:S(2)}, u32[]{:S(2)}) %collective-permute-start.17) | collective-permute-done | bytes 487456 | tf_op jit(solution)/shard_map/ppermute | solution.py:25
  246.7 2.5 collective-permute-start.23
  252.4 2.5 convolution_convert_fusion.13
  257.1 3.5 %all-to-all-start.3 = ((bf16[4,40,3584]{2,1,0:T(8,128)(2,1)}), bf16[4,40,3584]{2,1,0:T(8,128)(2,1)S(1)}, u32[]{:S(2)}, u32[]{:S(2)}) async-start(bf16[4,40,3584]{2,1,0:T(8,128)(2,1)} %bitcast.18), calls=%async_computation.3 | async-start | bytes 2293760 | tf_op jit(solution)/shard_map/all_to_all | solution.py:32
  263.4 2.6 add_convert_fusion.1
  278.3 7.4 %all-to-all-done.3 = bf16[4,40,3584]{2,1,0:T(8,128)(2,1)S(1)} async-done(((bf16[4,40,3584]{2,1,0:T(8,128)(2,1)}), bf16[4,40,3584]{2,1,0:T(8,128)(2,1)S(1)}, u32[]{:S(2)}, u32[]{:S(2)}) %all-to-all-start.3) | async-done | bytes 1146912 | tf_op jit(solution)/shard_map/all_to_all | solution.py:32
  285.7 3.6 %all-to-all-start.4 = ((bf16[4,40,3584]{2,1,0:T(8,128)(2,1)}), bf16[4,40,3584]{2,1,0:T(8,128)(2,1)S(1)}, u32[]{:S(2)}, u32[]{:S(2)}) async-start(bf16[4,40,3584]{2,1,0:T(8,128)(2,1)} %bitcast.29), calls=%async_computation.4 | async-start | bytes 2293760 | tf_op jit(solution)/shard_map/all_to_all | solution.py:32
  289.4 2.7 convolution_convert_fusion.7
  297.7 8.6 %all-to-all-done.4 = bf16[4,40,3584]{2,1,0:T(8,128)(2,1)S(1)} async-done(((bf16[4,40,3584]{2,1,0:T(8,128)(2,1)}), bf16[4,40,3584]{2,1,0:T(8,128)(2,1)S(1)}, u32[]{:S(2)}, u32[]{:S(2)}) %all-to-all-start.4) | async-done | bytes 1146912 | tf_op jit(solution)/shard_map/all_to_all | solution.py:32
  306.8 2.7 fusion.61
  (227 shorter events, 100.2 us)
Async XLA Ops:
  7.7 34.5 %all-to-all-start = ((bf16[4,40,3584]{2,1,0:T(8,128)(2,1)}), bf16[4,40,3584]{2,1,0:T(8,128)(2,1)S(1)}, u32[]{:S(2)}, u32[]{:S(2)}) async-start(bf16[4,40,3584]{2,1,0:T(8,128)(2,1)} %bitcast.4), calls=%async_computation | async-start | bytes 2293760 | tf_op jit(solution)/shard_map/all_to_all | solution.py:32
  42.2 32.1 %all-to-all-start.2 = ((bf16[4,40,3584]{2,1,0:T(8,128)(2,1)}), bf16[4,40,3584]{2,1,0:T(8,128)(2,1)}, u32[]{:S(2)}, u32[]{:S(2)}) async-start(bf16[4,40,3584]{2,1,0:T(8,128)(2,1)} %bitcast.15), calls=%async_computation.2 | async-start | bytes 2293760 | tf_op jit(solution)/shard_map/all_to_all | solution.py:32
  74.3 31.6 %all-to-all-start.1 = ((bf16[4,40,3584]{2,1,0:T(8,128)(2,1)}), bf16[4,40,3584]{2,1,0:T(8,128)(2,1)}, u32[]{:S(2)}, u32[]{:S(2)}) async-start(bf16[4,40,3584]{2,1,0:T(8,128)(2,1)} %bitcast.12), calls=%async_computation.1 | async-start | bytes 2293760 | tf_op jit(solution)/shard_map/all_to_all | solution.py:32
  80.7 26.9 %collective-permute-start.3 = (bf16[136,3584]{1,0:T(8,128)(2,1)}, bf16[136,3584]{1,0:T(8,128)(2,1)}, u32[]{:S(2)}, u32[]{:S(2)}) collective-permute-start(bf16[136,3584]{1,0:T(8,128)(2,1)} %convolution_convert_fusion.5), channel_id=1, source_target_pairs={{0,2},{1,3},{2,0},{3,1},{4,6},{5,7},{6,4},{7,5},{8,10},{9,11},{10,... | collective-permute-start | bytes 2924552 | tf_op jit(solution)/shard_map/ppermute | solution.py:25
  82.2 25.4 %collective-permute-start.2 = (bf16[136,3584]{1,0:T(8,128)(2,1)}, bf16[136,3584]{1,0:T(8,128)(2,1)}, u32[]{:S(2)}, u32[]{:S(2)}) collective-permute-start(bf16[136,3584]{1,0:T(8,128)(2,1)} %convolution_convert_fusion.5), channel_id=1, source_target_pairs={{0,1},{1,0},{2,3},{3,2},{4,5},{5,4},{6,7},{7,6},{8,9},{9,8},{10,11... | collective-permute-start | bytes 2924552 | tf_op jit(solution)/shard_map/ppermute | solution.py:25
  112.8 34.3 %collective-permute-start.6 = (bf16[136,3584]{1,0:T(8,128)(2,1)S(1)}, bf16[136,3584]{1,0:T(8,128)(2,1)S(1)}, u32[]{:S(2)}, u32[]{:S(2)}) collective-permute-start(bf16[136,3584]{1,0:T(8,128)(2,1)S(1)} %convolution_convert_fusion.4), channel_id=1, source_target_pairs={{0,2},{1,3},{2,0},{3,1},{4,6},{5,7},{6,4},{7,5},{8,10},{9,11},{10,... | collective-permute-start | bytes 2924552 | tf_op jit(solution)/shard_map/ppermute | solution.py:25
  114.3 32.7 %collective-permute-start.5 = (bf16[136,3584]{1,0:T(8,128)(2,1)S(1)}, bf16[136,3584]{1,0:T(8,128)(2,1)S(1)}, u32[]{:S(2)}, u32[]{:S(2)}) collective-permute-start(bf16[136,3584]{1,0:T(8,128)(2,1)S(1)} %convolution_convert_fusion.4), channel_id=1, source_target_pairs={{0,1},{1,0},{2,3},{3,2},{4,5},{5,4},{6,7},{7,6},{8,9},{9,8},{10,11... | collective-permute-start | bytes 2924552 | tf_op jit(solution)/shard_map/ppermute | solution.py:25
  118.8 28.2 %collective-permute-start.8 = (bf16[136,1792]{1,0:T(8,128)(2,1)S(1)}, bf16[136,1792]{1,0:T(8,128)(2,1)S(1)}, u32[]{:S(2)}, u32[]{:S(2)}) collective-permute-start(bf16[136,1792]{1,0:T(8,128)(2,1)S(1)} %slice.69), channel_id=1, source_target_pairs={{0,1},{1,0},{2,3},{3,2},{4,5},{5,4},{6,7},{7,6},{8,9},{9,8},{10,11... | collective-permute-start | bytes 1462280 | tf_op jit(solution)/shard_map/ppermute | solution.py:25
  119.4 27.6 %collective-permute-start.7 = (bf16[136,1792]{1,0:T(8,128)(2,1)S(1)}, bf16[136,1792]{1,0:T(8,128)(2,1)S(1)}, u32[]{:S(2)}, u32[]{:S(2)}) collective-permute-start(bf16[136,1792]{1,0:T(8,128)(2,1)S(1)} %slice.66), channel_id=1, source_target_pairs={{0,2},{1,3},{2,0},{3,1},{4,6},{5,7},{6,4},{7,5},{8,10},{9,11},{10,... | collective-permute-start | bytes 1462280 | tf_op jit(solution)/shard_map/ppermute | solution.py:25
  150.0 32.1 %collective-permute-start.10 = (bf16[136,3584]{1,0:T(8,128)(2,1)S(1)}, bf16[136,3584]{1,0:T(8,128)(2,1)S(1)}, u32[]{:S(2)}, u32[]{:S(2)}) collective-permute-start(bf16[136,3584]{1,0:T(8,128)(2,1)S(1)} %copy-done.3), channel_id=1, source_target_pairs={{0,2},{1,3},{2,0},{3,1},{4,6},{5,7},{6,4},{7,5},{8,10},{9,11},{10,... | collective-permute-start | bytes 2924552 | tf_op jit(solution)/shard_map/ppermute | solution.py:25
  150.5 31.5 %collective-permute-start.9 = (bf16[136,3584]{1,0:T(8,128)(2,1)S(1)}, bf16[136,3584]{1,0:T(8,128)(2,1)S(1)}, u32[]{:S(2)}, u32[]{:S(2)}) collective-permute-start(bf16[136,3584]{1,0:T(8,128)(2,1)S(1)} %copy-done.3), channel_id=1, source_target_pairs={{0,1},{1,0},{2,3},{3,2},{4,5},{5,4},{6,7},{7,6},{8,9},{9,8},{10,11... | collective-permute-start | bytes 2924552 | tf_op jit(solution)/shard_map/ppermute | solution.py:25
  153.0 29.0 %collective-permute-start.12 = (bf16[136,1792]{1,0:T(8,128)(2,1)S(1)}, bf16[136,1792]{1,0:T(8,128)(2,1)S(1)}, u32[]{:S(2)}, u32[]{:S(2)}) collective-permute-start(bf16[136,1792]{1,0:T(8,128)(2,1)S(1)} %get-tuple-element.47), channel_id=1, source_target_pairs={{0,1},{1,0},{2,3},{3,2},{4,5},{5,4},{6,7},{7,6},{8,9},{9,8},{10,11... | collective-permute-start | bytes 1462280 | tf_op jit(solution)/shard_map/ppermute | solution.py:25
  153.7 28.3 %collective-permute-start.11 = (bf16[136,1792]{1,0:T(8,128)(2,1)S(1)}, bf16[136,1792]{1,0:T(8,128)(2,1)S(1)}, u32[]{:S(2)}, u32[]{:S(2)}) collective-permute-start(bf16[136,1792]{1,0:T(8,128)(2,1)S(1)} %get-tuple-element.49), channel_id=1, source_target_pairs={{0,2},{1,3},{2,0},{3,1},{4,6},{5,7},{6,4},{7,5},{8,10},{9,11},{10,... | collective-permute-start | bytes 1462280 | tf_op jit(solution)/shard_map/ppermute | solution.py:25
  187.2 14.1 %collective-permute-start.14 = (bf16[136,1792]{1,0:T(8,128)(2,1)S(1)}, bf16[136,1792]{1,0:T(8,128)(2,1)S(1)}, u32[]{:S(2)}, u32[]{:S(2)}) collective-permute-start(bf16[136,1792]{1,0:T(8,128)(2,1)S(1)} %convolution_convert_fusion.16), channel_id=1, source_target_pairs={{0,1},{1,0},{2,3},{3,2},{4,5},{5,4},{6,7},{7,6},{8,9},{9,8},{10,11... | collective-permute-start | bytes 1462280 | tf_op jit(solution)/shard_map/ppermute | solution.py:25
  188.8 35.4 %collective-permute-start.16 = (bf16[136,1792]{1,0:T(8,128)(2,1)S(1)}, bf16[136,1792]{1,0:T(8,128)(2,1)S(1)}, u32[]{:S(2)}, u32[]{:S(2)}) collective-permute-start(bf16[136,1792]{1,0:T(8,128)(2,1)S(1)} %convolution_convert_fusion.15), channel_id=1, source_target_pairs={{0,2},{1,3},{2,0},{3,1},{4,6},{5,7},{6,4},{7,5},{8,10},{9,11},{10,... | collective-permute-start | bytes 1462280 | tf_op jit(solution)/shard_map/ppermute | solution.py:25
  190.2 50.3 %collective-permute-start.18 = (bf16[136,1792]{1,0:T(8,128)(2,1)S(1)}, bf16[136,1792]{1,0:T(8,128)(2,1)S(1)}, u32[]{:S(2)}, u32[]{:S(2)}) collective-permute-start(bf16[136,1792]{1,0:T(8,128)(2,1)S(1)} %convolution_convert_fusion.14), channel_id=1, source_target_pairs={{0,2},{1,3},{2,0},{3,1},{4,6},{5,7},{6,4},{7,5},{8,10},{9,11},{10,... | collective-permute-start | bytes 1462280 | tf_op jit(solution)/shard_map/ppermute | solution.py:25
  190.8 60.1 %collective-permute-start.13 = (bf16[136,1792]{1,0:T(8,128)(2,1)}, bf16[136,1792]{1,0:T(8,128)(2,1)}, u32[]{:S(2)}, u32[]{:S(2)}) collective-permute-start(bf16[136,1792]{1,0:T(8,128)(2,1)} %convolution_convert_fusion.17), channel_id=1, source_target_pairs={{0,1},{1,0},{2,3},{3,2},{4,5},{5,4},{6,7},{7,6},{8,9},{9,8},{10,11... | collective-permute-start | bytes 1462280 | tf_op jit(solution)/shard_map/ppermute | solution.py:25
  191.4 30.9 %collective-permute-start.22 = (bf16[136,1792]{1,0:T(8,128)(2,1)S(1)}, bf16[136,1792]{1,0:T(8,128)(2,1)S(1)}, u32[]{:S(2)}, u32[]{:S(2)}) collective-permute-start(bf16[136,1792]{1,0:T(8,128)(2,1)S(1)} %get-tuple-element.41), channel_id=1, source_target_pairs={{0,1},{1,0},{2,3},{3,2},{4,5},{5,4},{6,7},{7,6},{8,9},{9,8},{10,11... | collective-permute-start | bytes 1462280 | tf_op jit(solution)/shard_map/ppermute | solution.py:25
  201.4 67.9 %collective-permute-start.20 = (bf16[136,1792]{1,0:T(8,128)(2,1)}, bf16[136,1792]{1,0:T(8,128)(2,1)}, u32[]{:S(2)}, u32[]{:S(2)}) collective-permute-start(bf16[136,1792]{1,0:T(8,128)(2,1)} %fusion.8), channel_id=1, source_target_pairs={{0,1},{1,0},{2,3},{3,2},{4,5},{5,4},{6,7},{7,6},{8,9},{9,8},{10,11... | collective-permute-start | bytes 1462280 | tf_op jit(solution)/shard_map/ppermute | solution.py:25
  224.2 28.2 %collective-permute-start.15 = (bf16[136,1792]{1,0:T(8,128)(2,1)}, bf16[136,1792]{1,0:T(8,128)(2,1)}, u32[]{:S(2)}, u32[]{:S(2)}) collective-permute-start(bf16[136,1792]{1,0:T(8,128)(2,1)} %fusion.5), channel_id=1, source_target_pairs={{0,2},{1,3},{2,0},{3,1},{4,6},{5,7},{6,4},{7,5},{8,10},{9,11},{10,... | collective-permute-start | bytes 1462280 | tf_op jit(solution)/shard_map/ppermute | solution.py:25
  240.5 33.0 %collective-permute-start.27 = (bf16[136,1792]{1,0:T(8,128)(2,1)}, bf16[136,1792]{1,0:T(8,128)(2,1)}, u32[]{:S(2)}, u32[]{:S(2)}) collective-permute-start(bf16[136,1792]{1,0:T(8,128)(2,1)} %fusion.11), channel_id=1, source_target_pairs={{0,2},{1,3},{2,0},{3,1},{4,6},{5,7},{6,4},{7,5},{8,10},{9,11},{10,... | collective-permute-start | bytes 1462280 | tf_op jit(solution)/shard_map/ppermute | solution.py:25
  246.7 14.0 %collective-permute-start.23 = (bf16[136,1792]{1,0:T(8,128)(2,1)}, bf16[136,1792]{1,0:T(8,128)(2,1)}, u32[]{:S(2)}, u32[]{:S(2)}) collective-permute-start(bf16[136,1792]{1,0:T(8,128)(2,1)} %fusion.9), channel_id=1, source_target_pairs={{0,1},{1,0},{2,3},{3,2},{4,5},{5,4},{6,7},{7,6},{8,9},{9,8},{10,11... | collective-permute-start | bytes 1462280 | tf_op jit(solution)/shard_map/ppermute | solution.py:25
  257.1 28.6 %all-to-all-start.3 = ((bf16[4,40,3584]{2,1,0:T(8,128)(2,1)}), bf16[4,40,3584]{2,1,0:T(8,128)(2,1)S(1)}, u32[]{:S(2)}, u32[]{:S(2)}) async-start(bf16[4,40,3584]{2,1,0:T(8,128)(2,1)} %bitcast.18), calls=%async_computation.3 | async-start | bytes 2293760 | tf_op jit(solution)/shard_map/all_to_all | solution.py:32
  285.7 20.6 %all-to-all-start.4 = ((bf16[4,40,3584]{2,1,0:T(8,128)(2,1)}), bf16[4,40,3584]{2,1,0:T(8,128)(2,1)S(1)}, u32[]{:S(2)}, u32[]{:S(2)}) async-start(bf16[4,40,3584]{2,1,0:T(8,128)(2,1)} %bitcast.29), calls=%async_computation.4 | async-start | bytes 2293760 | tf_op jit(solution)/shard_map/all_to_all | solution.py:32
  (47 other events, 482.4 us)

commit v3 on v2

v3 whole, which is shorter than its diff:
```python
import jax
import jax.numpy as jnp
from jax import lax
from jax.sharding import PartitionSpec as P

EPS = 1e-06
F32 = jnp.float32
BF16 = jnp.bfloat16


def dot(a, b, dims=((1,), (0,))):
    return lax.dot_general(a, b, (dims, ((), ())), preferred_element_type=F32)


def pipe_move(array, target):
    count = lax.axis_size("pipe")
    pairs = [(i, target(i, count) % count) for i in range(count)]
    if all(a == b for a, b in pairs):
        return array
    return lax.ppermute(array, "pipe", pairs)


def plane_move(array, experts, bit):
    devices = lax.axis_size("expert")
    return lax.ppermute(array, "expert", [(i, i ^ bit) for i in range(devices)])


def depth_exchange(blocks, experts):
    devices = lax.axis_size("expert")
    group = devices // experts
    columns = [[e * group + m for e in range(experts)] for m in range(group)]
    return lax.all_to_all(
        blocks, "expert", split_axis=0, concat_axis=0, tiled=True, axis_index_groups=columns
    )


class Layout:
    def __init__(self, experts, capacity):
        self.experts = experts
        self.main = capacity // 8 * 8
        self.rest = capacity - self.main
        self.tail = -(-experts * self.rest // 8) * 8
        self.rows = self.main + self.tail
        self.packed = experts * self.main + self.tail


def selector(ids, layout, here):
    onehot = (ids[:, None] == jnp.arange(layout.experts, dtype=jnp.int32)).astype(jnp.int32)
    slot = jnp.sum(onehot * (jnp.cumsum(onehot, axis=0) - 1), axis=1)
    place = jnp.where(slot < layout.main, slot, slot + here * layout.rest)
    row = jnp.arange(layout.experts * layout.rows, dtype=jnp.int32)[:, None]
    return ((ids * layout.rows + place)[None, :] == row).astype(BF16)


def packer(layout):
    packed = jnp.arange(layout.packed, dtype=jnp.int32)[:, None]
    row = jnp.arange(layout.experts * layout.rows, dtype=jnp.int32)[None, :]
    block, place = row // layout.rows, row % layout.rows
    target = jnp.where(
        place < layout.main,
        block * layout.main + place,
        layout.experts * layout.main + place - layout.main,
    )
    return (target == packed).astype(BF16)


def statistics(features):
    feat = features.astype(F32)
    scale = lax.rsqrt(jnp.mean(feat * feat, axis=-1, keepdims=True) + EPS)
    return feat, scale, (feat * scale).astype(BF16)


def gate_of(normed, ids, router):
    scores = dot(normed, router)
    onehot = ids[:, None] == jnp.arange(router.shape[1], dtype=jnp.int32)
    return jax.nn.sigmoid(jnp.sum(jnp.where(onehot, scores, 0.0), axis=1, keepdims=True))


def select_rows(pick, rows, layout):
    return dot(pick, rows).astype(BF16).reshape(layout.experts, layout.rows, rows.shape[1])


def across_planes(blocks, layout):
    blocks = depth_exchange(blocks, layout.experts)
    blocks = blocks.reshape(layout.experts * layout.rows, blocks.shape[2])
    return dot(packer(layout), blocks).astype(BF16)


def to_neighbours(mine, experts):
    return plane_move(mine, experts, 1), plane_move(mine, experts, 2)


def to_diagonal(from_x, from_y, experts):
    cut = -(-from_x.shape[0] // 16) * 8
    return (
        plane_move(from_x[:cut], experts, 2),
        plane_move(from_y[cut:], experts, 1),
    )


def first_parts(part):
    return (
        jnp.concatenate([part(3, 0).astype(BF16), part(1, 0).astype(BF16)], axis=0),
        jnp.concatenate([part(3, 1).astype(BF16), part(2, 1).astype(BF16)], axis=0),
    )


def second_parts(part, got, rows):
    return (
        (part(1, 1) + got[1][:rows].astype(F32)).astype(BF16),
        (part(2, 0) + got[0][:rows].astype(F32)).astype(BF16),
    )


def swap_pair(pair, experts):
    return plane_move(pair[0], experts, 1), plane_move(pair[1], experts, 2)


def totals(part, first, second, rows):
    lo = part(0, 0) + first[0][rows:].astype(F32) + second[1].astype(F32)
    hi = part(0, 1) + first[1][rows:].astype(F32) + second[0].astype(F32)
    return lo.astype(BF16), hi.astype(BF16)


def for_tokens(total, layout):
    blocks = [dot(packer(layout), t, ((0,), (0,))).astype(BF16) for t in total]
    blocks = jnp.concatenate(blocks, axis=1)
    return blocks.reshape(layout.experts, layout.rows, blocks.shape[1])


def at_tokens(blocks, pick, layout):
    blocks = depth_exchange(blocks, layout.experts)
    blocks = blocks.reshape(layout.experts * layout.rows, blocks.shape[2])
    return dot(pick, blocks, ((0,), (0,)))


def body(a_input, a_route, b_saved, b_grad, b_route, up_weight, down_weight, router):
    devices = lax.axis_size("expert")
    experts = router.shape[2]
    group = devices // experts
    tokens, width = a_input.shape[1], a_input.shape[2]
    layout = Layout(experts, tokens * a_route.shape[2] // experts + 2)
    here = lax.axis_index("expert") // group
    up, down, cols_r = up_weight[0], down_weight[0], router[0]
    half = width // 2
    halves = (slice(0, half), slice(half, width))

    b_ids = pipe_move(b_route[0].astype(BF16), lambda i, n: n - 1 - i).astype(jnp.int32)[:, 0]
    b_x = pipe_move(b_saved[0], lambda i, n: n - 1 - i)
    b_c = pipe_move(b_grad[0], lambda i, n: n - 1 - i)
    a_ids = a_route[0][:, 0]

    after = lax.optimization_barrier
    rows = layout.packed

    own_col = jnp.sum(
        jnp.where(jnp.arange(experts) == here, cols_r.astype(F32), 0.0), axis=1, keepdims=True
    ).astype(BF16)
    col_row = own_col.astype(F32).reshape(1, width)

    a_float, _, a_normed = statistics(a_input[0])
    a_pick = selector(a_ids, layout, here)
    a_mine = across_planes(select_rows(a_pick, a_normed, layout), layout)

    b_float, b_scale, b_normed = statistics(b_x)
    b_pick = selector(b_ids, layout, here)
    b_send = select_rows(b_pick, b_normed, layout)
    b_send, a_mine = after((b_send, a_mine))
    a_near = to_neighbours(a_mine, experts)
    b_mine = across_planes(b_send, layout)

    b_gate = gate_of(b_normed, b_ids, cols_r)
    cot = (b_gate * b_c.astype(F32)).astype(BF16)
    c_send = select_rows(b_pick, cot, layout)
    c_send, a_near, b_mine = after((c_send, a_near, b_mine))
    c_mine = across_planes(c_send, layout)
    a_far = to_diagonal(a_near[0], a_near[1], experts)
    b_near = to_neighbours(b_mine, experts)

    def forward_act(block):
        hidden = dot(block, up)
        return (hidden * jax.nn.sigmoid(hidden)).astype(BF16)

    a_act = [forward_act(v) for v in (a_mine,) + a_near]
    a_act.append(jnp.concatenate([forward_act(v) for v in a_far], axis=0))

    def a_part(j, h):
        return dot(a_act[j], down[:, halves[h]])

    a_first = first_parts(a_part)
    a_first, b_near = after((a_first, b_near))
    a_first = swap_pair(a_first, experts)
    b_far = to_diagonal(b_near[0], b_near[1], experts)
    a_first, c_mine = after((a_first, c_mine))
    c_near = to_neighbours(c_mine, experts)
    a_second = second_parts(a_part, a_first, rows)
    a_second, b_far, c_near = after((a_second, b_far, c_near))
    c_far = to_diagonal(c_near[0], c_near[1], experts)
    a_second = swap_pair(a_second, experts)
    a_back = for_tokens(totals(a_part, a_first, a_second, rows), layout)

    act, hid_grad, score_grad = [], [], []
    for block, cots in zip((b_mine,) + b_near + b_far, (c_mine,) + c_near + c_far):
        hidden = dot(block, up)
        score = dot(block, own_col)
        sigma = jax.nn.sigmoid(hidden)
        active = hidden * sigma
        act_grad = dot(cots, down, ((1,), (1,)))
        act.append(active.astype(BF16))
        hid_grad.append((act_grad * sigma * (1.0 + hidden * (1.0 - sigma))).astype(BF16))
        term = jnp.sum(active * act_grad, axis=1, keepdims=True)
        score_grad.append(term * jax.nn.sigmoid(-score))
    parts_g = hid_grad[:3] + [jnp.concatenate(hid_grad[3:], axis=0)]
    scores = score_grad[:3] + [jnp.concatenate(score_grad[3:], axis=0)]

    def b_part(j, h):
        cols = halves[h]
        return dot(parts_g[j], up[cols], ((1,), (1,))) + scores[j] * col_row[:, cols]

    b_first, a_back = after((first_parts(b_part), a_back))
    b_first = swap_pair(b_first, experts)
    a_gate = gate_of(a_normed, a_ids, cols_r)
    a_out = (a_float + a_gate * at_tokens(a_back, a_pick, layout)).astype(BF16)
    a_next = pipe_move(a_out, lambda i, n: i + 1)
    b_second = swap_pair(second_parts(b_part, b_first, rows), experts)
    b_back = for_tokens(totals(b_part, b_first, b_second, rows), layout)
    normed_grad = at_tokens(b_back, b_pick, layout)
    along = jnp.sum(normed_grad * b_float, axis=-1, keepdims=True) / width
    feature_grad = b_scale * normed_grad - b_float * (b_scale * b_scale * b_scale) * along
    b_out = (b_c.astype(F32) + feature_grad).astype(BF16)
    b_next = pipe_move(b_out, lambda i, n: n - i)

    acts, hids = jnp.concatenate(act, axis=0), jnp.concatenate(hid_grad, axis=0)
    b_all = jnp.concatenate((b_mine,) + b_near + b_far, axis=0)
    c_all = jnp.concatenate((c_mine,) + c_near + c_far, axis=0)
    up_grad = dot(b_all, hids, ((0,), (0,))).astype(BF16)
    down_grad = dot(acts, c_all, ((0,), (0,))).astype(BF16)
    return (a_next[None], b_next[None], up_grad[None], down_grad[None])


def solution(mesh):
    return jax.shard_map(
        body,
        mesh=mesh,
        in_specs=(
            P("pipe", "expert", None),
            P("pipe", "expert", None),
            P("pipe", "expert", None),
            P("pipe", "expert", None),
            P("pipe", "expert", None),
            P("pipe", None, "expert"),
            P("pipe", "expert", None),
            P("pipe", None, None),
        ),
        out_specs=(
            P("pipe", "expert", None),
            P("pipe", "expert", None),
            P("pipe", None, "expert"),
            P("pipe", "expert", None),
        ),
        check_vma=False,
    )
```

time: 312 us -> 293 us (0.939)
  waiting for transfers between devices: 170 us -> 122 us
  local copies, waits for them, and re-layouts: 9.73 us -> 28.4 us
  matrix products: 62.5 us -> 75.7 us
  starting transfers between devices: 53 us -> 46 us
  other arithmetic: 13.8 us -> 17.6 us
    all_to_all x5, waiting for transfers between devices: 83.4 us -> 48.4 us  [depth_exchange(): lax.all_to_all(blocks, 'expert', split_axis=0, concat_axis=0, tiled=True,...]
    ppermute x24 -> x20, waiting for transfers between devices: 86.7 us -> 72.5 us  [plane_move(): return lax.ppermute(array, 'expert', [(i, i ^ bit) for i in range(devices)])]
    unnamed x77 -> x125, local copies, waits for them, and re-layouts: 2.66 us -> 16.6 us
    dot_general x62 -> x48, matrix products: 62.5 us -> 75.7 us  [dot(): return lax.dot_general(a, b, (dims, ((), ())), preferred_element_type=F32)]
    ppermute x24 -> x20, starting transfers between devices: 30.2 us -> 22 us  [plane_move(): return lax.ppermute(array, 'expert', [(i, i ^ bit) for i in range(devices)])]
    concatenate x2 -> x7, other arithmetic: 3.25 us -> 8.93 us  [the longest x2 4.69 us: for_tokens(): blocks = jnp.concatenate(blocks, axis=1)]
    broadcast_in_dim x3 -> x1, other arithmetic: 5.43 us -> 1.56 us  [body(): return (a_next[None], b_next[None], up_grad[None], down_grad[None])]
    slice x12 -> x7, local copies, waits for them, and re-layouts: 6.72 us -> 8.1 us  [the longest x3 3.78 us: to_diagonal(): from_x[:cut]]
  transfers between devices with their start and end apart: 33 -> 29, of which waited for: 13 -> 13; matrix products, arithmetic and copies ran while one was open for 22% -> 32% of each run, Pallas kernels for 0% -> 0%
where the time goes in v3:
time: 293 us; the launch traced here: 291 us
  waiting for transfers between devices  122 us (42%)
  matrix products  75.7 us (26%)
  starting transfers between devices  46 us (16%)
  local copies, waits for them, and re-layouts  28.4 us (10%)
  other arithmetic  17.6 us (6%)
    dot_general x48, matrix products, dot(): return lax.dot_general(a, b, (dims, ((), ())), preferred_element_type=F32)  75.7 us
    ppermute x20, waiting for transfers between devices, plane_move(): return lax.ppermute(array, 'expert', [(i, i ^ bit) for i in range(devices)])  72.5 us
    all_to_all x5, waiting for transfers between devices, depth_exchange(): lax.all_to_all(blocks, 'expert', split_axis=0, concat_axis=0, tiled=True,...  48.4 us
    all_to_all x5, starting transfers between devices, depth_exchange(): lax.all_to_all(blocks, 'expert', split_axis=0, concat_axis=0, tiled=True,...  23.1 us
    ppermute x20, starting transfers between devices, plane_move(): return lax.ppermute(array, 'expert', [(i, i ^ bit) for i in range(devices)])  22 us
    unnamed x125, local copies, waits for them, and re-layouts  16.6 us
  transfers between devices with their start and end apart: 29, of which 13 were waited for; matrix products, arithmetic and copies ran while one was open for 32% of the time, Pallas kernels for 0%

profile of v3, /device:TPU:0, one launch (start us, length us, event | category | flops | bytes accessed | tf_op | source)
XLA Modules:
  0.0 290.8 jit_solution(4594239799606765812)
XLA Ops:
  7.1 5.9 %all-to-all-start = ((bf16[4,40,3584]{2,1,0:T(8,128)(2,1)}), bf16[4,40,3584]{2,1,0:T(8,128)(2,1)S(1)}, u32[]{:S(2)}, u32[]{:S(2)}) async-start(bf16[4,40,3584]{2,1,0:T(8,128)(2,1)} %bitcast.11), calls=%async_computation | async-start | bytes 2293760 | tf_op jit(solution)/shard_map/all_to_all | solution.py:32
  17.0 24.5 %all-to-all-done = bf16[4,40,3584]{2,1,0:T(8,128)(2,1)S(1)} async-done(((bf16[4,40,3584]{2,1,0:T(8,128)(2,1)}), bf16[4,40,3584]{2,1,0:T(8,128)(2,1)S(1)}, u32[]{:S(2)}, u32[]{:S(2)}) %all-to-all-start) | async-done | bytes 1146912 | tf_op jit(solution)/shard_map/all_to_all | solution.py:32
  42.8 4.3 %all-to-all-start.1 = ((bf16[4,40,3584]{2,1,0:T(8,128)(2,1)}), bf16[4,40,3584]{2,1,0:T(8,128)(2,1)}, u32[]{:S(2)}, u32[]{:S(2)}) async-start(bf16[4,40,3584]{2,1,0:T(8,128)(2,1)} %bitcast.10), calls=%async_computation.1 | async-start | bytes 2293760 | tf_op jit(solution)/shard_map/all_to_all | solution.py:32
  57.8 17.0 %all-to-all-done.1 = bf16[4,40,3584]{2,1,0:T(8,128)(2,1)} async-done(((bf16[4,40,3584]{2,1,0:T(8,128)(2,1)}), bf16[4,40,3584]{2,1,0:T(8,128)(2,1)}, u32[]{:S(2)}, u32[]{:S(2)}) %all-to-all-start.1) | async-done | bytes 1146912 | tf_op jit(solution)/shard_map/all_to_all | solution.py:32
  74.8 2.7 convolution_convert_fusion.6
  90.2 4.6 %all-to-all-start.2 = ((bf16[4,40,3584]{2,1,0:T(8,128)(2,1)}), bf16[4,40,3584]{2,1,0:T(8,128)(2,1)}, u32[]{:S(2)}, u32[]{:S(2)}) async-start(bf16[4,40,3584]{2,1,0:T(8,128)(2,1)} %bitcast.218), calls=%async_computation.2 | async-start | bytes 2293760 | tf_op jit(solution)/shard_map/all_to_all | solution.py:32
  98.7 20.0 %collective-permute-done.6 = bf16[64,3584]{1,0:T(8,128)(2,1)S(1)} collective-permute-done((bf16[64,3584]{1,0:T(8,128)(2,1)}, bf16[64,3584]{1,0:T(8,128)(2,1)S(1)}, u32[]{:S(2)}, u32[]{:S(2)}) %collective-permute-start.6) | collective-permute-done | bytes 458784 | tf_op jit(solution)/shard_map/ppermute | solution.py:25
  139.9 15.3 %collective-permute-done.9 = bf16[272,1792]{1,0:T(8,128)(2,1)} collective-permute-done((bf16[272,1792]{1,0:T(8,128)(2,1)}, bf16[272,1792]{1,0:T(8,128)(2,1)}, u32[]{:S(2)}, u32[]{:S(2)}) %collective-permute-start.9) | collective-permute-done | bytes 974880 | tf_op jit(solution)/shard_map/ppermute | solution.py:25
  155.2 4.3 %collective-permute-done.10 = bf16[272,1792]{1,0:T(8,128)(2,1)} collective-permute-done((bf16[272,1792]{1,0:T(8,128)(2,1)}, bf16[272,1792]{1,0:T(8,128)(2,1)}, u32[]{:S(2)}, u32[]{:S(2)}) %collective-permute-start.10) | collective-permute-done | bytes 974880 | tf_op jit(solution)/shard_map/ppermute | solution.py:25
  169.7 10.7 %collective-permute-done.14 = bf16[136,3584]{1,0:T(8,128)(2,1)S(1)} collective-permute-done((bf16[136,3584]{1,0:T(8,128)(2,1)S(1)}, bf16[136,3584]{1,0:T(8,128)(2,1)S(1)}, u32[]{:S(2)}, u32[]{:S(2)}) %collective-permute-start.14) | collective-permute-done | bytes 974880 | tf_op jit(solution)/shard_map/ppermute | solution.py:25
  197.1 6.7 %collective-permute-done.16 = bf16[64,3584]{1,0:T(8,128)(2,1)S(1)} collective-permute-done((bf16[64,3584]{1,0:T(8,128)(2,1)S(1)}, bf16[64,3584]{1,0:T(8,128)(2,1)S(1)}, u32[]{:S(2)}, u32[]{:S(2)}) %collective-permute-start.16) | collective-permute-done | bytes 458784 | tf_op jit(solution)/shard_map/ppermute | solution.py:25
  207.9 2.6 convolution_convert_fusion.11
  210.4 2.6 convolution_convert_fusion.10
  226.2 4.6 %all-to-all-start.3 = ((bf16[4,40,3584]{2,1,0:T(8,128)(2,1)}), bf16[4,40,3584]{2,1,0:T(8,128)(2,1)}, u32[]{:S(2)}, u32[]{:S(2)}) async-start(bf16[4,40,3584]{2,1,0:T(8,128)(2,1)} %bitcast.219), calls=%async_computation.3 | async-start | bytes 2293760 | tf_op jit(solution)/shard_map/all_to_all | solution.py:32
  230.8 8.8 %collective-permute-done.20 = bf16[272,1792]{1,0:T(8,128)(2,1)} collective-permute-done((bf16[272,1792]{1,0:T(8,128)(2,1)}, bf16[272,1792]{1,0:T(8,128)(2,1)}, u32[]{:S(2)}, u32[]{:S(2)}) %collective-permute-start.20) | collective-permute-done | bytes 974880 | tf_op jit(solution)/shard_map/ppermute | solution.py:25
  242.3 2.7 collective-permute-done.22
  247.3 2.5 collective-permute-start.23
  251.7 2.6 convolution_convert_fusion.9
  254.3 2.6 collective-permute-done.23
  256.9 2.7 convolution_convert_fusion.8
  262.0 3.7 %all-to-all-start.4 = ((bf16[4,40,3584]{2,1,0:T(8,128)(2,1)}), bf16[4,40,3584]{2,1,0:T(8,128)(2,1)S(1)}, u32[]{:S(2)}, u32[]{:S(2)}) async-start(bf16[4,40,3584]{2,1,0:T(8,128)(2,1)} %bitcast.30), calls=%async_computation.4 | async-start | bytes 2293760 | tf_op jit(solution)/shard_map/all_to_all | solution.py:32
  270.2 5.0 %fusion.2 = bf16[1,256,3584]{2,1,0:T(8,128)(2,1)} fusion(bf16[544,256]{1,0:T(8,128)(2,1)S(1)} %get-tuple-element.64, bf16[544,3584]{1,0:T(8,128)(2,1)} %constant_dynamic-update-slice_fusion.12), kind=kOutput, calls=%fused_computation.5 | convolution fusion | flops 999161856 | bytes 6012928 | tf_op jit(solution)/shard_map/dot_general | solution.py:12
  275.2 5.0 %fusion.1 = bf16[1,3584,256]{2,1,0:T(8,128)(2,1)} fusion(bf16[544,3584]{1,0:T(8,128)(2,1)} %constant_dynamic-update-slice_fusion, bf16[544,256]{1,0:T(8,128)(2,1)S(1)} %copy-done.52), kind=kOutput, calls=%fused_computation.4 | convolution fusion | flops 999161856 | bytes 6012928 | tf_op jit(solution)/shard_map/dot_general | solution.py:12
  280.2 6.9 %all-to-all-done.4 = bf16[4,40,3584]{2,1,0:T(8,128)(2,1)S(1)} async-done(((bf16[4,40,3584]{2,1,0:T(8,128)(2,1)}), bf16[4,40,3584]{2,1,0:T(8,128)(2,1)S(1)}, u32[]{:S(2)}, u32[]{:S(2)}) %all-to-all-start.4) | async-done | bytes 1146912 | tf_op jit(solution)/shard_map/all_to_all | solution.py:32
  (257 shorter events, 121.3 us)
Async XLA Ops:
  0.6 14.0 %collective-permute-start.1 = (bf16[128,3584]{1,0:T(8,128)(2,1)}, bf16[128,3584]{1,0:T(8,128)(2,1)S(1)}, u32[]{:S(2)}, u32[]{:S(2)}) collective-permute-start(bf16[128,3584]{1,0:T(8,128)(2,1)} %bitcast.231), channel_id=1, source_target_pairs={{0,16},{16,0},{1,17},{17,1},{2,18},{18,2},{3,19},{19,3},{4,20},{20... | collective-permute-start | bytes 2752520 | tf_op jit(solution)/shard_map/ppermute | solution.py:20
  7.1 34.4 %all-to-all-start = ((bf16[4,40,3584]{2,1,0:T(8,128)(2,1)}), bf16[4,40,3584]{2,1,0:T(8,128)(2,1)S(1)}, u32[]{:S(2)}, u32[]{:S(2)}) async-start(bf16[4,40,3584]{2,1,0:T(8,128)(2,1)} %bitcast.11), calls=%async_computation | async-start | bytes 2293760 | tf_op jit(solution)/shard_map/all_to_all | solution.py:32
  42.8 31.9 %all-to-all-start.1 = ((bf16[4,40,3584]{2,1,0:T(8,128)(2,1)}), bf16[4,40,3584]{2,1,0:T(8,128)(2,1)}, u32[]{:S(2)}, u32[]{:S(2)}) async-start(bf16[4,40,3584]{2,1,0:T(8,128)(2,1)} %bitcast.10), calls=%async_computation.1 | async-start | bytes 2293760 | tf_op jit(solution)/shard_map/all_to_all | solution.py:32
  50.0 27.5 %collective-permute-start.4 = (bf16[136,3584]{1,0:T(8,128)(2,1)}, bf16[136,3584]{1,0:T(8,128)(2,1)}, u32[]{:S(2)}, u32[]{:S(2)}) collective-permute-start(bf16[136,3584]{1,0:T(8,128)(2,1)} %convolution_convert_fusion.7), channel_id=1, source_target_pairs={{0,2},{1,3},{2,0},{3,1},{4,6},{5,7},{6,4},{7,5},{8,10},{9,11},{10,... | collective-permute-start | bytes 2924552 | tf_op jit(solution)/shard_map/ppermute | solution.py:25
  51.5 26.0 %collective-permute-start.3 = (bf16[136,3584]{1,0:T(8,128)(2,1)}, bf16[136,3584]{1,0:T(8,128)(2,1)}, u32[]{:S(2)}, u32[]{:S(2)}) collective-permute-start(bf16[136,3584]{1,0:T(8,128)(2,1)} %convolution_convert_fusion.7), channel_id=1, source_target_pairs={{0,1},{1,0},{2,3},{3,2},{4,5},{5,4},{6,7},{7,6},{8,9},{9,8},{10,11... | collective-permute-start | bytes 2924552 | tf_op jit(solution)/shard_map/ppermute | solution.py:25
  85.0 36.8 %collective-permute-start.8 = (bf16[136,3584]{1,0:T(8,128)(2,1)}, bf16[136,3584]{1,0:T(8,128)(2,1)}, u32[]{:S(2)}, u32[]{:S(2)}) collective-permute-start(bf16[136,3584]{1,0:T(8,128)(2,1)} %convolution_convert_fusion.6), channel_id=1, source_target_pairs={{0,2},{1,3},{2,0},{3,1},{4,6},{5,7},{6,4},{7,5},{8,10},{9,11},{10,... | collective-permute-start | bytes 2924552 | tf_op jit(solution)/shard_map/ppermute | solution.py:25
  86.5 35.3 %collective-permute-start.7 = (bf16[136,3584]{1,0:T(8,128)(2,1)}, bf16[136,3584]{1,0:T(8,128)(2,1)}, u32[]{:S(2)}, u32[]{:S(2)}) collective-permute-start(bf16[136,3584]{1,0:T(8,128)(2,1)} %convolution_convert_fusion.6), channel_id=1, source_target_pairs={{0,1},{1,0},{2,3},{3,2},{4,5},{5,4},{6,7},{7,6},{8,9},{9,8},{10,11... | collective-permute-start | bytes 2924552 | tf_op jit(solution)/shard_map/ppermute | solution.py:25
  90.2 48.0 %all-to-all-start.2 = ((bf16[4,40,3584]{2,1,0:T(8,128)(2,1)}), bf16[4,40,3584]{2,1,0:T(8,128)(2,1)}, u32[]{:S(2)}, u32[]{:S(2)}) async-start(bf16[4,40,3584]{2,1,0:T(8,128)(2,1)} %bitcast.218), calls=%async_computation.2 | async-start | bytes 2293760 | tf_op jit(solution)/shard_map/all_to_all | solution.py:32
  94.8 23.9 %collective-permute-start.6 = (bf16[64,3584]{1,0:T(8,128)(2,1)}, bf16[64,3584]{1,0:T(8,128)(2,1)S(1)}, u32[]{:S(2)}, u32[]{:S(2)}) collective-permute-start(bf16[64,3584]{1,0:T(8,128)(2,1)} %slice.86), channel_id=1, source_target_pairs={{0,1},{1,0},{2,3},{3,2},{4,5},{5,4},{6,7},{7,6},{8,9},{9,8},{10,11... | collective-permute-start | bytes 1376264 | tf_op jit(solution)/shard_map/ppermute | solution.py:25
  95.4 23.8 %collective-permute-start.5 = (bf16[72,3584]{1,0:T(8,128)(2,1)S(1)}, bf16[72,3584]{1,0:T(8,128)(2,1)S(1)}, u32[]{:S(2)}, u32[]{:S(2)}) collective-permute-start(bf16[72,3584]{1,0:T(8,128)(2,1)S(1)} %slice.85), channel_id=1, source_target_pairs={{0,2},{1,3},{2,0},{3,1},{4,6},{5,7},{6,4},{7,5},{8,10},{9,11},{10,... | collective-permute-start | bytes 1548296 | tf_op jit(solution)/shard_map/ppermute | solution.py:25
  123.6 46.1 %collective-permute-start.12 = (bf16[64,3584]{1,0:T(8,128)(2,1)}, bf16[64,3584]{1,0:T(8,128)(2,1)}, u32[]{:S(2)}, u32[]{:S(2)}) collective-permute-start(bf16[64,3584]{1,0:T(8,128)(2,1)} %slice.91), channel_id=1, source_target_pairs={{0,1},{1,0},{2,3},{3,2},{4,5},{5,4},{6,7},{7,6},{8,9},{9,8},{10,11... | collective-permute-start | bytes 1376264 | tf_op jit(solution)/shard_map/ppermute | solution.py:25
  126.9 42.8 %collective-permute-start.11 = (bf16[72,3584]{1,0:T(8,128)(2,1)}, bf16[72,3584]{1,0:T(8,128)(2,1)S(1)}, u32[]{:S(2)}, u32[]{:S(2)}) collective-permute-start(bf16[72,3584]{1,0:T(8,128)(2,1)} %slice.90), channel_id=1, source_target_pairs={{0,2},{1,3},{2,0},{3,1},{4,6},{5,7},{6,4},{7,5},{8,10},{9,11},{10,... | collective-permute-start | bytes 1548296 | tf_op jit(solution)/shard_map/ppermute | solution.py:25
  127.9 27.2 %collective-permute-start.9 = (bf16[272,1792]{1,0:T(8,128)(2,1)}, bf16[272,1792]{1,0:T(8,128)(2,1)}, u32[]{:S(2)}, u32[]{:S(2)}) collective-permute-start(bf16[272,1792]{1,0:T(8,128)(2,1)} %get-tuple-element.31), channel_id=1, source_target_pairs={{0,1},{1,0},{2,3},{3,2},{4,5},{5,4},{6,7},{7,6},{8,9},{9,8},{10,11... | collective-permute-start | bytes 2924552 | tf_op jit(solution)/shard_map/ppermute | solution.py:25
  128.5 30.9 %collective-permute-start.10 = (bf16[272,1792]{1,0:T(8,128)(2,1)}, bf16[272,1792]{1,0:T(8,128)(2,1)}, u32[]{:S(2)}, u32[]{:S(2)}) collective-permute-start(bf16[272,1792]{1,0:T(8,128)(2,1)} %get-tuple-element.32), channel_id=1, source_target_pairs={{0,2},{1,3},{2,0},{3,1},{4,6},{5,7},{6,4},{7,5},{8,10},{9,11},{10,... | collective-permute-start | bytes 2924552 | tf_op jit(solution)/shard_map/ppermute | solution.py:25
  160.1 20.3 %collective-permute-start.14 = (bf16[136,3584]{1,0:T(8,128)(2,1)S(1)}, bf16[136,3584]{1,0:T(8,128)(2,1)S(1)}, u32[]{:S(2)}, u32[]{:S(2)}) collective-permute-start(bf16[136,3584]{1,0:T(8,128)(2,1)S(1)} %convolution_convert_fusion.5), channel_id=1, source_target_pairs={{0,2},{1,3},{2,0},{3,1},{4,6},{5,7},{6,4},{7,5},{8,10},{9,11},{10,... | collective-permute-start | bytes 2924552 | tf_op jit(solution)/shard_map/ppermute | solution.py:25
  161.5 20.2 %collective-permute-start.13 = (bf16[136,3584]{1,0:T(8,128)(2,1)S(1)}, bf16[136,3584]{1,0:T(8,128)(2,1)S(1)}, u32[]{:S(2)}, u32[]{:S(2)}) collective-permute-start(bf16[136,3584]{1,0:T(8,128)(2,1)S(1)} %convolution_convert_fusion.5), channel_id=1, source_target_pairs={{0,1},{1,0},{2,3},{3,2},{4,5},{5,4},{6,7},{7,6},{8,9},{9,8},{10,11... | collective-permute-start | bytes 2924552 | tf_op jit(solution)/shard_map/ppermute | solution.py:25
  190.3 13.5 %collective-permute-start.16 = (bf16[64,3584]{1,0:T(8,128)(2,1)S(1)}, bf16[64,3584]{1,0:T(8,128)(2,1)S(1)}, u32[]{:S(2)}, u32[]{:S(2)}) collective-permute-start(bf16[64,3584]{1,0:T(8,128)(2,1)S(1)} %slice.93), channel_id=1, source_target_pairs={{0,1},{1,0},{2,3},{3,2},{4,5},{5,4},{6,7},{7,6},{8,9},{9,8},{10,11... | collective-permute-start | bytes 1376264 | tf_op jit(solution)/shard_map/ppermute | solution.py:25
  191.0 16.9 %collective-permute-start.17 = (bf16[136,1792]{1,0:T(8,128)(2,1)S(1)}, bf16[136,1792]{1,0:T(8,128)(2,1)}, u32[]{:S(2)}, u32[]{:S(2)}) collective-permute-start(bf16[136,1792]{1,0:T(8,128)(2,1)S(1)} %add_convert_fusion.6), channel_id=1, source_target_pairs={{0,2},{1,3},{2,0},{3,1},{4,6},{5,7},{6,4},{7,5},{8,10},{9,11},{10,... | collective-permute-start | bytes 1462280 | tf_op jit(solution)/shard_map/ppermute | solution.py:25
  191.5 18.9 %collective-permute-start.18 = (bf16[136,1792]{1,0:T(8,128)(2,1)}, bf16[136,1792]{1,0:T(8,128)(2,1)}, u32[]{:S(2)}, u32[]{:S(2)}) collective-permute-start(bf16[136,1792]{1,0:T(8,128)(2,1)} %add_convert_fusion.7), channel_id=1, source_target_pairs={{0,1},{1,0},{2,3},{3,2},{4,5},{5,4},{6,7},{7,6},{8,9},{9,8},{10,11... | collective-permute-start | bytes 1462280 | tf_op jit(solution)/shard_map/ppermute | solution.py:25
  193.0 22.4 %collective-permute-start.15 = (bf16[72,3584]{1,0:T(8,128)(2,1)}, bf16[72,3584]{1,0:T(8,128)(2,1)}, u32[]{:S(2)}, u32[]{:S(2)}) collective-permute-start(bf16[72,3584]{1,0:T(8,128)(2,1)} %slice.92), channel_id=1, source_target_pairs={{0,2},{1,3},{2,0},{3,1},{4,6},{5,7},{6,4},{7,5},{8,10},{9,11},{10,... | collective-permute-start | bytes 1548296 | tf_op jit(solution)/shard_map/ppermute | solution.py:25
  222.2 17.5 %collective-permute-start.20 = (bf16[272,1792]{1,0:T(8,128)(2,1)}, bf16[272,1792]{1,0:T(8,128)(2,1)}, u32[]{:S(2)}, u32[]{:S(2)}) collective-permute-start(bf16[272,1792]{1,0:T(8,128)(2,1)} %pad_maximum_fusion.4), channel_id=1, source_target_pairs={{0,1},{1,0},{2,3},{3,2},{4,5},{5,4},{6,7},{7,6},{8,9},{9,8},{10,11... | collective-permute-start | bytes 2924552 | tf_op jit(solution)/shard_map/ppermute | solution.py:25
  223.7 21.3 %collective-permute-start.22 = (bf16[272,1792]{1,0:T(8,128)(2,1)}, bf16[272,1792]{1,0:T(8,128)(2,1)}, u32[]{:S(2)}, u32[]{:S(2)}) collective-permute-start(bf16[272,1792]{1,0:T(8,128)(2,1)} %pad_maximum_fusion.5), channel_id=1, source_target_pairs={{0,2},{1,3},{2,0},{3,1},{4,6},{5,7},{6,4},{7,5},{8,10},{9,11},{10,... | collective-permute-start | bytes 2924552 | tf_op jit(solution)/shard_map/ppermute | solution.py:25
  226.2 35.8 %all-to-all-start.3 = ((bf16[4,40,3584]{2,1,0:T(8,128)(2,1)}), bf16[4,40,3584]{2,1,0:T(8,128)(2,1)}, u32[]{:S(2)}, u32[]{:S(2)}) async-start(bf16[4,40,3584]{2,1,0:T(8,128)(2,1)} %bitcast.219), calls=%async_computation.3 | async-start | bytes 2293760 | tf_op jit(solution)/shard_map/all_to_all | solution.py:32
  262.0 25.1 %all-to-all-start.4 = ((bf16[4,40,3584]{2,1,0:T(8,128)(2,1)}), bf16[4,40,3584]{2,1,0:T(8,128)(2,1)S(1)}, u32[]{:S(2)}, u32[]{:S(2)}) async-start(bf16[4,40,3584]{2,1,0:T(8,128)(2,1)} %bitcast.30), calls=%async_computation.4 | async-start | bytes 2293760 | tf_op jit(solution)/shard_map/all_to_all | solution.py:32
  (63 other events, 479.0 us)

commit v4 on v3

--- a/solution.py
+++ b/solution.py
@@ -80,14 +80,18 @@
     return dot(pick, rows).astype(BF16).reshape(layout.experts, layout.rows, rows.shape[1])
 
 
+def pack_rows(blocks, layout):
+    return dot(
+        packer(layout), blocks.reshape(layout.experts * layout.rows, blocks.shape[2])
+    ).astype(BF16)
+
+
 def across_planes(blocks, layout):
-    blocks = depth_exchange(blocks, layout.experts)
-    blocks = blocks.reshape(layout.experts * layout.rows, blocks.shape[2])
-    return dot(packer(layout), blocks).astype(BF16)
-
-
-def to_neighbours(mine, experts):
-    return plane_move(mine, experts, 1), plane_move(mine, experts, 2)
+    return pack_rows(depth_exchange(blocks, layout.experts), layout)
+
+
+def swap_pair(pair, experts):
+    return plane_move(pair[0], experts, 1), plane_move(pair[1], experts, 2)
 
 
 def to_diagonal(from_x, from_y, experts):
@@ -98,33 +102,15 @@
     )
 
 
-def first_parts(part):
-    return (
-        jnp.concatenate([part(3, 0).astype(BF16), part(1, 0).astype(BF16)], axis=0),
-        jnp.concatenate([part(3, 1).astype(BF16), part(2, 1).astype(BF16)], axis=0),
-    )
-
-
-def second_parts(part, got, rows):
-    return (
-        (part(1, 1) + got[1][:rows].astype(F32)).astype(BF16),
-        (part(2, 0) + got[0][:rows].astype(F32)).astype(BF16),
-    )
-
-
-def swap_pair(pair, experts):
-    return plane_move(pair[0], experts, 1), plane_move(pair[1], experts, 2)
-
-
-def totals(part, first, second, rows):
-    lo = part(0, 0) + first[0][rows:].astype(F32) + second[1].astype(F32)
-    hi = part(0, 1) + first[1][rows:].astype(F32) + second[0].astype(F32)
-    return lo.astype(BF16), hi.astype(BF16)
+def add(value, *got):
+    for term in got:
+        value = value + term.astype(F32)
+    return value.astype(BF16)
 
 
 def for_tokens(total, layout):
-    blocks = [dot(packer(layout), t, ((0,), (0,))).astype(BF16) for t in total]
-    blocks = jnp.concatenate(blocks, axis=1)
+    total = jnp.concatenate(total, axis=1)
+    blocks = dot(packer(layout), total, ((0,), (0,))).astype(BF16)
     return blocks.reshape(layout.experts, layout.rows, blocks.shape[1])
 
 
@@ -160,77 +146,120 @@
 
     a_float, _, a_normed = statistics(a_input[0])
     a_pick = selector(a_ids, layout, here)
-    a_mine = across_planes(select_rows(a_pick, a_normed, layout), layout)
+    a_mine = [
+        across_planes(select_rows(a_pick, a_normed[:, cols], layout), layout) for cols in halves
+    ]
+    a_x, a_y = [None, None], [None, None]
+    a_x[0], a_y[0] = swap_pair((a_mine[0], a_mine[0]), experts)
 
     b_float, b_scale, b_normed = statistics(b_x)
     b_pick = selector(b_ids, layout, here)
     b_send = select_rows(b_pick, b_normed, layout)
     b_send, a_mine = after((b_send, a_mine))
-    a_near = to_neighbours(a_mine, experts)
-    b_mine = across_planes(b_send, layout)
+    a_x[1], a_y[1] = swap_pair((a_mine[1], a_mine[1]), experts)
+    a_far = plane_move(a_x[0], experts, 2), plane_move(a_y[1], experts, 1)
+    b_got = depth_exchange(b_send, experts)
+
+    def forward_act(block):
+        hidden = dot(block[0], up[:half]) + dot(block[1], up[half:])
+        return (hidden * jax.nn.sigmoid(hidden)).astype(BF16)
+
+    a_act = [forward_act(v) for v in (a_mine, a_x, a_y, a_far)]
+
+    def a_part(j, h):
+        return dot(a_act[j], down[:, halves[h]])
+
+    a_first = tuple(
+        dot(jnp.concatenate([a_act[3], a_act[1 + h]], axis=0), down[:, halves[h]]).astype(BF16)
+        for h in range(2)
+    )
+    a_first, b_got = after((a_first, b_got))
+    a_first = swap_pair(a_first, experts)
+    b_mine = pack_rows(b_got, layout)
+    b_near = swap_pair((b_mine, b_mine), experts)
 
     b_gate = gate_of(b_normed, b_ids, cols_r)
     cot = (b_gate * b_c.astype(F32)).astype(BF16)
     c_send = select_rows(b_pick, cot, layout)
-    c_send, a_near, b_mine = after((c_send, a_near, b_mine))
+    c_send, b_mine = after((c_send, b_mine))
     c_mine = across_planes(c_send, layout)
-    a_far = to_diagonal(a_near[0], a_near[1], experts)
-    b_near = to_neighbours(b_mine, experts)
-
-    def forward_act(block):
-        hidden = dot(block, up)
-        return (hidden * jax.nn.sigmoid(hidden)).astype(BF16)
-
-    a_act = [forward_act(v) for v in (a_mine,) + a_near]
-    a_act.append(jnp.concatenate([forward_act(v) for v in a_far], axis=0))
-
-    def a_part(j, h):
-        return dot(a_act[j], down[:, halves[h]])
-
-    a_first = first_parts(a_part)
-    a_first, b_near = after((a_first, b_near))
-    a_first = swap_pair(a_first, experts)
+
+    a_second = (
+        add(a_part(1, 1), a_first[1][:rows]),
+        add(a_part(2, 0), a_first[0][:rows]),
+    )
+    a_second, b_near = after((a_second, b_near))
     b_far = to_diagonal(b_near[0], b_near[1], experts)
-    a_first, c_mine = after((a_first, c_mine))
-    c_near = to_neighbours(c_mine, experts)
-    a_second = second_parts(a_part, a_first, rows)
-    a_second, b_far, c_near = after((a_second, b_far, c_near))
+    a_second = swap_pair(a_second, experts)
+    c_mine, a_second = after((c_mine, a_second))
+    c_near = swap_pair((c_mine, c_mine), experts)
+    a_back = for_tokens(
+        [
+            add(a_part(0, 0), a_first[0][rows:], a_second[1]),
+            add(a_part(0, 1), a_first[1][rows:], a_second[0]),
+        ],
+        layout,
+    )
+    c_near, b_far, a_back = after((c_near, b_far, a_back))
     c_far = to_diagonal(c_near[0], c_near[1], experts)
-    a_second = swap_pair(a_second, experts)
-    a_back = for_tokens(totals(a_part, a_first, a_second, rows), layout)
-
-    act, hid_grad, score_grad = [], [], []
-    for block, cots in zip((b_mine,) + b_near + b_far, (c_mine,) + c_near + c_far):
+
+    def backward(block, cots):
         hidden = dot(block, up)
         score = dot(block, own_col)
         sigma = jax.nn.sigmoid(hidden)
         active = hidden * sigma
         act_grad = dot(cots, down, ((1,), (1,)))
-        act.append(active.astype(BF16))
-        hid_grad.append((act_grad * sigma * (1.0 + hidden * (1.0 - sigma))).astype(BF16))
+        hid_grad = (act_grad * sigma * (1.0 + hidden * (1.0 - sigma))).astype(BF16)
         term = jnp.sum(active * act_grad, axis=1, keepdims=True)
-        score_grad.append(term * jax.nn.sigmoid(-score))
-    parts_g = hid_grad[:3] + [jnp.concatenate(hid_grad[3:], axis=0)]
-    scores = score_grad[:3] + [jnp.concatenate(score_grad[3:], axis=0)]
-
-    def b_part(j, h):
-        cols = halves[h]
-        return dot(parts_g[j], up[cols], ((1,), (1,))) + scores[j] * col_row[:, cols]
-
-    b_first, a_back = after((first_parts(b_part), a_back))
-    b_first = swap_pair(b_first, experts)
+        return active.astype(BF16), hid_grad, term * jax.nn.sigmoid(-score)
+
+    done = [backward(v, w) for v, w in zip((b_mine,) + b_near, (c_mine,) + c_near)]
+    quarter = half // 2
+
+    def piece(c, side):
+        begin = c * half + side * quarter
+        return slice(begin, begin + quarter)
+
+    def b_part(j, c, side):
+        cols = piece(c, side)
+        return dot(done[j][1], up[cols], ((1,), (1,))) + done[j][2] * col_row[:, cols]
+
+    b_plain = [tuple(add(b_part(1 + side, c, side)) for side in range(2)) for c in range(2)]
+    b_plain = [swap_pair(pair, experts) for pair in b_plain]
+    ends = [backward(v, w) for v, w in zip(b_far, c_far)]
+    done.append(tuple(jnp.concatenate(pair, axis=0) for pair in zip(*ends)))
+
     a_gate = gate_of(a_normed, a_ids, cols_r)
     a_out = (a_float + a_gate * at_tokens(a_back, a_pick, layout)).astype(BF16)
     a_next = pipe_move(a_out, lambda i, n: i + 1)
-    b_second = swap_pair(second_parts(b_part, b_first, rows), experts)
-    b_back = for_tokens(totals(b_part, b_first, b_second, rows), layout)
-    normed_grad = at_tokens(b_back, b_pick, layout)
+
+    b_relay = [tuple(add(b_part(3, c, side)) for side in range(2)) for c in range(2)]
+    b_relay[0], b_plain[0] = after((b_relay[0], b_plain[0]))
+    b_relay = [swap_pair(pair, experts) for pair in b_relay]
+    b_second = [
+        swap_pair(
+            (
+                add(b_part(1, c, 1), b_relay[c][1]),
+                add(b_part(2, c, 0), b_relay[c][0]),
+            ),
+            experts,
+        )
+        for c in range(2)
+    ]
+    pieces = []
+    for c in range(2):
+        total = [
+            add(b_part(0, c, 0), b_plain[c][0], b_second[c][1]),
+            add(b_part(0, c, 1), b_plain[c][1], b_second[c][0]),
+        ]
+        pieces.append(at_tokens(for_tokens(total, layout), b_pick, layout))
+    normed_grad = jnp.concatenate(pieces, axis=1)
     along = jnp.sum(normed_grad * b_float, axis=-1, keepdims=True) / width
     feature_grad = b_scale * normed_grad - b_float * (b_scale * b_scale * b_scale) * along
     b_out = (b_c.astype(F32) + feature_grad).astype(BF16)
     b_next = pipe_move(b_out, lambda i, n: n - i)
 
-    acts, hids = jnp.concatenate(act, axis=0), jnp.concatenate(hid_grad, axis=0)
+    acts, hids = [jnp.concatenate([d[i] for d in done], axis=0) for i in range(2)]
     b_all = jnp.concatenate((b_mine,) + b_near + b_far, axis=0)
     c_all = jnp.concatenate((c_mine,) + c_near + c_far, axis=0)
     up_grad = dot(b_all, hids, ((0,), (0,))).astype(BF16)

time: 293 us -> 296 us (1.010)
  starting transfers between devices: 46 us -> 60.1 us
  waiting for transfers between devices: 122 us -> 115 us
  local copies, waits for them, and re-layouts: 28.4 us -> 22.8 us
  matrix products: 75.7 us -> 80.7 us
  other arithmetic: 17.6 us -> 13.5 us
    all_to_all x5 -> x7, waiting for transfers between devices: 48.4 us -> 29.2 us  [depth_exchange(): lax.all_to_all(blocks, 'expert', split_axis=0, concat_axis=0, tiled=True,...]
    ppermute x20 -> x30, waiting for transfers between devices: 72.5 us -> 86 us  [plane_move(): return lax.ppermute(array, 'expert', [(i, i ^ bit) for i in range(devices)])]
    all_to_all x5 -> x7, starting transfers between devices: 23.1 us -> 32.5 us  [depth_exchange(): lax.all_to_all(blocks, 'expert', split_axis=0, concat_axis=0, tiled=True,...]
    concatenate x7 -> x2, other arithmetic: 8.93 us -> 0.14 us  [the longest x1 0.1 us: body(): done.append(tuple((jnp.concatenate(pair, axis=0) for pair in zip(*ends))))]
    dot_general x48 -> x63, matrix products: 75.7 us -> 80.7 us  [dot(): return lax.dot_general(a, b, (dims, ((), ())), preferred_element_type=F32)]
    ppermute x20 -> x30, starting transfers between devices: 22 us -> 26.7 us  [plane_move(): return lax.ppermute(array, 'expert', [(i, i ^ bit) for i in range(devices)])]
    convert_element_type x0 -> x8, other arithmetic: none -> 4.31 us  [the longest x7 4.09 us: add(): return value.astype(BF16)]
  transfers between devices with their start and end apart: 29 -> 41, of which waited for: 13 -> 14; matrix products, arithmetic and copies ran while one was open for 32% -> 35% of each run, Pallas kernels for 0% -> 0%
where the time goes in v4:
time: 296 us; the launch traced here: 294 us
  waiting for transfers between devices  115 us (39%)
  matrix products  80.7 us (27%)
  starting transfers between devices  60.1 us (20%)
  local copies, waits for them, and re-layouts  22.8 us (8%)
  other arithmetic  13.5 us (5%)
    ppermute x30, waiting for transfers between devices, plane_move(): return lax.ppermute(array, 'expert', [(i, i ^ bit) for i in range(devices)])  86 us
    dot_general x63, matrix products, dot(): return lax.dot_general(a, b, (dims, ((), ())), preferred_element_type=F32)  80.7 us
    all_to_all x7, starting transfers between devices, depth_exchange(): lax.all_to_all(blocks, 'expert', split_axis=0, concat_axis=0, tiled=True,...  32.5 us
    all_to_all x7, waiting for transfers between devices, depth_exchange(): lax.all_to_all(blocks, 'expert', split_axis=0, concat_axis=0, tiled=True,...  29.2 us
    ppermute x30, starting transfers between devices, plane_move(): return lax.ppermute(array, 'expert', [(i, i ^ bit) for i in range(devices)])  26.7 us
    unnamed x125, local copies, waits for them, and re-layouts  13.8 us
  transfers between devices with their start and end apart: 41, of which 14 were waited for; matrix products, arithmetic and copies ran while one was open for 35% of the time, Pallas kernels for 0%

profile of v4, /device:TPU:0, one launch (start us, length us, event | category | flops | bytes accessed | tf_op | source)
XLA Modules:
  0.0 293.9 jit_solution(10625372472867355835)
XLA Ops:
  6.4 5.9 %all-to-all-start = ((bf16[4,40,1792]{2,1,0:T(8,128)(2,1)}), bf16[4,40,1792]{2,1,0:T(8,128)(2,1)S(1)}, u32[]{:S(2)}, u32[]{:S(2)}) async-start(bf16[4,40,1792]{2,1,0:T(8,128)(2,1)} %bitcast.10), calls=%async_computation | async-start | bytes 1146880 | tf_op jit(solution)/shard_map/all_to_all | solution.py:32
  15.7 12.7 %all-to-all-done = bf16[4,40,1792]{2,1,0:T(8,128)(2,1)S(1)} async-done(((bf16[4,40,1792]{2,1,0:T(8,128)(2,1)}), bf16[4,40,1792]{2,1,0:T(8,128)(2,1)S(1)}, u32[]{:S(2)}, u32[]{:S(2)}) %all-to-all-start) | async-done | bytes 573472 | tf_op jit(solution)/shard_map/all_to_all | solution.py:32
  28.5 3.5 %all-to-all-start.1 = ((bf16[4,40,1792]{2,1,0:T(8,128)(2,1)}), bf16[4,40,1792]{2,1,0:T(8,128)(2,1)S(1)}, u32[]{:S(2)}, u32[]{:S(2)}) async-start(bf16[4,40,1792]{2,1,0:T(8,128)(2,1)} %bitcast.14), calls=%async_computation.1 | async-start | bytes 1146880 | tf_op jit(solution)/shard_map/all_to_all | solution.py:32
  36.5 10.8 %all-to-all-done.1 = bf16[4,40,1792]{2,1,0:T(8,128)(2,1)S(1)} async-done(((bf16[4,40,1792]{2,1,0:T(8,128)(2,1)}), bf16[4,40,1792]{2,1,0:T(8,128)(2,1)S(1)}, u32[]{:S(2)}, u32[]{:S(2)}) %all-to-all-start.1) | async-done | bytes 573472 | tf_op jit(solution)/shard_map/all_to_all | solution.py:32
  53.0 4.3 %all-to-all-start.2 = ((bf16[4,40,3584]{2,1,0:T(8,128)(2,1)}), bf16[4,40,3584]{2,1,0:T(8,128)(2,1)}, u32[]{:S(2)}, u32[]{:S(2)}) async-start(bf16[4,40,3584]{2,1,0:T(8,128)(2,1)} %bitcast.241), calls=%async_computation.2 | async-start | bytes 2293760 | tf_op jit(solution)/shard_map/all_to_all | solution.py:32
  63.3 2.7 convolution_convert_fusion.4
  72.6 8.2 %collective-permute-done.6 = bf16[136,1792]{1,0:T(8,128)(2,1)S(1)} collective-permute-done((bf16[136,1792]{1,0:T(8,128)(2,1)}, bf16[136,1792]{1,0:T(8,128)(2,1)S(1)}, u32[]{:S(2)}, u32[]{:S(2)}) %collective-permute-start.6) | collective-permute-done | bytes 487456 | tf_op jit(solution)/shard_map/ppermute | solution.py:25
  89.5 4.8 %all-to-all-start.3 = ((bf16[4,40,3584]{2,1,0:T(8,128)(2,1)}), bf16[4,40,3584]{2,1,0:T(8,128)(2,1)}, u32[]{:S(2)}, u32[]{:S(2)}) async-start(bf16[4,40,3584]{2,1,0:T(8,128)(2,1)} %bitcast.240), calls=%async_computation.3 | async-start | bytes 2293760 | tf_op jit(solution)/shard_map/all_to_all | solution.py:32
  100.1 8.9 %collective-permute-done.9 = bf16[272,1792]{1,0:T(8,128)(2,1)} collective-permute-done((bf16[272,1792]{1,0:T(8,128)(2,1)}, bf16[272,1792]{1,0:T(8,128)(2,1)}, u32[]{:S(2)}, u32[]{:S(2)}) %collective-permute-start.9) | collective-permute-done | bytes 974880 | tf_op jit(solution)/shard_map/ppermute | solution.py:25
  111.2 20.7 %collective-permute-done.10 = bf16[272,1792]{1,0:T(8,128)(2,1)S(1)} collective-permute-done((bf16[272,1792]{1,0:T(8,128)(2,1)}, bf16[272,1792]{1,0:T(8,128)(2,1)S(1)}, u32[]{:S(2)}, u32[]{:S(2)}) %collective-permute-start.10) | collective-permute-done | bytes 974880 | tf_op jit(solution)/shard_map/ppermute | solution.py:25
  151.0 4.4 %collective-permute-done.13 = bf16[136,1792]{1,0:T(8,128)(2,1)} collective-permute-done((bf16[136,1792]{1,0:T(8,128)(2,1)}, bf16[136,1792]{1,0:T(8,128)(2,1)}, u32[]{:S(2)}, u32[]{:S(2)}) %collective-permute-start.13) | collective-permute-done | bytes 487456 | tf_op jit(solution)/shard_map/ppermute | solution.py:25
  167.5 11.4 %collective-permute-done.16 = bf16[136,3584]{1,0:T(8,128)(2,1)S(1)} collective-permute-done((bf16[136,3584]{1,0:T(8,128)(2,1)S(1)}, bf16[136,3584]{1,0:T(8,128)(2,1)S(1)}, u32[]{:S(2)}, u32[]{:S(2)}) %collective-permute-start.16) | collective-permute-done | bytes 974880 | tf_op jit(solution)/shard_map/ppermute | solution.py:25
  189.8 4.5 %all-to-all-start.4 = ((bf16[4,40,3584]{2,1,0:T(8,128)(2,1)}), bf16[4,40,3584]{2,1,0:T(8,128)(2,1)}, u32[]{:S(2)}, u32[]{:S(2)}) async-start(bf16[4,40,3584]{2,1,0:T(8,128)(2,1)} %bitcast.246), calls=%async_computation.4 | async-start | bytes 2293760 | tf_op jit(solution)/shard_map/all_to_all | solution.py:32
  207.9 9.6 %collective-permute-done.21 = bf16[64,3584]{1,0:T(8,128)(2,1)S(1)} collective-permute-done((bf16[64,3584]{1,0:T(8,128)(2,1)S(1)}, bf16[64,3584]{1,0:T(8,128)(2,1)S(1)}, u32[]{:S(2)}, u32[]{:S(2)}) %collective-permute-start.21) | collective-permute-done | bytes 458784 | tf_op jit(solution)/shard_map/ppermute | solution.py:25
  227.9 5.1 %fusion.1 = bf16[1,3584,256]{2,1,0:T(8,128)(2,1)} fusion(bf16[544,3584]{1,0:T(8,128)(2,1)} %constant_dynamic-update-slice_fusion, bf16[544,256]{1,0:T(8,128)(2,1)S(1)} %get-tuple-element.56), kind=kOutput, calls=%fused_computation.4 | convolution fusion | flops 999161856 | bytes 6012928 | tf_op jit(solution)/shard_map/dot_general | solution.py:12
  234.9 6.7 %collective-permute-done.26 = bf16[136,896]{1,0:T(8,128)(2,1)S(1)} collective-permute-done((bf16[136,896]{1,0:T(8,128)(2,1)S(1)}, bf16[136,896]{1,0:T(8,128)(2,1)S(1)}, u32[]{:S(2)}, u32[]{:S(2)}) %collective-permute-start.26) | collective-permute-done | bytes 243744 | tf_op jit(solution)/shard_map/ppermute | solution.py:25
  241.9 5.8 %collective-permute-done.25 = bf16[136,896]{1,0:T(8,128)(2,1)S(1)} collective-permute-done((bf16[136,896]{1,0:T(8,128)(2,1)S(1)}, bf16[136,896]{1,0:T(8,128)(2,1)S(1)}, u32[]{:S(2)}, u32[]{:S(2)}) %collective-permute-start.25) | collective-permute-done | bytes 243744 | tf_op jit(solution)/shard_map/ppermute | solution.py:25
  248.4 5.5 %collective-permute-done.27 = bf16[136,896]{1,0:T(8,128)(2,1)S(1)} collective-permute-done((bf16[136,896]{1,0:T(8,128)(2,1)S(1)}, bf16[136,896]{1,0:T(8,128)(2,1)S(1)}, u32[]{:S(2)}, u32[]{:S(2)}) %collective-permute-start.27) | collective-permute-done | bytes 243744 | tf_op jit(solution)/shard_map/ppermute | solution.py:25
  255.2 4.4 %all-to-all-start.5 = ((bf16[4,40,1792]{2,1,0:T(8,128)(2,1)}), bf16[4,40,1792]{2,1,0:T(8,128)(2,1)S(1)}, u32[]{:S(2)}, u32[]{:S(2)}) async-start(bf16[4,40,1792]{2,1,0:T(8,128)(2,1)} %bitcast.247), calls=%async_computation.5 | async-start | bytes 1146880 | tf_op jit(solution)/shard_map/all_to_all | solution.py:32
  262.4 4.8 %collective-permute-done.30 = bf16[136,896]{1,0:T(8,128)(2,1)S(1)} collective-permute-done((bf16[136,896]{1,0:T(8,128)(2,1)S(1)}, bf16[136,896]{1,0:T(8,128)(2,1)S(1)}, u32[]{:S(2)}, u32[]{:S(2)}) %collective-permute-start.30) | collective-permute-done | bytes 243744 | tf_op jit(solution)/shard_map/ppermute | solution.py:25
  269.5 2.9 all-to-all-done.5
  272.4 5.2 %all-to-all-start.6 = ((bf16[4,40,1792]{2,1,0:T(8,128)(2,1)}), bf16[4,40,1792]{2,1,0:T(8,128)(2,1)S(1)}, u32[]{:S(2)}, u32[]{:S(2)}) async-start(bf16[4,40,1792]{2,1,0:T(8,128)(2,1)} %bitcast.38), calls=%async_computation.6 | async-start | bytes 1146880 | tf_op jit(solution)/shard_map/all_to_all | solution.py:32
  277.6 5.0 %fusion.2 = bf16[1,256,3584]{2,1,0:T(8,128)(2,1)} fusion(bf16[544,256]{1,0:T(8,128)(2,1)S(1)} %get-tuple-element.70, bf16[544,3584]{1,0:T(8,128)(2,1)} %constant_dynamic-update-slice_fusion.12), kind=kOutput, calls=%fused_computation.5 | convolution fusion | flops 999161856 | bytes 6012928 | tf_op jit(solution)/shard_map/dot_general | solution.py:12
  285.6 2.8 all-to-all-done.6
  (298 shorter events, 131.9 us)
Async XLA Ops:
  1.4 30.6 %collective-permute-start = (bf16[128,1]{0,1:T(2,128)(2,1)S(1)}, bf16[128,1]{0,1:T(2,128)(2,1)S(1)}, u32[]{:S(2)}, u32[]{:S(2)}) collective-permute-start(bf16[128,1]{0,1:T(2,128)(2,1)S(1)} %convert_bitcast_fusion.1), channel_id=1, source_target_pairs={{0,16},{16,0},{1,17},{17,1},{2,18},{18,2},{3,19},{19,3},{4,20},{20... | collective-permute-start | bytes 776 | tf_op jit(solution)/shard_map/ppermute | solution.py:20
  6.4 22.1 %all-to-all-start = ((bf16[4,40,1792]{2,1,0:T(8,128)(2,1)}), bf16[4,40,1792]{2,1,0:T(8,128)(2,1)S(1)}, u32[]{:S(2)}, u32[]{:S(2)}) async-start(bf16[4,40,1792]{2,1,0:T(8,128)(2,1)} %bitcast.10), calls=%async_computation | async-start | bytes 1146880 | tf_op jit(solution)/shard_map/all_to_all | solution.py:32
  12.3 35.4 %collective-permute-start.1 = (bf16[128,3584]{1,0:T(8,128)(2,1)}, bf16[128,3584]{1,0:T(8,128)(2,1)S(1)}, u32[]{:S(2)}, u32[]{:S(2)}) collective-permute-start(bf16[128,3584]{1,0:T(8,128)(2,1)} %bitcast.258), channel_id=1, source_target_pairs={{0,16},{16,0},{1,17},{17,1},{2,18},{18,2},{3,19},{19,3},{4,20},{20... | collective-permute-start | bytes 2752520 | tf_op jit(solution)/shard_map/ppermute | solution.py:20
  12.5 50.8 %collective-permute-start.2 = (bf16[128,3584]{1,0:T(8,128)(2,1)}, bf16[128,3584]{1,0:T(8,128)(2,1)}, u32[]{:S(2)}, u32[]{:S(2)}) collective-permute-start(bf16[128,3584]{1,0:T(8,128)(2,1)} %bitcast.259), channel_id=1, source_target_pairs={{0,16},{16,0},{1,17},{17,1},{2,18},{18,2},{3,19},{19,3},{4,20},{20... | collective-permute-start | bytes 2752520 | tf_op jit(solution)/shard_map/ppermute | solution.py:20
  33.5 37.8 %collective-permute-start.8 = (bf16[136,1792]{1,0:T(8,128)(2,1)}, bf16[136,1792]{1,0:T(8,128)(2,1)}, u32[]{:S(2)}, u32[]{:S(2)}) collective-permute-start(bf16[136,1792]{1,0:T(8,128)(2,1)} %convolution_convert_fusion.14), channel_id=1, source_target_pairs={{0,2},{1,3},{2,0},{3,1},{4,6},{5,7},{6,4},{7,5},{8,10},{9,11},{10,... | collective-permute-start | bytes 1462280 | tf_op jit(solution)/shard_map/ppermute | solution.py:25
  35.0 31.0 %collective-permute-start.3 = (bf16[136,1792]{1,0:T(8,128)(2,1)}, bf16[136,1792]{1,0:T(8,128)(2,1)}, u32[]{:S(2)}, u32[]{:S(2)}) collective-permute-start(bf16[136,1792]{1,0:T(8,128)(2,1)} %convolution_convert_fusion.14), channel_id=1, source_target_pairs={{0,1},{1,0},{2,3},{3,2},{4,5},{5,4},{6,7},{7,6},{8,9},{9,8},{10,11... | collective-permute-start | bytes 1462280 | tf_op jit(solution)/shard_map/ppermute | solution.py:25
  53.0 31.2 %all-to-all-start.2 = ((bf16[4,40,3584]{2,1,0:T(8,128)(2,1)}), bf16[4,40,3584]{2,1,0:T(8,128)(2,1)}, u32[]{:S(2)}, u32[]{:S(2)}) async-start(bf16[4,40,3584]{2,1,0:T(8,128)(2,1)} %bitcast.241), calls=%async_computation.2 | async-start | bytes 2293760 | tf_op jit(solution)/shard_map/all_to_all | solution.py:32
  84.2 24.8 %collective-permute-start.9 = (bf16[272,1792]{1,0:T(8,128)(2,1)}, bf16[272,1792]{1,0:T(8,128)(2,1)}, u32[]{:S(2)}, u32[]{:S(2)}) collective-permute-start(bf16[272,1792]{1,0:T(8,128)(2,1)} %convolution_convert_fusion.7), channel_id=1, source_target_pairs={{0,2},{1,3},{2,0},{3,1},{4,6},{5,7},{6,4},{7,5},{8,10},{9,11},{10,... | collective-permute-start | bytes 2924552 | tf_op jit(solution)/shard_map/ppermute | solution.py:25
  88.4 44.6 %collective-permute-start.12 = (bf16[136,3584]{1,0:T(8,128)(2,1)}, bf16[136,3584]{1,0:T(8,128)(2,1)}, u32[]{:S(2)}, u32[]{:S(2)}) collective-permute-start(bf16[136,3584]{1,0:T(8,128)(2,1)} %convolution_convert_fusion.6), channel_id=1, source_target_pairs={{0,2},{1,3},{2,0},{3,1},{4,6},{5,7},{6,4},{7,5},{8,10},{9,11},{10,... | collective-permute-start | bytes 2924552 | tf_op jit(solution)/shard_map/ppermute | solution.py:25
  88.9 44.1 %collective-permute-start.11 = (bf16[136,3584]{1,0:T(8,128)(2,1)}, bf16[136,3584]{1,0:T(8,128)(2,1)}, u32[]{:S(2)}, u32[]{:S(2)}) collective-permute-start(bf16[136,3584]{1,0:T(8,128)(2,1)} %convolution_convert_fusion.6), channel_id=1, source_target_pairs={{0,1},{1,0},{2,3},{3,2},{4,5},{5,4},{6,7},{7,6},{8,9},{9,8},{10,11... | collective-permute-start | bytes 2924552 | tf_op jit(solution)/shard_map/ppermute | solution.py:25
  89.5 59.9 %all-to-all-start.3 = ((bf16[4,40,3584]{2,1,0:T(8,128)(2,1)}), bf16[4,40,3584]{2,1,0:T(8,128)(2,1)}, u32[]{:S(2)}, u32[]{:S(2)}) async-start(bf16[4,40,3584]{2,1,0:T(8,128)(2,1)} %bitcast.240), calls=%async_computation.3 | async-start | bytes 2293760 | tf_op jit(solution)/shard_map/all_to_all | solution.py:32
  94.2 37.6 %collective-permute-start.10 = (bf16[272,1792]{1,0:T(8,128)(2,1)}, bf16[272,1792]{1,0:T(8,128)(2,1)S(1)}, u32[]{:S(2)}, u32[]{:S(2)}) collective-permute-start(bf16[272,1792]{1,0:T(8,128)(2,1)} %convolution_convert_fusion.8), channel_id=1, source_target_pairs={{0,1},{1,0},{2,3},{3,2},{4,5},{5,4},{6,7},{7,6},{8,9},{9,8},{10,11... | collective-permute-start | bytes 2924552 | tf_op jit(solution)/shard_map/ppermute | solution.py:25
  134.8 32.7 %collective-permute-start.18 = (bf16[64,3584]{1,0:T(8,128)(2,1)}, bf16[64,3584]{1,0:T(8,128)(2,1)}, u32[]{:S(2)}, u32[]{:S(2)}) collective-permute-start(bf16[64,3584]{1,0:T(8,128)(2,1)} %slice.129), channel_id=1, source_target_pairs={{0,1},{1,0},{2,3},{3,2},{4,5},{5,4},{6,7},{7,6},{8,9},{9,8},{10,11... | collective-permute-start | bytes 1376264 | tf_op jit(solution)/shard_map/ppermute | solution.py:25
  135.3 20.1 %collective-permute-start.13 = (bf16[136,1792]{1,0:T(8,128)(2,1)}, bf16[136,1792]{1,0:T(8,128)(2,1)}, u32[]{:S(2)}, u32[]{:S(2)}) collective-permute-start(bf16[136,1792]{1,0:T(8,128)(2,1)} %add_convert_fusion.3), channel_id=1, source_target_pairs={{0,1},{1,0},{2,3},{3,2},{4,5},{5,4},{6,7},{7,6},{8,9},{9,8},{10,11... | collective-permute-start | bytes 1462280 | tf_op jit(solution)/shard_map/ppermute | solution.py:25
  139.2 28.3 %collective-permute-start.17 = (bf16[72,3584]{1,0:T(8,128)(2,1)}, bf16[72,3584]{1,0:T(8,128)(2,1)S(1)}, u32[]{:S(2)}, u32[]{:S(2)}) collective-permute-start(bf16[72,3584]{1,0:T(8,128)(2,1)} %slice.128), channel_id=1, source_target_pairs={{0,2},{1,3},{2,0},{3,1},{4,6},{5,7},{6,4},{7,5},{8,10},{9,11},{10,... | collective-permute-start | bytes 1548296 | tf_op jit(solution)/shard_map/ppermute | solution.py:25
  156.1 22.7 %collective-permute-start.16 = (bf16[136,3584]{1,0:T(8,128)(2,1)S(1)}, bf16[136,3584]{1,0:T(8,128)(2,1)S(1)}, u32[]{:S(2)}, u32[]{:S(2)}) collective-permute-start(bf16[136,3584]{1,0:T(8,128)(2,1)S(1)} %convolution_convert_fusion.5), channel_id=1, source_target_pairs={{0,2},{1,3},{2,0},{3,1},{4,6},{5,7},{6,4},{7,5},{8,10},{9,11},{10,... | collective-permute-start | bytes 2924552 | tf_op jit(solution)/shard_map/ppermute | solution.py:25
  156.2 22.7 %collective-permute-start.15 = (bf16[136,3584]{1,0:T(8,128)(2,1)S(1)}, bf16[136,3584]{1,0:T(8,128)(2,1)S(1)}, u32[]{:S(2)}, u32[]{:S(2)}) collective-permute-start(bf16[136,3584]{1,0:T(8,128)(2,1)S(1)} %convolution_convert_fusion.5), channel_id=1, source_target_pairs={{0,1},{1,0},{2,3},{3,2},{4,5},{5,4},{6,7},{7,6},{8,9},{9,8},{10,11... | collective-permute-start | bytes 2924552 | tf_op jit(solution)/shard_map/ppermute | solution.py:25
  189.8 65.4 %all-to-all-start.4 = ((bf16[4,40,3584]{2,1,0:T(8,128)(2,1)}), bf16[4,40,3584]{2,1,0:T(8,128)(2,1)}, u32[]{:S(2)}, u32[]{:S(2)}) async-start(bf16[4,40,3584]{2,1,0:T(8,128)(2,1)} %bitcast.246), calls=%async_computation.4 | async-start | bytes 2293760 | tf_op jit(solution)/shard_map/all_to_all | solution.py:32
  197.1 25.3 %collective-permute-start.22 = (bf16[136,896]{1,0:T(8,128)(2,1)S(1)}, bf16[136,896]{1,0:T(8,128)(2,1)S(1)}, u32[]{:S(2)}, u32[]{:S(2)}) collective-permute-start(bf16[136,896]{1,0:T(8,128)(2,1)S(1)} %copy-done.56), channel_id=1, source_target_pairs={{0,1},{1,0},{2,3},{3,2},{4,5},{5,4},{6,7},{7,6},{8,9},{9,8},{10,11... | collective-permute-start | bytes 731144 | tf_op jit(solution)/shard_map/ppermute | solution.py:25
  197.7 64.7 %collective-permute-start.28 = (bf16[136,896]{1,0:T(8,128)(2,1)}, bf16[136,896]{1,0:T(8,128)(2,1)}, u32[]{:S(2)}, u32[]{:S(2)}) collective-permute-start(bf16[136,896]{1,0:T(8,128)(2,1)} %fusion.30), channel_id=1, source_target_pairs={{0,1},{1,0},{2,3},{3,2},{4,5},{5,4},{6,7},{7,6},{8,9},{9,8},{10,11... | collective-permute-start | bytes 731144 | tf_op jit(solution)/shard_map/ppermute | solution.py:25
  199.2 23.2 %collective-permute-start.23 = (bf16[136,896]{1,0:T(8,128)(2,1)S(1)}, bf16[136,896]{1,0:T(8,128)(2,1)S(1)}, u32[]{:S(2)}, u32[]{:S(2)}) collective-permute-start(bf16[136,896]{1,0:T(8,128)(2,1)S(1)} %copy-done.57), channel_id=1, source_target_pairs={{0,2},{1,3},{2,0},{3,1},{4,6},{5,7},{6,4},{7,5},{8,10},{9,11},{10,... | collective-permute-start | bytes 731144 | tf_op jit(solution)/shard_map/ppermute | solution.py:25
  217.5 43.8 %collective-permute-start.31 = (bf16[136,896]{1,0:T(8,128)(2,1)}, bf16[136,896]{1,0:T(8,128)(2,1)}, u32[]{:S(2)}, u32[]{:S(2)}) collective-permute-start(bf16[136,896]{1,0:T(8,128)(2,1)} %fusion.32), channel_id=1, source_target_pairs={{0,2},{1,3},{2,0},{3,1},{4,6},{5,7},{6,4},{7,5},{8,10},{9,11},{10,... | collective-permute-start | bytes 731144 | tf_op jit(solution)/shard_map/ppermute | solution.py:25
  224.3 35.3 %collective-permute-start.29 = (bf16[136,896]{1,0:T(8,128)(2,1)S(1)}, bf16[136,896]{1,0:T(8,128)(2,1)}, u32[]{:S(2)}, u32[]{:S(2)}) collective-permute-start(bf16[136,896]{1,0:T(8,128)(2,1)S(1)} %fusion.31), channel_id=1, source_target_pairs={{0,1},{1,0},{2,3},{3,2},{4,5},{5,4},{6,7},{7,6},{8,9},{9,8},{10,11... | collective-permute-start | bytes 731144 | tf_op jit(solution)/shard_map/ppermute | solution.py:25
  234.2 27.1 %collective-permute-start.33 = (bf16[136,896]{1,0:T(8,128)(2,1)}, bf16[136,896]{1,0:T(8,128)(2,1)S(1)}, u32[]{:S(2)}, u32[]{:S(2)}) collective-permute-start(bf16[136,896]{1,0:T(8,128)(2,1)} %add_convert_fusion.5), channel_id=1, source_target_pairs={{0,1},{1,0},{2,3},{3,2},{4,5},{5,4},{6,7},{7,6},{8,9},{9,8},{10,11... | collective-permute-start | bytes 731144 | tf_op jit(solution)/shard_map/ppermute | solution.py:25
  (75 other events, 818.9 us)

commit v5 on v3

v5 whole, which is shorter than its diff:
```python
import jax
import jax.numpy as jnp
from jax import lax
from jax.experimental import pallas as pl
from jax.experimental.pallas import tpu as pltpu
from jax.sharding import PartitionSpec as P

EPS = 1e-06
F32 = jnp.float32
BF16 = jnp.bfloat16


def dot(a, b, dims=((1,), (0,))):
    return lax.dot_general(a, b, (dims, ((), ())), preferred_element_type=F32)


def pipe_move(array, target):
    count = lax.axis_size("pipe")
    pairs = [(i, target(i, count) % count) for i in range(count)]
    if all(a == b for a, b in pairs):
        return array
    return lax.ppermute(array, "pipe", pairs)


def plane_move(array, experts, bit):
    devices = lax.axis_size("expert")
    return lax.ppermute(array, "expert", [(i, i ^ bit) for i in range(devices)])


def depth_exchange(blocks, experts):
    devices = lax.axis_size("expert")
    group = devices // experts
    columns = [[e * group + m for e in range(experts)] for m in range(group)]
    return lax.all_to_all(
        blocks, "expert", split_axis=0, concat_axis=0, tiled=True, axis_index_groups=columns
    )


class Layout:
    def __init__(self, experts, capacity):
        self.experts = experts
        self.main = capacity // 8 * 8
        self.rest = capacity - self.main
        self.tail = -(-experts * self.rest // 8) * 8
        self.rows = self.main + self.tail
        self.packed = experts * self.main + self.tail


def selector(ids, layout, here):
    onehot = (ids[:, None] == jnp.arange(layout.experts, dtype=jnp.int32)).astype(jnp.int32)
    slot = jnp.sum(onehot * (jnp.cumsum(onehot, axis=0) - 1), axis=1)
    place = jnp.where(slot < layout.main, slot, slot + here * layout.rest)
    row = jnp.arange(layout.experts * layout.rows, dtype=jnp.int32)[:, None]
    return ((ids * layout.rows + place)[None, :] == row).astype(BF16)


def packer(layout):
    packed = jnp.arange(layout.packed, dtype=jnp.int32)[:, None]
    row = jnp.arange(layout.experts * layout.rows, dtype=jnp.int32)[None, :]
    block, place = row // layout.rows, row % layout.rows
    target = jnp.where(
        place < layout.main,
        block * layout.main + place,
        layout.experts * layout.main + place - layout.main,
    )
    return (target == packed).astype(BF16)


def on_core(name, work, outs, *args):
    def kernel(*refs):
        work(refs[: len(args)], refs[len(args) :])

    space = pl.BlockSpec(memory_space=pltpu.VMEM)
    return pl.pallas_call(
        kernel,
        out_shape=[jax.ShapeDtypeStruct(shape, kind) for shape, kind in outs],
        in_specs=[space] * len(args),
        out_specs=[space] * len(outs),
        compiler_params=pltpu.CompilerParams(vmem_limit_bytes=40 * 2**20),
        cost_estimate=pl.CostEstimate(flops=10**6, bytes_accessed=10**5, transcendentals=0),
        name=name,
    )(*args)


NT = ((1,), (1,))
TN = ((0,), (0,))


def pack_halves(blocks, select):
    rows, half = select.shape[0], blocks.shape[1] // 2

    def work(ins, outs):
        for h in range(2):
            outs[h][...] = dot(ins[1][...], ins[0][:, h * half : (h + 1) * half]).astype(BF16)

    return on_core("pack", work, [((rows, half), BF16)] * 2, blocks, select)


def a_near_rows(blocks, up):
    half, hidden_units = up.shape[0] // 2, up.shape[1]
    rows = blocks[0][0].shape[0]

    def work(ins, outs):
        for j in range(3):
            hidden = dot(ins[2 * j][...], ins[6][:half]) + dot(ins[2 * j + 1][...], ins[6][half:])
            outs[0][j] = (hidden * jax.nn.sigmoid(hidden)).astype(BF16)

    flat = [half_block for block in blocks for half_block in block]
    return on_core("a_near", work, [((3, rows, hidden_units), BF16)], *flat, up)[0]


def a_far_rows(block, act, up, down):
    half, rows = up.shape[0] // 2, act.shape[1]

    def work(ins, outs):
        lo, hi, acts, up_ref, down_ref = ins
        hidden = dot(lo[...], up_ref[:half]) + dot(hi[...], up_ref[half:])
        far = (hidden * jax.nn.sigmoid(hidden)).astype(BF16)
        for h in range(2):
            weights = down_ref[:, h * half : (h + 1) * half]
            outs[h][0] = dot(far, weights).astype(BF16)
            outs[h][1] = dot(acts[1 + h], weights).astype(BF16)

    return on_core("a_far", work, [((2, rows, half), BF16)] * 2, *block, act, up, down)


def a_second_rows(act, down, got):
    half, rows = down.shape[1] // 2, act.shape[1]

    def work(ins, outs):
        acts, down_ref, by_x, by_y = ins
        outs[0][...] = (dot(acts[1], down_ref[:, half:]) + by_y[0].astype(F32)).astype(BF16)
        outs[1][...] = (dot(acts[2], down_ref[:, :half]) + by_x[0].astype(F32)).astype(BF16)

    return on_core("a_second", work, [((rows, half), BF16)] * 2, act, down, *got)


def a_total_rows(act, down, first, second, place):
    half = down.shape[1] // 2

    def work(ins, outs):
        acts, down_ref, first_x, first_y, second_x, second_y, place_ref = ins
        for h, (one, two) in enumerate(((first_x, second_y), (first_y, second_x))):
            cols = slice(h * half, (h + 1) * half)
            total = dot(acts[0], down_ref[:, cols]) + one[1].astype(F32) + two[...].astype(F32)
            outs[0][:, cols] = dot(place_ref[...], total.astype(BF16)).astype(BF16)

    outs = [((place.shape[0], 2 * half), BF16)]
    return on_core("a_total", work, outs, act, down, *first, *second, place)[0]


def back_rows(x_lo, x_hi, c_lo, c_hi, up_ref, down_ref, col_ref):
    half = x_lo.shape[1]
    hidden = dot(x_lo, up_ref[:half]) + dot(x_hi, up_ref[half:])
    score = (dot(x_lo, col_ref[:half]) + dot(x_hi, col_ref[half:]))[:, :1]
    act_grad = dot(c_lo, down_ref[:, :half], NT) + dot(c_hi, down_ref[:, half:], NT)
    sigma = jax.nn.sigmoid(hidden)
    active = hidden * sigma
    hid_grad = (act_grad * sigma * (1.0 + hidden * (1.0 - sigma))).astype(BF16)
    term = jnp.sum(active * act_grad, axis=1, keepdims=True) * jax.nn.sigmoid(-score)
    return active.astype(BF16), hid_grad, term


def grad_rows(hid_grad, term, up_ref, line_ref, cols):
    return dot(hid_grad, up_ref[cols], NT) + term * line_ref[:, cols]


def piece(c, side, half):
    begin = c * half + side * (half // 2)
    return slice(begin, begin + half // 2)


def b_near_rows(blocks, cots, up, down, col, line):
    half, units, rows = up.shape[0] // 2, up.shape[1], blocks[0][0].shape[0]

    def work(ins, outs):
        up_ref, down_ref, col_ref, line_ref = ins[12:]
        for j in range(3):
            act, hid, term = back_rows(
                ins[2 * j][...],
                ins[2 * j + 1][...],
                ins[6 + 2 * j][...],
                ins[7 + 2 * j][...],
                up_ref,
                down_ref,
                col_ref,
            )
            outs[0][j], outs[1][j] = act, hid
            outs[2][j] = jnp.broadcast_to(term, (rows, 128))
            if j:
                for c in range(2):
                    cols = piece(c, j - 1, half)
                    part = grad_rows(hid, term, up_ref, line_ref, cols)
                    outs[2 + j][c] = part.astype(BF16)

    flat = [v for block in blocks for v in block] + [v for block in cots for v in block]
    outs = [((3, rows, units), BF16)] * 2 + [((3, rows, 128), F32)]
    outs += [((2, rows, half // 2), BF16)] * 2
    act, hid, term, by_x, by_y = on_core("b_near", work, outs, *flat, up, down, col, line)
    return (act, hid, term), (by_x, by_y)


def b_far_rows(block, cots, up, down, col, line):
    half, units, rows = up.shape[0] // 2, up.shape[1], block[0].shape[0]

    def work(ins, outs):
        up_ref, down_ref, col_ref, line_ref = ins[4:]
        values = [ref[...] for ref in ins[:4]]
        act, hid, term = back_rows(*values, up_ref, down_ref, col_ref)
        outs[0][...], outs[1][...] = act, hid
        for c in range(2):
            for side in range(2):
                part = grad_rows(hid, term, up_ref, line_ref, piece(c, side, half))
                outs[2 + 2 * c + side][...] = part.astype(BF16)

    outs = [((rows, units), BF16)] * 2 + [((rows, half // 2), BF16)] * 4
    act, hid, x0, y0, x1, y1 = on_core("b_far", work, outs, *block, *cots, up, down, col, line)
    return (act, hid), [(x0, y0), (x1, y1)]


def b_second_rows(near, up, line, got, c):
    half, rows = up.shape[0] // 2, got[0].shape[0]

    def work(ins, outs):
        hids, terms, up_ref, line_ref, by_x, by_y = ins
        for side, ref in enumerate((by_y, by_x)):
            j, cols = 1 + side, piece(c, 1 - side, half)
            part = grad_rows(hids[j], terms[j][:, :1], up_ref, line_ref, cols)
            outs[side][...] = (part + ref[...].astype(F32)).astype(BF16)

    outs = [((rows, half // 2), BF16)] * 2
    return on_core("b_second", work, outs, near[1], near[2], up, line, *got)


def b_total_rows(near, up, line, plain, second, place, c):
    half = up.shape[0] // 2
    quarter = half // 2

    def work(ins, outs):
        hids, terms, up_ref, line_ref, plain_x, plain_y, second_x, second_y, place_ref = ins
        for side, (one, two) in enumerate(((plain_x, second_y), (plain_y, second_x))):
            part = grad_rows(hids[0], terms[0][:, :1], up_ref, line_ref, piece(c, side, half))
            total = (part + one[c].astype(F32) + two[...].astype(F32)).astype(BF16)
            cols = slice(side * quarter, (side + 1) * quarter)
            outs[0][:, cols] = dot(place_ref[...], total).astype(BF16)

    outs = [((place.shape[0], half), BF16)]
    return on_core("b_total", work, outs, near[1], near[2], up, line, *plain, *second, place)[0]


def weight_grads(blocks, cots, near, far):
    half, units = blocks[0][0].shape[1], far[0].shape[1]
    tile = 256

    def work(ins, outs):
        xs, cs = ins[0:8], ins[8:16]
        acts = [ins[16][j] for j in range(3)] + [ins[18][...]]
        hids = [ins[17][j] for j in range(3)] + [ins[19][...]]
        for h in range(2):
            for begin in range(0, half, tile):
                cols, out = slice(begin, begin + tile), slice(h * half + begin, h * half + begin + tile)
                up_sum, down_sum = 0.0, 0.0
                for j in range(4):
                    up_sum = up_sum + dot(xs[2 * j + h][:, cols], hids[j], TN)
                    down_sum = down_sum + dot(acts[j], cs[2 * j + h][:, cols], TN)
                outs[0][out, :] = up_sum.astype(BF16)
                outs[1][:, out] = down_sum.astype(BF16)

    flat = [v for block in blocks for v in block] + [v for block in cots for v in block]
    outs = [((2 * half, units), BF16), ((units, 2 * half), BF16)]
    return on_core("weight_grads", work, outs, *flat, near[0], near[1], *far)


def statistics(features):
    feat = features.astype(F32)
    scale = lax.rsqrt(jnp.mean(feat * feat, axis=-1, keepdims=True) + EPS)
    return feat, scale, (feat * scale).astype(BF16)


def gate_of(normed, ids, router):
    scores = dot(normed, router)
    onehot = ids[:, None] == jnp.arange(router.shape[1], dtype=jnp.int32)
    return jax.nn.sigmoid(jnp.sum(jnp.where(onehot, scores, 0.0), axis=1, keepdims=True))


def select_rows(pick, rows, layout):
    return dot(pick, rows).astype(BF16).reshape(layout.experts, layout.rows, rows.shape[1])


def across_planes(blocks, layout):
    blocks = depth_exchange(blocks, layout.experts)
    return blocks.reshape(layout.experts * layout.rows, blocks.shape[2])


def swap_pair(pair, experts):
    return plane_move(pair[0], experts, 1), plane_move(pair[1], experts, 2)


def at_tokens(blocks, pick, layout):
    blocks = blocks.reshape(layout.experts, layout.rows, blocks.shape[1])
    return dot(pick, across_planes(blocks, layout), TN)


def spread_halves(mine, experts):
    x_lo, y_hi = swap_pair(mine, experts)
    x_hi, y_lo = swap_pair((mine[1], mine[0]), experts)
    return (x_lo, x_hi), (y_lo, y_hi)


def relay_halves(near, experts):
    return plane_move(near[0][0], experts, 2), plane_move(near[1][1], experts, 1)


def body(a_input, a_route, b_saved, b_grad, b_route, up_weight, down_weight, router):
    devices = lax.axis_size("expert")
    experts = router.shape[2]
    group = devices // experts
    tokens, width = a_input.shape[1], a_input.shape[2]
    layout = Layout(experts, tokens * a_route.shape[2] // experts + 2)
    here = lax.axis_index("expert") // group
    up, down, cols_r = up_weight[0], down_weight[0], router[0]
    half = width // 2

    b_ids = pipe_move(b_route[0].astype(BF16), lambda i, n: n - 1 - i).astype(jnp.int32)[:, 0]
    b_x = pipe_move(b_saved[0], lambda i, n: n - 1 - i)
    b_c = pipe_move(b_grad[0], lambda i, n: n - 1 - i)
    a_ids = a_route[0][:, 0]

    after = lax.optimization_barrier
    own = jnp.where(jnp.arange(experts) == here, cols_r.astype(F32), 0.0)
    own = jnp.sum(own, axis=1, keepdims=True)
    line = own.reshape(1, width)
    col = jnp.where(jnp.arange(128)[None, :] == 0, own, 0.0).astype(BF16)
    select = packer(layout)
    place = select.T

    a_float, _, a_normed = statistics(a_input[0])
    a_pick = selector(a_ids, layout, here)
    a_blocks = across_planes(select_rows(a_pick, a_normed, layout), layout)
    a_mine = tuple(pack_halves(a_blocks, select))

    b_float, b_scale, b_normed = statistics(b_x)
    b_pick = selector(b_ids, layout, here)
    b_send = select_rows(b_pick, b_normed, layout)
    b_send, a_mine = after((b_send, a_mine))
    a_near = spread_halves(a_mine, experts)
    a_far = relay_halves(a_near, experts)
    b_blocks = across_planes(b_send, layout)

    act = a_near_rows((a_mine,) + a_near, up)
    a_first = a_far_rows(a_far, act, up, down)
    a_first, b_blocks = after((a_first, b_blocks))
    a_first = swap_pair(a_first, experts)
    b_mine = tuple(pack_halves(b_blocks, select))

    b_gate = gate_of(b_normed, b_ids, cols_r)
    cot = (b_gate * b_c.astype(F32)).astype(BF16)
    c_send = select_rows(b_pick, cot, layout)
    c_send, b_mine = after((c_send, b_mine))
    b_near = spread_halves(b_mine, experts)
    b_far = relay_halves(b_near, experts)
    c_blocks = across_planes(c_send, layout)

    a_second = a_second_rows(act, down, a_first)
    a_second, c_blocks = after((a_second, c_blocks))
    a_second = swap_pair(a_second, experts)
    c_mine = tuple(pack_halves(c_blocks, select))
    c_near = spread_halves(c_mine, experts)
    c_far = relay_halves(c_near, experts)
    a_back = a_total_rows(act, down, a_first, a_second, place)
    a_gate = gate_of(a_normed, a_ids, cols_r)
    a_out = (a_float + a_gate * at_tokens(a_back, a_pick, layout)).astype(BF16)
    a_next = pipe_move(a_out, lambda i, n: i + 1)

    near, b_plain = b_near_rows((b_mine,) + b_near, (c_mine,) + c_near, up, down, col, line)
    b_plain = swap_pair(b_plain, experts)
    far, b_relay = b_far_rows(b_far, c_far, up, down, col, line)
    b_relay = [swap_pair(pair, experts) for pair in b_relay]
    pieces = []
    for c in range(2):
        second = swap_pair(b_second_rows(near, up, line, b_relay[c], c), experts)
        b_back = b_total_rows(near, up, line, b_plain, second, place, c)
        pieces.append(at_tokens(b_back, b_pick, layout))
    normed_grad = jnp.concatenate(pieces, axis=1)
    along = jnp.sum(normed_grad * b_float, axis=-1, keepdims=True) / width
    feature_grad = b_scale * normed_grad - b_float * (b_scale * b_scale * b_scale) * along
    b_out = (b_c.astype(F32) + feature_grad).astype(BF16)
    b_next = pipe_move(b_out, lambda i, n: n - i)

    up_grad, down_grad = weight_grads(
        (b_mine,) + b_near + (b_far,), (c_mine,) + c_near + (c_far,), near, far
    )
    return (a_next[None], b_next[None], up_grad[None], down_grad[None])


def solution(mesh):
    return jax.shard_map(
        body,
        mesh=mesh,
        in_specs=(
            P("pipe", "expert", None),
            P("pipe", "expert", None),
            P("pipe", "expert", None),
            P("pipe", "expert", None),
            P("pipe", "expert", None),
            P("pipe", None, "expert"),
            P("pipe", "expert", None),
            P("pipe", None, None),
        ),
        out_specs=(
            P("pipe", "expert", None),
            P("pipe", "expert", None),
            P("pipe", None, "expert"),
            P("pipe", "expert", None),
        ),
        check_vma=False,
    )
```

time: 293 us -> 276 us (0.942)
  matrix products: 75.7 us -> 12.3 us
  Pallas kernels: 0 us -> 29.8 us
  starting transfers between devices: 46 us -> 65.5 us
  waiting for transfers between devices: 122 us -> 134 us
  other arithmetic: 17.6 us -> 7.96 us
  local copies, waits for them, and re-layouts: 28.4 us -> 24.1 us
    dot_general x48 -> x8, matrix products: 75.7 us -> 12.3 us  [dot(): return lax.dot_general(a, b, (dims, ((), ())), preferred_element_type=F32)]
    ppermute x20 -> x32, waiting for transfers between devices: 72.5 us -> 109 us  [plane_move(): return lax.ppermute(array, 'expert', [(i, i ^ bit) for i in range(devices)])]
    pallas_call x0 -> x14, Pallas kernels: none -> 29.8 us  [on_core(): pl.pallas_call(kernel, out_shape=[jax.ShapeDtypeStruct(shape, kind) for s...]
    all_to_all x5 -> x6, waiting for transfers between devices: 48.4 us -> 25.2 us  [depth_exchange(): lax.all_to_all(blocks, 'expert', split_axis=0, concat_axis=0, tiled=True,...]
    ppermute x20 -> x32, starting transfers between devices: 22 us -> 34.9 us  [plane_move(): return lax.ppermute(array, 'expert', [(i, i ^ bit) for i in range(devices)])]
    concatenate x7 -> x0, other arithmetic: 8.93 us -> none  [the longest x2 4.69 us: for_tokens(): blocks = jnp.concatenate(blocks, axis=1)]
    slice x7 -> x0, local copies, waits for them, and re-layouts: 8.1 us -> none  [the longest x3 3.78 us: to_diagonal(): from_x[:cut]]
    unnamed x125 -> x103, local copies, waits for them, and re-layouts: 16.6 us -> 23.7 us
  transfers between devices with their start and end apart: 29 -> 42, of which waited for: 13 -> 19; matrix products, arithmetic and copies ran while one was open for 32% -> 7% of each run, Pallas kernels for 0% -> 11%
where the time goes in v5:
time: 276 us; the launch traced here: 275 us
  waiting for transfers between devices  134 us (49%)
  starting transfers between devices  65.5 us (24%)
  Pallas kernels  29.8 us (11%)
  local copies, waits for them, and re-layouts  24.1 us (9%)
  matrix products  12.3 us (4%)
  other arithmetic  7.96 us (3%)
    ppermute x32, waiting for transfers between devices, plane_move(): return lax.ppermute(array, 'expert', [(i, i ^ bit) for i in range(devices)])  109 us
    ppermute x32, starting transfers between devices, plane_move(): return lax.ppermute(array, 'expert', [(i, i ^ bit) for i in range(devices)])  34.9 us
    all_to_all x6, starting transfers between devices, depth_exchange(): lax.all_to_all(blocks, 'expert', split_axis=0, concat_axis=0, tiled=True,...  29.9 us
    pallas_call x14, Pallas kernels, on_core(): pl.pallas_call(kernel, out_shape=[jax.ShapeDtypeStruct(shape, kind) for s...  29.8 us
    all_to_all x6, waiting for transfers between devices, depth_exchange(): lax.all_to_all(blocks, 'expert', split_axis=0, concat_axis=0, tiled=True,...  25.2 us
    unnamed x103, local copies, waits for them, and re-layouts  23.7 us
    dot_general x8, matrix products, dot(): return lax.dot_general(a, b, (dims, ((), ())), preferred_element_type=F32)  12.3 us
  transfers between devices with their start and end apart: 42, of which 19 were waited for; matrix products, arithmetic and copies ran while one was open for 7% of the time, Pallas kernels for 11%

profile of v5, /device:TPU:0, one launch (start us, length us, event | category | flops | bytes accessed | tf_op | source)
XLA Modules:
  0.0 274.7 jit_solution(3703199918084045165)
XLA Ops:
  7.3 6.3 %all-to-all-start = ((bf16[4,40,3584]{2,1,0:T(8,128)(2,1)}), bf16[4,40,3584]{2,1,0:T(8,128)(2,1)S(1)}, u32[]{:S(2)}, u32[]{:S(2)}) async-start(bf16[4,40,3584]{2,1,0:T(8,128)(2,1)} %bitcast.73), calls=%async_computation | async-start | bytes 2293760 | tf_op jit(solution)/shard_map/all_to_all | solution.py:34
  16.4 25.2 %all-to-all-done = bf16[4,40,3584]{2,1,0:T(8,128)(2,1)S(1)} async-done(((bf16[4,40,3584]{2,1,0:T(8,128)(2,1)}), bf16[4,40,3584]{2,1,0:T(8,128)(2,1)S(1)}, u32[]{:S(2)}, u32[]{:S(2)}) %all-to-all-start) | async-done | bytes 1146912 | tf_op jit(solution)/shard_map/all_to_all | solution.py:34
  43.6 3.5 %all-to-all-start.1 = ((bf16[4,40,3584]{2,1,0:T(8,128)(2,1)}), bf16[4,40,3584]{2,1,0:T(8,128)(2,1)S(1)}, u32[]{:S(2)}, u32[]{:S(2)}) async-start(bf16[4,40,3584]{2,1,0:T(8,128)(2,1)} %bitcast.71), calls=%async_computation.1 | async-start | bytes 2293760 | tf_op jit(solution)/shard_map/all_to_all | solution.py:34
  53.0 8.5 %collective-permute-done.2.refs_2_ = bf16[136,1792]{1,0:T(8,128)(2,1)S(1)} collective-permute-done((bf16[136,1792]{1,0:T(8,128)(2,1)}, bf16[136,1792]{1,0:T(8,128)(2,1)S(1)}, u32[]{:S(2)}, u32[]{:S(2)}) %collective-permute-start.2) | collective-permute-done | bytes 487456 | tf_op jit(solution)/shard_map/ppermute | solution.py:27
  66.1 5.9 %collective-permute-done.3.refs_3_ = bf16[136,1792]{1,0:T(8,128)(2,1)S(1)} collective-permute-done((bf16[136,1792]{1,0:T(8,128)(2,1)}, bf16[136,1792]{1,0:T(8,128)(2,1)S(1)}, u32[]{:S(2)}, u32[]{:S(2)}) %collective-permute-start.3) | collective-permute-done | bytes 487456 | tf_op jit(solution)/shard_map/ppermute | solution.py:27
  74.5 8.6 %collective-permute-done.6.refs_0_ = bf16[136,1792]{1,0:T(8,128)(2,1)S(1)} collective-permute-done((bf16[136,1792]{1,0:T(8,128)(2,1)S(1)}, bf16[136,1792]{1,0:T(8,128)(2,1)S(1)}, u32[]{:S(2)}, u32[]{:S(2)}) %collective-permute-start.6) | collective-permute-done | bytes 487456 | tf_op jit(solution)/shard_map/ppermute | solution.py:27
  88.7 5.0 %all-to-all-start.2 = ((bf16[4,40,3584]{2,1,0:T(8,128)(2,1)}), bf16[4,40,3584]{2,1,0:T(8,128)(2,1)S(1)}, u32[]{:S(2)}, u32[]{:S(2)}) async-start(bf16[4,40,3584]{2,1,0:T(8,128)(2,1)} %bitcast.72), calls=%async_computation.2 | async-start | bytes 2293760 | tf_op jit(solution)/shard_map/all_to_all | solution.py:34
  97.7 20.7 %collective-permute-done.8.refs_2_ = bf16[2,136,1792]{2,1,0:T(8,128)(2,1)S(1)} collective-permute-done((bf16[2,136,1792]{2,1,0:T(8,128)(2,1)}, bf16[2,136,1792]{2,1,0:T(8,128)(2,1)S(1)}, u32[]{:S(2)}, u32[]{:S(2)}) %collective-permute-start.8) | collective-permute-done | bytes 974880 | tf_op jit(solution)/shard_map/ppermute | solution.py:27
  131.1 8.2 %collective-permute-done.11.refs_4_ = bf16[136,1792]{1,0:T(8,128)(2,1)S(1)} collective-permute-done((bf16[136,1792]{1,0:T(8,128)(2,1)}, bf16[136,1792]{1,0:T(8,128)(2,1)S(1)}, u32[]{:S(2)}, u32[]{:S(2)}) %collective-permute-start.11) | collective-permute-done | bytes 487456 | tf_op jit(solution)/shard_map/ppermute | solution.py:27
  140.8 9.0 %collective-permute-done.18.refs_8_.refs_10_ = bf16[136,1792]{1,0:T(8,128)(2,1)} collective-permute-done((bf16[136,1792]{1,0:T(8,128)(2,1)S(1)}, bf16[136,1792]{1,0:T(8,128)(2,1)}, u32[]{:S(2)}, u32[]{:S(2)}) %collective-permute-start.18) | collective-permute-done | bytes 487456 | tf_op jit(solution)/shard_map/ppermute | solution.py:27
  156.0 5.2 %all-to-all-start.3 = ((bf16[4,40,3584]{2,1,0:T(8,128)(2,1)}), bf16[4,40,3584]{2,1,0:T(8,128)(2,1)}, u32[]{:S(2)}, u32[]{:S(2)}) async-start(bf16[4,40,3584]{2,1,0:T(8,128)(2,1)} %bitcast.17), calls=%async_computation.3 | async-start | bytes 2293760 | tf_op jit(solution)/shard_map/all_to_all | solution.py:34
  165.5 7.8 %collective-permute-done.26.refs_2_.refs_14_ = bf16[136,1792]{1,0:T(8,128)(2,1)} collective-permute-done((bf16[136,1792]{1,0:T(8,128)(2,1)}, bf16[136,1792]{1,0:T(8,128)(2,1)}, u32[]{:S(2)}, u32[]{:S(2)}) %collective-permute-start.26) | collective-permute-done | bytes 487456 | tf_op jit(solution)/shard_map/ppermute | solution.py:27
  175.3 15.3 %collective-permute-done.27.refs_3_.refs_15_ = bf16[136,1792]{1,0:T(8,128)(2,1)S(1)} collective-permute-done((bf16[136,1792]{1,0:T(8,128)(2,1)}, bf16[136,1792]{1,0:T(8,128)(2,1)S(1)}, u32[]{:S(2)}, u32[]{:S(2)}) %collective-permute-start.27) | collective-permute-done | bytes 487456 | tf_op jit(solution)/shard_map/ppermute | solution.py:27
  192.1 4.2 %b_far.1 = (bf16[136,256]{1,0:T(8,128)(2,1)S(1)}, bf16[136,256]{1,0:T(8,128)(2,1)S(1)}, bf16[136,896]{1,0:T(8,128)(2,1)S(1)}, bf16[136,896]{1,0:T(8,128)(2,1)S(1...) custom-call(bf16[136,1792]{1,0:T(8,128)(2,1)} %collective-permute-done.24.refs_0_.refs_6_, ...), custom_call_target="tpu_custom_call" | custom-call | flops 1000000 | bytes 100000 | tf_op jit(solution)/shard_map/b_far/pallas_call | solution.py:74
  200.1 6.5 %b_near.1 = (bf16[3,136,256]{2,1,0:T(8,128)(2,1)S(1)}, bf16[3,136,256]{2,1,0:T(8,128)(2,1)S(1)}, f32[3,136,128]{2,1,0:T(8,128)S(1)}, bf16[2,136,896]{2,1,0:T(8,128)(2,1)S(1)}, bf16[2,136,896]{2,1,0:T(8,128)(2,1)S(1)}) custom-call(bf16[136,1792]{1,0:T(8,128)(2,1)S(1)} %copy-done.10, bf16[136,1792]{1,0:T(8,128)(2,1)S(1)} %copy-done.13, ...), custom_call_target="tpu_custom_call" | custom-call | flops 1000000 | bytes 100000 | tf_op jit(solution)/shard_map/b_near/pallas_call | solution.py:74
  211.3 6.9 %collective-permute-done.22.refs_4_ = bf16[2,136,896]{2,1,0:T(8,128)(2,1)S(1)} collective-permute-done((bf16[2,136,896]{2,1,0:T(8,128)(2,1)S(1)}, bf16[2,136,896]{2,1,0:T(8,128)(2,1)S(1)}, u32[]{:S(2)}, u32[]{:S(2)}) %collective-permute-start.22) | collective-permute-done | bytes 487456 | tf_op jit(solution)/shard_map/ppermute | solution.py:27
  218.6 2.3 collective-permute-done.34.refs_6_
  222.8 4.6 %all-to-all-start.5 = ((bf16[4,40,1792]{2,1,0:T(8,128)(2,1)}), bf16[4,40,1792]{2,1,0:T(8,128)(2,1)}, u32[]{:S(2)}, u32[]{:S(2)}) async-start(bf16[4,40,1792]{2,1,0:T(8,128)(2,1)} %bitcast.22), calls=%async_computation.5 | async-start | bytes 1146880 | tf_op jit(solution)/shard_map/all_to_all | solution.py:34
  229.7 6.3 %collective-permute-done.28.refs_4_ = bf16[136,896]{1,0:T(8,128)(2,1)S(1)} collective-permute-done((bf16[136,896]{1,0:T(8,128)(2,1)}, bf16[136,896]{1,0:T(8,128)(2,1)S(1)}, u32[]{:S(2)}, u32[]{:S(2)}) %collective-permute-start.28) | collective-permute-done | bytes 243744 | tf_op jit(solution)/shard_map/ppermute | solution.py:27
  239.5 4.2 %collective-permute-done.30.refs_6_ = bf16[136,896]{1,0:T(8,128)(2,1)S(1)} collective-permute-done((bf16[136,896]{1,0:T(8,128)(2,1)S(1)}, bf16[136,896]{1,0:T(8,128)(2,1)S(1)}, u32[]{:S(2)}, u32[]{:S(2)}) %collective-permute-start.30) | collective-permute-done | bytes 243744 | tf_op jit(solution)/shard_map/ppermute | solution.py:27
  246.6 5.3 %all-to-all-start.4 = ((bf16[4,40,1792]{2,1,0:T(8,128)(2,1)}), bf16[4,40,1792]{2,1,0:T(8,128)(2,1)S(1)}, u32[]{:S(2)}, u32[]{:S(2)}) async-start(bf16[4,40,1792]{2,1,0:T(8,128)(2,1)} %bitcast.20), calls=%async_computation.4 | async-start | bytes 1146880 | tf_op jit(solution)/shard_map/all_to_all | solution.py:34
  257.7 8.1 %weight_grads.1 = (bf16[3584,256]{1,0:T(8,128)(2,1)}, bf16[256,3584]{1,0:T(8,128)(2,1)}) custom-call(bf16[136,1792]{1,0:T(8,128)(2,1)S(1)} %copy-done.11, bf16[136,1792]{1,0:T(8,128)(2,1)S(1)} %copy-done.14, bf16[136,1792]{1,0:T(8,128)(2,1)} %collective-permute-done.14.refs_2_, bf16[136,1792]{1,0:T(8,128)(2,1)S(1)} %copy-done.19, ...), custom_call_target="tpu_custom_call" | custom-call | flops 1000000 | bytes 100000 | tf_op jit(solution)/shard_map/weight_grads/pallas_call | solution.py:74
  265.7 2.6 fusion.1
  272.6 2.2 copy.17
  (216 shorter events, 91.1 us)
Async XLA Ops:
  7.3 34.3 %all-to-all-start = ((bf16[4,40,3584]{2,1,0:T(8,128)(2,1)}), bf16[4,40,3584]{2,1,0:T(8,128)(2,1)S(1)}, u32[]{:S(2)}, u32[]{:S(2)}) async-start(bf16[4,40,3584]{2,1,0:T(8,128)(2,1)} %bitcast.73), calls=%async_computation | async-start | bytes 2293760 | tf_op jit(solution)/shard_map/all_to_all | solution.py:34
  43.6 43.0 %all-to-all-start.1 = ((bf16[4,40,3584]{2,1,0:T(8,128)(2,1)}), bf16[4,40,3584]{2,1,0:T(8,128)(2,1)S(1)}, u32[]{:S(2)}, u32[]{:S(2)}) async-start(bf16[4,40,3584]{2,1,0:T(8,128)(2,1)} %bitcast.71), calls=%async_computation.1 | async-start | bytes 2293760 | tf_op jit(solution)/shard_map/all_to_all | solution.py:34
  52.0 20.0 %collective-permute-start.3 = (bf16[136,1792]{1,0:T(8,128)(2,1)}, bf16[136,1792]{1,0:T(8,128)(2,1)S(1)}, u32[]{:S(2)}, u32[]{:S(2)}) collective-permute-start(bf16[136,1792]{1,0:T(8,128)(2,1)} %copy-done.30), channel_id=1, source_target_pairs={{0,1},{1,0},{2,3},{3,2},{4,5},{5,4},{6,7},{7,6},{8,9},{9,8},{10,11... | collective-permute-start | bytes 1462280 | tf_op jit(solution)/shard_map/ppermute | solution.py:27
  52.5 21.0 %collective-permute-start.4 = (bf16[136,1792]{1,0:T(8,128)(2,1)}, bf16[136,1792]{1,0:T(8,128)(2,1)S(1)}, u32[]{:S(2)}, u32[]{:S(2)}) collective-permute-start(bf16[136,1792]{1,0:T(8,128)(2,1)} %copy-done.28), channel_id=1, source_target_pairs={{0,2},{1,3},{2,0},{3,1},{4,6},{5,7},{6,4},{7,5},{8,10},{9,11},{10,... | collective-permute-start | bytes 1462280 | tf_op jit(solution)/shard_map/ppermute | solution.py:27
  61.5 21.6 %collective-permute-start.6 = (bf16[136,1792]{1,0:T(8,128)(2,1)S(1)}, bf16[136,1792]{1,0:T(8,128)(2,1)S(1)}, u32[]{:S(2)}, u32[]{:S(2)}) collective-permute-start(bf16[136,1792]{1,0:T(8,128)(2,1)S(1)} %collective-permute-done.2.refs_2_), channel_id=1, source_target_pairs={{0,2},{1,3},{2,0},{3,1},{4,6},{5,7},{6,4},{7,5},{8,10},{9,11},{10,... | collective-permute-start | bytes 1462280 | tf_op jit(solution)/shard_map/ppermute | solution.py:27
  63.0 20.1 %collective-permute-start.7 = (bf16[136,1792]{1,0:T(8,128)(2,1)S(1)}, bf16[136,1792]{1,0:T(8,128)(2,1)S(1)}, u32[]{:S(2)}, u32[]{:S(2)}) collective-permute-start(bf16[136,1792]{1,0:T(8,128)(2,1)S(1)} %collective-permute-done.5.refs_5_), channel_id=1, source_target_pairs={{0,1},{1,0},{2,3},{3,2},{4,5},{5,4},{6,7},{7,6},{8,9},{9,8},{10,11... | collective-permute-start | bytes 1462280 | tf_op jit(solution)/shard_map/ppermute | solution.py:27
  88.7 35.7 %all-to-all-start.2 = ((bf16[4,40,3584]{2,1,0:T(8,128)(2,1)}), bf16[4,40,3584]{2,1,0:T(8,128)(2,1)S(1)}, u32[]{:S(2)}, u32[]{:S(2)}) async-start(bf16[4,40,3584]{2,1,0:T(8,128)(2,1)} %bitcast.72), calls=%async_computation.2 | async-start | bytes 2293760 | tf_op jit(solution)/shard_map/all_to_all | solution.py:34
  93.6 24.7 %collective-permute-start.8 = (bf16[2,136,1792]{2,1,0:T(8,128)(2,1)}, bf16[2,136,1792]{2,1,0:T(8,128)(2,1)S(1)}, u32[]{:S(2)}, u32[]{:S(2)}) collective-permute-start(bf16[2,136,1792]{2,1,0:T(8,128)(2,1)} %copy-done.37), channel_id=1, source_target_pairs={{0,1},{1,0},{2,3},{3,2},{4,5},{5,4},{6,7},{7,6},{8,9},{9,8},{10,11... | collective-permute-start | bytes 2924552 | tf_op jit(solution)/shard_map/ppermute | solution.py:27
  94.2 24.7 %collective-permute-start.9 = (bf16[2,136,1792]{2,1,0:T(8,128)(2,1)}, bf16[2,136,1792]{2,1,0:T(8,128)(2,1)S(1)}, u32[]{:S(2)}, u32[]{:S(2)}) collective-permute-start(bf16[2,136,1792]{2,1,0:T(8,128)(2,1)} %copy-done.36), channel_id=1, source_target_pairs={{0,2},{1,3},{2,0},{3,1},{4,6},{5,7},{6,4},{7,5},{8,10},{9,11},{10,... | collective-permute-start | bytes 2924552 | tf_op jit(solution)/shard_map/ppermute | solution.py:27
  95.7 33.4 %collective-permute-start.14 = (bf16[136,1792]{1,0:T(8,128)(2,1)}, bf16[136,1792]{1,0:T(8,128)(2,1)}, u32[]{:S(2)}, u32[]{:S(2)}) collective-permute-start(bf16[136,1792]{1,0:T(8,128)(2,1)} %copy-done.9), channel_id=1, source_target_pairs={{0,1},{1,0},{2,3},{3,2},{4,5},{5,4},{6,7},{7,6},{8,9},{9,8},{10,11... | collective-permute-start | bytes 1462280 | tf_op jit(solution)/shard_map/ppermute | solution.py:27
  97.2 33.3 %collective-permute-start.17 = (bf16[136,1792]{1,0:T(8,128)(2,1)}, bf16[136,1792]{1,0:T(8,128)(2,1)}, u32[]{:S(2)}, u32[]{:S(2)}) collective-permute-start(bf16[136,1792]{1,0:T(8,128)(2,1)} %copy-done.12), channel_id=1, source_target_pairs={{0,2},{1,3},{2,0},{3,1},{4,6},{5,7},{6,4},{7,5},{8,10},{9,11},{10,... | collective-permute-start | bytes 1462280 | tf_op jit(solution)/shard_map/ppermute | solution.py:27
  127.0 22.8 %collective-permute-start.18 = (bf16[136,1792]{1,0:T(8,128)(2,1)S(1)}, bf16[136,1792]{1,0:T(8,128)(2,1)}, u32[]{:S(2)}, u32[]{:S(2)}) collective-permute-start(bf16[136,1792]{1,0:T(8,128)(2,1)S(1)} %get-tuple-element.63.refs_6_.refs_8_), channel_id=1, source_target_pairs={{0,1},{1,0},{2,3},{3,2},{4,5},{5,4},{6,7},{7,6},{8,9},{9,8},{10,11... | collective-permute-start | bytes 1462280 | tf_op jit(solution)/shard_map/ppermute | solution.py:27
  127.6 23.8 %collective-permute-start.12 = (bf16[136,1792]{1,0:T(8,128)(2,1)}, bf16[136,1792]{1,0:T(8,128)(2,1)S(1)}, u32[]{:S(2)}, u32[]{:S(2)}) collective-permute-start(bf16[136,1792]{1,0:T(8,128)(2,1)} %copy-done.38), channel_id=1, source_target_pairs={{0,2},{1,3},{2,0},{3,1},{4,6},{5,7},{6,4},{7,5},{8,10},{9,11},{10,... | collective-permute-start | bytes 1462280 | tf_op jit(solution)/shard_map/ppermute | solution.py:27
  129.1 33.2 %collective-permute-start.24 = (bf16[136,1792]{1,0:T(8,128)(2,1)}, bf16[136,1792]{1,0:T(8,128)(2,1)}, u32[]{:S(2)}, u32[]{:S(2)}) collective-permute-start(bf16[136,1792]{1,0:T(8,128)(2,1)} %collective-permute-done.14.refs_2_), channel_id=1, source_target_pairs={{0,2},{1,3},{2,0},{3,1},{4,6},{5,7},{6,4},{7,5},{8,10},{9,11},{10,... | collective-permute-start | bytes 1462280 | tf_op jit(solution)/shard_map/ppermute | solution.py:27
  130.4 32.4 %collective-permute-start.25 = (bf16[136,1792]{1,0:T(8,128)(2,1)}, bf16[136,1792]{1,0:T(8,128)(2,1)}, u32[]{:S(2)}, u32[]{:S(2)}) collective-permute-start(bf16[136,1792]{1,0:T(8,128)(2,1)} %collective-permute-done.17.refs_5_), channel_id=1, source_target_pairs={{0,1},{1,0},{2,3},{3,2},{4,5},{5,4},{6,7},{7,6},{8,9},{9,8},{10,11... | collective-permute-start | bytes 1462280 | tf_op jit(solution)/shard_map/ppermute | solution.py:27
  139.2 24.7 %collective-permute-start.21 = (bf16[136,1792]{1,0:T(8,128)(2,1)}, bf16[136,1792]{1,0:T(8,128)(2,1)}, u32[]{:S(2)}, u32[]{:S(2)}) collective-permute-start(bf16[136,1792]{1,0:T(8,128)(2,1)} %get-tuple-element.64.refs_7_.refs_9_), channel_id=1, source_target_pairs={{0,2},{1,3},{2,0},{3,1},{4,6},{5,7},{6,4},{7,5},{8,10},{9,11},{10,... | collective-permute-start | bytes 1462280 | tf_op jit(solution)/shard_map/ppermute | solution.py:27
  149.8 23.5 %collective-permute-start.26 = (bf16[136,1792]{1,0:T(8,128)(2,1)}, bf16[136,1792]{1,0:T(8,128)(2,1)}, u32[]{:S(2)}, u32[]{:S(2)}) collective-permute-start(bf16[136,1792]{1,0:T(8,128)(2,1)} %collective-permute-done.18.refs_8_.refs_10_), channel_id=1, source_target_pairs={{0,2},{1,3},{2,0},{3,1},{4,6},{5,7},{6,4},{7,5},{8,10},{9,11},{10,... | collective-permute-start | bytes 1462280 | tf_op jit(solution)/shard_map/ppermute | solution.py:27
  156.0 66.9 %all-to-all-start.3 = ((bf16[4,40,3584]{2,1,0:T(8,128)(2,1)}), bf16[4,40,3584]{2,1,0:T(8,128)(2,1)}, u32[]{:S(2)}, u32[]{:S(2)}) async-start(bf16[4,40,3584]{2,1,0:T(8,128)(2,1)} %bitcast.17), calls=%async_computation.3 | async-start | bytes 2293760 | tf_op jit(solution)/shard_map/all_to_all | solution.py:34
  161.4 38.0 %collective-permute-start.15 = (bf16[136,1792]{1,0:T(8,128)(2,1)S(1)}, bf16[136,1792]{1,0:T(8,128)(2,1)S(1)}, u32[]{:S(2)}, u32[]{:S(2)}) collective-permute-start(bf16[136,1792]{1,0:T(8,128)(2,1)S(1)} %copy-done.13), channel_id=1, source_target_pairs={{0,1},{1,0},{2,3},{3,2},{4,5},{5,4},{6,7},{7,6},{8,9},{9,8},{10,11... | collective-permute-start | bytes 1462280 | tf_op jit(solution)/shard_map/ppermute | solution.py:27
  162.3 37.7 %collective-permute-start.16 = (bf16[136,1792]{1,0:T(8,128)(2,1)S(1)}, bf16[136,1792]{1,0:T(8,128)(2,1)S(1)}, u32[]{:S(2)}, u32[]{:S(2)}) collective-permute-start(bf16[136,1792]{1,0:T(8,128)(2,1)S(1)} %copy-done.10), channel_id=1, source_target_pairs={{0,2},{1,3},{2,0},{3,1},{4,6},{5,7},{6,4},{7,5},{8,10},{9,11},{10,... | collective-permute-start | bytes 1462280 | tf_op jit(solution)/shard_map/ppermute | solution.py:27
  162.8 37.2 %collective-permute-start.19 = (bf16[136,1792]{1,0:T(8,128)(2,1)}, bf16[136,1792]{1,0:T(8,128)(2,1)S(1)}, u32[]{:S(2)}, u32[]{:S(2)}) collective-permute-start(bf16[136,1792]{1,0:T(8,128)(2,1)} %get-tuple-element.64.refs_7_.refs_9_), channel_id=1, source_target_pairs={{0,1},{1,0},{2,3},{3,2},{4,5},{5,4},{6,7},{7,6},{8,9},{9,8},{10,11... | collective-permute-start | bytes 1462280 | tf_op jit(solution)/shard_map/ppermute | solution.py:27
  164.0 36.1 %collective-permute-start.20 = (bf16[136,1792]{1,0:T(8,128)(2,1)}, bf16[136,1792]{1,0:T(8,128)(2,1)S(1)}, u32[]{:S(2)}, u32[]{:S(2)}) collective-permute-start(bf16[136,1792]{1,0:T(8,128)(2,1)} %copy-done.15), channel_id=1, source_target_pairs={{0,2},{1,3},{2,0},{3,1},{4,6},{5,7},{6,4},{7,5},{8,10},{9,11},{10,... | collective-permute-start | bytes 1462280 | tf_op jit(solution)/shard_map/ppermute | solution.py:27
  222.8 23.7 %all-to-all-start.5 = ((bf16[4,40,1792]{2,1,0:T(8,128)(2,1)}), bf16[4,40,1792]{2,1,0:T(8,128)(2,1)}, u32[]{:S(2)}, u32[]{:S(2)}) async-start(bf16[4,40,1792]{2,1,0:T(8,128)(2,1)} %bitcast.22), calls=%async_computation.5 | async-start | bytes 1146880 | tf_op jit(solution)/shard_map/all_to_all | solution.py:34
  246.6 23.3 %all-to-all-start.4 = ((bf16[4,40,1792]{2,1,0:T(8,128)(2,1)}), bf16[4,40,1792]{2,1,0:T(8,128)(2,1)S(1)}, u32[]{:S(2)}, u32[]{:S(2)}) async-start(bf16[4,40,1792]{2,1,0:T(8,128)(2,1)} %bitcast.20), calls=%async_computation.4 | async-start | bytes 1146880 | tf_op jit(solution)/shard_map/all_to_all | solution.py:34
  (69 other events, 557.0 us)

commit v6 on v5

--- a/solution.py
+++ b/solution.py
@@ -76,7 +76,7 @@
         out_shape=[jax.ShapeDtypeStruct(shape, kind) for shape, kind in outs],
         in_specs=[space] * len(args),
         out_specs=[space] * len(outs),
-        compiler_params=pltpu.CompilerParams(vmem_limit_bytes=40 * 2**20),
+        compiler_params=pltpu.CompilerParams(vmem_limit_bytes=16 * 2**20),
         cost_estimate=pl.CostEstimate(flops=10**6, bytes_accessed=10**5, transcendentals=0),
         name=name,
     )(*args)
@@ -86,6 +86,13 @@
 TN = ((0,), (0,))
 
 
+def pack_part(blocks, select):
+    def work(ins, outs):
+        outs[0][...] = dot(ins[1][...], ins[0][...]).astype(BF16)
+
+    return on_core("pack", work, [((select.shape[0], blocks.shape[1]), BF16)], blocks, select)[0]
+
+
 def pack_halves(blocks, select):
     rows, half = select.shape[0], blocks.shape[1] // 2
 
@@ -93,35 +100,39 @@
         for h in range(2):
             outs[h][...] = dot(ins[1][...], ins[0][:, h * half : (h + 1) * half]).astype(BF16)
 
-    return on_core("pack", work, [((rows, half), BF16)] * 2, blocks, select)
-
-
-def a_near_rows(blocks, up):
-    half, hidden_units = up.shape[0] // 2, up.shape[1]
-    rows = blocks[0][0].shape[0]
-
-    def work(ins, outs):
+    return tuple(on_core("pack", work, [((rows, half), BF16)] * 2, blocks, select))
+
+
+def a_near_rows(blocks, up, down):
+    half, units, rows = up.shape[0] // 2, up.shape[1], blocks[0][0].shape[0]
+
+    def work(ins, outs):
+        up_ref, down_ref = ins[6:]
         for j in range(3):
-            hidden = dot(ins[2 * j][...], ins[6][:half]) + dot(ins[2 * j + 1][...], ins[6][half:])
-            outs[0][j] = (hidden * jax.nn.sigmoid(hidden)).astype(BF16)
-
-    flat = [half_block for block in blocks for half_block in block]
-    return on_core("a_near", work, [((3, rows, hidden_units), BF16)], *flat, up)[0]
+            hidden = dot(ins[2 * j][...], up_ref[:half]) + dot(ins[2 * j + 1][...], up_ref[half:])
+            act = (hidden * jax.nn.sigmoid(hidden)).astype(BF16)
+            outs[0][j] = act
+            if j:
+                cols = slice((j - 1) * half, j * half)
+                outs[j][...] = dot(act, down_ref[:, cols]).astype(BF16)
+
+    flat = [v for block in blocks for v in block]
+    outs = [((3, rows, units), BF16)] + [((rows, half), BF16)] * 2
+    act, by_x, by_y = on_core("a_near", work, outs, *flat, up, down)
+    return act, (by_x, by_y)
 
 
 def a_far_rows(block, act, up, down):
     half, rows = up.shape[0] // 2, act.shape[1]
 
     def work(ins, outs):
-        lo, hi, acts, up_ref, down_ref = ins
+        lo, hi, _, up_ref, down_ref = ins
         hidden = dot(lo[...], up_ref[:half]) + dot(hi[...], up_ref[half:])
         far = (hidden * jax.nn.sigmoid(hidden)).astype(BF16)
         for h in range(2):
-            weights = down_ref[:, h * half : (h + 1) * half]
-            outs[h][0] = dot(far, weights).astype(BF16)
-            outs[h][1] = dot(acts[1 + h], weights).astype(BF16)
-
-    return on_core("a_far", work, [((2, rows, half), BF16)] * 2, *block, act, up, down)
+            outs[h][...] = dot(far, down_ref[:, h * half : (h + 1) * half]).astype(BF16)
+
+    return tuple(on_core("a_far", work, [((rows, half), BF16)] * 2, *block, act, up, down))
 
 
 def a_second_rows(act, down, got):
@@ -129,40 +140,53 @@
 
     def work(ins, outs):
         acts, down_ref, by_x, by_y = ins
-        outs[0][...] = (dot(acts[1], down_ref[:, half:]) + by_y[0].astype(F32)).astype(BF16)
-        outs[1][...] = (dot(acts[2], down_ref[:, :half]) + by_x[0].astype(F32)).astype(BF16)
-
-    return on_core("a_second", work, [((rows, half), BF16)] * 2, act, down, *got)
-
-
-def a_total_rows(act, down, first, second, place):
+        outs[0][...] = (dot(acts[1], down_ref[:, half:]) + by_y[...].astype(F32)).astype(BF16)
+        outs[1][...] = (dot(acts[2], down_ref[:, :half]) + by_x[...].astype(F32)).astype(BF16)
+
+    return tuple(on_core("a_second", work, [((rows, half), BF16)] * 2, act, down, *got))
+
+
+def a_total_rows(act, down, plain, second, place):
     half = down.shape[1] // 2
 
     def work(ins, outs):
-        acts, down_ref, first_x, first_y, second_x, second_y, place_ref = ins
-        for h, (one, two) in enumerate(((first_x, second_y), (first_y, second_x))):
+        acts, down_ref, plain_x, plain_y, second_x, second_y, place_ref = ins
+        for h, (one, two) in enumerate(((plain_x, second_y), (plain_y, second_x))):
             cols = slice(h * half, (h + 1) * half)
-            total = dot(acts[0], down_ref[:, cols]) + one[1].astype(F32) + two[...].astype(F32)
+            total = dot(acts[0], down_ref[:, cols]) + one[...].astype(F32) + two[...].astype(F32)
             outs[0][:, cols] = dot(place_ref[...], total.astype(BF16)).astype(BF16)
 
     outs = [((place.shape[0], 2 * half), BF16)]
-    return on_core("a_total", work, outs, act, down, *first, *second, place)[0]
-
-
-def back_rows(x_lo, x_hi, c_lo, c_hi, up_ref, down_ref, col_ref):
-    half = x_lo.shape[1]
-    hidden = dot(x_lo, up_ref[:half]) + dot(x_hi, up_ref[half:])
-    score = (dot(x_lo, col_ref[:half]) + dot(x_hi, col_ref[half:]))[:, :1]
-    act_grad = dot(c_lo, down_ref[:, :half], NT) + dot(c_hi, down_ref[:, half:], NT)
+    return on_core("a_total", work, outs, act, down, *plain, *second, place)[0]
+
+
+def b_hidden_rows(blocks, up, col):
+    half, units, rows = up.shape[0] // 2, up.shape[1], blocks[0][0].shape[0]
+
+    def work(ins, outs):
+        up_ref, col_ref = ins[8:]
+        for j in range(4):
+            lo, hi = ins[2 * j][...], ins[2 * j + 1][...]
+            outs[0][j] = dot(lo, up_ref[:half]) + dot(hi, up_ref[half:])
+            outs[1][j] = dot(lo, col_ref[:half]) + dot(hi, col_ref[half:])
+
+    flat = [v for block in blocks for v in block]
+    outs = [((4, rows, units), F32), ((4, rows, 128), F32)]
+    return tuple(on_core("b_hidden", work, outs, *flat, up, col))
+
+
+def back_rows(hidden, score, c_lo, c_hi, down_ref):
+    half = c_lo.shape[1]
+    act_grad = dot(c_lo, down_ref[:half]) + dot(c_hi, down_ref[half:])
     sigma = jax.nn.sigmoid(hidden)
     active = hidden * sigma
     hid_grad = (act_grad * sigma * (1.0 + hidden * (1.0 - sigma))).astype(BF16)
-    term = jnp.sum(active * act_grad, axis=1, keepdims=True) * jax.nn.sigmoid(-score)
+    term = jnp.sum(active * act_grad, axis=1, keepdims=True) * jax.nn.sigmoid(-score[:, :1])
     return active.astype(BF16), hid_grad, term
 
 
 def grad_rows(hid_grad, term, up_ref, line_ref, cols):
-    return dot(hid_grad, up_ref[cols], NT) + term * line_ref[:, cols]
+    return dot(hid_grad, up_ref[:, cols]) + term * line_ref[:, cols]
 
 
 def piece(c, side, half):
@@ -170,21 +194,14 @@
     return slice(begin, begin + half // 2)
 
 
-def b_near_rows(blocks, cots, up, down, col, line):
-    half, units, rows = up.shape[0] // 2, up.shape[1], blocks[0][0].shape[0]
-
-    def work(ins, outs):
-        up_ref, down_ref, col_ref, line_ref = ins[12:]
+def b_near_rows(cots, early, up, down, line):
+    half, units, rows = up.shape[1] // 2, up.shape[0], cots[0][0].shape[0]
+
+    def work(ins, outs):
+        hidden, score, up_ref, down_ref, line_ref = ins[6:]
         for j in range(3):
-            act, hid, term = back_rows(
-                ins[2 * j][...],
-                ins[2 * j + 1][...],
-                ins[6 + 2 * j][...],
-                ins[7 + 2 * j][...],
-                up_ref,
-                down_ref,
-                col_ref,
-            )
+            lo, hi = ins[2 * j][...], ins[2 * j + 1][...]
+            act, hid, term = back_rows(hidden[j], score[j], lo, hi, down_ref)
             outs[0][j], outs[1][j] = act, hid
             outs[2][j] = jnp.broadcast_to(term, (rows, 128))
             if j:
@@ -193,20 +210,19 @@
                     part = grad_rows(hid, term, up_ref, line_ref, cols)
                     outs[2 + j][c] = part.astype(BF16)
 
-    flat = [v for block in blocks for v in block] + [v for block in cots for v in block]
+    flat = [v for block in cots for v in block]
     outs = [((3, rows, units), BF16)] * 2 + [((3, rows, 128), F32)]
     outs += [((2, rows, half // 2), BF16)] * 2
-    act, hid, term, by_x, by_y = on_core("b_near", work, outs, *flat, up, down, col, line)
+    act, hid, term, by_x, by_y = on_core("b_near", work, outs, *flat, *early, up, down, line)
     return (act, hid, term), (by_x, by_y)
 
 
-def b_far_rows(block, cots, up, down, col, line):
-    half, units, rows = up.shape[0] // 2, up.shape[1], block[0].shape[0]
-
-    def work(ins, outs):
-        up_ref, down_ref, col_ref, line_ref = ins[4:]
-        values = [ref[...] for ref in ins[:4]]
-        act, hid, term = back_rows(*values, up_ref, down_ref, col_ref)
+def b_far_rows(cots, early, near, up, down, line):
+    half, units, rows = up.shape[1] // 2, up.shape[0], cots[0].shape[0]
+
+    def work(ins, outs):
+        lo, hi, hidden, score, _, up_ref, down_ref, line_ref = ins
+        act, hid, term = back_rows(hidden[3], score[3], lo[...], hi[...], down_ref)
         outs[0][...], outs[1][...] = act, hid
         for c in range(2):
             for side in range(2):
@@ -214,12 +230,13 @@
                 outs[2 + 2 * c + side][...] = part.astype(BF16)
 
     outs = [((rows, units), BF16)] * 2 + [((rows, half // 2), BF16)] * 4
-    act, hid, x0, y0, x1, y1 = on_core("b_far", work, outs, *block, *cots, up, down, col, line)
+    args = (*cots, *early, near[2], up, down, line)
+    act, hid, x0, y0, x1, y1 = on_core("b_far", work, outs, *args)
     return (act, hid), [(x0, y0), (x1, y1)]
 
 
 def b_second_rows(near, up, line, got, c):
-    half, rows = up.shape[0] // 2, got[0].shape[0]
+    half, rows = up.shape[1] // 2, got[0].shape[0]
 
     def work(ins, outs):
         hids, terms, up_ref, line_ref, by_x, by_y = ins
@@ -233,7 +250,7 @@
 
 
 def b_total_rows(near, up, line, plain, second, place, c):
-    half = up.shape[0] // 2
+    half = up.shape[1] // 2
     quarter = half // 2
 
     def work(ins, outs):
@@ -336,52 +353,61 @@
 
     a_float, _, a_normed = statistics(a_input[0])
     a_pick = selector(a_ids, layout, here)
-    a_blocks = across_planes(select_rows(a_pick, a_normed, layout), layout)
-    a_mine = tuple(pack_halves(a_blocks, select))
+    a_mine = []
+    for h in range(2):
+        send = select_rows(a_pick, a_normed[:, h * half : (h + 1) * half], layout)
+        a_mine.append(pack_part(across_planes(send, layout), select))
+    a_mine = tuple(a_mine)
 
     b_float, b_scale, b_normed = statistics(b_x)
     b_pick = selector(b_ids, layout, here)
     b_send = select_rows(b_pick, b_normed, layout)
-    b_send, a_mine = after((b_send, a_mine))
-    a_near = spread_halves(a_mine, experts)
+    a_x_lo, a_y_lo = swap_pair((a_mine[0], a_mine[0]), experts)
+    up_turned, down_turned = up.T, down.T
+    b_send, a_mine, up_turned, down_turned = after((b_send, a_mine, up_turned, down_turned))
+    a_x_hi, a_y_hi = swap_pair((a_mine[1], a_mine[1]), experts)
+    a_near = ((a_x_lo, a_x_hi), (a_y_lo, a_y_hi))
     a_far = relay_halves(a_near, experts)
     b_blocks = across_planes(b_send, layout)
 
-    act = a_near_rows((a_mine,) + a_near, up)
-    a_first = a_far_rows(a_far, act, up, down)
-    a_first, b_blocks = after((a_first, b_blocks))
-    a_first = swap_pair(a_first, experts)
-    b_mine = tuple(pack_halves(b_blocks, select))
+    act, a_plain = a_near_rows((a_mine,) + a_near, up, down)
+    a_plain = swap_pair(a_plain, experts)
+    a_relay = a_far_rows(a_far, act, up, down)
+    a_relay, a_plain, b_blocks = after((a_relay, a_plain, b_blocks))
+    a_relay = swap_pair(a_relay, experts)
+    b_mine = pack_halves(b_blocks, select)
 
     b_gate = gate_of(b_normed, b_ids, cols_r)
     cot = (b_gate * b_c.astype(F32)).astype(BF16)
     c_send = select_rows(b_pick, cot, layout)
-    c_send, b_mine = after((c_send, b_mine))
     b_near = spread_halves(b_mine, experts)
+    c_send, _, a_relay = after((c_send, b_mine, a_relay))
     b_far = relay_halves(b_near, experts)
     c_blocks = across_planes(c_send, layout)
 
-    a_second = a_second_rows(act, down, a_first)
+    a_second = a_second_rows(act, down, a_relay)
     a_second, c_blocks = after((a_second, c_blocks))
     a_second = swap_pair(a_second, experts)
-    c_mine = tuple(pack_halves(c_blocks, select))
+    c_mine = pack_halves(c_blocks, select)
     c_near = spread_halves(c_mine, experts)
     c_far = relay_halves(c_near, experts)
-    a_back = a_total_rows(act, down, a_first, a_second, place)
+    a_back = a_total_rows(act, down, a_plain, a_second, place)
     a_gate = gate_of(a_normed, a_ids, cols_r)
     a_out = (a_float + a_gate * at_tokens(a_back, a_pick, layout)).astype(BF16)
     a_next = pipe_move(a_out, lambda i, n: i + 1)
 
-    near, b_plain = b_near_rows((b_mine,) + b_near, (c_mine,) + c_near, up, down, col, line)
+    early = b_hidden_rows((b_mine,) + b_near + (b_far,), up, col)
+    near, b_plain = b_near_rows((c_mine,) + c_near, early, up_turned, down_turned, line)
     b_plain = swap_pair(b_plain, experts)
-    far, b_relay = b_far_rows(b_far, c_far, up, down, col, line)
+    far, b_relay = b_far_rows(c_far, early, near, up_turned, down_turned, line)
+    b_relay[1], b_plain = after((b_relay[1], b_plain))
     b_relay = [swap_pair(pair, experts) for pair in b_relay]
-    pieces = []
+    backs = []
     for c in range(2):
-        second = swap_pair(b_second_rows(near, up, line, b_relay[c], c), experts)
-        b_back = b_total_rows(near, up, line, b_plain, second, place, c)
-        pieces.append(at_tokens(b_back, b_pick, layout))
-    normed_grad = jnp.concatenate(pieces, axis=1)
+        second = swap_pair(b_second_rows(near, up_turned, line, b_relay[c], c), experts)
+        backs.append(b_total_rows(near, up_turned, line, b_plain, second, place, c))
+    backs[1], far = after((backs[1], far))
+    normed_grad = jnp.concatenate([at_tokens(back, b_pick, layout) for back in backs], axis=1)
     along = jnp.sum(normed_grad * b_float, axis=-1, keepdims=True) / width
     feature_grad = b_scale * normed_grad - b_float * (b_scale * b_scale * b_scale) * along
     b_out = (b_c.astype(F32) + feature_grad).astype(BF16)

time: 276 us -> 286 us (1.036)
  waiting for transfers between devices: 134 us -> 121 us
  local copies, waits for them, and re-layouts: 24.1 us -> 35.4 us
  other arithmetic: 7.96 us -> 12.6 us
  matrix products: 12.3 us -> 16.3 us
  starting transfers between devices: 65.5 us -> 68.4 us
    ppermute x32 -> x34, waiting for transfers between devices: 109 us -> 97.3 us  [plane_move(): return lax.ppermute(array, 'expert', [(i, i ^ bit) for i in range(devices)])]
    unnamed x103 -> x143, local copies, waits for them, and re-layouts: 23.7 us -> 35 us
    dot_general x8 -> x9, matrix products: 12.3 us -> 16.3 us  [dot(): return lax.dot_general(a, b, (dims, ((), ())), preferred_element_type=F32)]
    all_to_all x6 -> x7, starting transfers between devices: 29.9 us -> 33.1 us  [depth_exchange(): lax.all_to_all(blocks, 'expert', split_axis=0, concat_axis=0, tiled=True,...]
    all_to_all x6 -> x7, waiting for transfers between devices: 25.2 us -> 23.9 us  [depth_exchange(): lax.all_to_all(blocks, 'expert', split_axis=0, concat_axis=0, tiled=True,...]
    pallas_call x14 -> x16, Pallas kernels: 29.8 us -> 29.1 us  [on_core(): pl.pallas_call(kernel, out_shape=[jax.ShapeDtypeStruct(shape, kind) for s...]
    ppermute x32 -> x34, starting transfers between devices: 34.9 us -> 34.8 us  [plane_move(): return lax.ppermute(array, 'expert', [(i, i ^ bit) for i in range(devices)])]
  transfers between devices with their start and end apart: 42 -> 45, of which waited for: 19 -> 25; matrix products, arithmetic and copies ran while one was open for 7% -> 9% of each run, Pallas kernels for 11% -> 10%
where the time goes in v6:
time: 286 us; the launch traced here: 284 us
  waiting for transfers between devices  121 us (42%)
  starting transfers between devices  68.4 us (24%)
  local copies, waits for them, and re-layouts  35.4 us (12%)
  Pallas kernels  29.1 us (10%)
  matrix products  16.3 us (6%)
  other arithmetic  12.6 us (4%)
    ppermute x34, waiting for transfers between devices, plane_move(): return lax.ppermute(array, 'expert', [(i, i ^ bit) for i in range(devices)])  97.3 us
    unnamed x143, local copies, waits for them, and re-layouts  35 us
    ppermute x34, starting transfers between devices, plane_move(): return lax.ppermute(array, 'expert', [(i, i ^ bit) for i in range(devices)])  34.8 us
    all_to_all x7, starting transfers between devices, depth_exchange(): lax.all_to_all(blocks, 'expert', split_axis=0, concat_axis=0, tiled=True,...  33.1 us
    pallas_call x16, Pallas kernels, on_core(): pl.pallas_call(kernel, out_shape=[jax.ShapeDtypeStruct(shape, kind) for s...  29.1 us
    all_to_all x7, waiting for transfers between devices, depth_exchange(): lax.all_to_all(blocks, 'expert', split_axis=0, concat_axis=0, tiled=True,...  23.9 us
    dot_general x9, matrix products, dot(): return lax.dot_general(a, b, (dims, ((), ())), preferred_element_type=F32)  16.3 us
  transfers between devices with their start and end apart: 45, of which 25 were waited for; matrix products, arithmetic and copies ran while one was open for 9% of the time, Pallas kernels for 10%

profile of v6, /device:TPU:0, one launch (start us, length us, event | category | flops | bytes accessed | tf_op | source)
XLA Modules:
  0.0 284.4 jit_solution(17453157843552899026)
XLA Ops:
  5.3 6.3 %all-to-all-start.1 = ((bf16[4,40,1792]{2,1,0:T(8,128)(2,1)}), bf16[4,40,1792]{2,1,0:T(8,128)(2,1)S(1)}, u32[]{:S(2)}, u32[]{:S(2)}) async-start(bf16[4,40,1792]{2,1,0:T(8,128)(2,1)} %bitcast.11), calls=%async_computation.1 | async-start | bytes 1146880 | tf_op jit(solution)/shard_map/all_to_all | solution.py:34
  13.3 13.8 %all-to-all-done.1 = bf16[4,40,1792]{2,1,0:T(8,128)(2,1)S(1)} async-done(((bf16[4,40,1792]{2,1,0:T(8,128)(2,1)}), bf16[4,40,1792]{2,1,0:T(8,128)(2,1)S(1)}, u32[]{:S(2)}, u32[]{:S(2)}) %all-to-all-start.1) | async-done | bytes 573472 | tf_op jit(solution)/shard_map/all_to_all | solution.py:34
  33.5 3.8 %copy.17 = bf16[1,256,3584]{1,2,0:T(8,128)(2,1)} copy(bf16[1,256,3584]{2,1,0:T(8,128)(2,1)} %param.14) | data formatting | bytes 3670016 | tf_op args[6]
  38.0 7.7 %all-to-all-done = bf16[4,40,1792]{2,1,0:T(8,128)(2,1)S(1)} async-done(((bf16[4,40,1792]{2,1,0:T(8,128)(2,1)}), bf16[4,40,1792]{2,1,0:T(8,128)(2,1)S(1)}, u32[]{:S(2)}, u32[]{:S(2)}) %all-to-all-start) | async-done | bytes 573472 | tf_op jit(solution)/shard_map/all_to_all | solution.py:34
  59.1 10.2 %collective-permute-done.2.refs_2_ = bf16[136,1792]{1,0:T(8,128)(2,1)S(1)} collective-permute-done((bf16[136,1792]{1,0:T(8,128)(2,1)}, bf16[136,1792]{1,0:T(8,128)(2,1)S(1)}, u32[]{:S(2)}, u32[]{:S(2)}) %collective-permute-start.2) | collective-permute-done | bytes 487456 | tf_op jit(solution)/shard_map/ppermute | solution.py:27
  72.4 8.7 %collective-permute-done.4.refs_4_ = bf16[136,1792]{1,0:T(8,128)(2,1)S(1)} collective-permute-done((bf16[136,1792]{1,0:T(8,128)(2,1)}, bf16[136,1792]{1,0:T(8,128)(2,1)S(1)}, u32[]{:S(2)}, u32[]{:S(2)}) %collective-permute-start.4) | collective-permute-done | bytes 487456 | tf_op jit(solution)/shard_map/ppermute | solution.py:27
  93.6 5.1 %collective-permute-done.8.refs_2_ = bf16[136,1792]{1,0:T(8,128)(2,1)S(1)} collective-permute-done((bf16[136,1792]{1,0:T(8,128)(2,1)S(1)}, bf16[136,1792]{1,0:T(8,128)(2,1)S(1)}, u32[]{:S(2)}, u32[]{:S(2)}) %collective-permute-start.8) | collective-permute-done | bytes 487456 | tf_op jit(solution)/shard_map/ppermute | solution.py:27
  107.3 4.3 %collective-permute-done.11.refs_2_ = bf16[136,1792]{1,0:T(8,128)(2,1)S(1)} collective-permute-done((bf16[136,1792]{1,0:T(8,128)(2,1)}, bf16[136,1792]{1,0:T(8,128)(2,1)S(1)}, u32[]{:S(2)}, u32[]{:S(2)}) %collective-permute-start.11) | collective-permute-done | bytes 487456 | tf_op jit(solution)/shard_map/ppermute | solution.py:27
  113.6 4.4 %all-to-all-start.3 = ((bf16[4,40,3584]{2,1,0:T(8,128)(2,1)}), bf16[4,40,3584]{2,1,0:T(8,128)(2,1)S(1)}, u32[]{:S(2)}, u32[]{:S(2)}) async-start(bf16[4,40,3584]{2,1,0:T(8,128)(2,1)} %bitcast.87), calls=%async_computation.3 | async-start | bytes 2293760 | tf_op jit(solution)/shard_map/all_to_all | solution.py:34
  122.1 10.1 %collective-permute-done.20.refs_2_ = bf16[136,1792]{1,0:T(8,128)(2,1)} collective-permute-done((bf16[136,1792]{1,0:T(8,128)(2,1)S(1)}, bf16[136,1792]{1,0:T(8,128)(2,1)}, u32[]{:S(2)}, u32[]{:S(2)}) %collective-permute-start.20) | collective-permute-done | bytes 487456 | tf_op jit(solution)/shard_map/ppermute | solution.py:27
  149.6 4.8 %collective-permute-done.13.refs_4_ = bf16[136,1792]{1,0:T(8,128)(2,1)S(1)} collective-permute-done((bf16[136,1792]{1,0:T(8,128)(2,1)}, bf16[136,1792]{1,0:T(8,128)(2,1)S(1)}, u32[]{:S(2)}, u32[]{:S(2)}) %collective-permute-start.13) | collective-permute-done | bytes 487456 | tf_op jit(solution)/shard_map/ppermute | solution.py:27
  156.1 5.2 %collective-permute-done.14.refs_5_ = bf16[136,1792]{1,0:T(8,128)(2,1)S(1)} collective-permute-done((bf16[136,1792]{1,0:T(8,128)(2,1)}, bf16[136,1792]{1,0:T(8,128)(2,1)S(1)}, u32[]{:S(2)}, u32[]{:S(2)}) %collective-permute-start.14) | collective-permute-done | bytes 487456 | tf_op jit(solution)/shard_map/ppermute | solution.py:27
  169.2 5.7 %all-to-all-start.4 = ((bf16[4,40,3584]{2,1,0:T(8,128)(2,1)}), bf16[4,40,3584]{2,1,0:T(8,128)(2,1)}, u32[]{:S(2)}, u32[]{:S(2)}) async-start(bf16[4,40,3584]{2,1,0:T(8,128)(2,1)} %bitcast.27), calls=%async_computation.4 | async-start | bytes 2293760 | tf_op jit(solution)/shard_map/all_to_all | solution.py:34
  179.5 4.2 %b_hidden.1 = (f32[4,136,256]{2,1,0:T(8,128)S(1)}, f32[4,136,128]{2,1,0:T(8,128)S(1)}) custom-call(bf16[136,1792]{1,0:T(8,128)(2,1)S(1)} %get-tuple-element.68.refs_0_, bf16[136,1792]{1,0:T(8,128)(2,1)S(1)} %copy-done.11, bf16[136,1792]{1,0:T(8,128)(2,1)} %collective-permute-done.20.refs_2_, bf16[136,1792]{1,0:T(8,128)(2,1)} %collective-permute-done.21.refs_3_, ...), custom_call_target="tpu_custom_call" | custom-call | flops 1000000 | bytes 100000 | tf_op jit(solution)/shard_map/b_hidden/pallas_call | solution.py:74
  183.7 5.5 %collective-permute-done.16.refs_2_.refs_10_ = bf16[136,1792]{1,0:T(8,128)(2,1)S(1)} collective-permute-done((bf16[136,1792]{1,0:T(8,128)(2,1)}, bf16[136,1792]{1,0:T(8,128)(2,1)S(1)}, u32[]{:S(2)}, u32[]{:S(2)}) %collective-permute-start.16) | collective-permute-done | bytes 487456 | tf_op jit(solution)/shard_map/ppermute | solution.py:27
  190.5 9.1 %collective-permute-done.17.refs_3_.refs_11_ = bf16[136,1792]{1,0:T(8,128)(2,1)S(1)} collective-permute-done((bf16[136,1792]{1,0:T(8,128)(2,1)}, bf16[136,1792]{1,0:T(8,128)(2,1)S(1)}, u32[]{:S(2)}, u32[]{:S(2)}) %collective-permute-start.17) | collective-permute-done | bytes 487456 | tf_op jit(solution)/shard_map/ppermute | solution.py:27
  209.7 5.8 %collective-permute-done.28.refs_4_ = bf16[2,136,896]{2,1,0:T(8,128)(2,1)S(1)} collective-permute-done((bf16[2,136,896]{2,1,0:T(8,128)(2,1)S(1)}, bf16[2,136,896]{2,1,0:T(8,128)(2,1)S(1)}, u32[]{:S(2)}, u32[]{:S(2)}) %collective-permute-start.28) | collective-permute-done | bytes 487456 | tf_op jit(solution)/shard_map/ppermute | solution.py:27
  217.1 4.6 %collective-permute-done.34.refs_4_ = bf16[136,896]{1,0:T(8,128)(2,1)S(1)} collective-permute-done((bf16[136,896]{1,0:T(8,128)(2,1)S(1)}, bf16[136,896]{1,0:T(8,128)(2,1)S(1)}, u32[]{:S(2)}, u32[]{:S(2)}) %collective-permute-start.34) | collective-permute-done | bytes 243744 | tf_op jit(solution)/shard_map/ppermute | solution.py:27
  224.6 5.2 %collective-permute-done.36.refs_6_ = bf16[136,896]{1,0:T(8,128)(2,1)S(1)} collective-permute-done((bf16[136,896]{1,0:T(8,128)(2,1)S(1)}, bf16[136,896]{1,0:T(8,128)(2,1)S(1)}, u32[]{:S(2)}, u32[]{:S(2)}) %collective-permute-start.36) | collective-permute-done | bytes 243744 | tf_op jit(solution)/shard_map/ppermute | solution.py:27
  232.5 4.3 %all-to-all-start.6 = ((bf16[4,40,1792]{2,1,0:T(8,128)(2,1)}), bf16[4,40,1792]{2,1,0:T(8,128)(2,1)}, u32[]{:S(2)}, u32[]{:S(2)}) async-start(bf16[4,40,1792]{2,1,0:T(8,128)(2,1)} %bitcast.33), calls=%async_computation.6 | async-start | bytes 1146880 | tf_op jit(solution)/shard_map/all_to_all | solution.py:34
  238.8 4.5 %collective-permute-done.30.refs_4_ = bf16[136,896]{1,0:T(8,128)(2,1)S(1)} collective-permute-done((bf16[136,896]{1,0:T(8,128)(2,1)}, bf16[136,896]{1,0:T(8,128)(2,1)S(1)}, u32[]{:S(2)}, u32[]{:S(2)}) %collective-permute-start.30) | collective-permute-done | bytes 243744 | tf_op jit(solution)/shard_map/ppermute | solution.py:27
  246.2 5.1 %collective-permute-done.32.refs_6_ = bf16[136,896]{1,0:T(8,128)(2,1)S(1)} collective-permute-done((bf16[136,896]{1,0:T(8,128)(2,1)S(1)}, bf16[136,896]{1,0:T(8,128)(2,1)S(1)}, u32[]{:S(2)}, u32[]{:S(2)}) %collective-permute-start.32) | collective-permute-done | bytes 243744 | tf_op jit(solution)/shard_map/ppermute | solution.py:27
  253.5 5.3 %all-to-all-start.5 = ((bf16[4,40,1792]{2,1,0:T(8,128)(2,1)}), bf16[4,40,1792]{2,1,0:T(8,128)(2,1)}, u32[]{:S(2)}, u32[]{:S(2)}) async-start(bf16[4,40,1792]{2,1,0:T(8,128)(2,1)} %bitcast.31), calls=%async_computation.5 | async-start | bytes 1146880 | tf_op jit(solution)/shard_map/all_to_all | solution.py:34
  265.6 7.9 %weight_grads.1 = (bf16[3584,256]{1,0:T(8,128)(2,1)}, bf16[256,3584]{1,0:T(8,128)(2,1)}) custom-call(bf16[136,1792]{1,0:T(8,128)(2,1)S(1)} %copy-done.9, bf16[136,1792]{1,0:T(8,128)(2,1)S(1)} %copy-done.12, bf16[136,1792]{1,0:T(8,128)(2,1)} %collective-permute-done.20.refs_2_, bf16[136,1792]{1,0:T(8,128)(2,1)} %collective-permute-done.21.refs_3_, ...), custom_call_target="tpu_custom_call" | custom-call | flops 1000000 | bytes 100000 | tf_op jit(solution)/shard_map/weight_grads/pallas_call | solution.py:74
  (266 shorter events, 131.4 us)
Async XLA Ops:
  5.3 21.9 %all-to-all-start.1 = ((bf16[4,40,1792]{2,1,0:T(8,128)(2,1)}), bf16[4,40,1792]{2,1,0:T(8,128)(2,1)S(1)}, u32[]{:S(2)}, u32[]{:S(2)}) async-start(bf16[4,40,1792]{2,1,0:T(8,128)(2,1)} %bitcast.11), calls=%async_computation.1 | async-start | bytes 1146880 | tf_op jit(solution)/shard_map/all_to_all | solution.py:34
  11.6 25.6 %collective-permute-start = (bf16[128,1]{0,1:T(2,128)(2,1)S(1)}, bf16[128,1]{0,1:T(2,128)(2,1)S(1)}, u32[]{:S(2)}, u32[]{:S(2)}) collective-permute-start(bf16[128,1]{0,1:T(2,128)(2,1)S(1)} %convert_bitcast_fusion.1), channel_id=1, source_target_pairs={{0,16},{16,0},{1,17},{17,1},{2,18},{18,2},{3,19},{19,3},{4,20},{20... | collective-permute-start | bytes 776 | tf_op jit(solution)/shard_map/ppermute | solution.py:22
  11.7 35.0 %collective-permute-start.1 = (bf16[128,3584]{1,0:T(8,128)(2,1)}, bf16[128,3584]{1,0:T(8,128)(2,1)}, u32[]{:S(2)}, u32[]{:S(2)}) collective-permute-start(bf16[128,3584]{1,0:T(8,128)(2,1)} %bitcast.7), channel_id=1, source_target_pairs={{0,16},{16,0},{1,17},{17,1},{2,18},{18,2},{3,19},{19,3},{4,20},{20... | collective-permute-start | bytes 2752520 | tf_op jit(solution)/shard_map/ppermute | solution.py:22
  27.2 18.5 %all-to-all-start = ((bf16[4,40,1792]{2,1,0:T(8,128)(2,1)}), bf16[4,40,1792]{2,1,0:T(8,128)(2,1)S(1)}, u32[]{:S(2)}, u32[]{:S(2)}) async-start(bf16[4,40,1792]{2,1,0:T(8,128)(2,1)} %bitcast.9), calls=%async_computation | async-start | bytes 1146880 | tf_op jit(solution)/shard_map/all_to_all | solution.py:34
  51.5 49.0 %all-to-all-start.2 = ((bf16[4,40,3584]{2,1,0:T(8,128)(2,1)}), bf16[4,40,3584]{2,1,0:T(8,128)(2,1)S(1)}, u32[]{:S(2)}, u32[]{:S(2)}) async-start(bf16[4,40,3584]{2,1,0:T(8,128)(2,1)} %bitcast.86), calls=%async_computation.2 | async-start | bytes 2293760 | tf_op jit(solution)/shard_map/all_to_all | solution.py:34
  58.1 23.0 %collective-permute-start.4 = (bf16[136,1792]{1,0:T(8,128)(2,1)}, bf16[136,1792]{1,0:T(8,128)(2,1)S(1)}, u32[]{:S(2)}, u32[]{:S(2)}) collective-permute-start(bf16[136,1792]{1,0:T(8,128)(2,1)} %copy-done.6), channel_id=1, source_target_pairs={{0,2},{1,3},{2,0},{3,1},{4,6},{5,7},{6,4},{7,5},{8,10},{9,11},{10,... | collective-permute-start | bytes 1462280 | tf_op jit(solution)/shard_map/ppermute | solution.py:27
  58.6 22.5 %collective-permute-start.3 = (bf16[136,1792]{1,0:T(8,128)(2,1)S(1)}, bf16[136,1792]{1,0:T(8,128)(2,1)S(1)}, u32[]{:S(2)}, u32[]{:S(2)}) collective-permute-start(bf16[136,1792]{1,0:T(8,128)(2,1)S(1)} %pack.5.refs_1_), channel_id=1, source_target_pairs={{0,1},{1,0},{2,3},{3,2},{4,5},{5,4},{6,7},{7,6},{8,9},{9,8},{10,11... | collective-permute-start | bytes 1462280 | tf_op jit(solution)/shard_map/ppermute | solution.py:27
  59.1 44.2 %collective-permute-start.10 = (bf16[128,3584]{1,0:T(8,128)(2,1)}, bf16[128,3584]{1,0:T(8,128)(2,1)}, u32[]{:S(2)}, u32[]{:S(2)}) collective-permute-start(bf16[128,3584]{1,0:T(8,128)(2,1)} %bitcast.94), channel_id=1, source_target_pairs={{0,16},{16,0},{1,17},{17,1},{2,18},{18,2},{3,19},{19,3},{4,20},{20... | collective-permute-start | bytes 2752520 | tf_op jit(solution)/shard_map/ppermute | solution.py:22
  69.4 22.2 %collective-permute-start.6 = (bf16[136,1792]{1,0:T(8,128)(2,1)S(1)}, bf16[136,1792]{1,0:T(8,128)(2,1)S(1)}, u32[]{:S(2)}, u32[]{:S(2)}) collective-permute-start(bf16[136,1792]{1,0:T(8,128)(2,1)S(1)} %collective-permute-done.2.refs_2_), channel_id=1, source_target_pairs={{0,2},{1,3},{2,0},{3,1},{4,6},{5,7},{6,4},{7,5},{8,10},{9,11},{10,... | collective-permute-start | bytes 1462280 | tf_op jit(solution)/shard_map/ppermute | solution.py:27
  70.9 20.7 %collective-permute-start.7 = (bf16[136,1792]{1,0:T(8,128)(2,1)S(1)}, bf16[136,1792]{1,0:T(8,128)(2,1)S(1)}, u32[]{:S(2)}, u32[]{:S(2)}) collective-permute-start(bf16[136,1792]{1,0:T(8,128)(2,1)S(1)} %collective-permute-done.5.refs_5_), channel_id=1, source_target_pairs={{0,1},{1,0},{2,3},{3,2},{4,5},{5,4},{6,7},{7,6},{8,9},{9,8},{10,11... | collective-permute-start | bytes 1462280 | tf_op jit(solution)/shard_map/ppermute | solution.py:27
  113.6 29.1 %all-to-all-start.3 = ((bf16[4,40,3584]{2,1,0:T(8,128)(2,1)}), bf16[4,40,3584]{2,1,0:T(8,128)(2,1)S(1)}, u32[]{:S(2)}, u32[]{:S(2)}) async-start(bf16[4,40,3584]{2,1,0:T(8,128)(2,1)} %bitcast.87), calls=%async_computation.3 | async-start | bytes 2293760 | tf_op jit(solution)/shard_map/all_to_all | solution.py:34
  119.1 24.9 %collective-permute-start.23 = (bf16[136,1792]{1,0:T(8,128)(2,1)}, bf16[136,1792]{1,0:T(8,128)(2,1)}, u32[]{:S(2)}, u32[]{:S(2)}) collective-permute-start(bf16[136,1792]{1,0:T(8,128)(2,1)} %copy-done.10), channel_id=1, source_target_pairs={{0,2},{1,3},{2,0},{3,1},{4,6},{5,7},{6,4},{7,5},{8,10},{9,11},{10,... | collective-permute-start | bytes 1462280 | tf_op jit(solution)/shard_map/ppermute | solution.py:27
  120.7 54.2 %collective-permute-start.22 = (bf16[136,1792]{1,0:T(8,128)(2,1)S(1)}, bf16[136,1792]{1,0:T(8,128)(2,1)}, u32[]{:S(2)}, u32[]{:S(2)}) collective-permute-start(bf16[136,1792]{1,0:T(8,128)(2,1)S(1)} %get-tuple-element.68.refs_0_), channel_id=1, source_target_pairs={{0,2},{1,3},{2,0},{3,1},{4,6},{5,7},{6,4},{7,5},{8,10},{9,11},{10,... | collective-permute-start | bytes 1462280 | tf_op jit(solution)/shard_map/ppermute | solution.py:27
  121.2 54.6 %collective-permute-start.21 = (bf16[136,1792]{1,0:T(8,128)(2,1)}, bf16[136,1792]{1,0:T(8,128)(2,1)}, u32[]{:S(2)}, u32[]{:S(2)}) collective-permute-start(bf16[136,1792]{1,0:T(8,128)(2,1)} %copy-done.10), channel_id=1, source_target_pairs={{0,1},{1,0},{2,3},{3,2},{4,5},{5,4},{6,7},{7,6},{8,9},{9,8},{10,11... | collective-permute-start | bytes 1462280 | tf_op jit(solution)/shard_map/ppermute | solution.py:27
  132.2 44.0 %collective-permute-start.24 = (bf16[136,1792]{1,0:T(8,128)(2,1)}, bf16[136,1792]{1,0:T(8,128)(2,1)}, u32[]{:S(2)}, u32[]{:S(2)}) collective-permute-start(bf16[136,1792]{1,0:T(8,128)(2,1)} %collective-permute-done.20.refs_2_), channel_id=1, source_target_pairs={{0,2},{1,3},{2,0},{3,1},{4,6},{5,7},{6,4},{7,5},{8,10},{9,11},{10,... | collective-permute-start | bytes 1462280 | tf_op jit(solution)/shard_map/ppermute | solution.py:27
  144.1 17.2 %collective-permute-start.14 = (bf16[136,1792]{1,0:T(8,128)(2,1)}, bf16[136,1792]{1,0:T(8,128)(2,1)S(1)}, u32[]{:S(2)}, u32[]{:S(2)}) collective-permute-start(bf16[136,1792]{1,0:T(8,128)(2,1)} %copy-done.47), channel_id=1, source_target_pairs={{0,2},{1,3},{2,0},{3,1},{4,6},{5,7},{6,4},{7,5},{8,10},{9,11},{10,... | collective-permute-start | bytes 1462280 | tf_op jit(solution)/shard_map/ppermute | solution.py:27
  154.5 23.5 %collective-permute-start.25 = (bf16[136,1792]{1,0:T(8,128)(2,1)}, bf16[136,1792]{1,0:T(8,128)(2,1)S(1)}, u32[]{:S(2)}, u32[]{:S(2)}) collective-permute-start(bf16[136,1792]{1,0:T(8,128)(2,1)} %collective-permute-done.23.refs_5_), channel_id=1, source_target_pairs={{0,1},{1,0},{2,3},{3,2},{4,5},{5,4},{6,7},{7,6},{8,9},{9,8},{10,11... | collective-permute-start | bytes 1462280 | tf_op jit(solution)/shard_map/ppermute | solution.py:27
  161.3 29.2 %collective-permute-start.18 = (bf16[136,1792]{1,0:T(8,128)(2,1)}, bf16[136,1792]{1,0:T(8,128)(2,1)}, u32[]{:S(2)}, u32[]{:S(2)}) collective-permute-start(bf16[136,1792]{1,0:T(8,128)(2,1)} %get-tuple-element.80.refs_0_.refs_8_), channel_id=1, source_target_pairs={{0,2},{1,3},{2,0},{3,1},{4,6},{5,7},{6,4},{7,5},{8,10},{9,11},{10,... | collective-permute-start | bytes 1462280 | tf_op jit(solution)/shard_map/ppermute | solution.py:27
  169.2 63.4 %all-to-all-start.4 = ((bf16[4,40,3584]{2,1,0:T(8,128)(2,1)}), bf16[4,40,3584]{2,1,0:T(8,128)(2,1)}, u32[]{:S(2)}, u32[]{:S(2)}) async-start(bf16[4,40,3584]{2,1,0:T(8,128)(2,1)} %bitcast.27), calls=%async_computation.4 | async-start | bytes 2293760 | tf_op jit(solution)/shard_map/all_to_all | solution.py:34
  176.2 23.4 %collective-permute-start.17 = (bf16[136,1792]{1,0:T(8,128)(2,1)}, bf16[136,1792]{1,0:T(8,128)(2,1)S(1)}, u32[]{:S(2)}, u32[]{:S(2)}) collective-permute-start(bf16[136,1792]{1,0:T(8,128)(2,1)} %copy-done.19), channel_id=1, source_target_pairs={{0,1},{1,0},{2,3},{3,2},{4,5},{5,4},{6,7},{7,6},{8,9},{9,8},{10,11... | collective-permute-start | bytes 1462280 | tf_op jit(solution)/shard_map/ppermute | solution.py:27
  189.2 15.3 %collective-permute-start.26 = (bf16[136,1792]{1,0:T(8,128)(2,1)S(1)}, bf16[136,1792]{1,0:T(8,128)(2,1)S(1)}, u32[]{:S(2)}, u32[]{:S(2)}) collective-permute-start(bf16[136,1792]{1,0:T(8,128)(2,1)S(1)} %collective-permute-done.16.refs_2_.refs_10_), channel_id=1, source_target_pairs={{0,2},{1,3},{2,0},{3,1},{4,6},{5,7},{6,4},{7,5},{8,10},{9,11},{10,... | collective-permute-start | bytes 1462280 | tf_op jit(solution)/shard_map/ppermute | solution.py:27
  189.7 18.0 %collective-permute-start.27 = (bf16[136,1792]{1,0:T(8,128)(2,1)S(1)}, bf16[136,1792]{1,0:T(8,128)(2,1)S(1)}, u32[]{:S(2)}, u32[]{:S(2)}) collective-permute-start(bf16[136,1792]{1,0:T(8,128)(2,1)S(1)} %collective-permute-done.19.refs_5_.refs_13_), channel_id=1, source_target_pairs={{0,1},{1,0},{2,3},{3,2},{4,5},{5,4},{6,7},{7,6},{8,9},{9,8},{10,11... | collective-permute-start | bytes 1462280 | tf_op jit(solution)/shard_map/ppermute | solution.py:27
  232.5 21.0 %all-to-all-start.6 = ((bf16[4,40,1792]{2,1,0:T(8,128)(2,1)}), bf16[4,40,1792]{2,1,0:T(8,128)(2,1)}, u32[]{:S(2)}, u32[]{:S(2)}) async-start(bf16[4,40,1792]{2,1,0:T(8,128)(2,1)} %bitcast.33), calls=%async_computation.6 | async-start | bytes 1146880 | tf_op jit(solution)/shard_map/all_to_all | solution.py:34
  253.5 24.1 %all-to-all-start.5 = ((bf16[4,40,1792]{2,1,0:T(8,128)(2,1)}), bf16[4,40,1792]{2,1,0:T(8,128)(2,1)}, u32[]{:S(2)}, u32[]{:S(2)}) async-start(bf16[4,40,1792]{2,1,0:T(8,128)(2,1)} %bitcast.31), calls=%async_computation.5 | async-start | bytes 1146880 | tf_op jit(solution)/shard_map/all_to_all | solution.py:34
  (91 other events, 831.5 us)

commit v7 on v6

v7 whole, which is shorter than its diff:
```python
import jax
import jax.numpy as jnp
import numpy as np
from jax import lax
from jax.experimental import pallas as pl
from jax.experimental.pallas import tpu as pltpu
from jax.sharding import PartitionSpec as P

EPS = 1e-06
F32 = jnp.float32
BF16 = jnp.bfloat16


def dot(a, b, dims=((1,), (0,))):
    return lax.dot_general(a, b, (dims, ((), ())), preferred_element_type=F32)


def pipe_move(array, target):
    count = lax.axis_size("pipe")
    pairs = [(i, target(i, count) % count) for i in range(count)]
    if all(a == b for a, b in pairs):
        return array
    return lax.ppermute(array, "pipe", pairs)


def plane_move(array, experts, bit):
    devices = lax.axis_size("expert")
    return lax.ppermute(array, "expert", [(i, i ^ bit) for i in range(devices)])


def depth_exchange(blocks, experts):
    devices = lax.axis_size("expert")
    group = devices // experts
    columns = [[e * group + m for e in range(experts)] for m in range(group)]
    return lax.all_to_all(
        blocks, "expert", split_axis=0, concat_axis=0, tiled=True, axis_index_groups=columns
    )


class Layout:
    cuts = 4

    def __init__(self, experts, capacity):
        self.experts = experts
        self.slots = capacity
        self.block = self.cuts * capacity
        self.sent = experts * self.block
        self.packed = experts * capacity

    def places(self):
        packed = np.arange(self.packed)
        found = np.zeros((self.cuts, self.sent, self.packed), np.float32)
        for c in range(self.cuts):
            row = packed // self.slots * self.block + c * self.slots + packed % self.slots
            found[c, row, packed] = 1.0
        return jnp.asarray(found, BF16), jnp.asarray(found.transpose(0, 2, 1), BF16)


def target_rows(ids, layout):
    onehot = (ids[:, None] == jnp.arange(layout.experts, dtype=jnp.int32)).astype(jnp.int32)
    slot = jnp.sum(onehot * (jnp.cumsum(onehot, axis=0) - 1), axis=1)
    first = (ids * layout.block + slot)[:, None]
    return first + layout.slots * jnp.arange(layout.cuts, dtype=jnp.int32)[None, :]


def on_core(name, work, outs, *args):
    def kernel(*refs):
        work(refs[: len(args)], refs[len(args) :])

    space = pl.BlockSpec(memory_space=pltpu.VMEM)
    return pl.pallas_call(
        kernel,
        out_shape=[jax.ShapeDtypeStruct(shape, kind) for shape, kind in outs],
        in_specs=[space] * len(args),
        out_specs=[space] * len(outs),
        compiler_params=pltpu.CompilerParams(vmem_limit_bytes=16 * 2**20),
        cost_estimate=pl.CostEstimate(flops=10**6, bytes_accessed=10**5, transcendentals=0),
        name=name,
    )(*args)


NT = ((1,), (1,))
TN = ((0,), (0,))


TOKEN = ((8, 128), F32)


def sent_rows(values, target, sent):
    cuts, tokens = target.shape
    part = values.shape[1] // cuts
    rows = lax.broadcasted_iota(jnp.int32, (sent, tokens), 0)
    total = 0.0
    for c in range(cuts):
        pick = jnp.where(rows == target[c : c + 1, :], 1.0, 0.0).astype(BF16)
        total = total + dot(pick, values[:, c * part : (c + 1) * part])
    return total.astype(BF16)


def token_rows(ref, target):
    tokens, cuts = target.shape
    rows = lax.broadcasted_iota(jnp.int32, (tokens, ref.shape[0]), 1)
    parts = []
    for c in range(cuts):
        pick = jnp.where(rows == target[:, c : c + 1], 1.0, 0.0).astype(BF16)
        parts.append(dot(pick, ref[...]))
    return jnp.concatenate(parts, axis=1)


def send_normed(x, ids, router, target, layout, after=()):
    tokens, width = x.shape

    def work(ins, outs):
        x_ref, ids_ref, router_ref, target_ref = ins[:4]
        feat = x_ref[...].astype(F32)
        scale = lax.rsqrt(jnp.mean(feat * feat, axis=1, keepdims=True) + EPS)
        normed = (feat * scale).astype(BF16)
        outs[0][...] = sent_rows(normed, target_ref[...], layout.sent)
        scores = dot(normed, router_ref[...])
        expert = lax.broadcasted_iota(jnp.int32, scores.shape, 1)
        score = jnp.sum(jnp.where(expert == ids_ref[...], scores, 0.0), axis=1, keepdims=True)
        outs[1][...] = jnp.broadcast_to(jax.nn.sigmoid(score), (tokens, 128))

    outs = [((layout.sent, width // layout.cuts), BF16), ((tokens, 128), F32)]
    return on_core("send_normed", work, outs, x, ids, router, target.T, *after)


def send_cotangents(cot, gate, target, layout, after=()):
    def work(ins, outs):
        values = (ins[1][:, :1] * ins[0][...].astype(F32)).astype(BF16)
        outs[0][...] = sent_rows(values, ins[2][...], layout.sent)
        outs[1][...] = jnp.zeros(TOKEN[0], F32)

    outs = [((layout.sent, cot.shape[1] // layout.cuts), BF16), TOKEN]
    return on_core("send_cotangents", work, outs, cot, gate, target.T, *after)


def forward_out(x, gate, back, target):
    def work(ins, outs):
        rows = token_rows(ins[2], ins[3][...])
        outs[0][...] = (ins[0][...].astype(F32) + ins[1][:, :1] * rows).astype(BF16)

    return on_core("forward_out", work, [(x.shape, BF16)], x, gate, back, target)[0]


def backward_out(x, cot, back, target):
    width = x.shape[1]

    def work(ins, outs):
        feat = ins[0][...].astype(F32)
        scale = lax.rsqrt(jnp.mean(feat * feat, axis=1, keepdims=True) + EPS)
        normed_grad = token_rows(ins[2], ins[3][...])
        along = jnp.sum(normed_grad * feat, axis=1, keepdims=True) / width
        feature_grad = scale * normed_grad - feat * (scale * scale * scale) * along
        outs[0][...] = (ins[1][...].astype(F32) + feature_grad).astype(BF16)

    return on_core("backward_out", work, [(x.shape, BF16)], x, cot, back, target)[0]


def pack_halves(blocks, select, after=()):
    cuts, rows, _ = select.shape
    part = blocks.shape[1]
    half = cuts * part // 2

    def work(ins, outs):
        for c in range(cuts):
            begin = c * part % half
            outs[c * part // half][:, begin : begin + part] = dot(ins[1][c], ins[0][...]).astype(
                BF16
            )
        outs[2][...] = jnp.zeros(TOKEN[0], F32)

    lo, hi, token = on_core(
        "pack", work, [((rows, half), BF16)] * 2 + [TOKEN], blocks, select, *after
    )
    return (lo, hi), token


def placed(parts, place_ref):
    cuts = place_ref.shape[0]
    part = 2 * parts[0].shape[1] // cuts
    rows = 0.0
    for c in range(cuts):
        begin = c * part % parts[0].shape[1]
        rows = rows + dot(
            place_ref[c], parts[c * part // parts[0].shape[1]][:, begin : begin + part]
        )
    return rows.astype(BF16)


def a_near_rows(blocks, up, after):
    half, hidden_units = up.shape[0] // 2, up.shape[1]
    rows = blocks[0][0].shape[0]

    def work(ins, outs):
        for j in range(3):
            hidden = dot(ins[2 * j][...], ins[6][:half]) + dot(ins[2 * j + 1][...], ins[6][half:])
            outs[0][j] = (hidden * jax.nn.sigmoid(hidden)).astype(BF16)

    flat = [half_block for block in blocks for half_block in block]
    return on_core("a_near", work, [((3, rows, hidden_units), BF16)], *flat, up, after)[0]


def a_far_rows(block, act, up, down):
    half, rows = up.shape[0] // 2, act.shape[1]

    def work(ins, outs):
        lo, hi, acts, up_ref, down_ref = ins
        hidden = dot(lo[...], up_ref[:half]) + dot(hi[...], up_ref[half:])
        far = (hidden * jax.nn.sigmoid(hidden)).astype(BF16)
        for h in range(2):
            weights = down_ref[:, h * half : (h + 1) * half]
            outs[h][0] = dot(far, weights).astype(BF16)
            outs[h][1] = dot(acts[1 + h], weights).astype(BF16)
        outs[2][...] = jnp.zeros(TOKEN[0], F32)

    outs = [((2, rows, half), BF16)] * 2 + [TOKEN]
    by_x, by_y, token = on_core("a_far", work, outs, *block, act, up, down)
    return (by_x, by_y), token


def a_second_rows(act, down, got, after):
    half, rows = down.shape[1] // 2, act.shape[1]

    def work(ins, outs):
        acts, down_ref, by_x, by_y = ins[:4]
        outs[0][...] = (dot(acts[1], down_ref[:, half:]) + by_y[0].astype(F32)).astype(BF16)
        outs[1][...] = (dot(acts[2], down_ref[:, :half]) + by_x[0].astype(F32)).astype(BF16)
        outs[2][...] = jnp.zeros(TOKEN[0], F32)

    outs = [((rows, half), BF16)] * 2 + [TOKEN]
    by_x, by_y, token = on_core("a_second", work, outs, act, down, *got, after)
    return (by_x, by_y), token


def a_total_rows(act, down, first, second, place):
    half = down.shape[1] // 2

    def work(ins, outs):
        acts, down_ref, first_x, first_y, second_x, second_y, place_ref = ins
        parts = []
        for h, (one, two) in enumerate(((first_x, second_y), (first_y, second_x))):
            cols = slice(h * half, (h + 1) * half)
            total = dot(acts[0], down_ref[:, cols]) + one[1].astype(F32) + two[...].astype(F32)
            parts.append(total.astype(BF16))
        outs[0][...] = placed(parts, place_ref)
        outs[1][...] = jnp.zeros(TOKEN[0], F32)

    outs = [((place.shape[1], 2 * half // place.shape[0]), BF16), TOKEN]
    return on_core("a_total", work, outs, act, down, *first, *second, place)


def b_hidden_rows(blocks, up, col, after):
    half, units, rows = up.shape[0] // 2, up.shape[1], blocks[0][0].shape[0]

    def work(ins, outs):
        up_ref, col_ref = ins[8:10]
        for j in range(4):
            lo, hi = ins[2 * j][...], ins[2 * j + 1][...]
            outs[0][j] = dot(lo, up_ref[:half]) + dot(hi, up_ref[half:])
            outs[1][j] = dot(lo, col_ref[:half]) + dot(hi, col_ref[half:])

    flat = [v for block in blocks for v in block]
    outs = [((4, rows, units), F32), ((4, rows, 128), F32)]
    return tuple(on_core("b_hidden", work, outs, *flat, up, col, after))


def back_rows(hidden, score, c_lo, c_hi, down_ref):
    half = c_lo.shape[1]
    act_grad = dot(c_lo, down_ref[:half]) + dot(c_hi, down_ref[half:])
    sigma = jax.nn.sigmoid(hidden)
    active = hidden * sigma
    hid_grad = (act_grad * sigma * (1.0 + hidden * (1.0 - sigma))).astype(BF16)
    term = jnp.sum(active * act_grad, axis=1, keepdims=True) * jax.nn.sigmoid(-score[:, :1])
    return active.astype(BF16), hid_grad, term


def grad_rows(hid_grad, term, up_ref, line_ref, cols):
    return dot(hid_grad, up_ref[:, cols]) + term * line_ref[:, cols]


def b_near_rows(cots, early, up, down, line):
    half, units, rows = up.shape[1] // 2, up.shape[0], cots[0][0].shape[0]

    def work(ins, outs):
        hidden, score, up_ref, down_ref, line_ref = ins[6:]
        for j in range(3):
            lo, hi = ins[2 * j][...], ins[2 * j + 1][...]
            act, hid, term = back_rows(hidden[j], score[j], lo, hi, down_ref)
            outs[0][j], outs[1][j] = act, hid
            outs[2][j] = jnp.broadcast_to(term, (rows, 128))
            if j:
                cols = slice((j - 1) * half, j * half)
                outs[2 + j][...] = grad_rows(hid, term, up_ref, line_ref, cols).astype(BF16)

    flat = [v for block in cots for v in block]
    outs = [((3, rows, units), BF16)] * 2 + [((3, rows, 128), F32)]
    outs += [((rows, half), BF16)] * 2
    act, hid, term, by_x, by_y = on_core("b_near", work, outs, *flat, *early, up, down, line)
    return (act, hid, term), (by_x, by_y)


def b_far_rows(cots, early, near, up, down, line):
    half, units, rows = up.shape[1] // 2, up.shape[0], cots[0].shape[0]

    def work(ins, outs):
        lo, hi, hidden, score, _, up_ref, down_ref, line_ref = ins
        act, hid, term = back_rows(hidden[3], score[3], lo[...], hi[...], down_ref)
        outs[0][...], outs[1][...] = act, hid
        for h in range(2):
            part = grad_rows(hid, term, up_ref, line_ref, slice(h * half, (h + 1) * half))
            outs[2 + h][...] = part.astype(BF16)

    outs = [((rows, units), BF16)] * 2 + [((rows, half), BF16)] * 2
    args = (*cots, *early, near[2], up, down, line)
    act, hid, by_x, by_y = on_core("b_far", work, outs, *args)
    return (act, hid), (by_x, by_y)


def b_second_rows(near, up, line, got, plain):
    half, rows = up.shape[1] // 2, got[0].shape[0]

    def work(ins, outs):
        hids, terms, up_ref, line_ref, by_x, by_y = ins[:6]
        for side, ref in enumerate((by_y, by_x)):
            j, cols = 1 + side, slice((1 - side) * half, (2 - side) * half)
            part = grad_rows(hids[j], terms[j][:, :1], up_ref, line_ref, cols)
            outs[side][...] = (part + ref[...].astype(F32)).astype(BF16)

    outs = [((rows, half), BF16)] * 2
    return on_core("b_second", work, outs, near[1], near[2], up, line, *got, *plain)


def b_total_rows(near, up, line, plain, second, place):
    half = up.shape[1] // 2

    def work(ins, outs):
        hids, terms, up_ref, line_ref, plain_x, plain_y, second_x, second_y, place_ref = ins
        parts = []
        for h, (one, two) in enumerate(((plain_x, second_y), (plain_y, second_x))):
            cols = slice(h * half, (h + 1) * half)
            part = grad_rows(hids[0], terms[0][:, :1], up_ref, line_ref, cols)
            parts.append((part + one[...].astype(F32) + two[...].astype(F32)).astype(BF16))
        outs[0][...] = placed(parts, place_ref)
        outs[1][...] = jnp.zeros(TOKEN[0], F32)

    outs = [((place.shape[1], 2 * half // place.shape[0]), BF16), TOKEN]
    return on_core("b_total", work, outs, near[1], near[2], up, line, *plain, *second, place)


def weight_grads(blocks, cots, near, far, after):
    half, units = blocks[0][0].shape[1], far[0].shape[1]
    tile = 256

    def work(ins, outs):
        xs, cs = ins[0:8], ins[8:16]
        acts = [ins[16][j] for j in range(3)] + [ins[18][...]]
        hids = [ins[17][j] for j in range(3)] + [ins[19][...]]
        for h in range(2):
            for begin in range(0, half, tile):
                cols, out = slice(begin, begin + tile), slice(h * half + begin, h * half + begin + tile)
                up_sum, down_sum = 0.0, 0.0
                for j in range(4):
                    up_sum = up_sum + dot(xs[2 * j + h][:, cols], hids[j], TN)
                    down_sum = down_sum + dot(acts[j], cs[2 * j + h][:, cols], TN)
                outs[0][out, :] = up_sum.astype(BF16)
                outs[1][:, out] = down_sum.astype(BF16)

    flat = [v for block in blocks for v in block] + [v for block in cots for v in block]
    outs = [((2 * half, units), BF16), ((units, 2 * half), BF16)]
    return on_core("weight_grads", work, outs, *flat, near[0], near[1], *far, after)


def across_planes(rows, layout):
    blocks = rows.reshape(layout.experts, layout.block, rows.shape[1])
    return depth_exchange(blocks, layout.experts).reshape(rows.shape)


def swap_pair(pair, experts):
    return plane_move(pair[0], experts, 1), plane_move(pair[1], experts, 2)


def spread_halves(mine, experts):
    x_lo, y_hi = swap_pair(mine, experts)
    x_hi, y_lo = swap_pair((mine[1], mine[0]), experts)
    return (x_lo, x_hi), (y_lo, y_hi)


def relay_halves(near, experts):
    return plane_move(near[0][0], experts, 2), plane_move(near[1][1], experts, 1)


def body(a_input, a_route, b_saved, b_grad, b_route, up_weight, down_weight, router):
    devices = lax.axis_size("expert")
    experts = router.shape[2]
    group = devices // experts
    tokens, width = a_input.shape[1], a_input.shape[2]
    layout = Layout(experts, tokens * a_route.shape[2] // experts + 2)
    here = lax.axis_index("expert") // group
    up, down, cols_r = up_weight[0], down_weight[0], router[0]
    b_ids = pipe_move(b_route[0].astype(BF16), lambda i, n: n - 1 - i).astype(jnp.int32)
    b_x = pipe_move(b_saved[0], lambda i, n: n - 1 - i)
    b_c = pipe_move(b_grad[0], lambda i, n: n - 1 - i)
    a_ids = a_route[0]
    own = jnp.where(jnp.arange(experts) == here, cols_r.astype(F32), 0.0)
    own = jnp.sum(own, axis=1, keepdims=True)
    line = own.reshape(1, width)
    col = jnp.where(jnp.arange(128)[None, :] == 0, own, 0.0).astype(BF16)
    place, select = layout.places()
    a_target, b_target = target_rows(a_ids[:, 0], layout), target_rows(b_ids[:, 0], layout)

    a_send, a_gate = send_normed(a_input[0], a_ids, cols_r, a_target, layout)
    a_mine, a_packed = pack_halves(across_planes(a_send, layout), select)
    b_send, b_gate = send_normed(b_x, b_ids, cols_r, b_target, layout, (a_packed,))
    a_near = spread_halves(a_mine, experts)
    a_far = relay_halves(a_near, experts)
    b_blocks = across_planes(b_send, layout)

    act = a_near_rows((a_mine,) + a_near, up, b_gate)
    a_first, a_ready = a_far_rows(a_far, act, up, down)
    a_first = swap_pair(a_first, experts)
    b_mine, b_packed = pack_halves(b_blocks, select, (a_ready,))
    b_near = spread_halves(b_mine, experts)
    b_far = relay_halves(b_near, experts)
    c_send, c_sent = send_cotangents(b_c, b_gate, b_target, layout, (b_packed,))
    c_blocks = across_planes(c_send, layout)

    a_second, a_done = a_second_rows(act, down, a_first, c_sent)
    a_second = swap_pair(a_second, experts)
    c_mine, _ = pack_halves(c_blocks, select, (a_done,))
    c_near = spread_halves(c_mine, experts)
    c_far = relay_halves(c_near, experts)
    a_total, a_summed = a_total_rows(act, down, a_first, a_second, place)
    a_back = across_planes(a_total, layout)
    a_out = forward_out(a_input[0], a_gate, a_back, a_target)
    a_next = pipe_move(a_out, lambda i, n: i + 1)

    up_turned, down_turned = up.T, down.T
    early = b_hidden_rows((b_mine,) + b_near + (b_far,), up, col, a_summed)
    near, b_plain = b_near_rows((c_mine,) + c_near, early, up_turned, down_turned, line)
    b_plain = swap_pair(b_plain, experts)
    far, b_relay = b_far_rows(c_far, early, near, up_turned, down_turned, line)
    b_relay = swap_pair(b_relay, experts)
    b_second = b_second_rows(near, up_turned, line, b_relay, b_plain)
    b_second = swap_pair(b_second, experts)
    b_total, b_done = b_total_rows(near, up_turned, line, b_plain, b_second, place)
    b_out = backward_out(b_x, b_c, across_planes(b_total, layout), b_target)
    b_next = pipe_move(b_out, lambda i, n: n - i)
    up_grad, down_grad = weight_grads(
        (b_mine,) + b_near + (b_far,), (c_mine,) + c_near + (c_far,), near, far, b_done
    )
    return (a_next[None], b_next[None], up_grad[None], down_grad[None])


def solution(mesh):
    return jax.shard_map(
        body,
        mesh=mesh,
        in_specs=(
            P("pipe", "expert", None),
            P("pipe", "expert", None),
            P("pipe", "expert", None),
            P("pipe", "expert", None),
            P("pipe", "expert", None),
            P("pipe", None, "expert"),
            P("pipe", "expert", None),
            P("pipe", None, None),
        ),
        out_specs=(
            P("pipe", "expert", None),
            P("pipe", "expert", None),
            P("pipe", None, "expert"),
            P("pipe", "expert", None),
        ),
        check_vma=False,
    )
```

time: 286 us -> 270 us (0.944)
  matrix products: 16.3 us -> 0 us
  Pallas kernels: 29.1 us -> 45 us
  starting transfers between devices: 68.4 us -> 55.9 us
  other arithmetic: 12.6 us -> 5.49 us
  local copies, waits for them, and re-layouts: 35.4 us -> 40.1 us
    dot_general x9 -> x0, matrix products: 16.3 us -> none  [dot(): return lax.dot_general(a, b, (dims, ((), ())), preferred_element_type=F32)]
    pallas_call x16 -> x18, Pallas kernels: 29.1 us -> 45 us  [on_core(): pl.pallas_call(kernel, out_shape=[jax.ShapeDtypeStruct(shape, kind) for s...]
    all_to_all x7 -> x5, starting transfers between devices: 33.1 us -> 25.5 us  [depth_exchange(): lax.all_to_all(blocks, 'expert', split_axis=0, concat_axis=0, tiled=True,...]
    ppermute x34 -> x28, starting transfers between devices: 34.8 us -> 29.6 us  [plane_move(): return lax.ppermute(array, 'expert', [(i, i ^ bit) for i in range(devices)])]
    reduce_sum x5 -> x2, other arithmetic: 5.13 us -> 0.99 us  [target_rows(): slot = jnp.sum(onehot * (jnp.cumsum(onehot, axis=0) - 1), axis=1)]
    unnamed x143 -> x112, local copies, waits for them, and re-layouts: 35 us -> 39.1 us
    broadcast_in_dim x1 -> x0, other arithmetic: 2.95 us -> none  [body(): return (a_next[None], b_next[None], up_grad[None], down_grad[None])]
    ppermute x34 -> x28, waiting for transfers between devices: 97.3 us -> 94.6 us  [plane_move(): return lax.ppermute(array, 'expert', [(i, i ^ bit) for i in range(devices)])]
  transfers between devices with their start and end apart: 45 -> 37, of which waited for: 25 -> 17; matrix products, arithmetic and copies ran while one was open for 9% -> 5% of each run, Pallas kernels for 10% -> 13%
where the time goes in v7:
time: 270 us; the launch traced here: 269 us
  waiting for transfers between devices  121 us (45%)
  starting transfers between devices  55.9 us (21%)
  Pallas kernels  45 us (17%)
  local copies, waits for them, and re-layouts  40.1 us (15%)
  other arithmetic  5.49 us (2%)
    ppermute x28, waiting for transfers between devices, plane_move(): return lax.ppermute(array, 'expert', [(i, i ^ bit) for i in range(devices)])  94.6 us
    pallas_call x18, Pallas kernels, on_core(): pl.pallas_call(kernel, out_shape=[jax.ShapeDtypeStruct(shape, kind) for s...  45 us
    unnamed x112, local copies, waits for them, and re-layouts  39.1 us
    ppermute x28, starting transfers between devices, plane_move(): return lax.ppermute(array, 'expert', [(i, i ^ bit) for i in range(devices)])  29.6 us
    all_to_all x5, starting transfers between devices, depth_exchange(): lax.all_to_all(blocks, 'expert', split_axis=0, concat_axis=0, tiled=True,...  25.5 us
    all_to_all x5, waiting for transfers between devices, depth_exchange(): lax.all_to_all(blocks, 'expert', split_axis=0, concat_axis=0, tiled=True,...  24 us
  transfers between devices with their start and end apart: 37, of which 17 were waited for; matrix products, arithmetic and copies ran while one was open for 5% of the time, Pallas kernels for 13%

profile of v7, /device:TPU:0, one launch (start us, length us, event | category | flops | bytes accessed | tf_op | source)
XLA Modules:
  0.0 268.7 jit_solution(5879349773988556924)
XLA Ops:
  10.1 5.9 %all-to-all-start = ((bf16[4,136,896]{2,1,0:T(8,128)(2,1)}), bf16[4,136,896]{2,1,0:T(8,128)(2,1)S(1)}, u32[]{:S(2)}, u32[]{:S(2)}) async-start(bf16[4,136,896]{2,1,0:T(8,128)(2,1)} %bitcast.56), calls=%async_computation | async-start | bytes 1949696 | tf_op jit(solution)/shard_map/all_to_all | solution.py:35
  16.8 24.0 %all-to-all-done = bf16[4,136,896]{2,1,0:T(8,128)(2,1)S(1)} async-done(((bf16[4,136,896]{2,1,0:T(8,128)(2,1)}), bf16[4,136,896]{2,1,0:T(8,128)(2,1)S(1)}, u32[]{:S(2)}, u32[]{:S(2)}) %all-to-all-start) | async-done | bytes 974880 | tf_op jit(solution)/shard_map/all_to_all | solution.py:35
  48.3 4.2 %all-to-all-start.1 = ((bf16[4,136,896]{2,1,0:T(8,128)(2,1)}), bf16[4,136,896]{2,1,0:T(8,128)(2,1)}, u32[]{:S(2)}, u32[]{:S(2)}) async-start(bf16[4,136,896]{2,1,0:T(8,128)(2,1)} %bitcast.53), calls=%async_computation.1 | async-start | bytes 1949696 | tf_op jit(solution)/shard_map/all_to_all | solution.py:35
  56.7 10.2 %collective-permute-done.refs_2_ = bf16[136,1792]{1,0:T(8,128)(2,1)S(1)} collective-permute-done((bf16[136,1792]{1,0:T(8,128)(2,1)}, bf16[136,1792]{1,0:T(8,128)(2,1)S(1)}, u32[]{:S(2)}, u32[]{:S(2)}) %collective-permute-start) | collective-permute-done | bytes 487456 | tf_op jit(solution)/shard_map/ppermute | solution.py:28
  69.9 8.9 %collective-permute-done.2.refs_4_ = bf16[136,1792]{1,0:T(8,128)(2,1)S(1)} collective-permute-done((bf16[136,1792]{1,0:T(8,128)(2,1)}, bf16[136,1792]{1,0:T(8,128)(2,1)S(1)}, u32[]{:S(2)}, u32[]{:S(2)}) %collective-permute-start.2) | collective-permute-done | bytes 487456 | tf_op jit(solution)/shard_map/ppermute | solution.py:28
  81.9 5.5 %collective-permute-done.6.refs_0_ = bf16[136,1792]{1,0:T(8,128)(2,1)S(1)} collective-permute-done((bf16[136,1792]{1,0:T(8,128)(2,1)S(1)}, bf16[136,1792]{1,0:T(8,128)(2,1)S(1)}, u32[]{:S(2)}, u32[]{:S(2)}) %collective-permute-start.6) | collective-permute-done | bytes 487456 | tf_op jit(solution)/shard_map/ppermute | solution.py:28
  99.0 4.7 %all-to-all-start.3 = ((bf16[4,136,896]{2,1,0:T(8,128)(2,1)}), bf16[4,136,896]{2,1,0:T(8,128)(2,1)}, u32[]{:S(2)}, u32[]{:S(2)}) async-start(bf16[4,136,896]{2,1,0:T(8,128)(2,1)} %bitcast.55), calls=%async_computation.3 | async-start | bytes 1949696 | tf_op jit(solution)/shard_map/all_to_all | solution.py:35
  107.7 20.7 %collective-permute-done.8.refs_2_ = bf16[2,136,1792]{2,1,0:T(8,128)(2,1)S(1)} collective-permute-done((bf16[2,136,1792]{2,1,0:T(8,128)(2,1)}, bf16[2,136,1792]{2,1,0:T(8,128)(2,1)S(1)}, u32[]{:S(2)}, u32[]{:S(2)}) %collective-permute-start.8) | collective-permute-done | bytes 974880 | tf_op jit(solution)/shard_map/ppermute | solution.py:28
  134.9 3.1 %pack.5 = (bf16[136,1792]{1,0:T(8,128)(2,1)}, bf16[136,1792]{1,0:T(8,128)(2,1)}, f32[8,128]{1,0:T(8,128)}) custom-call(bf16[544,896]{1,0:T(8,128)(2,1)} %bitcast.20.refs_0_, bf16[4,136,544]{2,1,0:T(8,128)(2,1)S(1)} %copy-done.6, f32[8,128]{1,0:T(8,128)S(1)} %get-tuple-element.59.refs_2_), custom_call_target="tpu_custom_call" | custom-call | flops 1000000 | bytes 100000 | tf_op jit(solution)/shard_map/pack/pallas_call | solution.py:71
  142.5 6.8 %collective-permute-done.11.refs_4_ = bf16[136,1792]{1,0:T(8,128)(2,1)S(1)} collective-permute-done((bf16[136,1792]{1,0:T(8,128)(2,1)}, bf16[136,1792]{1,0:T(8,128)(2,1)S(1)}, u32[]{:S(2)}, u32[]{:S(2)}) %collective-permute-start.11) | collective-permute-done | bytes 487456 | tf_op jit(solution)/shard_map/ppermute | solution.py:28
  155.7 3.9 %copy.32 = bf16[1,256,3584]{1,2,0:T(8,128)(2,1)} copy(bf16[1,256,3584]{2,1,0:T(8,128)(2,1)} %param.16) | data formatting | bytes 3670016 | tf_op args[6]
  168.8 5.1 %all-to-all-start.2 = ((bf16[4,136,896]{2,1,0:T(8,128)(2,1)}), bf16[4,136,896]{2,1,0:T(8,128)(2,1)S(1)}, u32[]{:S(2)}, u32[]{:S(2)}) async-start(bf16[4,136,896]{2,1,0:T(8,128)(2,1)} %bitcast.52), calls=%async_computation.2 | async-start | bytes 1949696 | tf_op jit(solution)/shard_map/all_to_all | solution.py:35
  177.9 3.3 %collective-permute-done.17.refs_5_.refs_13_ = bf16[136,1792]{1,0:T(8,128)(2,1)} collective-permute-done((bf16[136,1792]{1,0:T(8,128)(2,1)}, bf16[136,1792]{1,0:T(8,128)(2,1)}, u32[]{:S(2)}, u32[]{:S(2)}) %collective-permute-start.17) | collective-permute-done | bytes 487456 | tf_op jit(solution)/shard_map/ppermute | solution.py:28
  183.3 4.8 %collective-permute-done.23.refs_7_ = bf16[136,1792]{1,0:T(8,128)(2,1)S(1)} collective-permute-done((bf16[136,1792]{1,0:T(8,128)(2,1)}, bf16[136,1792]{1,0:T(8,128)(2,1)S(1)}, u32[]{:S(2)}, u32[]{:S(2)}) %collective-permute-start.23) | collective-permute-done | bytes 487456 | tf_op jit(solution)/shard_map/ppermute | solution.py:28
  189.8 4.2 %b_hidden.1 = (f32[4,136,256]{2,1,0:T(8,128)S(1)}, f32[4,136,128]{2,1,0:T(8,128)S(1)}) custom-call(bf16[136,1792]{1,0:T(8,128)(2,1)S(1)} %copy-done.19, bf16[136,1792]{1,0:T(8,128)(2,1)} %get-tuple-element.63.refs_1_, bf16[136,1792]{1,0:T(8,128)(2,1)} %collective-permute-done.18.refs_2_, bf16[136,1792]{1,0:T(8,128)(2,1)} %collective-permute-done.19.refs_3_, ...), custom_call_target="tpu_custom_call" | custom-call | flops 1000000 | bytes 100000 | tf_op jit(solution)/shard_map/b_hidden/pallas_call | solution.py:71
  194.1 3.9 %collective-permute-done.15.refs_3_.refs_11_ = bf16[136,1792]{1,0:T(8,128)(2,1)S(1)} collective-permute-done((bf16[136,1792]{1,0:T(8,128)(2,1)}, bf16[136,1792]{1,0:T(8,128)(2,1)S(1)}, u32[]{:S(2)}, u32[]{:S(2)}) %collective-permute-start.15) | collective-permute-done | bytes 487456 | tf_op jit(solution)/shard_map/ppermute | solution.py:28
  198.0 3.7 %b_near.1 = (bf16[3,136,256]{2,1,0:T(8,128)(2,1)S(1)}, bf16[3,136,256]{2,1,0:T(8,128)(2,1)S(1)}, f32[3,136,128]{2,1,0:T(8,128)S(1)}, bf16[136,1792]{1,0:T(8,128)(2,1)S(1)}, bf16[136,1792]{1,0:T(8,128)(2,1)S(1)}) custom-call(bf16[136,1792]{1,0:T(8,128)(2,1)} %get-tuple-element.60.refs_0_.refs_8_, bf16[136,1792]{1,0:T(8,128)(2,1)} %get-tuple-element.61.refs_1_.refs_9_, ...), custom_call_target="tpu_custom_call" | custom-call | flops 1000000 | bytes 100000 | tf_op jit(solution)/shard_map/b_near/pallas_call | solution.py:71
  203.2 5.2 %collective-permute-done.27.refs_1_.refs_15_ = bf16[136,1792]{1,0:T(8,128)(2,1)S(1)} collective-permute-done((bf16[136,1792]{1,0:T(8,128)(2,1)}, bf16[136,1792]{1,0:T(8,128)(2,1)S(1)}, u32[]{:S(2)}, u32[]{:S(2)}) %collective-permute-start.27) | collective-permute-done | bytes 487456 | tf_op jit(solution)/shard_map/ppermute | solution.py:28
  211.3 4.4 %collective-permute-done.24.refs_6_.refs_4_ = bf16[136,1792]{1,0:T(8,128)(2,1)S(1)} collective-permute-done((bf16[136,1792]{1,0:T(8,128)(2,1)S(1)}, bf16[136,1792]{1,0:T(8,128)(2,1)S(1)}, u32[]{:S(2)}, u32[]{:S(2)}) %collective-permute-start.24) | collective-permute-done | bytes 487456 | tf_op jit(solution)/shard_map/ppermute | solution.py:28
  215.7 10.0 %collective-permute-done.28.refs_4_ = bf16[136,1792]{1,0:T(8,128)(2,1)S(1)} collective-permute-done((bf16[136,1792]{1,0:T(8,128)(2,1)S(1)}, bf16[136,1792]{1,0:T(8,128)(2,1)S(1)}, u32[]{:S(2)}, u32[]{:S(2)}) %collective-permute-start.28) | collective-permute-done | bytes 487456 | tf_op jit(solution)/shard_map/ppermute | solution.py:28
  227.6 7.6 %collective-permute-done.30.refs_6_ = bf16[136,1792]{1,0:T(8,128)(2,1)S(1)} collective-permute-done((bf16[136,1792]{1,0:T(8,128)(2,1)S(1)}, bf16[136,1792]{1,0:T(8,128)(2,1)S(1)}, u32[]{:S(2)}, u32[]{:S(2)}) %collective-permute-start.30) | collective-permute-done | bytes 487456 | tf_op jit(solution)/shard_map/ppermute | solution.py:28
  239.3 5.6 %all-to-all-start.4 = ((bf16[4,136,896]{2,1,0:T(8,128)(2,1)}), bf16[4,136,896]{2,1,0:T(8,128)(2,1)S(1)}, u32[]{:S(2)}, u32[]{:S(2)}) async-start(bf16[4,136,896]{2,1,0:T(8,128)(2,1)} %bitcast.54), calls=%async_computation.4 | async-start | bytes 1949696 | tf_op jit(solution)/shard_map/all_to_all | solution.py:35
  255.6 8.3 %weight_grads.1 = (bf16[3584,256]{1,0:T(8,128)(2,1)}, bf16[256,3584]{1,0:T(8,128)(2,1)}) custom-call(bf16[136,1792]{1,0:T(8,128)(2,1)S(1)} %copy-done.19, bf16[136,1792]{1,0:T(8,128)(2,1)} %get-tuple-element.63.refs_1_, bf16[136,1792]{1,0:T(8,128)(2,1)} %collective-permute-done.18.refs_2_, bf16[136,1792]{1,0:T(8,128)(2,1)} %collective-permute-done.19.refs_3_, ...), custom_call_target="tpu_custom_call" | custom-call | flops 1000000 | bytes 100000 | tf_op jit(solution)/shard_map/weight_grads/pallas_call | solution.py:71
  263.9 3.9 %backward_out.1 = bf16[128,3584]{1,0:T(8,128)(2,1)} custom-call(bf16[128,3584]{1,0:T(8,128)(2,1)} %collective-permute-done.4.refs_0_, bf16[128,3584]{1,0:T(8,128)(2,1)} %collective-permute-done.10.refs_0_.refs_1_, bf16[544,896]{1,0:T(8,128)(2,1)S(1)} %bitcast.49, s32[128,4]{1,0:T(8,128)S(1)} %get-tuple-element.82.refs_3_), custom_call_target="tpu_custom_call" | custom-call | flops 1000000 | bytes 100000 | tf_op jit(solution)/shard_map/backward_out/pallas_call | solution.py:71
  (202 shorter events, 99.7 us)
Async XLA Ops:
  10.1 30.7 %all-to-all-start = ((bf16[4,136,896]{2,1,0:T(8,128)(2,1)}), bf16[4,136,896]{2,1,0:T(8,128)(2,1)S(1)}, u32[]{:S(2)}, u32[]{:S(2)}) async-start(bf16[4,136,896]{2,1,0:T(8,128)(2,1)} %bitcast.56), calls=%async_computation | async-start | bytes 1949696 | tf_op jit(solution)/shard_map/all_to_all | solution.py:35
  16.0 27.5 %collective-permute-start.4 = (bf16[128,3584]{1,0:T(8,128)(2,1)}, bf16[128,3584]{1,0:T(8,128)(2,1)}, u32[]{:S(2)}, u32[]{:S(2)}) collective-permute-start(bf16[128,3584]{1,0:T(8,128)(2,1)} %bitcast.65), channel_id=1, source_target_pairs={{0,16},{16,0},{1,17},{17,1},{2,18},{18,2},{3,19},{19,3},{4,20},{20... | collective-permute-start | bytes 2752520 | tf_op jit(solution)/shard_map/ppermute | solution.py:23
  48.3 43.2 %all-to-all-start.1 = ((bf16[4,136,896]{2,1,0:T(8,128)(2,1)}), bf16[4,136,896]{2,1,0:T(8,128)(2,1)}, u32[]{:S(2)}, u32[]{:S(2)}) async-start(bf16[4,136,896]{2,1,0:T(8,128)(2,1)} %bitcast.53), calls=%async_computation.1 | async-start | bytes 1949696 | tf_op jit(solution)/shard_map/all_to_all | solution.py:35
  55.6 39.8 %collective-permute-start.10 = (bf16[128,3584]{1,0:T(8,128)(2,1)}, bf16[128,3584]{1,0:T(8,128)(2,1)}, u32[]{:S(2)}, u32[]{:S(2)}) collective-permute-start(bf16[128,3584]{1,0:T(8,128)(2,1)} %bitcast.66), channel_id=1, source_target_pairs={{0,16},{16,0},{1,17},{17,1},{2,18},{18,2},{3,19},{19,3},{4,20},{20... | collective-permute-start | bytes 2752520 | tf_op jit(solution)/shard_map/ppermute | solution.py:23
  55.6 23.2 %collective-permute-start.2 = (bf16[136,1792]{1,0:T(8,128)(2,1)}, bf16[136,1792]{1,0:T(8,128)(2,1)S(1)}, u32[]{:S(2)}, u32[]{:S(2)}) collective-permute-start(bf16[136,1792]{1,0:T(8,128)(2,1)} %copy-done.39), channel_id=1, source_target_pairs={{0,2},{1,3},{2,0},{3,1},{4,6},{5,7},{6,4},{7,5},{8,10},{9,11},{10,... | collective-permute-start | bytes 1462280 | tf_op jit(solution)/shard_map/ppermute | solution.py:28
  56.1 22.7 %collective-permute-start.1 = (bf16[136,1792]{1,0:T(8,128)(2,1)}, bf16[136,1792]{1,0:T(8,128)(2,1)S(1)}, u32[]{:S(2)}, u32[]{:S(2)}) collective-permute-start(bf16[136,1792]{1,0:T(8,128)(2,1)} %copy-done.41), channel_id=1, source_target_pairs={{0,1},{1,0},{2,3},{3,2},{4,5},{5,4},{6,7},{7,6},{8,9},{9,8},{10,11... | collective-permute-start | bytes 1462280 | tf_op jit(solution)/shard_map/ppermute | solution.py:28
  66.9 20.5 %collective-permute-start.6 = (bf16[136,1792]{1,0:T(8,128)(2,1)S(1)}, bf16[136,1792]{1,0:T(8,128)(2,1)S(1)}, u32[]{:S(2)}, u32[]{:S(2)}) collective-permute-start(bf16[136,1792]{1,0:T(8,128)(2,1)S(1)} %collective-permute-done.refs_2_), channel_id=1, source_target_pairs={{0,2},{1,3},{2,0},{3,1},{4,6},{5,7},{6,4},{7,5},{8,10},{9,11},{10,... | collective-permute-start | bytes 1462280 | tf_op jit(solution)/shard_map/ppermute | solution.py:28
  68.4 18.9 %collective-permute-start.7 = (bf16[136,1792]{1,0:T(8,128)(2,1)S(1)}, bf16[136,1792]{1,0:T(8,128)(2,1)S(1)}, u32[]{:S(2)}, u32[]{:S(2)}) collective-permute-start(bf16[136,1792]{1,0:T(8,128)(2,1)S(1)} %collective-permute-done.3.refs_5_), channel_id=1, source_target_pairs={{0,1},{1,0},{2,3},{3,2},{4,5},{5,4},{6,7},{7,6},{8,9},{9,8},{10,11... | collective-permute-start | bytes 1462280 | tf_op jit(solution)/shard_map/ppermute | solution.py:28
  99.0 35.9 %all-to-all-start.3 = ((bf16[4,136,896]{2,1,0:T(8,128)(2,1)}), bf16[4,136,896]{2,1,0:T(8,128)(2,1)}, u32[]{:S(2)}, u32[]{:S(2)}) async-start(bf16[4,136,896]{2,1,0:T(8,128)(2,1)} %bitcast.55), calls=%async_computation.3 | async-start | bytes 1949696 | tf_op jit(solution)/shard_map/all_to_all | solution.py:35
  103.7 24.7 %collective-permute-start.8 = (bf16[2,136,1792]{2,1,0:T(8,128)(2,1)}, bf16[2,136,1792]{2,1,0:T(8,128)(2,1)S(1)}, u32[]{:S(2)}, u32[]{:S(2)}) collective-permute-start(bf16[2,136,1792]{2,1,0:T(8,128)(2,1)} %copy-done.53), channel_id=1, source_target_pairs={{0,1},{1,0},{2,3},{3,2},{4,5},{5,4},{6,7},{7,6},{8,9},{9,8},{10,11... | collective-permute-start | bytes 2924552 | tf_op jit(solution)/shard_map/ppermute | solution.py:28
  104.2 24.7 %collective-permute-start.9 = (bf16[2,136,1792]{2,1,0:T(8,128)(2,1)}, bf16[2,136,1792]{2,1,0:T(8,128)(2,1)S(1)}, u32[]{:S(2)}, u32[]{:S(2)}) collective-permute-start(bf16[2,136,1792]{2,1,0:T(8,128)(2,1)} %copy-done.52), channel_id=1, source_target_pairs={{0,2},{1,3},{2,0},{3,1},{4,6},{5,7},{6,4},{7,5},{8,10},{9,11},{10,... | collective-permute-start | bytes 2924552 | tf_op jit(solution)/shard_map/ppermute | solution.py:28
  105.7 33.8 %collective-permute-start.20 = (bf16[136,1792]{1,0:T(8,128)(2,1)}, bf16[136,1792]{1,0:T(8,128)(2,1)}, u32[]{:S(2)}, u32[]{:S(2)}) collective-permute-start(bf16[136,1792]{1,0:T(8,128)(2,1)} %copy-done.18), channel_id=1, source_target_pairs={{0,2},{1,3},{2,0},{3,1},{4,6},{5,7},{6,4},{7,5},{8,10},{9,11},{10,... | collective-permute-start | bytes 1462280 | tf_op jit(solution)/shard_map/ppermute | solution.py:28
  106.2 34.8 %collective-permute-start.18 = (bf16[136,1792]{1,0:T(8,128)(2,1)}, bf16[136,1792]{1,0:T(8,128)(2,1)}, u32[]{:S(2)}, u32[]{:S(2)}) collective-permute-start(bf16[136,1792]{1,0:T(8,128)(2,1)} %copy-done.18), channel_id=1, source_target_pairs={{0,1},{1,0},{2,3},{3,2},{4,5},{5,4},{6,7},{7,6},{8,9},{9,8},{10,11... | collective-permute-start | bytes 1462280 | tf_op jit(solution)/shard_map/ppermute | solution.py:28
  134.4 39.5 %collective-permute-start.21 = (bf16[136,1792]{1,0:T(8,128)(2,1)}, bf16[136,1792]{1,0:T(8,128)(2,1)}, u32[]{:S(2)}, u32[]{:S(2)}) collective-permute-start(bf16[136,1792]{1,0:T(8,128)(2,1)} %get-tuple-element.63.refs_1_), channel_id=1, source_target_pairs={{0,2},{1,3},{2,0},{3,1},{4,6},{5,7},{6,4},{7,5},{8,10},{9,11},{10,... | collective-permute-start | bytes 1462280 | tf_op jit(solution)/shard_map/ppermute | solution.py:28
  139.5 35.9 %collective-permute-start.19 = (bf16[136,1792]{1,0:T(8,128)(2,1)}, bf16[136,1792]{1,0:T(8,128)(2,1)}, u32[]{:S(2)}, u32[]{:S(2)}) collective-permute-start(bf16[136,1792]{1,0:T(8,128)(2,1)} %get-tuple-element.63.refs_1_), channel_id=1, source_target_pairs={{0,1},{1,0},{2,3},{3,2},{4,5},{5,4},{6,7},{7,6},{8,9},{9,8},{10,11... | collective-permute-start | bytes 1462280 | tf_op jit(solution)/shard_map/ppermute | solution.py:28
  141.0 34.9 %collective-permute-start.22 = (bf16[136,1792]{1,0:T(8,128)(2,1)}, bf16[136,1792]{1,0:T(8,128)(2,1)}, u32[]{:S(2)}, u32[]{:S(2)}) collective-permute-start(bf16[136,1792]{1,0:T(8,128)(2,1)} %collective-permute-done.18.refs_2_), channel_id=1, source_target_pairs={{0,2},{1,3},{2,0},{3,1},{4,6},{5,7},{6,4},{7,5},{8,10},{9,11},{10,... | collective-permute-start | bytes 1462280 | tf_op jit(solution)/shard_map/ppermute | solution.py:28
  150.1 26.3 %collective-permute-start.14 = (bf16[136,1792]{1,0:T(8,128)(2,1)}, bf16[136,1792]{1,0:T(8,128)(2,1)}, u32[]{:S(2)}, u32[]{:S(2)}) collective-permute-start(bf16[136,1792]{1,0:T(8,128)(2,1)} %get-tuple-element.60.refs_0_.refs_8_), channel_id=1, source_target_pairs={{0,1},{1,0},{2,3},{3,2},{4,5},{5,4},{6,7},{7,6},{8,9},{9,8},{10,11... | collective-permute-start | bytes 1462280 | tf_op jit(solution)/shard_map/ppermute | solution.py:28
  151.4 29.9 %collective-permute-start.17 = (bf16[136,1792]{1,0:T(8,128)(2,1)}, bf16[136,1792]{1,0:T(8,128)(2,1)}, u32[]{:S(2)}, u32[]{:S(2)}) collective-permute-start(bf16[136,1792]{1,0:T(8,128)(2,1)} %get-tuple-element.61.refs_1_.refs_9_), channel_id=1, source_target_pairs={{0,2},{1,3},{2,0},{3,1},{4,6},{5,7},{6,4},{7,5},{8,10},{9,11},{10,... | collective-permute-start | bytes 1462280 | tf_op jit(solution)/shard_map/ppermute | solution.py:28
  168.8 70.5 %all-to-all-start.2 = ((bf16[4,136,896]{2,1,0:T(8,128)(2,1)}), bf16[4,136,896]{2,1,0:T(8,128)(2,1)S(1)}, u32[]{:S(2)}, u32[]{:S(2)}) async-start(bf16[4,136,896]{2,1,0:T(8,128)(2,1)} %bitcast.52), calls=%async_computation.2 | async-start | bytes 1949696 | tf_op jit(solution)/shard_map/all_to_all | solution.py:35
  175.4 18.7 %collective-permute-start.16 = (bf16[136,1792]{1,0:T(8,128)(2,1)}, bf16[136,1792]{1,0:T(8,128)(2,1)S(1)}, u32[]{:S(2)}, u32[]{:S(2)}) collective-permute-start(bf16[136,1792]{1,0:T(8,128)(2,1)} %get-tuple-element.60.refs_0_.refs_8_), channel_id=1, source_target_pairs={{0,2},{1,3},{2,0},{3,1},{4,6},{5,7},{6,4},{7,5},{8,10},{9,11},{10,... | collective-permute-start | bytes 1462280 | tf_op jit(solution)/shard_map/ppermute | solution.py:28
  175.9 22.1 %collective-permute-start.15 = (bf16[136,1792]{1,0:T(8,128)(2,1)}, bf16[136,1792]{1,0:T(8,128)(2,1)S(1)}, u32[]{:S(2)}, u32[]{:S(2)}) collective-permute-start(bf16[136,1792]{1,0:T(8,128)(2,1)} %get-tuple-element.61.refs_1_.refs_9_), channel_id=1, source_target_pairs={{0,1},{1,0},{2,3},{3,2},{4,5},{5,4},{6,7},{7,6},{8,9},{9,8},{10,11... | collective-permute-start | bytes 1462280 | tf_op jit(solution)/shard_map/ppermute | solution.py:28
  176.4 26.8 %collective-permute-start.26 = (bf16[136,1792]{1,0:T(8,128)(2,1)}, bf16[136,1792]{1,0:T(8,128)(2,1)S(1)}, u32[]{:S(2)}, u32[]{:S(2)}) collective-permute-start(bf16[136,1792]{1,0:T(8,128)(2,1)} %collective-permute-done.14.refs_2_.refs_10_), channel_id=1, source_target_pairs={{0,2},{1,3},{2,0},{3,1},{4,6},{5,7},{6,4},{7,5},{8,10},{9,11},{10,... | collective-permute-start | bytes 1462280 | tf_op jit(solution)/shard_map/ppermute | solution.py:28
  181.3 27.1 %collective-permute-start.27 = (bf16[136,1792]{1,0:T(8,128)(2,1)}, bf16[136,1792]{1,0:T(8,128)(2,1)S(1)}, u32[]{:S(2)}, u32[]{:S(2)}) collective-permute-start(bf16[136,1792]{1,0:T(8,128)(2,1)} %collective-permute-done.17.refs_5_.refs_13_), channel_id=1, source_target_pairs={{0,1},{1,0},{2,3},{3,2},{4,5},{5,4},{6,7},{7,6},{8,9},{9,8},{10,11... | collective-permute-start | bytes 1462280 | tf_op jit(solution)/shard_map/ppermute | solution.py:28
  239.3 24.6 %all-to-all-start.4 = ((bf16[4,136,896]{2,1,0:T(8,128)(2,1)}), bf16[4,136,896]{2,1,0:T(8,128)(2,1)S(1)}, u32[]{:S(2)}, u32[]{:S(2)}) async-start(bf16[4,136,896]{2,1,0:T(8,128)(2,1)} %bitcast.54), calls=%async_computation.4 | async-start | bytes 1949696 | tf_op jit(solution)/shard_map/all_to_all | solution.py:35
  (67 other events, 484.1 us)

commit v8 on v7

--- a/solution.py
+++ b/solution.py
@@ -63,20 +63,22 @@
     return first + layout.slots * jnp.arange(layout.cuts, dtype=jnp.int32)[None, :]
 
 
-def on_core(name, work, outs, *args):
+def on_core(name, work, outs, *args, after=()):
+    first_out = len(args) + len(after)
+
     def kernel(*refs):
-        work(refs[: len(args)], refs[len(args) :])
+        work(refs[: len(args)], refs[first_out:])
 
     space = pl.BlockSpec(memory_space=pltpu.VMEM)
     return pl.pallas_call(
         kernel,
         out_shape=[jax.ShapeDtypeStruct(shape, kind) for shape, kind in outs],
-        in_specs=[space] * len(args),
+        in_specs=[space] * len(args) + [pl.BlockSpec(memory_space=pl.ANY)] * len(after),
         out_specs=[space] * len(outs),
         compiler_params=pltpu.CompilerParams(vmem_limit_bytes=16 * 2**20),
         cost_estimate=pl.CostEstimate(flops=10**6, bytes_accessed=10**5, transcendentals=0),
         name=name,
-    )(*args)
+    )(*args, *after)
 
 
 NT = ((1,), (1,))
@@ -122,7 +124,7 @@
         outs[1][...] = jnp.broadcast_to(jax.nn.sigmoid(score), (tokens, 128))
 
     outs = [((layout.sent, width // layout.cuts), BF16), ((tokens, 128), F32)]
-    return on_core("send_normed", work, outs, x, ids, router, target.T, *after)
+    return on_core("send_normed", work, outs, x, ids, router, target.T, after=after)
 
 
 def send_cotangents(cot, gate, target, layout, after=()):
@@ -132,7 +134,7 @@
         outs[1][...] = jnp.zeros(TOKEN[0], F32)
 
     outs = [((layout.sent, cot.shape[1] // layout.cuts), BF16), TOKEN]
-    return on_core("send_cotangents", work, outs, cot, gate, target.T, *after)
+    return on_core("send_cotangents", work, outs, cot, gate, target.T, after=after)
 
 
 def forward_out(x, gate, back, target):
@@ -171,7 +173,7 @@
         outs[2][...] = jnp.zeros(TOKEN[0], F32)
 
     lo, hi, token = on_core(
-        "pack", work, [((rows, half), BF16)] * 2 + [TOKEN], blocks, select, *after
+        "pack", work, [((rows, half), BF16)] * 2 + [TOKEN], blocks, select, after=after
     )
     return (lo, hi), token
 
@@ -198,7 +200,7 @@
             outs[0][j] = (hidden * jax.nn.sigmoid(hidden)).astype(BF16)
 
     flat = [half_block for block in blocks for half_block in block]
-    return on_core("a_near", work, [((3, rows, hidden_units), BF16)], *flat, up, after)[0]
+    return on_core("a_near", work, [((3, rows, hidden_units), BF16)], *flat, up, after=(after,))[0]
 
 
 def a_far_rows(block, act, up, down):
@@ -219,21 +221,21 @@
     return (by_x, by_y), token
 
 
-def a_second_rows(act, down, got, after):
+def a_second_rows(act, down, got, after=()):
     half, rows = down.shape[1] // 2, act.shape[1]
 
     def work(ins, outs):
-        acts, down_ref, by_x, by_y = ins[:4]
+        acts, down_ref, by_x, by_y = ins
         outs[0][...] = (dot(acts[1], down_ref[:, half:]) + by_y[0].astype(F32)).astype(BF16)
         outs[1][...] = (dot(acts[2], down_ref[:, :half]) + by_x[0].astype(F32)).astype(BF16)
         outs[2][...] = jnp.zeros(TOKEN[0], F32)
 
     outs = [((rows, half), BF16)] * 2 + [TOKEN]
-    by_x, by_y, token = on_core("a_second", work, outs, act, down, *got, after)
+    by_x, by_y, token = on_core("a_second", work, outs, act, down, *got, after=after)
     return (by_x, by_y), token
 
 
-def a_total_rows(act, down, first, second, place):
+def a_total_rows(act, down, first, second, place, after):
     half = down.shape[1] // 2
 
     def work(ins, outs):
@@ -247,22 +249,25 @@
         outs[1][...] = jnp.zeros(TOKEN[0], F32)
 
     outs = [((place.shape[1], 2 * half // place.shape[0]), BF16), TOKEN]
-    return on_core("a_total", work, outs, act, down, *first, *second, place)
-
-
-def b_hidden_rows(blocks, up, col, after):
+    return on_core("a_total", work, outs, act, down, *first, *second, place, after=after)
+
+
+def b_hidden_rows(blocks, up, col):
     half, units, rows = up.shape[0] // 2, up.shape[1], blocks[0][0].shape[0]
 
     def work(ins, outs):
-        up_ref, col_ref = ins[8:10]
+        up_ref, col_ref = ins[8:]
         for j in range(4):
             lo, hi = ins[2 * j][...], ins[2 * j + 1][...]
             outs[0][j] = dot(lo, up_ref[:half]) + dot(hi, up_ref[half:])
             outs[1][j] = dot(lo, col_ref[:half]) + dot(hi, col_ref[half:])
 
+        outs[2][...] = jnp.zeros(TOKEN[0], F32)
+
     flat = [v for block in blocks for v in block]
-    outs = [((4, rows, units), F32), ((4, rows, 128), F32)]
-    return tuple(on_core("b_hidden", work, outs, *flat, up, col, after))
+    outs = [((4, rows, units), F32), ((4, rows, 128), F32), TOKEN]
+    hidden, score, token = on_core("b_hidden", work, outs, *flat, up, col)
+    return (hidden, score), token
 
 
 def back_rows(hidden, score, c_lo, c_hi, down_ref):
@@ -279,7 +284,7 @@
     return dot(hid_grad, up_ref[:, cols]) + term * line_ref[:, cols]
 
 
-def b_near_rows(cots, early, up, down, line):
+def b_near_rows(cots, early, up, down, line, after):
     half, units, rows = up.shape[1] // 2, up.shape[0], cots[0][0].shape[0]
 
     def work(ins, outs):
@@ -296,7 +301,7 @@
     flat = [v for block in cots for v in block]
     outs = [((3, rows, units), BF16)] * 2 + [((3, rows, 128), F32)]
     outs += [((rows, half), BF16)] * 2
-    act, hid, term, by_x, by_y = on_core("b_near", work, outs, *flat, *early, up, down, line)
+    act, hid, term, by_x, by_y = on_core("b_near", work, outs, *flat, *early, up, down, line, after=after)
     return (act, hid, term), (by_x, by_y)
 
 
@@ -304,7 +309,7 @@
     half, units, rows = up.shape[1] // 2, up.shape[0], cots[0].shape[0]
 
     def work(ins, outs):
-        lo, hi, hidden, score, _, up_ref, down_ref, line_ref = ins
+        lo, hi, hidden, score, up_ref, down_ref, line_ref = ins
         act, hid, term = back_rows(hidden[3], score[3], lo[...], hi[...], down_ref)
         outs[0][...], outs[1][...] = act, hid
         for h in range(2):
@@ -312,8 +317,8 @@
             outs[2 + h][...] = part.astype(BF16)
 
     outs = [((rows, units), BF16)] * 2 + [((rows, half), BF16)] * 2
-    args = (*cots, *early, near[2], up, down, line)
-    act, hid, by_x, by_y = on_core("b_far", work, outs, *args)
+    args = (*cots, *early, up, down, line)
+    act, hid, by_x, by_y = on_core("b_far", work, outs, *args, after=(near[2],))
     return (act, hid), (by_x, by_y)
 
 
@@ -321,14 +326,14 @@
     half, rows = up.shape[1] // 2, got[0].shape[0]
 
     def work(ins, outs):
-        hids, terms, up_ref, line_ref, by_x, by_y = ins[:6]
+        hids, terms, up_ref, line_ref, by_x, by_y = ins
         for side, ref in enumerate((by_y, by_x)):
             j, cols = 1 + side, slice((1 - side) * half, (2 - side) * half)
             part = grad_rows(hids[j], terms[j][:, :1], up_ref, line_ref, cols)
             outs[side][...] = (part + ref[...].astype(F32)).astype(BF16)
 
     outs = [((rows, half), BF16)] * 2
-    return on_core("b_second", work, outs, near[1], near[2], up, line, *got, *plain)
+    return on_core("b_second", work, outs, near[1], near[2], up, line, *got, after=plain)
 
 
 def b_total_rows(near, up, line, plain, second, place):
@@ -368,7 +373,7 @@
 
     flat = [v for block in blocks for v in block] + [v for block in cots for v in block]
     outs = [((2 * half, units), BF16), ((units, 2 * half), BF16)]
-    return on_core("weight_grads", work, outs, *flat, near[0], near[1], *far, after)
+    return on_core("weight_grads", work, outs, *flat, near[0], near[1], *far, after=(after,))
 
 
 def across_planes(rows, layout):
@@ -410,34 +415,36 @@
     a_target, b_target = target_rows(a_ids[:, 0], layout), target_rows(b_ids[:, 0], layout)
 
     a_send, a_gate = send_normed(a_input[0], a_ids, cols_r, a_target, layout)
-    a_mine, a_packed = pack_halves(across_planes(a_send, layout), select)
-    b_send, b_gate = send_normed(b_x, b_ids, cols_r, b_target, layout, (a_packed,))
+    up_turned, down_turned = up.T, down.T
+    a_blocks = across_planes(a_send, layout)
+    a_mine, _ = pack_halves(a_blocks, select, (up_turned, down_turned))
     a_near = spread_halves(a_mine, experts)
     a_far = relay_halves(a_near, experts)
+    b_send, b_gate = send_normed(b_x, b_ids, cols_r, b_target, layout, (a_near[0][0],))
     b_blocks = across_planes(b_send, layout)
 
     act = a_near_rows((a_mine,) + a_near, up, b_gate)
     a_first, a_ready = a_far_rows(a_far, act, up, down)
     a_first = swap_pair(a_first, experts)
-    b_mine, b_packed = pack_halves(b_blocks, select, (a_ready,))
+    b_mine, _ = pack_halves(b_blocks, select, (a_ready,))
     b_near = spread_halves(b_mine, experts)
     b_far = relay_halves(b_near, experts)
-    c_send, c_sent = send_cotangents(b_c, b_gate, b_target, layout, (b_packed,))
+
+    a_second, a_done = a_second_rows(act, down, a_first)
+    a_second = swap_pair(a_second, experts)
+    c_send, _ = send_cotangents(b_c, b_gate, b_target, layout, (a_done,))
     c_blocks = across_planes(c_send, layout)
-
-    a_second, a_done = a_second_rows(act, down, a_first, c_sent)
-    a_second = swap_pair(a_second, experts)
-    c_mine, _ = pack_halves(c_blocks, select, (a_done,))
+    c_mine, _ = pack_halves(c_blocks, select)
     c_near = spread_halves(c_mine, experts)
     c_far = relay_halves(c_near, experts)
-    a_total, a_summed = a_total_rows(act, down, a_first, a_second, place)
+    early, b_ready = b_hidden_rows((b_mine,) + b_near + (b_far,), up, col)
+    a_total, a_summed = a_total_rows(act, down, a_first, a_second, place, (b_ready,))
     a_back = across_planes(a_total, layout)
     a_out = forward_out(a_input[0], a_gate, a_back, a_target)
     a_next = pipe_move(a_out, lambda i, n: i + 1)
 
-    up_turned, down_turned = up.T, down.T
-    early = b_hidden_rows((b_mine,) + b_near + (b_far,), up, col, a_summed)
-    near, b_plain = b_near_rows((c_mine,) + c_near, early, up_turned, down_turned, line)
+    cots = (c_mine,) + c_near
+    near, b_plain = b_near_rows(cots, early, up_turned, down_turned, line, (a_summed,))
     b_plain = swap_pair(b_plain, experts)
     far, b_relay = b_far_rows(c_far, early, near, up_turned, down_turned, line)
     b_relay = swap_pair(b_relay, experts)

time: 270 us -> 261 us (0.967)
  local copies, waits for them, and re-layouts: 40.1 us -> 27.9 us
  Pallas kernels: 45 us -> 53.8 us
  waiting for transfers between devices: 121 us -> 114 us
    unnamed x112 -> x84, local copies, waits for them, and re-layouts: 39.1 us -> 26.9 us
    pallas_call x18, Pallas kernels: 45 us -> 53.8 us  [on_core(): pl.pallas_call(kernel, out_shape=[jax.ShapeDtypeStruct(shape, kind) for s...]
    all_to_all x5, waiting for transfers between devices: 24 us -> 19.4 us  [depth_exchange(): lax.all_to_all(blocks, 'expert', split_axis=0, concat_axis=0, tiled=True,...]
    ppermute x28, starting transfers between devices: 29.6 us -> 32.8 us  [plane_move(): return lax.ppermute(array, 'expert', [(i, i ^ bit) for i in range(devices)])]
  transfers between devices with their start and end apart: 37 -> 37, of which waited for: 17 -> 19; matrix products, arithmetic and copies ran while one was open for 5% -> 5% of each run, Pallas kernels for 13% -> 18%
where the time goes in v8:
time: 261 us; the launch traced here: 260 us
  waiting for transfers between devices  114 us (44%)
  starting transfers between devices  58 us (22%)
  Pallas kernels  53.8 us (21%)
  local copies, waits for them, and re-layouts  27.9 us (11%)
  other arithmetic  4.79 us (2%)
    ppermute x28, waiting for transfers between devices, plane_move(): return lax.ppermute(array, 'expert', [(i, i ^ bit) for i in range(devices)])  92.2 us
    pallas_call x18, Pallas kernels, on_core(): pl.pallas_call(kernel, out_shape=[jax.ShapeDtypeStruct(shape, kind) for s...  53.8 us
    ppermute x28, starting transfers between devices, plane_move(): return lax.ppermute(array, 'expert', [(i, i ^ bit) for i in range(devices)])  32.8 us
    unnamed x84, local copies, waits for them, and re-layouts  26.9 us
    all_to_all x5, starting transfers between devices, depth_exchange(): lax.all_to_all(blocks, 'expert', split_axis=0, concat_axis=0, tiled=True,...  24.4 us
    all_to_all x5, waiting for transfers between devices, depth_exchange(): lax.all_to_all(blocks, 'expert', split_axis=0, concat_axis=0, tiled=True,...  19.4 us
  transfers between devices with their start and end apart: 37, of which 19 were waited for; matrix products, arithmetic and copies ran while one was open for 5% of the time, Pallas kernels for 18%

profile of v8, /device:TPU:0, one launch (start us, length us, event | category | flops | bytes accessed | tf_op | source)
XLA Modules:
  0.0 259.6 jit_solution(6560293466446331857)
XLA Ops:
  11.0 5.9 %all-to-all-start = ((bf16[4,136,896]{2,1,0:T(8,128)(2,1)}), bf16[4,136,896]{2,1,0:T(8,128)(2,1)}, u32[]{:S(2)}, u32[]{:S(2)}) async-start(bf16[4,136,896]{2,1,0:T(8,128)(2,1)} %bitcast.4), calls=%async_computation | async-start | bytes 1949696 | tf_op jit(solution)/shard_map/all_to_all | solution.py:35
  19.9 3.9 %copy.29 = bf16[1,256,3584]{1,2,0:T(8,128)(2,1)} copy(bf16[1,256,3584]{2,1,0:T(8,128)(2,1)} %param.16) | data formatting | bytes 3670016 | tf_op args[6]
  23.7 18.1 %all-to-all-done = bf16[4,136,896]{2,1,0:T(8,128)(2,1)} async-done(((bf16[4,136,896]{2,1,0:T(8,128)(2,1)}), bf16[4,136,896]{2,1,0:T(8,128)(2,1)}, u32[]{:S(2)}, u32[]{:S(2)}) %all-to-all-start) | async-done | bytes 974880 | tf_op jit(solution)/shard_map/all_to_all | solution.py:35
  43.3 3.1 %pack.3 = (bf16[136,1792]{1,0:T(8,128)(2,1)}, bf16[136,1792]{1,0:T(8,128)(2,1)}, f32[8,128]{1,0:T(8,128)}) custom-call(bf16[544,896]{1,0:T(8,128)(2,1)} %bitcast.5.refs_0_, bf16[4,136,544]{2,1,0:T(8,128)(2,1)S(1)} %copy-done.7, bf16[256,3584]{1,0:T(8,128)(2,1)S(1)} %bitcast.33, bf16[3584,256]{1,0:T(8,128)(2,1)S(1)} %bitcast.44), custom_call_target="tpu_custom_call" | custom-call | flops 1000000 | bytes 100000 | tf_op jit(solution)/shard_map/pack/pallas_call | solution.py:73
  50.4 10.3 %collective-permute-done.refs_4_.refs_2_ = bf16[136,1792]{1,0:T(8,128)(2,1)} collective-permute-done((bf16[136,1792]{1,0:T(8,128)(2,1)}, bf16[136,1792]{1,0:T(8,128)(2,1)}, u32[]{:S(2)}, u32[]{:S(2)}) %collective-permute-start) | collective-permute-done | bytes 487456 | tf_op jit(solution)/shard_map/ppermute | solution.py:28
  67.7 4.2 %all-to-all-start.1 = ((bf16[4,136,896]{2,1,0:T(8,128)(2,1)}), bf16[4,136,896]{2,1,0:T(8,128)(2,1)}, u32[]{:S(2)}, u32[]{:S(2)}) async-start(bf16[4,136,896]{2,1,0:T(8,128)(2,1)} %bitcast.53), calls=%async_computation.1 | async-start | bytes 1949696 | tf_op jit(solution)/shard_map/all_to_all | solution.py:35
  77.1 4.1 %collective-permute-done.6.refs_0_ = bf16[136,1792]{1,0:T(8,128)(2,1)} collective-permute-done((bf16[136,1792]{1,0:T(8,128)(2,1)}, bf16[136,1792]{1,0:T(8,128)(2,1)}, u32[]{:S(2)}, u32[]{:S(2)}) %collective-permute-start.6) | collective-permute-done | bytes 487456 | tf_op jit(solution)/shard_map/ppermute | solution.py:28
  86.2 19.6 %collective-permute-done.8.refs_2_ = bf16[2,136,1792]{2,1,0:T(8,128)(2,1)S(1)} collective-permute-done((bf16[2,136,1792]{2,1,0:T(8,128)(2,1)S(1)}, bf16[2,136,1792]{2,1,0:T(8,128)(2,1)S(1)}, u32[]{:S(2)}, u32[]{:S(2)}) %collective-permute-start.8) | collective-permute-done | bytes 974880 | tf_op jit(solution)/shard_map/ppermute | solution.py:28
  112.4 4.4 %all-to-all-start.3 = ((bf16[4,136,896]{2,1,0:T(8,128)(2,1)}), bf16[4,136,896]{2,1,0:T(8,128)(2,1)}, u32[]{:S(2)}, u32[]{:S(2)}) async-start(bf16[4,136,896]{2,1,0:T(8,128)(2,1)} %bitcast.55), calls=%async_computation.3 | async-start | bytes 1949696 | tf_op jit(solution)/shard_map/all_to_all | solution.py:35
  116.8 3.1 %pack.4 = (bf16[136,1792]{1,0:T(8,128)(2,1)}, bf16[136,1792]{1,0:T(8,128)(2,1)}, f32[8,128]{1,0:T(8,128)}) custom-call(bf16[544,896]{1,0:T(8,128)(2,1)} %bitcast.16.refs_0_, bf16[4,136,544]{2,1,0:T(8,128)(2,1)S(1)} %copy-done.7, f32[8,128]{1,0:T(8,128)S(1)} %get-tuple-element.51.refs_2_), custom_call_target="tpu_custom_call" | custom-call | flops 1000000 | bytes 100000 | tf_op jit(solution)/shard_map/pack/pallas_call | solution.py:73
  125.4 8.9 %collective-permute-done.12.refs_2_ = bf16[136,1792]{1,0:T(8,128)(2,1)} collective-permute-done((bf16[136,1792]{1,0:T(8,128)(2,1)}, bf16[136,1792]{1,0:T(8,128)(2,1)}, u32[]{:S(2)}, u32[]{:S(2)}) %collective-permute-start.12) | collective-permute-done | bytes 487456 | tf_op jit(solution)/shard_map/ppermute | solution.py:28
  138.5 3.1 %pack.5 = (bf16[136,1792]{1,0:T(8,128)(2,1)}, bf16[136,1792]{1,0:T(8,128)(2,1)}, f32[8,128]{1,0:T(8,128)}) custom-call(bf16[544,896]{1,0:T(8,128)(2,1)} %bitcast.22.refs_0_, bf16[4,136,544]{2,1,0:T(8,128)(2,1)S(1)} %copy-done.7), custom_call_target="tpu_custom_call" | custom-call | flops 1000000 | bytes 100000 | tf_op jit(solution)/shard_map/pack/pallas_call | solution.py:73
  141.6 4.5 %collective-permute-done.14.refs_4_ = bf16[136,1792]{1,0:T(8,128)(2,1)} collective-permute-done((bf16[136,1792]{1,0:T(8,128)(2,1)}, bf16[136,1792]{1,0:T(8,128)(2,1)}, u32[]{:S(2)}, u32[]{:S(2)}) %collective-permute-start.14) | collective-permute-done | bytes 487456 | tf_op jit(solution)/shard_map/ppermute | solution.py:28
  148.6 6.5 %collective-permute-done.10.refs_4_ = bf16[136,1792]{1,0:T(8,128)(2,1)} collective-permute-done((bf16[136,1792]{1,0:T(8,128)(2,1)}, bf16[136,1792]{1,0:T(8,128)(2,1)}, u32[]{:S(2)}, u32[]{:S(2)}) %collective-permute-start.10) | collective-permute-done | bytes 487456 | tf_op jit(solution)/shard_map/ppermute | solution.py:28
  158.1 7.5 %collective-permute-done.17.refs_7_ = bf16[136,1792]{1,0:T(8,128)(2,1)} collective-permute-done((bf16[136,1792]{1,0:T(8,128)(2,1)}, bf16[136,1792]{1,0:T(8,128)(2,1)}, u32[]{:S(2)}, u32[]{:S(2)}) %collective-permute-start.17) | collective-permute-done | bytes 487456 | tf_op jit(solution)/shard_map/ppermute | solution.py:28
  167.0 9.0 %collective-permute-done.20.refs_2_.refs_10_ = bf16[136,1792]{1,0:T(8,128)(2,1)} collective-permute-done((bf16[136,1792]{1,0:T(8,128)(2,1)}, bf16[136,1792]{1,0:T(8,128)(2,1)}, u32[]{:S(2)}, u32[]{:S(2)}) %collective-permute-start.20) | collective-permute-done | bytes 487456 | tf_op jit(solution)/shard_map/ppermute | solution.py:28
  179.6 4.5 %b_hidden.1 = (f32[4,136,256]{2,1,0:T(8,128)S(1)}, f32[4,136,128]{2,1,0:T(8,128)S(1)}, f32[8,128]{1,0:T(8,128)S(1)}) custom-call(bf16[136,1792]{1,0:T(8,128)(2,1)} %get-tuple-element.52.refs_0_, bf16[136,1792]{1,0:T(8,128)(2,1)} %get-tuple-element.53.refs_1_, bf16[136,1792]{1,0:T(8,128)(2,1)} %collective-permute-done.12.refs_2_, ...), custom_call_target="tpu_custom_call" | custom-call | flops 1000000 | bytes 100000 | tf_op jit(solution)/shard_map/b_hidden/pallas_call | solution.py:73
  187.9 4.9 %all-to-all-start.2 = ((bf16[4,136,896]{2,1,0:T(8,128)(2,1)}), bf16[4,136,896]{2,1,0:T(8,128)(2,1)}, u32[]{:S(2)}, u32[]{:S(2)}) async-start(bf16[4,136,896]{2,1,0:T(8,128)(2,1)} %bitcast.52), calls=%async_computation.2 | async-start | bytes 1949696 | tf_op jit(solution)/shard_map/all_to_all | solution.py:35
  195.3 3.8 %b_near.1 = (bf16[3,136,256]{2,1,0:T(8,128)(2,1)S(1)}, bf16[3,136,256]{2,1,0:T(8,128)(2,1)S(1)}, f32[3,136,128]{2,1,0:T(8,128)S(1)}, bf16[136,1792]{1,0:T(8,128)(2,1)S(1)}, bf16[136,1792]{1,0:T(8,128)(2,1)S(1)}) custom-call(bf16[136,1792]{1,0:T(8,128)(2,1)} %get-tuple-element.58.refs_0_.refs_8_, bf16[136,1792]{1,0:T(8,128)(2,1)} %get-tuple-element.59.refs_1_.refs_9_, ...), custom_call_target="tpu_custom_call" | custom-call | flops 1000000 | bytes 100000 | tf_op jit(solution)/shard_map/b_near/pallas_call | solution.py:73
  209.6 9.4 %collective-permute-done.28.refs_4_ = bf16[136,1792]{1,0:T(8,128)(2,1)S(1)} collective-permute-done((bf16[136,1792]{1,0:T(8,128)(2,1)S(1)}, bf16[136,1792]{1,0:T(8,128)(2,1)S(1)}, u32[]{:S(2)}, u32[]{:S(2)}) %collective-permute-start.28) | collective-permute-done | bytes 487456 | tf_op jit(solution)/shard_map/ppermute | solution.py:28
  221.9 7.2 %collective-permute-done.30.refs_6_ = bf16[136,1792]{1,0:T(8,128)(2,1)S(1)} collective-permute-done((bf16[136,1792]{1,0:T(8,128)(2,1)S(1)}, bf16[136,1792]{1,0:T(8,128)(2,1)S(1)}, u32[]{:S(2)}, u32[]{:S(2)}) %collective-permute-start.30) | collective-permute-done | bytes 487456 | tf_op jit(solution)/shard_map/ppermute | solution.py:28
  232.5 5.0 %all-to-all-start.4 = ((bf16[4,136,896]{2,1,0:T(8,128)(2,1)}), bf16[4,136,896]{2,1,0:T(8,128)(2,1)S(1)}, u32[]{:S(2)}, u32[]{:S(2)}) async-start(bf16[4,136,896]{2,1,0:T(8,128)(2,1)} %bitcast.54), calls=%async_computation.4 | async-start | bytes 1949696 | tf_op jit(solution)/shard_map/all_to_all | solution.py:35
  244.6 9.3 %weight_grads.1 = (bf16[3584,256]{1,0:T(8,128)(2,1)}, bf16[256,3584]{1,0:T(8,128)(2,1)}) custom-call(bf16[136,1792]{1,0:T(8,128)(2,1)} %get-tuple-element.52.refs_0_, bf16[136,1792]{1,0:T(8,128)(2,1)} %get-tuple-element.53.refs_1_, bf16[136,1792]{1,0:T(8,128)(2,1)} %collective-permute-done.12.refs_2_, bf16[136,1792]{1,0:T(8,128)(2,1)} %collective-permute-done.13.refs_3_, ...), custom_call_target="tpu_custom_call" | custom-call | flops 1000000 | bytes 100000 | tf_op jit(solution)/shard_map/weight_grads/pallas_call | solution.py:73
  255.0 3.7 %backward_out.1 = bf16[128,3584]{1,0:T(8,128)(2,1)} custom-call(bf16[128,3584]{1,0:T(8,128)(2,1)} %collective-permute-done.4.refs_0_, bf16[128,3584]{1,0:T(8,128)(2,1)S(1)} %copy-done.16, bf16[544,896]{1,0:T(8,128)(2,1)S(1)} %bitcast.49, s32[128,4]{1,0:T(8,128)S(1)} %get-tuple-element.78.refs_3_), custom_call_target="tpu_custom_call" | custom-call | flops 1000000 | bytes 100000 | tf_op jit(solution)/shard_map/backward_out/pallas_call | solution.py:73
  (174 shorter events, 94.5 us)
Async XLA Ops:
  11.0 30.8 %all-to-all-start = ((bf16[4,136,896]{2,1,0:T(8,128)(2,1)}), bf16[4,136,896]{2,1,0:T(8,128)(2,1)}, u32[]{:S(2)}, u32[]{:S(2)}) async-start(bf16[4,136,896]{2,1,0:T(8,128)(2,1)} %bitcast.4), calls=%async_computation | async-start | bytes 1949696 | tf_op jit(solution)/shard_map/all_to_all | solution.py:35
  16.9 46.9 %collective-permute-start.4 = (bf16[128,3584]{1,0:T(8,128)(2,1)}, bf16[128,3584]{1,0:T(8,128)(2,1)}, u32[]{:S(2)}, u32[]{:S(2)}) collective-permute-start(bf16[128,3584]{1,0:T(8,128)(2,1)} %bitcast.11), channel_id=1, source_target_pairs={{0,16},{16,0},{1,17},{17,1},{2,18},{18,2},{3,19},{19,3},{4,20},{20... | collective-permute-start | bytes 2752520 | tf_op jit(solution)/shard_map/ppermute | solution.py:23
  49.4 23.3 %collective-permute-start.2 = (bf16[136,1792]{1,0:T(8,128)(2,1)}, bf16[136,1792]{1,0:T(8,128)(2,1)}, u32[]{:S(2)}, u32[]{:S(2)}) collective-permute-start(bf16[136,1792]{1,0:T(8,128)(2,1)} %get-tuple-element.43.refs_0_), channel_id=1, source_target_pairs={{0,2},{1,3},{2,0},{3,1},{4,6},{5,7},{6,4},{7,5},{8,10},{9,11},{10,... | collective-permute-start | bytes 1462280 | tf_op jit(solution)/shard_map/ppermute | solution.py:28
  49.9 22.8 %collective-permute-start.1 = (bf16[136,1792]{1,0:T(8,128)(2,1)}, bf16[136,1792]{1,0:T(8,128)(2,1)}, u32[]{:S(2)}, u32[]{:S(2)}) collective-permute-start(bf16[136,1792]{1,0:T(8,128)(2,1)} %get-tuple-element.44.refs_1_), channel_id=1, source_target_pairs={{0,1},{1,0},{2,3},{3,2},{4,5},{5,4},{6,7},{7,6},{8,9},{9,8},{10,11... | collective-permute-start | bytes 1462280 | tf_op jit(solution)/shard_map/ppermute | solution.py:28
  60.8 20.5 %collective-permute-start.6 = (bf16[136,1792]{1,0:T(8,128)(2,1)}, bf16[136,1792]{1,0:T(8,128)(2,1)}, u32[]{:S(2)}, u32[]{:S(2)}) collective-permute-start(bf16[136,1792]{1,0:T(8,128)(2,1)} %collective-permute-done.refs_4_.refs_2_), channel_id=1, source_target_pairs={{0,2},{1,3},{2,0},{3,1},{4,6},{5,7},{6,4},{7,5},{8,10},{9,11},{10,... | collective-permute-start | bytes 1462280 | tf_op jit(solution)/shard_map/ppermute | solution.py:28
  67.7 44.7 %all-to-all-start.1 = ((bf16[4,136,896]{2,1,0:T(8,128)(2,1)}), bf16[4,136,896]{2,1,0:T(8,128)(2,1)}, u32[]{:S(2)}, u32[]{:S(2)}) async-start(bf16[4,136,896]{2,1,0:T(8,128)(2,1)} %bitcast.53), calls=%async_computation.1 | async-start | bytes 1949696 | tf_op jit(solution)/shard_map/all_to_all | solution.py:35
  84.1 21.7 %collective-permute-start.8 = (bf16[2,136,1792]{2,1,0:T(8,128)(2,1)S(1)}, bf16[2,136,1792]{2,1,0:T(8,128)(2,1)S(1)}, u32[]{:S(2)}, u32[]{:S(2)}) collective-permute-start(bf16[2,136,1792]{2,1,0:T(8,128)(2,1)S(1)} %get-tuple-element.46), channel_id=1, source_target_pairs={{0,1},{1,0},{2,3},{3,2},{4,5},{5,4},{6,7},{7,6},{8,9},{9,8},{10,11... | collective-permute-start | bytes 2924552 | tf_op jit(solution)/shard_map/ppermute | solution.py:28
  84.7 21.4 %collective-permute-start.9 = (bf16[2,136,1792]{2,1,0:T(8,128)(2,1)S(1)}, bf16[2,136,1792]{2,1,0:T(8,128)(2,1)S(1)}, u32[]{:S(2)}, u32[]{:S(2)}) collective-permute-start(bf16[2,136,1792]{2,1,0:T(8,128)(2,1)S(1)} %get-tuple-element.47), channel_id=1, source_target_pairs={{0,2},{1,3},{2,0},{3,1},{4,6},{5,7},{6,4},{7,5},{8,10},{9,11},{10,... | collective-permute-start | bytes 2924552 | tf_op jit(solution)/shard_map/ppermute | solution.py:28
  86.2 22.5 %collective-permute-start.19 = (bf16[128,3584]{1,0:T(8,128)(2,1)S(1)}, bf16[128,3584]{1,0:T(8,128)(2,1)S(1)}, u32[]{:S(2)}, u32[]{:S(2)}) collective-permute-start(bf16[128,3584]{1,0:T(8,128)(2,1)S(1)} %bitcast.64), channel_id=1, source_target_pairs={{0,16},{16,0},{1,17},{17,1},{2,18},{18,2},{3,19},{19,3},{4,20},{20... | collective-permute-start | bytes 2752520 | tf_op jit(solution)/shard_map/ppermute | solution.py:23
  112.4 26.2 %all-to-all-start.3 = ((bf16[4,136,896]{2,1,0:T(8,128)(2,1)}), bf16[4,136,896]{2,1,0:T(8,128)(2,1)}, u32[]{:S(2)}, u32[]{:S(2)}) async-start(bf16[4,136,896]{2,1,0:T(8,128)(2,1)} %bitcast.55), calls=%async_computation.3 | async-start | bytes 1949696 | tf_op jit(solution)/shard_map/all_to_all | solution.py:35
  122.8 23.3 %collective-permute-start.14 = (bf16[136,1792]{1,0:T(8,128)(2,1)}, bf16[136,1792]{1,0:T(8,128)(2,1)}, u32[]{:S(2)}, u32[]{:S(2)}) collective-permute-start(bf16[136,1792]{1,0:T(8,128)(2,1)} %get-tuple-element.52.refs_0_), channel_id=1, source_target_pairs={{0,2},{1,3},{2,0},{3,1},{4,6},{5,7},{6,4},{7,5},{8,10},{9,11},{10,... | collective-permute-start | bytes 1462280 | tf_op jit(solution)/shard_map/ppermute | solution.py:28
  123.3 23.4 %collective-permute-start.13 = (bf16[136,1792]{1,0:T(8,128)(2,1)}, bf16[136,1792]{1,0:T(8,128)(2,1)}, u32[]{:S(2)}, u32[]{:S(2)}) collective-permute-start(bf16[136,1792]{1,0:T(8,128)(2,1)} %get-tuple-element.53.refs_1_), channel_id=1, source_target_pairs={{0,1},{1,0},{2,3},{3,2},{4,5},{5,4},{6,7},{7,6},{8,9},{9,8},{10,11... | collective-permute-start | bytes 1462280 | tf_op jit(solution)/shard_map/ppermute | solution.py:28
  123.9 31.2 %collective-permute-start.10 = (bf16[136,1792]{1,0:T(8,128)(2,1)}, bf16[136,1792]{1,0:T(8,128)(2,1)}, u32[]{:S(2)}, u32[]{:S(2)}) collective-permute-start(bf16[136,1792]{1,0:T(8,128)(2,1)} %copy-done.36), channel_id=1, source_target_pairs={{0,1},{1,0},{2,3},{3,2},{4,5},{5,4},{6,7},{7,6},{8,9},{9,8},{10,11... | collective-permute-start | bytes 1462280 | tf_op jit(solution)/shard_map/ppermute | solution.py:28
  134.3 22.4 %collective-permute-start.16 = (bf16[136,1792]{1,0:T(8,128)(2,1)}, bf16[136,1792]{1,0:T(8,128)(2,1)}, u32[]{:S(2)}, u32[]{:S(2)}) collective-permute-start(bf16[136,1792]{1,0:T(8,128)(2,1)} %collective-permute-done.12.refs_2_), channel_id=1, source_target_pairs={{0,2},{1,3},{2,0},{3,1},{4,6},{5,7},{6,4},{7,5},{8,10},{9,11},{10,... | collective-permute-start | bytes 1462280 | tf_op jit(solution)/shard_map/ppermute | solution.py:28
  135.8 29.8 %collective-permute-start.17 = (bf16[136,1792]{1,0:T(8,128)(2,1)}, bf16[136,1792]{1,0:T(8,128)(2,1)}, u32[]{:S(2)}, u32[]{:S(2)}) collective-permute-start(bf16[136,1792]{1,0:T(8,128)(2,1)} %collective-permute-done.15.refs_5_), channel_id=1, source_target_pairs={{0,1},{1,0},{2,3},{3,2},{4,5},{5,4},{6,7},{7,6},{8,9},{9,8},{10,11... | collective-permute-start | bytes 1462280 | tf_op jit(solution)/shard_map/ppermute | solution.py:28
  146.1 29.9 %collective-permute-start.20 = (bf16[136,1792]{1,0:T(8,128)(2,1)}, bf16[136,1792]{1,0:T(8,128)(2,1)}, u32[]{:S(2)}, u32[]{:S(2)}) collective-permute-start(bf16[136,1792]{1,0:T(8,128)(2,1)} %get-tuple-element.58.refs_0_.refs_8_), channel_id=1, source_target_pairs={{0,1},{1,0},{2,3},{3,2},{4,5},{5,4},{6,7},{7,6},{8,9},{9,8},{10,11... | collective-permute-start | bytes 1462280 | tf_op jit(solution)/shard_map/ppermute | solution.py:28
  146.7 30.8 %collective-permute-start.23 = (bf16[136,1792]{1,0:T(8,128)(2,1)}, bf16[136,1792]{1,0:T(8,128)(2,1)}, u32[]{:S(2)}, u32[]{:S(2)}) collective-permute-start(bf16[136,1792]{1,0:T(8,128)(2,1)} %get-tuple-element.59.refs_1_.refs_9_), channel_id=1, source_target_pairs={{0,2},{1,3},{2,0},{3,1},{4,6},{5,7},{6,4},{7,5},{8,10},{9,11},{10,... | collective-permute-start | bytes 1462280 | tf_op jit(solution)/shard_map/ppermute | solution.py:28
  155.1 29.0 %collective-permute-start.11 = (bf16[136,1792]{1,0:T(8,128)(2,1)}, bf16[136,1792]{1,0:T(8,128)(2,1)S(1)}, u32[]{:S(2)}, u32[]{:S(2)}) collective-permute-start(bf16[136,1792]{1,0:T(8,128)(2,1)} %copy-done.35), channel_id=1, source_target_pairs={{0,2},{1,3},{2,0},{3,1},{4,6},{5,7},{6,4},{7,5},{8,10},{9,11},{10,... | collective-permute-start | bytes 1462280 | tf_op jit(solution)/shard_map/ppermute | solution.py:28
  156.7 36.1 %collective-permute-start.22 = (bf16[136,1792]{1,0:T(8,128)(2,1)}, bf16[136,1792]{1,0:T(8,128)(2,1)}, u32[]{:S(2)}, u32[]{:S(2)}) collective-permute-start(bf16[136,1792]{1,0:T(8,128)(2,1)} %get-tuple-element.58.refs_0_.refs_8_), channel_id=1, source_target_pairs={{0,2},{1,3},{2,0},{3,1},{4,6},{5,7},{6,4},{7,5},{8,10},{9,11},{10,... | collective-permute-start | bytes 1462280 | tf_op jit(solution)/shard_map/ppermute | solution.py:28
  165.6 27.2 %collective-permute-start.21 = (bf16[136,1792]{1,0:T(8,128)(2,1)}, bf16[136,1792]{1,0:T(8,128)(2,1)}, u32[]{:S(2)}, u32[]{:S(2)}) collective-permute-start(bf16[136,1792]{1,0:T(8,128)(2,1)} %get-tuple-element.59.refs_1_.refs_9_), channel_id=1, source_target_pairs={{0,1},{1,0},{2,3},{3,2},{4,5},{5,4},{6,7},{7,6},{8,9},{9,8},{10,11... | collective-permute-start | bytes 1462280 | tf_op jit(solution)/shard_map/ppermute | solution.py:28
  176.0 24.2 %collective-permute-start.26 = (bf16[136,1792]{1,0:T(8,128)(2,1)}, bf16[136,1792]{1,0:T(8,128)(2,1)}, u32[]{:S(2)}, u32[]{:S(2)}) collective-permute-start(bf16[136,1792]{1,0:T(8,128)(2,1)} %collective-permute-done.20.refs_2_.refs_10_), channel_id=1, source_target_pairs={{0,2},{1,3},{2,0},{3,1},{4,6},{5,7},{6,4},{7,5},{8,10},{9,11},{10,... | collective-permute-start | bytes 1462280 | tf_op jit(solution)/shard_map/ppermute | solution.py:28
  177.6 22.7 %collective-permute-start.27 = (bf16[136,1792]{1,0:T(8,128)(2,1)}, bf16[136,1792]{1,0:T(8,128)(2,1)}, u32[]{:S(2)}, u32[]{:S(2)}) collective-permute-start(bf16[136,1792]{1,0:T(8,128)(2,1)} %collective-permute-done.23.refs_5_.refs_13_), channel_id=1, source_target_pairs={{0,1},{1,0},{2,3},{3,2},{4,5},{5,4},{6,7},{7,6},{8,9},{9,8},{10,11... | collective-permute-start | bytes 1462280 | tf_op jit(solution)/shard_map/ppermute | solution.py:28
  187.9 44.6 %all-to-all-start.2 = ((bf16[4,136,896]{2,1,0:T(8,128)(2,1)}), bf16[4,136,896]{2,1,0:T(8,128)(2,1)}, u32[]{:S(2)}, u32[]{:S(2)}) async-start(bf16[4,136,896]{2,1,0:T(8,128)(2,1)} %bitcast.52), calls=%async_computation.2 | async-start | bytes 1949696 | tf_op jit(solution)/shard_map/all_to_all | solution.py:35
  232.5 21.3 %all-to-all-start.4 = ((bf16[4,136,896]{2,1,0:T(8,128)(2,1)}), bf16[4,136,896]{2,1,0:T(8,128)(2,1)S(1)}, u32[]{:S(2)}, u32[]{:S(2)}) async-start(bf16[4,136,896]{2,1,0:T(8,128)(2,1)} %bitcast.54), calls=%async_computation.4 | async-start | bytes 1949696 | tf_op jit(solution)/shard_map/all_to_all | solution.py:35
  (53 other events, 389.5 us)

commit v9 on v8

--- a/solution.py
+++ b/solution.py
@@ -284,7 +284,7 @@
     return dot(hid_grad, up_ref[:, cols]) + term * line_ref[:, cols]
 
 
-def b_near_rows(cots, early, up, down, line, after):
+def b_near_rows(cots, early, up, down, line):
     half, units, rows = up.shape[1] // 2, up.shape[0], cots[0][0].shape[0]
 
     def work(ins, outs):
@@ -301,11 +301,11 @@
     flat = [v for block in cots for v in block]
     outs = [((3, rows, units), BF16)] * 2 + [((3, rows, 128), F32)]
     outs += [((rows, half), BF16)] * 2
-    act, hid, term, by_x, by_y = on_core("b_near", work, outs, *flat, *early, up, down, line, after=after)
+    act, hid, term, by_x, by_y = on_core("b_near", work, outs, *flat, *early, up, down, line)
     return (act, hid, term), (by_x, by_y)
 
 
-def b_far_rows(cots, early, near, up, down, line):
+def b_far_rows(cots, early, up, down, line, after):
     half, units, rows = up.shape[1] // 2, up.shape[0], cots[0].shape[0]
 
     def work(ins, outs):
@@ -318,7 +318,7 @@
 
     outs = [((rows, units), BF16)] * 2 + [((rows, half), BF16)] * 2
     args = (*cots, *early, up, down, line)
-    act, hid, by_x, by_y = on_core("b_far", work, outs, *args, after=(near[2],))
+    act, hid, by_x, by_y = on_core("b_far", work, outs, *args, after=after)
     return (act, hid), (by_x, by_y)
 
 
@@ -430,9 +430,9 @@
     b_near = spread_halves(b_mine, experts)
     b_far = relay_halves(b_near, experts)
 
-    a_second, a_done = a_second_rows(act, down, a_first)
+    a_second, _ = a_second_rows(act, down, a_first)
     a_second = swap_pair(a_second, experts)
-    c_send, _ = send_cotangents(b_c, b_gate, b_target, layout, (a_done,))
+    c_send, _ = send_cotangents(b_c, b_gate, b_target, layout, (b_near[0][0],))
     c_blocks = across_planes(c_send, layout)
     c_mine, _ = pack_halves(c_blocks, select)
     c_near = spread_halves(c_mine, experts)
@@ -444,9 +444,9 @@
     a_next = pipe_move(a_out, lambda i, n: i + 1)
 
     cots = (c_mine,) + c_near
-    near, b_plain = b_near_rows(cots, early, up_turned, down_turned, line, (a_summed,))
+    near, b_plain = b_near_rows(cots, early, up_turned, down_turned, line)
     b_plain = swap_pair(b_plain, experts)
-    far, b_relay = b_far_rows(c_far, early, near, up_turned, down_turned, line)
+    far, b_relay = b_far_rows(c_far, early, up_turned, down_turned, line, (near[2], a_summed))
     b_relay = swap_pair(b_relay, experts)
     b_second = b_second_rows(near, up_turned, line, b_relay, b_plain)
     b_second = swap_pair(b_second, experts)

time: 261 us -> 286 us (1.096)
  waiting for transfers between devices: 114 us -> 133 us
  local copies, waits for them, and re-layouts: 27.9 us -> 36 us
    ppermute x28, waiting for transfers between devices: 92.2 us -> 111 us  [plane_move(): return lax.ppermute(array, 'expert', [(i, i ^ bit) for i in range(devices)])]
    unnamed x84 -> x104, local copies, waits for them, and re-layouts: 26.9 us -> 35 us
  transfers between devices with their start and end apart: 37 -> 37, of which waited for: 19 -> 23; matrix products, arithmetic and copies ran while one was open for 5% -> 4% of each run, Pallas kernels for 18% -> 14%
where the time goes in v9:
time: 286 us; the launch traced here: 285 us
  waiting for transfers between devices  133 us (47%)
  starting transfers between devices  57.9 us (20%)
  Pallas kernels  51 us (18%)
  local copies, waits for them, and re-layouts  36 us (13%)
  other arithmetic  5.43 us (2%)
    ppermute x28, waiting for transfers between devices, plane_move(): return lax.ppermute(array, 'expert', [(i, i ^ bit) for i in range(devices)])  111 us
    pallas_call x18, Pallas kernels, on_core(): pl.pallas_call(kernel, out_shape=[jax.ShapeDtypeStruct(shape, kind) for s...  51 us
    unnamed x104, local copies, waits for them, and re-layouts  35 us
    ppermute x28, starting transfers between devices, plane_move(): return lax.ppermute(array, 'expert', [(i, i ^ bit) for i in range(devices)])  32.4 us
    all_to_all x5, starting transfers between devices, depth_exchange(): lax.all_to_all(blocks, 'expert', split_axis=0, concat_axis=0, tiled=True,...  24.7 us
    all_to_all x5, waiting for transfers between devices, depth_exchange(): lax.all_to_all(blocks, 'expert', split_axis=0, concat_axis=0, tiled=True,...  19.4 us
  transfers between devices with their start and end apart: 37, of which 23 were waited for; matrix products, arithmetic and copies ran while one was open for 4% of the time, Pallas kernels for 14%

profile of v9, /device:TPU:0, one launch (start us, length us, event | category | flops | bytes accessed | tf_op | source)
XLA Modules:
  0.0 284.7 jit_solution(10576036907376283684)
XLA Ops:
  11.0 5.9 %all-to-all-start = ((bf16[4,136,896]{2,1,0:T(8,128)(2,1)}), bf16[4,136,896]{2,1,0:T(8,128)(2,1)}, u32[]{:S(2)}, u32[]{:S(2)}) async-start(bf16[4,136,896]{2,1,0:T(8,128)(2,1)} %bitcast.4), calls=%async_computation | async-start | bytes 1949696 | tf_op jit(solution)/shard_map/all_to_all | solution.py:35
  19.9 3.9 %copy.29 = bf16[1,256,3584]{1,2,0:T(8,128)(2,1)} copy(bf16[1,256,3584]{2,1,0:T(8,128)(2,1)} %param.16) | data formatting | bytes 3670016 | tf_op args[6]
  23.7 18.1 %all-to-all-done = bf16[4,136,896]{2,1,0:T(8,128)(2,1)} async-done(((bf16[4,136,896]{2,1,0:T(8,128)(2,1)}), bf16[4,136,896]{2,1,0:T(8,128)(2,1)}, u32[]{:S(2)}, u32[]{:S(2)}) %all-to-all-start) | async-done | bytes 974880 | tf_op jit(solution)/shard_map/all_to_all | solution.py:35
  47.9 10.9 %collective-permute-done.refs_4_.refs_2_ = bf16[136,1792]{1,0:T(8,128)(2,1)S(1)} collective-permute-done((bf16[136,1792]{1,0:T(8,128)(2,1)S(1)}, bf16[136,1792]{1,0:T(8,128)(2,1)S(1)}, u32[]{:S(2)}, u32[]{:S(2)}) %collective-permute-start) | collective-permute-done | bytes 487456 | tf_op jit(solution)/shard_map/ppermute | solution.py:28
  63.5 4.2 %all-to-all-start.1 = ((bf16[4,136,896]{2,1,0:T(8,128)(2,1)}), bf16[4,136,896]{2,1,0:T(8,128)(2,1)}, u32[]{:S(2)}, u32[]{:S(2)}) async-start(bf16[4,136,896]{2,1,0:T(8,128)(2,1)} %bitcast.54), calls=%async_computation.1 | async-start | bytes 1949696 | tf_op jit(solution)/shard_map/all_to_all | solution.py:35
  72.9 9.2 %collective-permute-done.3.refs_5_ = bf16[136,1792]{1,0:T(8,128)(2,1)S(1)} collective-permute-done((bf16[136,1792]{1,0:T(8,128)(2,1)}, bf16[136,1792]{1,0:T(8,128)(2,1)S(1)}, u32[]{:S(2)}, u32[]{:S(2)}) %collective-permute-start.3) | collective-permute-done | bytes 487456 | tf_op jit(solution)/shard_map/ppermute | solution.py:28
  83.6 8.9 %collective-permute-done.2.refs_4_ = bf16[136,1792]{1,0:T(8,128)(2,1)S(1)} collective-permute-done((bf16[136,1792]{1,0:T(8,128)(2,1)}, bf16[136,1792]{1,0:T(8,128)(2,1)S(1)}, u32[]{:S(2)}, u32[]{:S(2)}) %collective-permute-start.2) | collective-permute-done | bytes 487456 | tf_op jit(solution)/shard_map/ppermute | solution.py:28
  109.6 9.4 %collective-permute-done.12.refs_2_.refs_3_ = bf16[136,1792]{1,0:T(8,128)(2,1)} collective-permute-done((bf16[136,1792]{1,0:T(8,128)(2,1)}, bf16[136,1792]{1,0:T(8,128)(2,1)}, u32[]{:S(2)}, u32[]{:S(2)}) %collective-permute-start.12) | collective-permute-done | bytes 487456 | tf_op jit(solution)/shard_map/ppermute | solution.py:28
  119.0 2.9 %send_cotangents.1 = (bf16[544,896]{1,0:T(8,128)(2,1)S(1)}, f32[8,128]{1,0:T(8,128)}) custom-call(bf16[128,3584]{1,0:T(8,128)(2,1)} %collective-permute-done.19.refs_0_.refs_1_, f32[128,128]{1,0:T(8,128)S(1)} %get-tuple-element.44.refs_7_.refs_1_, s32[4,128]{1,0:T(4,128)S(1)} %get-tuple-element.78.refs_3_.refs_2_, ...), custom_call_target="tpu_custom_call" | custom-call | flops 1000000 | bytes 100000 | tf_op jit(solution)/shard_map/send_cotangents/pallas_call | solution.py:73
  122.9 4.4 %all-to-all-start.3 = ((bf16[4,136,896]{2,1,0:T(8,128)(2,1)}), bf16[4,136,896]{2,1,0:T(8,128)(2,1)}, u32[]{:S(2)}, u32[]{:S(2)}) async-start(bf16[4,136,896]{2,1,0:T(8,128)(2,1)} %bitcast.55), calls=%async_computation.3 | async-start | bytes 1949696 | tf_op jit(solution)/shard_map/all_to_all | solution.py:35
  133.0 19.1 %collective-permute-done.8.refs_2_ = bf16[2,136,1792]{2,1,0:T(8,128)(2,1)S(1)} collective-permute-done((bf16[2,136,1792]{2,1,0:T(8,128)(2,1)}, bf16[2,136,1792]{2,1,0:T(8,128)(2,1)S(1)}, u32[]{:S(2)}, u32[]{:S(2)}) %collective-permute-start.8) | collective-permute-done | bytes 974880 | tf_op jit(solution)/shard_map/ppermute | solution.py:28
  160.0 4.2 %collective-permute-done.15.refs_5_ = bf16[136,1792]{1,0:T(8,128)(2,1)} collective-permute-done((bf16[136,1792]{1,0:T(8,128)(2,1)}, bf16[136,1792]{1,0:T(8,128)(2,1)}, u32[]{:S(2)}, u32[]{:S(2)}) %collective-permute-start.15) | collective-permute-done | bytes 487456 | tf_op jit(solution)/shard_map/ppermute | solution.py:28
  164.7 3.1 %pack.5 = (bf16[136,1792]{1,0:T(8,128)(2,1)}, bf16[136,1792]{1,0:T(8,128)(2,1)}, f32[8,128]{1,0:T(8,128)}) custom-call(bf16[544,896]{1,0:T(8,128)(2,1)} %bitcast.22.refs_0_, bf16[4,136,544]{2,1,0:T(8,128)(2,1)S(1)} %copy-done.8), custom_call_target="tpu_custom_call" | custom-call | flops 1000000 | bytes 100000 | tf_op jit(solution)/shard_map/pack/pallas_call | solution.py:73
  169.3 5.3 %collective-permute-done.14.refs_4_ = bf16[136,1792]{1,0:T(8,128)(2,1)} collective-permute-done((bf16[136,1792]{1,0:T(8,128)(2,1)}, bf16[136,1792]{1,0:T(8,128)(2,1)}, u32[]{:S(2)}, u32[]{:S(2)}) %collective-permute-start.14) | collective-permute-done | bytes 487456 | tf_op jit(solution)/shard_map/ppermute | solution.py:28
  177.1 8.0 %collective-permute-done.16.refs_6_ = bf16[136,1792]{1,0:T(8,128)(2,1)} collective-permute-done((bf16[136,1792]{1,0:T(8,128)(2,1)}, bf16[136,1792]{1,0:T(8,128)(2,1)}, u32[]{:S(2)}, u32[]{:S(2)}) %collective-permute-start.16) | collective-permute-done | bytes 487456 | tf_op jit(solution)/shard_map/ppermute | solution.py:28
  187.2 6.9 %collective-permute-done.20.refs_2_.refs_10_ = bf16[136,1792]{1,0:T(8,128)(2,1)} collective-permute-done((bf16[136,1792]{1,0:T(8,128)(2,1)}, bf16[136,1792]{1,0:T(8,128)(2,1)}, u32[]{:S(2)}, u32[]{:S(2)}) %collective-permute-start.20) | collective-permute-done | bytes 487456 | tf_op jit(solution)/shard_map/ppermute | solution.py:28
  198.7 4.4 %b_hidden.1 = (f32[4,136,256]{2,1,0:T(8,128)S(1)}, f32[4,136,128]{2,1,0:T(8,128)S(1)}, f32[8,128]{1,0:T(8,128)S(1)}) custom-call(bf16[136,1792]{1,0:T(8,128)(2,1)} %get-tuple-element.51.refs_0_, bf16[136,1792]{1,0:T(8,128)(2,1)S(1)} %copy-done.22, bf16[136,1792]{1,0:T(8,128)(2,1)} %collective-permute-done.12.refs_2_.refs_3_, ...), custom_call_target="tpu_custom_call" | custom-call | flops 1000000 | bytes 100000 | tf_op jit(solution)/shard_map/b_hidden/pallas_call | solution.py:73
  209.6 5.0 %all-to-all-start.2 = ((bf16[4,136,896]{2,1,0:T(8,128)(2,1)}), bf16[4,136,896]{2,1,0:T(8,128)(2,1)}, u32[]{:S(2)}, u32[]{:S(2)}) async-start(bf16[4,136,896]{2,1,0:T(8,128)(2,1)} %bitcast.52), calls=%async_computation.2 | async-start | bytes 1949696 | tf_op jit(solution)/shard_map/all_to_all | solution.py:35
  218.9 3.8 %b_near.1 = (bf16[3,136,256]{2,1,0:T(8,128)(2,1)S(1)}, bf16[3,136,256]{2,1,0:T(8,128)(2,1)S(1)}, f32[3,136,128]{2,1,0:T(8,128)S(1)}, bf16[136,1792]{1,0:T(8,128)(2,1)S(1)}, bf16[136,1792]{1,0:T(8,128)(2,1)S(1)}) custom-call(bf16[136,1792]{1,0:T(8,128)(2,1)} %get-tuple-element.56.refs_0_.refs_8_, bf16[136,1792]{1,0:T(8,128)(2,1)} %get-tuple-element.57.refs_1_.refs_9_, ...), custom_call_target="tpu_custom_call" | custom-call | flops 1000000 | bytes 100000 | tf_op jit(solution)/shard_map/b_near/pallas_call | solution.py:73
  239.7 4.6 %collective-permute-done.29.refs_5_ = bf16[136,1792]{1,0:T(8,128)(2,1)S(1)} collective-permute-done((bf16[136,1792]{1,0:T(8,128)(2,1)S(1)}, bf16[136,1792]{1,0:T(8,128)(2,1)S(1)}, u32[]{:S(2)}, u32[]{:S(2)}) %collective-permute-start.29) | collective-permute-done | bytes 487456 | tf_op jit(solution)/shard_map/ppermute | solution.py:28
  246.5 7.1 %collective-permute-done.30.refs_6_ = bf16[136,1792]{1,0:T(8,128)(2,1)S(1)} collective-permute-done((bf16[136,1792]{1,0:T(8,128)(2,1)S(1)}, bf16[136,1792]{1,0:T(8,128)(2,1)S(1)}, u32[]{:S(2)}, u32[]{:S(2)}) %collective-permute-start.30) | collective-permute-done | bytes 487456 | tf_op jit(solution)/shard_map/ppermute | solution.py:28
  256.6 5.2 %all-to-all-start.4 = ((bf16[4,136,896]{2,1,0:T(8,128)(2,1)}), bf16[4,136,896]{2,1,0:T(8,128)(2,1)S(1)}, u32[]{:S(2)}, u32[]{:S(2)}) async-start(bf16[4,136,896]{2,1,0:T(8,128)(2,1)} %bitcast.53), calls=%async_computation.4 | async-start | bytes 1949696 | tf_op jit(solution)/shard_map/all_to_all | solution.py:35
  269.4 9.0 %weight_grads.1 = (bf16[3584,256]{1,0:T(8,128)(2,1)}, bf16[256,3584]{1,0:T(8,128)(2,1)}) custom-call(bf16[136,1792]{1,0:T(8,128)(2,1)} %get-tuple-element.51.refs_0_, bf16[136,1792]{1,0:T(8,128)(2,1)S(1)} %copy-done.23, bf16[136,1792]{1,0:T(8,128)(2,1)} %collective-permute-done.12.refs_2_.refs_3_, bf16[136,1792]{1,0:T(8,128)(2,1)} %collective-permute-done.13.refs_3_, ...), custom_call_target="tpu_custom_call" | custom-call | flops 1000000 | bytes 100000 | tf_op jit(solution)/shard_map/weight_grads/pallas_call | solution.py:73
  279.8 4.0 %backward_out.1 = bf16[128,3584]{1,0:T(8,128)(2,1)} custom-call(bf16[128,3584]{1,0:T(8,128)(2,1)} %collective-permute-done.4.refs_0_, bf16[128,3584]{1,0:T(8,128)(2,1)} %collective-permute-done.19.refs_0_.refs_1_, bf16[544,896]{1,0:T(8,128)(2,1)S(1)} %bitcast.49, s32[128,4]{1,0:T(8,128)S(1)} %copy-done.36), custom_call_target="tpu_custom_call" | custom-call | flops 1000000 | bytes 100000 | tf_op jit(solution)/shard_map/backward_out/pallas_call | solution.py:73
  (194 shorter events, 116.0 us)
Async XLA Ops:
  11.0 30.8 %all-to-all-start = ((bf16[4,136,896]{2,1,0:T(8,128)(2,1)}), bf16[4,136,896]{2,1,0:T(8,128)(2,1)}, u32[]{:S(2)}, u32[]{:S(2)}) async-start(bf16[4,136,896]{2,1,0:T(8,128)(2,1)} %bitcast.4), calls=%async_computation | async-start | bytes 1949696 | tf_op jit(solution)/shard_map/all_to_all | solution.py:35
  16.9 31.0 %collective-permute-start.4 = (bf16[128,3584]{1,0:T(8,128)(2,1)}, bf16[128,3584]{1,0:T(8,128)(2,1)}, u32[]{:S(2)}, u32[]{:S(2)}) collective-permute-start(bf16[128,3584]{1,0:T(8,128)(2,1)} %bitcast.11), channel_id=1, source_target_pairs={{0,16},{16,0},{1,17},{17,1},{2,18},{18,2},{3,19},{19,3},{4,20},{20... | collective-permute-start | bytes 2752520 | tf_op jit(solution)/shard_map/ppermute | solution.py:23
  63.5 41.2 %all-to-all-start.1 = ((bf16[4,136,896]{2,1,0:T(8,128)(2,1)}), bf16[4,136,896]{2,1,0:T(8,128)(2,1)}, u32[]{:S(2)}, u32[]{:S(2)}) async-start(bf16[4,136,896]{2,1,0:T(8,128)(2,1)} %bitcast.54), calls=%async_computation.1 | async-start | bytes 1949696 | tf_op jit(solution)/shard_map/all_to_all | solution.py:35
  70.8 21.7 %collective-permute-start.2 = (bf16[136,1792]{1,0:T(8,128)(2,1)}, bf16[136,1792]{1,0:T(8,128)(2,1)S(1)}, u32[]{:S(2)}, u32[]{:S(2)}) collective-permute-start(bf16[136,1792]{1,0:T(8,128)(2,1)} %copy-done.32), channel_id=1, source_target_pairs={{0,2},{1,3},{2,0},{3,1},{4,6},{5,7},{6,4},{7,5},{8,10},{9,11},{10,... | collective-permute-start | bytes 1462280 | tf_op jit(solution)/shard_map/ppermute | solution.py:28
  71.3 29.1 %collective-permute-start.6 = (bf16[136,1792]{1,0:T(8,128)(2,1)}, bf16[136,1792]{1,0:T(8,128)(2,1)S(1)}, u32[]{:S(2)}, u32[]{:S(2)}) collective-permute-start(bf16[136,1792]{1,0:T(8,128)(2,1)} %copy-done.19), channel_id=1, source_target_pairs={{0,2},{1,3},{2,0},{3,1},{4,6},{5,7},{6,4},{7,5},{8,10},{9,11},{10,... | collective-permute-start | bytes 1462280 | tf_op jit(solution)/shard_map/ppermute | solution.py:28
  83.6 26.0 %collective-permute-start.19 = (bf16[128,3584]{1,0:T(8,128)(2,1)}, bf16[128,3584]{1,0:T(8,128)(2,1)}, u32[]{:S(2)}, u32[]{:S(2)}) collective-permute-start(bf16[128,3584]{1,0:T(8,128)(2,1)} %bitcast.64), channel_id=1, source_target_pairs={{0,16},{16,0},{1,17},{17,1},{2,18},{18,2},{3,19},{19,3},{4,20},{20... | collective-permute-start | bytes 2752520 | tf_op jit(solution)/shard_map/ppermute | solution.py:23
  122.9 41.8 %all-to-all-start.3 = ((bf16[4,136,896]{2,1,0:T(8,128)(2,1)}), bf16[4,136,896]{2,1,0:T(8,128)(2,1)}, u32[]{:S(2)}, u32[]{:S(2)}) async-start(bf16[4,136,896]{2,1,0:T(8,128)(2,1)} %bitcast.55), calls=%async_computation.3 | async-start | bytes 1949696 | tf_op jit(solution)/shard_map/all_to_all | solution.py:35
  127.4 24.8 %collective-permute-start.8 = (bf16[2,136,1792]{2,1,0:T(8,128)(2,1)}, bf16[2,136,1792]{2,1,0:T(8,128)(2,1)S(1)}, u32[]{:S(2)}, u32[]{:S(2)}) collective-permute-start(bf16[2,136,1792]{2,1,0:T(8,128)(2,1)} %copy-done.46), channel_id=1, source_target_pairs={{0,1},{1,0},{2,3},{3,2},{4,5},{5,4},{6,7},{7,6},{8,9},{9,8},{10,11... | collective-permute-start | bytes 2924552 | tf_op jit(solution)/shard_map/ppermute | solution.py:28
  128.9 24.7 %collective-permute-start.9 = (bf16[2,136,1792]{2,1,0:T(8,128)(2,1)}, bf16[2,136,1792]{2,1,0:T(8,128)(2,1)S(1)}, u32[]{:S(2)}, u32[]{:S(2)}) collective-permute-start(bf16[2,136,1792]{2,1,0:T(8,128)(2,1)} %copy-done.45), channel_id=1, source_target_pairs={{0,2},{1,3},{2,0},{3,1},{4,6},{5,7},{6,4},{7,5},{8,10},{9,11},{10,... | collective-permute-start | bytes 2924552 | tf_op jit(solution)/shard_map/ppermute | solution.py:28
  130.4 33.8 %collective-permute-start.15 = (bf16[136,1792]{1,0:T(8,128)(2,1)}, bf16[136,1792]{1,0:T(8,128)(2,1)}, u32[]{:S(2)}, u32[]{:S(2)}) collective-permute-start(bf16[136,1792]{1,0:T(8,128)(2,1)} %copy-done.21), channel_id=1, source_target_pairs={{0,2},{1,3},{2,0},{3,1},{4,6},{5,7},{6,4},{7,5},{8,10},{9,11},{10,... | collective-permute-start | bytes 1462280 | tf_op jit(solution)/shard_map/ppermute | solution.py:28
  131.0 36.8 %collective-permute-start.13 = (bf16[136,1792]{1,0:T(8,128)(2,1)}, bf16[136,1792]{1,0:T(8,128)(2,1)}, u32[]{:S(2)}, u32[]{:S(2)}) collective-permute-start(bf16[136,1792]{1,0:T(8,128)(2,1)} %copy-done.21), channel_id=1, source_target_pairs={{0,1},{1,0},{2,3},{3,2},{4,5},{5,4},{6,7},{7,6},{8,9},{9,8},{10,11... | collective-permute-start | bytes 1462280 | tf_op jit(solution)/shard_map/ppermute | solution.py:28
  131.5 43.2 %collective-permute-start.14 = (bf16[136,1792]{1,0:T(8,128)(2,1)}, bf16[136,1792]{1,0:T(8,128)(2,1)}, u32[]{:S(2)}, u32[]{:S(2)}) collective-permute-start(bf16[136,1792]{1,0:T(8,128)(2,1)} %get-tuple-element.51.refs_0_), channel_id=1, source_target_pairs={{0,2},{1,3},{2,0},{3,1},{4,6},{5,7},{6,4},{7,5},{8,10},{9,11},{10,... | collective-permute-start | bytes 1462280 | tf_op jit(solution)/shard_map/ppermute | solution.py:28
  158.0 18.5 %collective-permute-start.10 = (bf16[136,1792]{1,0:T(8,128)(2,1)}, bf16[136,1792]{1,0:T(8,128)(2,1)}, u32[]{:S(2)}, u32[]{:S(2)}) collective-permute-start(bf16[136,1792]{1,0:T(8,128)(2,1)} %get-tuple-element.47), channel_id=1, source_target_pairs={{0,1},{1,0},{2,3},{3,2},{4,5},{5,4},{6,7},{7,6},{8,9},{9,8},{10,11... | collective-permute-start | bytes 1462280 | tf_op jit(solution)/shard_map/ppermute | solution.py:28
  158.5 26.6 %collective-permute-start.16 = (bf16[136,1792]{1,0:T(8,128)(2,1)}, bf16[136,1792]{1,0:T(8,128)(2,1)}, u32[]{:S(2)}, u32[]{:S(2)}) collective-permute-start(bf16[136,1792]{1,0:T(8,128)(2,1)} %collective-permute-done.12.refs_2_.refs_3_), channel_id=1, source_target_pairs={{0,2},{1,3},{2,0},{3,1},{4,6},{5,7},{6,4},{7,5},{8,10},{9,11},{10,... | collective-permute-start | bytes 1462280 | tf_op jit(solution)/shard_map/ppermute | solution.py:28
  164.2 21.4 %collective-permute-start.17 = (bf16[136,1792]{1,0:T(8,128)(2,1)}, bf16[136,1792]{1,0:T(8,128)(2,1)}, u32[]{:S(2)}, u32[]{:S(2)}) collective-permute-start(bf16[136,1792]{1,0:T(8,128)(2,1)} %collective-permute-done.15.refs_5_), channel_id=1, source_target_pairs={{0,1},{1,0},{2,3},{3,2},{4,5},{5,4},{6,7},{7,6},{8,9},{9,8},{10,11... | collective-permute-start | bytes 1462280 | tf_op jit(solution)/shard_map/ppermute | solution.py:28
  167.8 26.2 %collective-permute-start.20 = (bf16[136,1792]{1,0:T(8,128)(2,1)}, bf16[136,1792]{1,0:T(8,128)(2,1)}, u32[]{:S(2)}, u32[]{:S(2)}) collective-permute-start(bf16[136,1792]{1,0:T(8,128)(2,1)} %get-tuple-element.56.refs_0_.refs_8_), channel_id=1, source_target_pairs={{0,1},{1,0},{2,3},{3,2},{4,5},{5,4},{6,7},{7,6},{8,9},{9,8},{10,11... | collective-permute-start | bytes 1462280 | tf_op jit(solution)/shard_map/ppermute | solution.py:28
  174.7 20.9 %collective-permute-start.23 = (bf16[136,1792]{1,0:T(8,128)(2,1)}, bf16[136,1792]{1,0:T(8,128)(2,1)}, u32[]{:S(2)}, u32[]{:S(2)}) collective-permute-start(bf16[136,1792]{1,0:T(8,128)(2,1)} %get-tuple-element.57.refs_1_.refs_9_), channel_id=1, source_target_pairs={{0,2},{1,3},{2,0},{3,1},{4,6},{5,7},{6,4},{7,5},{8,10},{9,11},{10,... | collective-permute-start | bytes 1462280 | tf_op jit(solution)/shard_map/ppermute | solution.py:28
  176.5 29.3 %collective-permute-start.11 = (bf16[136,1792]{1,0:T(8,128)(2,1)}, bf16[136,1792]{1,0:T(8,128)(2,1)S(1)}, u32[]{:S(2)}, u32[]{:S(2)}) collective-permute-start(bf16[136,1792]{1,0:T(8,128)(2,1)} %copy-done.47), channel_id=1, source_target_pairs={{0,2},{1,3},{2,0},{3,1},{4,6},{5,7},{6,4},{7,5},{8,10},{9,11},{10,... | collective-permute-start | bytes 1462280 | tf_op jit(solution)/shard_map/ppermute | solution.py:28
  185.1 29.5 %collective-permute-start.21 = (bf16[136,1792]{1,0:T(8,128)(2,1)}, bf16[136,1792]{1,0:T(8,128)(2,1)}, u32[]{:S(2)}, u32[]{:S(2)}) collective-permute-start(bf16[136,1792]{1,0:T(8,128)(2,1)} %get-tuple-element.57.refs_1_.refs_9_), channel_id=1, source_target_pairs={{0,1},{1,0},{2,3},{3,2},{4,5},{5,4},{6,7},{7,6},{8,9},{9,8},{10,11... | collective-permute-start | bytes 1462280 | tf_op jit(solution)/shard_map/ppermute | solution.py:28
  185.6 30.8 %collective-permute-start.22 = (bf16[136,1792]{1,0:T(8,128)(2,1)}, bf16[136,1792]{1,0:T(8,128)(2,1)}, u32[]{:S(2)}, u32[]{:S(2)}) collective-permute-start(bf16[136,1792]{1,0:T(8,128)(2,1)} %get-tuple-element.56.refs_0_.refs_8_), channel_id=1, source_target_pairs={{0,2},{1,3},{2,0},{3,1},{4,6},{5,7},{6,4},{7,5},{8,10},{9,11},{10,... | collective-permute-start | bytes 1462280 | tf_op jit(solution)/shard_map/ppermute | solution.py:28
  194.0 32.8 %collective-permute-start.26 = (bf16[136,1792]{1,0:T(8,128)(2,1)}, bf16[136,1792]{1,0:T(8,128)(2,1)}, u32[]{:S(2)}, u32[]{:S(2)}) collective-permute-start(bf16[136,1792]{1,0:T(8,128)(2,1)} %collective-permute-done.20.refs_2_.refs_10_), channel_id=1, source_target_pairs={{0,2},{1,3},{2,0},{3,1},{4,6},{5,7},{6,4},{7,5},{8,10},{9,11},{10,... | collective-permute-start | bytes 1462280 | tf_op jit(solution)/shard_map/ppermute | solution.py:28
  195.6 31.3 %collective-permute-start.27 = (bf16[136,1792]{1,0:T(8,128)(2,1)}, bf16[136,1792]{1,0:T(8,128)(2,1)}, u32[]{:S(2)}, u32[]{:S(2)}) collective-permute-start(bf16[136,1792]{1,0:T(8,128)(2,1)} %collective-permute-done.23.refs_5_.refs_13_), channel_id=1, source_target_pairs={{0,1},{1,0},{2,3},{3,2},{4,5},{5,4},{6,7},{7,6},{8,9},{9,8},{10,11... | collective-permute-start | bytes 1462280 | tf_op jit(solution)/shard_map/ppermute | solution.py:28
  209.6 46.9 %all-to-all-start.2 = ((bf16[4,136,896]{2,1,0:T(8,128)(2,1)}), bf16[4,136,896]{2,1,0:T(8,128)(2,1)}, u32[]{:S(2)}, u32[]{:S(2)}) async-start(bf16[4,136,896]{2,1,0:T(8,128)(2,1)} %bitcast.52), calls=%async_computation.2 | async-start | bytes 1949696 | tf_op jit(solution)/shard_map/all_to_all | solution.py:35
  256.6 23.3 %all-to-all-start.4 = ((bf16[4,136,896]{2,1,0:T(8,128)(2,1)}), bf16[4,136,896]{2,1,0:T(8,128)(2,1)S(1)}, u32[]{:S(2)}, u32[]{:S(2)}) async-start(bf16[4,136,896]{2,1,0:T(8,128)(2,1)} %bitcast.53), calls=%async_computation.4 | async-start | bytes 1949696 | tf_op jit(solution)/shard_map/all_to_all | solution.py:35
  (63 other events, 407.0 us)

commit v10 on v8

--- a/solution.py
+++ b/solution.py
@@ -420,7 +420,7 @@
     a_mine, _ = pack_halves(a_blocks, select, (up_turned, down_turned))
     a_near = spread_halves(a_mine, experts)
     a_far = relay_halves(a_near, experts)
-    b_send, b_gate = send_normed(b_x, b_ids, cols_r, b_target, layout, (a_near[0][0],))
+    b_send, b_gate = send_normed(b_x, b_ids, cols_r, b_target, layout, a_near[0] + a_near[1])
     b_blocks = across_planes(b_send, layout)
 
     act = a_near_rows((a_mine,) + a_near, up, b_gate)
@@ -430,7 +430,7 @@
     b_near = spread_halves(b_mine, experts)
     b_far = relay_halves(b_near, experts)
 
-    a_second, a_done = a_second_rows(act, down, a_first)
+    a_second, a_done = a_second_rows(act, down, a_first, (b_near[0][0], b_near[1][1]))
     a_second = swap_pair(a_second, experts)
     c_send, _ = send_cotangents(b_c, b_gate, b_target, layout, (a_done,))
     c_blocks = across_planes(c_send, layout)

time: 261 us -> 273 us (1.046)
  local copies, waits for them, and re-layouts: 27.9 us -> 37.5 us
  waiting for transfers between devices: 114 us -> 118 us
    all_to_all x5, waiting for transfers between devices: 19.4 us -> 38.9 us  [depth_exchange(): lax.all_to_all(blocks, 'expert', split_axis=0, concat_axis=0, tiled=True,...]
    ppermute x28, waiting for transfers between devices: 92.2 us -> 77.1 us  [plane_move(): return lax.ppermute(array, 'expert', [(i, i ^ bit) for i in range(devices)])]
    unnamed x84 -> x118, local copies, waits for them, and re-layouts: 26.9 us -> 36.5 us
  transfers between devices with their start and end apart: 37 -> 37, of which waited for: 19 -> 22; matrix products, arithmetic and copies ran while one was open for 5% -> 4% of each run, Pallas kernels for 18% -> 15%
where the time goes in v10:
time: 273 us; the launch traced here: 272 us
  waiting for transfers between devices  118 us (43%)
  starting transfers between devices  56.6 us (21%)
  Pallas kernels  53 us (19%)
  local copies, waits for them, and re-layouts  37.5 us (14%)
  other arithmetic  4.79 us (2%)
    ppermute x28, waiting for transfers between devices, plane_move(): return lax.ppermute(array, 'expert', [(i, i ^ bit) for i in range(devices)])  77.1 us
    pallas_call x18, Pallas kernels, on_core(): pl.pallas_call(kernel, out_shape=[jax.ShapeDtypeStruct(shape, kind) for s...  53 us
    all_to_all x5, waiting for transfers between devices, depth_exchange(): lax.all_to_all(blocks, 'expert', split_axis=0, concat_axis=0, tiled=True,...  38.9 us
    unnamed x118, local copies, waits for them, and re-layouts  36.5 us
    ppermute x28, starting transfers between devices, plane_move(): return lax.ppermute(array, 'expert', [(i, i ^ bit) for i in range(devices)])  30.9 us
    all_to_all x5, starting transfers between devices, depth_exchange(): lax.all_to_all(blocks, 'expert', split_axis=0, concat_axis=0, tiled=True,...  24.8 us
  transfers between devices with their start and end apart: 37, of which 22 were waited for; matrix products, arithmetic and copies ran while one was open for 4% of the time, Pallas kernels for 15%

profile of v10, /device:TPU:0, one launch (start us, length us, event | category | flops | bytes accessed | tf_op | source)
XLA Modules:
  0.0 271.6 jit_solution(11124962556688448386)
XLA Ops:
  11.0 5.9 %all-to-all-start = ((bf16[4,136,896]{2,1,0:T(8,128)(2,1)}), bf16[4,136,896]{2,1,0:T(8,128)(2,1)}, u32[]{:S(2)}, u32[]{:S(2)}) async-start(bf16[4,136,896]{2,1,0:T(8,128)(2,1)} %bitcast.4), calls=%async_computation | async-start | bytes 1949696 | tf_op jit(solution)/shard_map/all_to_all | solution.py:35
  19.9 3.9 %copy.29 = bf16[1,256,3584]{1,2,0:T(8,128)(2,1)} copy(bf16[1,256,3584]{2,1,0:T(8,128)(2,1)} %param.16) | data formatting | bytes 3670016 | tf_op args[6]
  23.7 18.1 %all-to-all-done = bf16[4,136,896]{2,1,0:T(8,128)(2,1)} async-done(((bf16[4,136,896]{2,1,0:T(8,128)(2,1)}), bf16[4,136,896]{2,1,0:T(8,128)(2,1)}, u32[]{:S(2)}, u32[]{:S(2)}) %all-to-all-start) | async-done | bytes 974880 | tf_op jit(solution)/shard_map/all_to_all | solution.py:35
  50.5 9.2 %collective-permute-done.2.refs_6_.refs_4_ = bf16[136,1792]{1,0:T(8,128)(2,1)S(1)} collective-permute-done((bf16[136,1792]{1,0:T(8,128)(2,1)S(1)}, bf16[136,1792]{1,0:T(8,128)(2,1)S(1)}, u32[]{:S(2)}, u32[]{:S(2)}) %collective-permute-start.2) | collective-permute-done | bytes 487456 | tf_op jit(solution)/shard_map/ppermute | solution.py:28
  61.3 7.3 %collective-permute-done.3.refs_7_.refs_5_ = bf16[136,1792]{1,0:T(8,128)(2,1)S(1)} collective-permute-done((bf16[136,1792]{1,0:T(8,128)(2,1)S(1)}, bf16[136,1792]{1,0:T(8,128)(2,1)S(1)}, u32[]{:S(2)}, u32[]{:S(2)}) %collective-permute-start.3) | collective-permute-done | bytes 487456 | tf_op jit(solution)/shard_map/ppermute | solution.py:28
  73.9 4.2 %all-to-all-start.1 = ((bf16[4,136,896]{2,1,0:T(8,128)(2,1)}), bf16[4,136,896]{2,1,0:T(8,128)(2,1)}, u32[]{:S(2)}, u32[]{:S(2)}) async-start(bf16[4,136,896]{2,1,0:T(8,128)(2,1)} %bitcast.54), calls=%async_computation.1 | async-start | bytes 1949696 | tf_op jit(solution)/shard_map/all_to_all | solution.py:35
  95.7 5.4 %all-to-all-done.1 = bf16[4,136,896]{2,1,0:T(8,128)(2,1)} async-done(((bf16[4,136,896]{2,1,0:T(8,128)(2,1)}), bf16[4,136,896]{2,1,0:T(8,128)(2,1)}, u32[]{:S(2)}, u32[]{:S(2)}) %all-to-all-start.1) | async-done | bytes 974880 | tf_op jit(solution)/shard_map/all_to_all | solution.py:35
  105.6 12.1 %collective-permute-done.8.refs_2_ = bf16[2,136,1792]{2,1,0:T(8,128)(2,1)} collective-permute-done((bf16[2,136,1792]{2,1,0:T(8,128)(2,1)}, bf16[2,136,1792]{2,1,0:T(8,128)(2,1)}, u32[]{:S(2)}, u32[]{:S(2)}) %collective-permute-start.8) | collective-permute-done | bytes 974880 | tf_op jit(solution)/shard_map/ppermute | solution.py:28
  119.2 5.6 %collective-permute-done.10.refs_4_.refs_2_ = bf16[136,1792]{1,0:T(8,128)(2,1)S(1)} collective-permute-done((bf16[136,1792]{1,0:T(8,128)(2,1)S(1)}, bf16[136,1792]{1,0:T(8,128)(2,1)S(1)}, u32[]{:S(2)}, u32[]{:S(2)}) %collective-permute-start.10) | collective-permute-done | bytes 487456 | tf_op jit(solution)/shard_map/ppermute | solution.py:28
  130.2 3.3 %send_cotangents.1 = (bf16[544,896]{1,0:T(8,128)(2,1)S(1)}, f32[8,128]{1,0:T(8,128)}) custom-call(bf16[128,3584]{1,0:T(8,128)(2,1)} %collective-permute-done.19.refs_0_.refs_1_, f32[128,128]{1,0:T(8,128)S(1)} %get-tuple-element.45.refs_7_.refs_1_, s32[4,128]{1,0:T(4,128)S(1)} %get-tuple-element.80.refs_3_.refs_2_, f32[8,128]{1,0:T(8,128)S(1)} %get-tuple-element.56.refs_3_), custom_call_target="tpu_custom_call" | custom-call | flops 1000000 | bytes 100000 | tf_op jit(solution)/shard_map/send_cotangents/pallas_call | solution.py:73
  134.4 4.4 %all-to-all-start.3 = ((bf16[4,136,896]{2,1,0:T(8,128)(2,1)}), bf16[4,136,896]{2,1,0:T(8,128)(2,1)}, u32[]{:S(2)}, u32[]{:S(2)}) async-start(bf16[4,136,896]{2,1,0:T(8,128)(2,1)} %bitcast.55), calls=%async_computation.3 | async-start | bytes 1949696 | tf_op jit(solution)/shard_map/all_to_all | solution.py:35
  144.1 15.5 %all-to-all-done.3 = bf16[4,136,896]{2,1,0:T(8,128)(2,1)} async-done(((bf16[4,136,896]{2,1,0:T(8,128)(2,1)}), bf16[4,136,896]{2,1,0:T(8,128)(2,1)}, u32[]{:S(2)}, u32[]{:S(2)}) %all-to-all-start.3) | async-done | bytes 974880 | tf_op jit(solution)/shard_map/all_to_all | solution.py:35
  159.6 3.1 %pack.5 = (bf16[136,1792]{1,0:T(8,128)(2,1)}, bf16[136,1792]{1,0:T(8,128)(2,1)}, f32[8,128]{1,0:T(8,128)}) custom-call(bf16[544,896]{1,0:T(8,128)(2,1)} %bitcast.22.refs_0_, bf16[4,136,544]{2,1,0:T(8,128)(2,1)S(1)} %copy-done.8), custom_call_target="tpu_custom_call" | custom-call | flops 1000000 | bytes 100000 | tf_op jit(solution)/shard_map/pack/pallas_call | solution.py:73
  166.4 8.8 %collective-permute-done.17.refs_7_ = bf16[136,1792]{1,0:T(8,128)(2,1)} collective-permute-done((bf16[136,1792]{1,0:T(8,128)(2,1)}, bf16[136,1792]{1,0:T(8,128)(2,1)}, u32[]{:S(2)}, u32[]{:S(2)}) %collective-permute-start.17) | collective-permute-done | bytes 487456 | tf_op jit(solution)/shard_map/ppermute | solution.py:28
  177.3 8.3 %collective-permute-done.20.refs_2_.refs_10_ = bf16[136,1792]{1,0:T(8,128)(2,1)} collective-permute-done((bf16[136,1792]{1,0:T(8,128)(2,1)}, bf16[136,1792]{1,0:T(8,128)(2,1)}, u32[]{:S(2)}, u32[]{:S(2)}) %collective-permute-start.20) | collective-permute-done | bytes 487456 | tf_op jit(solution)/shard_map/ppermute | solution.py:28
  192.5 3.9 %b_hidden.1 = (f32[4,136,256]{2,1,0:T(8,128)S(1)}, f32[4,136,128]{2,1,0:T(8,128)S(1)}, f32[8,128]{1,0:T(8,128)S(1)}) custom-call(bf16[136,1792]{1,0:T(8,128)(2,1)S(1)} %copy-done.30, bf16[136,1792]{1,0:T(8,128)(2,1)S(1)} %copy-done.33, bf16[136,1792]{1,0:T(8,128)(2,1)S(1)} %copy-done.11, bf16[136,1792]{1,0:T(8,128)(2,1)} %collective-permute-done.14.refs_3_, ...), custom_call_target="tpu_custom_call" | custom-call | flops 1000000 | bytes 100000 | tf_op jit(solution)/shard_map/b_hidden/pallas_call | solution.py:73
  196.5 3.4 %a_total.1 = (bf16[544,896]{1,0:T(8,128)(2,1)S(1)}, f32[8,128]{1,0:T(8,128)S(1)}) custom-call(bf16[3,136,256]{2,1,0:T(8,128)(2,1)S(1)} %copy-done.20, bf16[256,3584]{1,0:T(8,128)(2,1)S(1)} %bitcast.43, bf16[2,136,1792]{2,1,0:T(8,128)(2,1)} %collective-permute-done.8.refs_2_, bf16[2,136,1792]{2,1,0:T(8,128)(2,1)} %collective-permute-done.9.refs_3_, ...), custom_call_target="tpu_custom_call" | custom-call | flops 1000000 | bytes 100000 | tf_op jit(solution)/shard_map/a_total/pallas_call | solution.py:73
  200.8 5.1 %all-to-all-start.2 = ((bf16[4,136,896]{2,1,0:T(8,128)(2,1)}), bf16[4,136,896]{2,1,0:T(8,128)(2,1)}, u32[]{:S(2)}, u32[]{:S(2)}) async-start(bf16[4,136,896]{2,1,0:T(8,128)(2,1)} %bitcast.52), calls=%async_computation.2 | async-start | bytes 1949696 | tf_op jit(solution)/shard_map/all_to_all | solution.py:35
  208.4 3.8 %b_near.1 = (bf16[3,136,256]{2,1,0:T(8,128)(2,1)S(1)}, bf16[3,136,256]{2,1,0:T(8,128)(2,1)S(1)}, f32[3,136,128]{2,1,0:T(8,128)S(1)}, bf16[136,1792]{1,0:T(8,128)(2,1)S(1)}, bf16[136,1792]{1,0:T(8,128)(2,1)S(1)}) custom-call(bf16[136,1792]{1,0:T(8,128)(2,1)} %get-tuple-element.58.refs_0_.refs_8_, bf16[136,1792]{1,0:T(8,128)(2,1)} %get-tuple-element.59.refs_1_.refs_9_, ...), custom_call_target="tpu_custom_call" | custom-call | flops 1000000 | bytes 100000 | tf_op jit(solution)/shard_map/b_near/pallas_call | solution.py:73
  223.2 8.3 %collective-permute-done.28.refs_4_ = bf16[136,1792]{1,0:T(8,128)(2,1)S(1)} collective-permute-done((bf16[136,1792]{1,0:T(8,128)(2,1)S(1)}, bf16[136,1792]{1,0:T(8,128)(2,1)S(1)}, u32[]{:S(2)}, u32[]{:S(2)}) %collective-permute-start.28) | collective-permute-done | bytes 487456 | tf_op jit(solution)/shard_map/ppermute | solution.py:28
  235.4 6.2 %collective-permute-done.30.refs_6_ = bf16[136,1792]{1,0:T(8,128)(2,1)S(1)} collective-permute-done((bf16[136,1792]{1,0:T(8,128)(2,1)S(1)}, bf16[136,1792]{1,0:T(8,128)(2,1)S(1)}, u32[]{:S(2)}, u32[]{:S(2)}) %collective-permute-start.30) | collective-permute-done | bytes 487456 | tf_op jit(solution)/shard_map/ppermute | solution.py:28
  245.8 5.2 %all-to-all-start.4 = ((bf16[4,136,896]{2,1,0:T(8,128)(2,1)}), bf16[4,136,896]{2,1,0:T(8,128)(2,1)S(1)}, u32[]{:S(2)}, u32[]{:S(2)}) async-start(bf16[4,136,896]{2,1,0:T(8,128)(2,1)} %bitcast.53), calls=%async_computation.4 | async-start | bytes 1949696 | tf_op jit(solution)/shard_map/all_to_all | solution.py:35
  258.2 8.6 %weight_grads.1 = (bf16[3584,256]{1,0:T(8,128)(2,1)}, bf16[256,3584]{1,0:T(8,128)(2,1)}) custom-call(bf16[136,1792]{1,0:T(8,128)(2,1)S(1)} %copy-done.31, bf16[136,1792]{1,0:T(8,128)(2,1)S(1)} %copy-done.34, bf16[136,1792]{1,0:T(8,128)(2,1)S(1)} %copy-done.12, bf16[136,1792]{1,0:T(8,128)(2,1)} %collective-permute-done.14.refs_3_, ...), custom_call_target="tpu_custom_call" | custom-call | flops 1000000 | bytes 100000 | tf_op jit(solution)/shard_map/weight_grads/pallas_call | solution.py:73
  266.8 3.9 %backward_out.1 = bf16[128,3584]{1,0:T(8,128)(2,1)} custom-call(bf16[128,3584]{1,0:T(8,128)(2,1)} %collective-permute-done.4.refs_0_, bf16[128,3584]{1,0:T(8,128)(2,1)} %collective-permute-done.19.refs_0_.refs_1_, bf16[544,896]{1,0:T(8,128)(2,1)S(1)} %bitcast.49, s32[128,4]{1,0:T(8,128)S(1)} %get-tuple-element.78.refs_3_), custom_call_target="tpu_custom_call" | custom-call | flops 1000000 | bytes 100000 | tf_op jit(solution)/shard_map/backward_out/pallas_call | solution.py:73
  (208 shorter events, 107.1 us)
Async XLA Ops:
  11.0 30.8 %all-to-all-start = ((bf16[4,136,896]{2,1,0:T(8,128)(2,1)}), bf16[4,136,896]{2,1,0:T(8,128)(2,1)}, u32[]{:S(2)}, u32[]{:S(2)}) async-start(bf16[4,136,896]{2,1,0:T(8,128)(2,1)} %bitcast.4), calls=%async_computation | async-start | bytes 1949696 | tf_op jit(solution)/shard_map/all_to_all | solution.py:35
  16.9 33.6 %collective-permute-start.4 = (bf16[128,3584]{1,0:T(8,128)(2,1)}, bf16[128,3584]{1,0:T(8,128)(2,1)}, u32[]{:S(2)}, u32[]{:S(2)}) collective-permute-start(bf16[128,3584]{1,0:T(8,128)(2,1)} %bitcast.11), channel_id=1, source_target_pairs={{0,16},{16,0},{1,17},{17,1},{2,18},{18,2},{3,19},{19,3},{4,20},{20... | collective-permute-start | bytes 2752520 | tf_op jit(solution)/shard_map/ppermute | solution.py:23
  49.2 20.6 %collective-permute-start.1 = (bf16[136,1792]{1,0:T(8,128)(2,1)S(1)}, bf16[136,1792]{1,0:T(8,128)(2,1)S(1)}, u32[]{:S(2)}, u32[]{:S(2)}) collective-permute-start(bf16[136,1792]{1,0:T(8,128)(2,1)S(1)} %get-tuple-element.44.refs_1_), channel_id=1, source_target_pairs={{0,1},{1,0},{2,3},{3,2},{4,5},{5,4},{6,7},{7,6},{8,9},{9,8},{10,11... | collective-permute-start | bytes 1462280 | tf_op jit(solution)/shard_map/ppermute | solution.py:28
  73.9 27.1 %all-to-all-start.1 = ((bf16[4,136,896]{2,1,0:T(8,128)(2,1)}), bf16[4,136,896]{2,1,0:T(8,128)(2,1)}, u32[]{:S(2)}, u32[]{:S(2)}) async-start(bf16[4,136,896]{2,1,0:T(8,128)(2,1)} %bitcast.54), calls=%async_computation.1 | async-start | bytes 1949696 | tf_op jit(solution)/shard_map/all_to_all | solution.py:35
  92.9 24.8 %collective-permute-start.8 = (bf16[2,136,1792]{2,1,0:T(8,128)(2,1)}, bf16[2,136,1792]{2,1,0:T(8,128)(2,1)}, u32[]{:S(2)}, u32[]{:S(2)}) collective-permute-start(bf16[2,136,1792]{2,1,0:T(8,128)(2,1)} %get-tuple-element.46), channel_id=1, source_target_pairs={{0,1},{1,0},{2,3},{3,2},{4,5},{5,4},{6,7},{7,6},{8,9},{9,8},{10,11... | collective-permute-start | bytes 2924552 | tf_op jit(solution)/shard_map/ppermute | solution.py:28
  94.4 24.8 %collective-permute-start.9 = (bf16[2,136,1792]{2,1,0:T(8,128)(2,1)}, bf16[2,136,1792]{2,1,0:T(8,128)(2,1)}, u32[]{:S(2)}, u32[]{:S(2)}) collective-permute-start(bf16[2,136,1792]{2,1,0:T(8,128)(2,1)} %get-tuple-element.47), channel_id=1, source_target_pairs={{0,2},{1,3},{2,0},{3,1},{4,6},{5,7},{6,4},{7,5},{8,10},{9,11},{10,... | collective-permute-start | bytes 2924552 | tf_op jit(solution)/shard_map/ppermute | solution.py:28
  95.7 34.5 %collective-permute-start.19 = (bf16[128,3584]{1,0:T(8,128)(2,1)}, bf16[128,3584]{1,0:T(8,128)(2,1)}, u32[]{:S(2)}, u32[]{:S(2)}) collective-permute-start(bf16[128,3584]{1,0:T(8,128)(2,1)} %bitcast.20), channel_id=1, source_target_pairs={{0,16},{16,0},{1,17},{17,1},{2,18},{18,2},{3,19},{19,3},{4,20},{20... | collective-permute-start | bytes 2752520 | tf_op jit(solution)/shard_map/ppermute | solution.py:23
  103.3 21.4 %collective-permute-start.10 = (bf16[136,1792]{1,0:T(8,128)(2,1)S(1)}, bf16[136,1792]{1,0:T(8,128)(2,1)S(1)}, u32[]{:S(2)}, u32[]{:S(2)}) collective-permute-start(bf16[136,1792]{1,0:T(8,128)(2,1)S(1)} %get-tuple-element.50.refs_0_), channel_id=1, source_target_pairs={{0,1},{1,0},{2,3},{3,2},{4,5},{5,4},{6,7},{7,6},{8,9},{9,8},{10,11... | collective-permute-start | bytes 1462280 | tf_op jit(solution)/shard_map/ppermute | solution.py:28
  104.9 20.6 %collective-permute-start.11 = (bf16[136,1792]{1,0:T(8,128)(2,1)S(1)}, bf16[136,1792]{1,0:T(8,128)(2,1)S(1)}, u32[]{:S(2)}, u32[]{:S(2)}) collective-permute-start(bf16[136,1792]{1,0:T(8,128)(2,1)S(1)} %get-tuple-element.51.refs_1_), channel_id=1, source_target_pairs={{0,2},{1,3},{2,0},{3,1},{4,6},{5,7},{6,4},{7,5},{8,10},{9,11},{10,... | collective-permute-start | bytes 1462280 | tf_op jit(solution)/shard_map/ppermute | solution.py:28
  134.4 25.2 %all-to-all-start.3 = ((bf16[4,136,896]{2,1,0:T(8,128)(2,1)}), bf16[4,136,896]{2,1,0:T(8,128)(2,1)}, u32[]{:S(2)}, u32[]{:S(2)}) async-start(bf16[4,136,896]{2,1,0:T(8,128)(2,1)} %bitcast.55), calls=%async_computation.3 | async-start | bytes 1949696 | tf_op jit(solution)/shard_map/all_to_all | solution.py:35
  138.8 23.9 %collective-permute-start.15 = (bf16[136,1792]{1,0:T(8,128)(2,1)}, bf16[136,1792]{1,0:T(8,128)(2,1)}, u32[]{:S(2)}, u32[]{:S(2)}) collective-permute-start(bf16[136,1792]{1,0:T(8,128)(2,1)} %copy-done.29), channel_id=1, source_target_pairs={{0,2},{1,3},{2,0},{3,1},{4,6},{5,7},{6,4},{7,5},{8,10},{9,11},{10,... | collective-permute-start | bytes 1462280 | tf_op jit(solution)/shard_map/ppermute | solution.py:28
  139.9 24.0 %collective-permute-start.14 = (bf16[136,1792]{1,0:T(8,128)(2,1)}, bf16[136,1792]{1,0:T(8,128)(2,1)}, u32[]{:S(2)}, u32[]{:S(2)}) collective-permute-start(bf16[136,1792]{1,0:T(8,128)(2,1)} %copy-done.32), channel_id=1, source_target_pairs={{0,1},{1,0},{2,3},{3,2},{4,5},{5,4},{6,7},{7,6},{8,9},{9,8},{10,11... | collective-permute-start | bytes 1462280 | tf_op jit(solution)/shard_map/ppermute | solution.py:28
  141.3 34.8 %collective-permute-start.12 = (bf16[136,1792]{1,0:T(8,128)(2,1)}, bf16[136,1792]{1,0:T(8,128)(2,1)}, u32[]{:S(2)}, u32[]{:S(2)}) collective-permute-start(bf16[136,1792]{1,0:T(8,128)(2,1)} %copy-done.56), channel_id=1, source_target_pairs={{0,1},{1,0},{2,3},{3,2},{4,5},{5,4},{6,7},{7,6},{8,9},{9,8},{10,11... | collective-permute-start | bytes 1462280 | tf_op jit(solution)/shard_map/ppermute | solution.py:28
  141.9 23.5 %collective-permute-start.16 = (bf16[136,1792]{1,0:T(8,128)(2,1)}, bf16[136,1792]{1,0:T(8,128)(2,1)}, u32[]{:S(2)}, u32[]{:S(2)}) collective-permute-start(bf16[136,1792]{1,0:T(8,128)(2,1)} %copy-done.10), channel_id=1, source_target_pairs={{0,2},{1,3},{2,0},{3,1},{4,6},{5,7},{6,4},{7,5},{8,10},{9,11},{10,... | collective-permute-start | bytes 1462280 | tf_op jit(solution)/shard_map/ppermute | solution.py:28
  142.9 32.3 %collective-permute-start.17 = (bf16[136,1792]{1,0:T(8,128)(2,1)}, bf16[136,1792]{1,0:T(8,128)(2,1)}, u32[]{:S(2)}, u32[]{:S(2)}) collective-permute-start(bf16[136,1792]{1,0:T(8,128)(2,1)} %copy-done.13), channel_id=1, source_target_pairs={{0,1},{1,0},{2,3},{3,2},{4,5},{5,4},{6,7},{7,6},{8,9},{9,8},{10,11... | collective-permute-start | bytes 1462280 | tf_op jit(solution)/shard_map/ppermute | solution.py:28
  162.7 23.0 %collective-permute-start.20 = (bf16[136,1792]{1,0:T(8,128)(2,1)}, bf16[136,1792]{1,0:T(8,128)(2,1)}, u32[]{:S(2)}, u32[]{:S(2)}) collective-permute-start(bf16[136,1792]{1,0:T(8,128)(2,1)} %get-tuple-element.58.refs_0_.refs_8_), channel_id=1, source_target_pairs={{0,1},{1,0},{2,3},{3,2},{4,5},{5,4},{6,7},{7,6},{8,9},{9,8},{10,11... | collective-permute-start | bytes 1462280 | tf_op jit(solution)/shard_map/ppermute | solution.py:28
  164.0 22.7 %collective-permute-start.23 = (bf16[136,1792]{1,0:T(8,128)(2,1)}, bf16[136,1792]{1,0:T(8,128)(2,1)}, u32[]{:S(2)}, u32[]{:S(2)}) collective-permute-start(bf16[136,1792]{1,0:T(8,128)(2,1)} %get-tuple-element.59.refs_1_.refs_9_), channel_id=1, source_target_pairs={{0,2},{1,3},{2,0},{3,1},{4,6},{5,7},{6,4},{7,5},{8,10},{9,11},{10,... | collective-permute-start | bytes 1462280 | tf_op jit(solution)/shard_map/ppermute | solution.py:28
  165.5 31.0 %collective-permute-start.13 = (bf16[136,1792]{1,0:T(8,128)(2,1)}, bf16[136,1792]{1,0:T(8,128)(2,1)S(1)}, u32[]{:S(2)}, u32[]{:S(2)}) collective-permute-start(bf16[136,1792]{1,0:T(8,128)(2,1)} %copy-done.55), channel_id=1, source_target_pairs={{0,2},{1,3},{2,0},{3,1},{4,6},{5,7},{6,4},{7,5},{8,10},{9,11},{10,... | collective-permute-start | bytes 1462280 | tf_op jit(solution)/shard_map/ppermute | solution.py:28
  175.2 30.7 %collective-permute-start.22 = (bf16[136,1792]{1,0:T(8,128)(2,1)}, bf16[136,1792]{1,0:T(8,128)(2,1)}, u32[]{:S(2)}, u32[]{:S(2)}) collective-permute-start(bf16[136,1792]{1,0:T(8,128)(2,1)} %get-tuple-element.58.refs_0_.refs_8_), channel_id=1, source_target_pairs={{0,2},{1,3},{2,0},{3,1},{4,6},{5,7},{6,4},{7,5},{8,10},{9,11},{10,... | collective-permute-start | bytes 1462280 | tf_op jit(solution)/shard_map/ppermute | solution.py:28
  176.2 29.7 %collective-permute-start.21 = (bf16[136,1792]{1,0:T(8,128)(2,1)}, bf16[136,1792]{1,0:T(8,128)(2,1)}, u32[]{:S(2)}, u32[]{:S(2)}) collective-permute-start(bf16[136,1792]{1,0:T(8,128)(2,1)} %get-tuple-element.59.refs_1_.refs_9_), channel_id=1, source_target_pairs={{0,1},{1,0},{2,3},{3,2},{4,5},{5,4},{6,7},{7,6},{8,9},{9,8},{10,11... | collective-permute-start | bytes 1462280 | tf_op jit(solution)/shard_map/ppermute | solution.py:28
  185.6 28.4 %collective-permute-start.26 = (bf16[136,1792]{1,0:T(8,128)(2,1)}, bf16[136,1792]{1,0:T(8,128)(2,1)}, u32[]{:S(2)}, u32[]{:S(2)}) collective-permute-start(bf16[136,1792]{1,0:T(8,128)(2,1)} %collective-permute-done.20.refs_2_.refs_10_), channel_id=1, source_target_pairs={{0,2},{1,3},{2,0},{3,1},{4,6},{5,7},{6,4},{7,5},{8,10},{9,11},{10,... | collective-permute-start | bytes 1462280 | tf_op jit(solution)/shard_map/ppermute | solution.py:28
  186.6 27.5 %collective-permute-start.27 = (bf16[136,1792]{1,0:T(8,128)(2,1)}, bf16[136,1792]{1,0:T(8,128)(2,1)}, u32[]{:S(2)}, u32[]{:S(2)}) collective-permute-start(bf16[136,1792]{1,0:T(8,128)(2,1)} %collective-permute-done.23.refs_5_.refs_13_), channel_id=1, source_target_pairs={{0,1},{1,0},{2,3},{3,2},{4,5},{5,4},{6,7},{7,6},{8,9},{9,8},{10,11... | collective-permute-start | bytes 1462280 | tf_op jit(solution)/shard_map/ppermute | solution.py:28
  200.8 44.9 %all-to-all-start.2 = ((bf16[4,136,896]{2,1,0:T(8,128)(2,1)}), bf16[4,136,896]{2,1,0:T(8,128)(2,1)}, u32[]{:S(2)}, u32[]{:S(2)}) async-start(bf16[4,136,896]{2,1,0:T(8,128)(2,1)} %bitcast.52), calls=%async_computation.2 | async-start | bytes 1949696 | tf_op jit(solution)/shard_map/all_to_all | solution.py:35
  245.8 21.0 %all-to-all-start.4 = ((bf16[4,136,896]{2,1,0:T(8,128)(2,1)}), bf16[4,136,896]{2,1,0:T(8,128)(2,1)S(1)}, u32[]{:S(2)}, u32[]{:S(2)}) async-start(bf16[4,136,896]{2,1,0:T(8,128)(2,1)} %bitcast.53), calls=%async_computation.4 | async-start | bytes 1949696 | tf_op jit(solution)/shard_map/all_to_all | solution.py:35
  (70 other events, 472.9 us)

commit v11 on v8

--- a/solution.py
+++ b/solution.py
@@ -54,13 +54,6 @@
             row = packed // self.slots * self.block + c * self.slots + packed % self.slots
             found[c, row, packed] = 1.0
         return jnp.asarray(found, BF16), jnp.asarray(found.transpose(0, 2, 1), BF16)
-
-
-def target_rows(ids, layout):
-    onehot = (ids[:, None] == jnp.arange(layout.experts, dtype=jnp.int32)).astype(jnp.int32)
-    slot = jnp.sum(onehot * (jnp.cumsum(onehot, axis=0) - 1), axis=1)
-    first = (ids * layout.block + slot)[:, None]
-    return first + layout.slots * jnp.arange(layout.cuts, dtype=jnp.int32)[None, :]
 
 
 def on_core(name, work, outs, *args, after=()):
@@ -88,75 +81,102 @@
 TOKEN = ((8, 128), F32)
 
 
-def sent_rows(values, target, sent):
-    cuts, tokens = target.shape
-    part = values.shape[1] // cuts
-    rows = lax.broadcasted_iota(jnp.int32, (sent, tokens), 0)
+def first_rows(ids, layout):
+    tokens = ids.shape[0]
+    named = lax.broadcasted_iota(jnp.int32, (tokens, 128), 1) == ids
+    row = lax.broadcasted_iota(jnp.int32, (tokens, tokens), 0)
+    other = lax.broadcasted_iota(jnp.int32, (tokens, tokens), 1)
+    earlier = jnp.where(other < row, 1.0, 0.0).astype(BF16)
+    count = dot(earlier, jnp.where(named, 1.0, 0.0).astype(BF16))
+    slot = jnp.sum(jnp.where(named, count, 0.0), axis=1, keepdims=True)
+    return ids * layout.block + slot.astype(jnp.int32)
+
+
+def picks(ids, layout):
+    first = first_rows(ids, layout)
+    place = lax.broadcasted_iota(jnp.int32, (ids.shape[0], layout.sent), 1)
+    return [
+        jnp.where(place == first + c * layout.slots, 1.0, 0.0).astype(BF16)
+        for c in range(layout.cuts)
+    ]
+
+
+def sent_rows(values, ids, layout):
+    part = values.shape[1] // layout.cuts
     total = 0.0
-    for c in range(cuts):
-        pick = jnp.where(rows == target[c : c + 1, :], 1.0, 0.0).astype(BF16)
-        total = total + dot(pick, values[:, c * part : (c + 1) * part])
+    for c, pick in enumerate(picks(ids, layout)):
+        total = total + dot(pick, values[:, c * part : (c + 1) * part], TN)
     return total.astype(BF16)
 
 
-def token_rows(ref, target):
-    tokens, cuts = target.shape
-    rows = lax.broadcasted_iota(jnp.int32, (tokens, ref.shape[0]), 1)
-    parts = []
-    for c in range(cuts):
-        pick = jnp.where(rows == target[:, c : c + 1], 1.0, 0.0).astype(BF16)
-        parts.append(dot(pick, ref[...]))
-    return jnp.concatenate(parts, axis=1)
-
-
-def send_normed(x, ids, router, target, layout, after=()):
+def token_rows(ref, ids, layout):
+    return jnp.concatenate([dot(pick, ref[...]) for pick in picks(ids, layout)], axis=1)
+
+
+def normed_rows(x_ref):
+    feat = x_ref[...].astype(F32)
+    scale = lax.rsqrt(jnp.mean(feat * feat, axis=1, keepdims=True) + EPS)
+    return (feat * scale).astype(BF16)
+
+
+def gate_rows(normed, ids, router_ref):
+    scores = dot(normed, router_ref[...])
+    expert = lax.broadcasted_iota(jnp.int32, scores.shape, 1)
+    score = jnp.sum(jnp.where(expert == ids, scores, 0.0), axis=1, keepdims=True)
+    return jax.nn.sigmoid(score)
+
+
+def send_rows(x, ids, layout):
+    def work(ins, outs):
+        outs[0][...] = sent_rows(normed_rows(ins[0]), ins[1][...], layout)
+
+    outs = [((layout.sent, x.shape[1] // layout.cuts), BF16)]
+    return on_core("send_rows", work, outs, x, ids)[0]
+
+
+def send_normed(x, ids, router, layout, after=()):
     tokens, width = x.shape
 
     def work(ins, outs):
-        x_ref, ids_ref, router_ref, target_ref = ins[:4]
-        feat = x_ref[...].astype(F32)
-        scale = lax.rsqrt(jnp.mean(feat * feat, axis=1, keepdims=True) + EPS)
-        normed = (feat * scale).astype(BF16)
-        outs[0][...] = sent_rows(normed, target_ref[...], layout.sent)
-        scores = dot(normed, router_ref[...])
-        expert = lax.broadcasted_iota(jnp.int32, scores.shape, 1)
-        score = jnp.sum(jnp.where(expert == ids_ref[...], scores, 0.0), axis=1, keepdims=True)
-        outs[1][...] = jnp.broadcast_to(jax.nn.sigmoid(score), (tokens, 128))
+        normed, named = normed_rows(ins[0]), ins[1][...]
+        outs[0][...] = sent_rows(normed, named, layout)
+        outs[1][...] = jnp.broadcast_to(gate_rows(normed, named, ins[2]), (tokens, 128))
 
     outs = [((layout.sent, width // layout.cuts), BF16), ((tokens, 128), F32)]
-    return on_core("send_normed", work, outs, x, ids, router, target.T, after=after)
-
-
-def send_cotangents(cot, gate, target, layout, after=()):
+    return on_core("send_normed", work, outs, x, ids, router, after=after)
+
+
+def send_cotangents(cot, gate, ids, layout, after=()):
     def work(ins, outs):
         values = (ins[1][:, :1] * ins[0][...].astype(F32)).astype(BF16)
-        outs[0][...] = sent_rows(values, ins[2][...], layout.sent)
-        outs[1][...] = jnp.zeros(TOKEN[0], F32)
-
-    outs = [((layout.sent, cot.shape[1] // layout.cuts), BF16), TOKEN]
-    return on_core("send_cotangents", work, outs, cot, gate, target.T, after=after)
-
-
-def forward_out(x, gate, back, target):
-    def work(ins, outs):
-        rows = token_rows(ins[2], ins[3][...])
-        outs[0][...] = (ins[0][...].astype(F32) + ins[1][:, :1] * rows).astype(BF16)
-
-    return on_core("forward_out", work, [(x.shape, BF16)], x, gate, back, target)[0]
-
-
-def backward_out(x, cot, back, target):
+        outs[0][...] = sent_rows(values, ins[2][...], layout)
+
+    outs = [((layout.sent, cot.shape[1] // layout.cuts), BF16)]
+    return on_core("send_cotangents", work, outs, cot, gate, ids, after=after)[0]
+
+
+def forward_out(x, router, back, ids, layout):
+    def work(ins, outs):
+        named = ins[3][...]
+        gate = gate_rows(normed_rows(ins[0]), named, ins[1])
+        rows = token_rows(ins[2], named, layout)
+        outs[0][...] = (ins[0][...].astype(F32) + gate * rows).astype(BF16)
+
+    return on_core("forward_out", work, [(x.shape, BF16)], x, router, back, ids)[0]
+
+
+def backward_out(x, cot, back, ids, layout):
     width = x.shape[1]
 
     def work(ins, outs):
         feat = ins[0][...].astype(F32)
         scale = lax.rsqrt(jnp.mean(feat * feat, axis=1, keepdims=True) + EPS)
-        normed_grad = token_rows(ins[2], ins[3][...])
+        normed_grad = token_rows(ins[2], ins[3][...], layout)
         along = jnp.sum(normed_grad * feat, axis=1, keepdims=True) / width
         feature_grad = scale * normed_grad - feat * (scale * scale * scale) * along
         outs[0][...] = (ins[1][...].astype(F32) + feature_grad).astype(BF16)
 
-    return on_core("backward_out", work, [(x.shape, BF16)], x, cot, back, target)[0]
+    return on_core("backward_out", work, [(x.shape, BF16)], x, cot, back, ids)[0]
 
 
 def pack_halves(blocks, select, after=()):
@@ -412,15 +432,14 @@
     line = own.reshape(1, width)
     col = jnp.where(jnp.arange(128)[None, :] == 0, own, 0.0).astype(BF16)
     place, select = layout.places()
-    a_target, b_target = target_rows(a_ids[:, 0], layout), target_rows(b_ids[:, 0], layout)
-
-    a_send, a_gate = send_normed(a_input[0], a_ids, cols_r, a_target, layout)
+
+    a_send = send_rows(a_input[0], a_ids, layout)
     up_turned, down_turned = up.T, down.T
     a_blocks = across_planes(a_send, layout)
     a_mine, _ = pack_halves(a_blocks, select, (up_turned, down_turned))
     a_near = spread_halves(a_mine, experts)
     a_far = relay_halves(a_near, experts)
-    b_send, b_gate = send_normed(b_x, b_ids, cols_r, b_target, layout, (a_near[0][0],))
+    b_send, b_gate = send_normed(b_x, b_ids, cols_r, layout, (a_near[0][0],))
     b_blocks = across_planes(b_send, layout)
 
     act = a_near_rows((a_mine,) + a_near, up, b_gate)
@@ -432,7 +451,7 @@
 
     a_second, a_done = a_second_rows(act, down, a_first)
     a_second = swap_pair(a_second, experts)
-    c_send, _ = send_cotangents(b_c, b_gate, b_target, layout, (a_done,))
+    c_send = send_cotangents(b_c, b_gate, b_ids, layout, (a_done,))
     c_blocks = across_planes(c_send, layout)
     c_mine, _ = pack_halves(c_blocks, select)
     c_near = spread_halves(c_mine, experts)
@@ -440,7 +459,7 @@
     early, b_ready = b_hidden_rows((b_mine,) + b_near + (b_far,), up, col)
     a_total, a_summed = a_total_rows(act, down, a_first, a_second, place, (b_ready,))
     a_back = across_planes(a_total, layout)
-    a_out = forward_out(a_input[0], a_gate, a_back, a_target)
+    a_out = forward_out(a_input[0], cols_r, a_back, a_ids, layout)
     a_next = pipe_move(a_out, lambda i, n: i + 1)
 
     cots = (c_mine,) + c_near
@@ -451,7 +470,7 @@
     b_second = b_second_rows(near, up_turned, line, b_relay, b_plain)
     b_second = swap_pair(b_second, experts)
     b_total, b_done = b_total_rows(near, up_turned, line, b_plain, b_second, place)
-    b_out = backward_out(b_x, b_c, across_planes(b_total, layout), b_target)
+    b_out = backward_out(b_x, b_c, across_planes(b_total, layout), b_ids, layout)
     b_next = pipe_move(b_out, lambda i, n: n - i)
     up_grad, down_grad = weight_grads(
         (b_mine,) + b_near + (b_far,), (c_mine,) + c_near + (c_far,), near, far, b_done

time: 261 us -> 256 us (0.981)
  other arithmetic: 4.79 us -> 0.91 us
  waiting for transfers between devices: 114 us -> 111 us
    ppermute x28, waiting for transfers between devices: 92.2 us -> 89.5 us  [plane_move(): return lax.ppermute(array, 'expert', [(i, i ^ bit) for i in range(devices)])]
    unnamed x84 -> x94, local copies, waits for them, and re-layouts: 26.9 us -> 26.4 us
  transfers between devices with their start and end apart: 37 -> 37, of which waited for: 19 -> 19; matrix products, arithmetic and copies ran while one was open for 5% -> 3% of each run, Pallas kernels for 18% -> 19%
where the time goes in v11:
time: 256 us; the launch traced here: 254 us
  waiting for transfers between devices  111 us (43%)
  starting transfers between devices  58.6 us (23%)
  Pallas kernels  55.2 us (22%)
  local copies, waits for them, and re-layouts  27.3 us (11%)
    ppermute x28, waiting for transfers between devices, plane_move(): return lax.ppermute(array, 'expert', [(i, i ^ bit) for i in range(devices)])  89.5 us
    pallas_call x18, Pallas kernels, on_core(): pl.pallas_call(kernel, out_shape=[jax.ShapeDtypeStruct(shape, kind) for s...  55.2 us
    ppermute x28, starting transfers between devices, plane_move(): return lax.ppermute(array, 'expert', [(i, i ^ bit) for i in range(devices)])  32.9 us
    unnamed x94, local copies, waits for them, and re-layouts  26.4 us
    all_to_all x5, starting transfers between devices, depth_exchange(): lax.all_to_all(blocks, 'expert', split_axis=0, concat_axis=0, tiled=True,...  25.5 us
    all_to_all x5, waiting for transfers between devices, depth_exchange(): lax.all_to_all(blocks, 'expert', split_axis=0, concat_axis=0, tiled=True,...  18.6 us
  transfers between devices with their start and end apart: 37, of which 19 were waited for; matrix products, arithmetic and copies ran while one was open for 3% of the time, Pallas kernels for 19%

profile of v11, /device:TPU:0, one launch (start us, length us, event | category | flops | bytes accessed | tf_op | source)
XLA Modules:
  0.0 254.4 jit_solution(4170012102615887970)
XLA Ops:
  5.1 6.3 %all-to-all-start = ((bf16[4,136,896]{2,1,0:T(8,128)(2,1)}), bf16[4,136,896]{2,1,0:T(8,128)(2,1)}, u32[]{:S(2)}, u32[]{:S(2)}) async-start(bf16[4,136,896]{2,1,0:T(8,128)(2,1)} %bitcast.3), calls=%async_computation | async-start | bytes 1949696 | tf_op jit(solution)/shard_map/all_to_all | solution.py:35
  14.2 3.9 %copy.17 = bf16[1,256,3584]{1,2,0:T(8,128)(2,1)} copy(bf16[1,256,3584]{2,1,0:T(8,128)(2,1)} %param.16) | data formatting | bytes 3670016 | tf_op args[6]
  18.1 17.6 %all-to-all-done = bf16[4,136,896]{2,1,0:T(8,128)(2,1)} async-done(((bf16[4,136,896]{2,1,0:T(8,128)(2,1)}), bf16[4,136,896]{2,1,0:T(8,128)(2,1)}, u32[]{:S(2)}, u32[]{:S(2)}) %all-to-all-start) | async-done | bytes 974880 | tf_op jit(solution)/shard_map/all_to_all | solution.py:35
  37.2 3.1 %pack.3 = (bf16[136,1792]{1,0:T(8,128)(2,1)}, bf16[136,1792]{1,0:T(8,128)(2,1)}, f32[8,128]{1,0:T(8,128)}) custom-call(bf16[544,896]{1,0:T(8,128)(2,1)} %bitcast.4.refs_0_, bf16[4,136,544]{2,1,0:T(8,128)(2,1)S(1)} %copy-done.7, bf16[256,3584]{1,0:T(8,128)(2,1)S(1)} %bitcast.30, bf16[3584,256]{1,0:T(8,128)(2,1)S(1)} %bitcast.41), custom_call_target="tpu_custom_call" | custom-call | flops 1000000 | bytes 100000 | tf_op jit(solution)/shard_map/pack/pallas_call | solution.py:66
  45.2 9.4 %collective-permute-done.refs_3_.refs_2_ = bf16[136,1792]{1,0:T(8,128)(2,1)} collective-permute-done((bf16[136,1792]{1,0:T(8,128)(2,1)}, bf16[136,1792]{1,0:T(8,128)(2,1)}, u32[]{:S(2)}, u32[]{:S(2)}) %collective-permute-start) | collective-permute-done | bytes 487456 | tf_op jit(solution)/shard_map/ppermute | solution.py:28
  58.2 3.1 %send_normed.1 = (bf16[544,896]{1,0:T(8,128)(2,1)S(1)}, f32[128,128]{1,0:T(8,128)S(1)}) custom-call(bf16[128,3584]{1,0:T(8,128)(2,1)} %collective-permute-done.4.refs_0_, s32[128,1]{1,0:T(8,128)S(1)} %convert_element_type.25.refs_1_.refs_2_.refs_3_, bf16[3584,4]{1,0:T(8,128)(2,1)S(1)} %bitcast.44, bf16[136,1792]{1,0:T(8,128)(2,1)} %collective-permute-done.refs_3_.refs_2_), custom_call_target="tpu_custom_call" | custom-call | flops 1000000 | bytes 100000 | tf_op jit(solution)/shard_map/send_normed/pallas_call | solution.py:66
  62.9 4.2 %all-to-all-start.1 = ((bf16[4,136,896]{2,1,0:T(8,128)(2,1)}), bf16[4,136,896]{2,1,0:T(8,128)(2,1)}, u32[]{:S(2)}, u32[]{:S(2)}) async-start(bf16[4,136,896]{2,1,0:T(8,128)(2,1)} %bitcast.50), calls=%async_computation.1 | async-start | bytes 1949696 | tf_op jit(solution)/shard_map/all_to_all | solution.py:35
  79.8 19.3 %collective-permute-done.8.refs_2_ = bf16[2,136,1792]{2,1,0:T(8,128)(2,1)S(1)} collective-permute-done((bf16[2,136,1792]{2,1,0:T(8,128)(2,1)S(1)}, bf16[2,136,1792]{2,1,0:T(8,128)(2,1)S(1)}, u32[]{:S(2)}, u32[]{:S(2)}) %collective-permute-start.8) | collective-permute-done | bytes 974880 | tf_op jit(solution)/shard_map/ppermute | solution.py:28
  105.5 4.4 %all-to-all-start.3 = ((bf16[4,136,896]{2,1,0:T(8,128)(2,1)}), bf16[4,136,896]{2,1,0:T(8,128)(2,1)}, u32[]{:S(2)}, u32[]{:S(2)}) async-start(bf16[4,136,896]{2,1,0:T(8,128)(2,1)} %bitcast.46), calls=%async_computation.3 | async-start | bytes 1949696 | tf_op jit(solution)/shard_map/all_to_all | solution.py:35
  118.4 8.9 %collective-permute-done.12.refs_2_ = bf16[136,1792]{1,0:T(8,128)(2,1)} collective-permute-done((bf16[136,1792]{1,0:T(8,128)(2,1)}, bf16[136,1792]{1,0:T(8,128)(2,1)}, u32[]{:S(2)}, u32[]{:S(2)}) %collective-permute-start.12) | collective-permute-done | bytes 487456 | tf_op jit(solution)/shard_map/ppermute | solution.py:28
  131.3 3.1 %pack.5 = (bf16[136,1792]{1,0:T(8,128)(2,1)}, bf16[136,1792]{1,0:T(8,128)(2,1)}, f32[8,128]{1,0:T(8,128)}) custom-call(bf16[544,896]{1,0:T(8,128)(2,1)} %bitcast.20.refs_0_, bf16[4,136,544]{2,1,0:T(8,128)(2,1)S(1)} %copy-done.7), custom_call_target="tpu_custom_call" | custom-call | flops 1000000 | bytes 100000 | tf_op jit(solution)/shard_map/pack/pallas_call | solution.py:66
  134.4 4.9 %collective-permute-done.14.refs_4_ = bf16[136,1792]{1,0:T(8,128)(2,1)} collective-permute-done((bf16[136,1792]{1,0:T(8,128)(2,1)}, bf16[136,1792]{1,0:T(8,128)(2,1)}, u32[]{:S(2)}, u32[]{:S(2)}) %collective-permute-start.14) | collective-permute-done | bytes 487456 | tf_op jit(solution)/shard_map/ppermute | solution.py:28
  141.7 6.5 %collective-permute-done.10.refs_4_ = bf16[136,1792]{1,0:T(8,128)(2,1)} collective-permute-done((bf16[136,1792]{1,0:T(8,128)(2,1)}, bf16[136,1792]{1,0:T(8,128)(2,1)}, u32[]{:S(2)}, u32[]{:S(2)}) %collective-permute-start.10) | collective-permute-done | bytes 487456 | tf_op jit(solution)/shard_map/ppermute | solution.py:28
  151.2 7.5 %collective-permute-done.17.refs_7_ = bf16[136,1792]{1,0:T(8,128)(2,1)} collective-permute-done((bf16[136,1792]{1,0:T(8,128)(2,1)}, bf16[136,1792]{1,0:T(8,128)(2,1)}, u32[]{:S(2)}, u32[]{:S(2)}) %collective-permute-start.17) | collective-permute-done | bytes 487456 | tf_op jit(solution)/shard_map/ppermute | solution.py:28
  160.1 9.0 %collective-permute-done.20.refs_2_.refs_10_ = bf16[136,1792]{1,0:T(8,128)(2,1)} collective-permute-done((bf16[136,1792]{1,0:T(8,128)(2,1)}, bf16[136,1792]{1,0:T(8,128)(2,1)}, u32[]{:S(2)}, u32[]{:S(2)}) %collective-permute-start.20) | collective-permute-done | bytes 487456 | tf_op jit(solution)/shard_map/ppermute | solution.py:28
  172.7 4.6 %b_hidden.1 = (f32[4,136,256]{2,1,0:T(8,128)S(1)}, f32[4,136,128]{2,1,0:T(8,128)S(1)}, f32[8,128]{1,0:T(8,128)S(1)}) custom-call(bf16[136,1792]{1,0:T(8,128)(2,1)} %get-tuple-element.47.refs_0_, bf16[136,1792]{1,0:T(8,128)(2,1)} %get-tuple-element.48.refs_1_, bf16[136,1792]{1,0:T(8,128)(2,1)} %collective-permute-done.12.refs_2_, ...), custom_call_target="tpu_custom_call" | custom-call | flops 1000000 | bytes 100000 | tf_op jit(solution)/shard_map/b_hidden/pallas_call | solution.py:66
  181.0 4.9 %all-to-all-start.2 = ((bf16[4,136,896]{2,1,0:T(8,128)(2,1)}), bf16[4,136,896]{2,1,0:T(8,128)(2,1)}, u32[]{:S(2)}, u32[]{:S(2)}) async-start(bf16[4,136,896]{2,1,0:T(8,128)(2,1)} %bitcast.49), calls=%async_computation.2 | async-start | bytes 1949696 | tf_op jit(solution)/shard_map/all_to_all | solution.py:35
  188.4 3.8 %b_near.1 = (bf16[3,136,256]{2,1,0:T(8,128)(2,1)S(1)}, bf16[3,136,256]{2,1,0:T(8,128)(2,1)S(1)}, f32[3,136,128]{2,1,0:T(8,128)S(1)}, bf16[136,1792]{1,0:T(8,128)(2,1)S(1)}, bf16[136,1792]{1,0:T(8,128)(2,1)S(1)}) custom-call(bf16[136,1792]{1,0:T(8,128)(2,1)} %get-tuple-element.52.refs_0_.refs_8_, bf16[136,1792]{1,0:T(8,128)(2,1)} %get-tuple-element.53.refs_1_.refs_9_, ...), custom_call_target="tpu_custom_call" | custom-call | flops 1000000 | bytes 100000 | tf_op jit(solution)/shard_map/b_near/pallas_call | solution.py:66
  202.4 9.6 %collective-permute-done.28.refs_4_ = bf16[136,1792]{1,0:T(8,128)(2,1)S(1)} collective-permute-done((bf16[136,1792]{1,0:T(8,128)(2,1)S(1)}, bf16[136,1792]{1,0:T(8,128)(2,1)S(1)}, u32[]{:S(2)}, u32[]{:S(2)}) %collective-permute-start.28) | collective-permute-done | bytes 487456 | tf_op jit(solution)/shard_map/ppermute | solution.py:28
  215.0 7.2 %collective-permute-done.30.refs_6_ = bf16[136,1792]{1,0:T(8,128)(2,1)S(1)} collective-permute-done((bf16[136,1792]{1,0:T(8,128)(2,1)S(1)}, bf16[136,1792]{1,0:T(8,128)(2,1)S(1)}, u32[]{:S(2)}, u32[]{:S(2)}) %collective-permute-start.30) | collective-permute-done | bytes 487456 | tf_op jit(solution)/shard_map/ppermute | solution.py:28
  225.3 5.7 %all-to-all-start.4 = ((bf16[4,136,896]{2,1,0:T(8,128)(2,1)}), bf16[4,136,896]{2,1,0:T(8,128)(2,1)}, u32[]{:S(2)}, u32[]{:S(2)}) async-start(bf16[4,136,896]{2,1,0:T(8,128)(2,1)} %bitcast.51), calls=%async_computation.4 | async-start | bytes 1949696 | tf_op jit(solution)/shard_map/all_to_all | solution.py:35
  232.2 3.1 %forward_out.1 = bf16[128,3584]{1,0:T(8,128)(2,1)S(1)} custom-call(bf16[128,3584]{1,0:T(8,128)(2,1)S(1)} %bitcast.48, bf16[3584,4]{1,0:T(8,128)(2,1)S(1)} %bitcast.45, bf16[544,896]{1,0:T(8,128)(2,1)} %bitcast.16.refs_2_, s32[128,1]{1,0:T(8,128)S(1)} %copy-done.29), custom_call_target="tpu_custom_call" | custom-call | flops 1000000 | bytes 100000 | tf_op jit(solution)/shard_map/forward_out/pallas_call | solution.py:66
  238.8 9.2 %weight_grads.1 = (bf16[3584,256]{1,0:T(8,128)(2,1)}, bf16[256,3584]{1,0:T(8,128)(2,1)}) custom-call(bf16[136,1792]{1,0:T(8,128)(2,1)} %get-tuple-element.47.refs_0_, bf16[136,1792]{1,0:T(8,128)(2,1)} %get-tuple-element.48.refs_1_, bf16[136,1792]{1,0:T(8,128)(2,1)} %collective-permute-done.12.refs_2_, bf16[136,1792]{1,0:T(8,128)(2,1)} %collective-permute-done.13.refs_3_, ...), custom_call_target="tpu_custom_call" | custom-call | flops 1000000 | bytes 100000 | tf_op jit(solution)/shard_map/weight_grads/pallas_call | solution.py:66
  249.2 4.3 %backward_out.1 = bf16[128,3584]{1,0:T(8,128)(2,1)} custom-call(bf16[128,3584]{1,0:T(8,128)(2,1)} %collective-permute-done.4.refs_0_, bf16[128,3584]{1,0:T(8,128)(2,1)S(1)} %copy-done.18, bf16[544,896]{1,0:T(8,128)(2,1)} %bitcast.24.refs_2_, s32[128,1]{1,0:T(8,128)S(1)} %copy-done.24), custom_call_target="tpu_custom_call" | custom-call | flops 1000000 | bytes 100000 | tf_op jit(solution)/shard_map/backward_out/pallas_call | solution.py:66
  (171 shorter events, 89.8 us)
Async XLA Ops:
  5.1 30.6 %all-to-all-start = ((bf16[4,136,896]{2,1,0:T(8,128)(2,1)}), bf16[4,136,896]{2,1,0:T(8,128)(2,1)}, u32[]{:S(2)}, u32[]{:S(2)}) async-start(bf16[4,136,896]{2,1,0:T(8,128)(2,1)} %bitcast.3), calls=%async_computation | async-start | bytes 1949696 | tf_op jit(solution)/shard_map/all_to_all | solution.py:35
  11.4 46.7 %collective-permute-start.4 = (bf16[128,3584]{1,0:T(8,128)(2,1)}, bf16[128,3584]{1,0:T(8,128)(2,1)}, u32[]{:S(2)}, u32[]{:S(2)}) collective-permute-start(bf16[128,3584]{1,0:T(8,128)(2,1)} %bitcast.10), channel_id=1, source_target_pairs={{0,16},{16,0},{1,17},{17,1},{2,18},{18,2},{3,19},{19,3},{4,20},{20... | collective-permute-start | bytes 2752520 | tf_op jit(solution)/shard_map/ppermute | solution.py:23
  43.5 23.6 %collective-permute-start.2 = (bf16[136,1792]{1,0:T(8,128)(2,1)}, bf16[136,1792]{1,0:T(8,128)(2,1)}, u32[]{:S(2)}, u32[]{:S(2)}) collective-permute-start(bf16[136,1792]{1,0:T(8,128)(2,1)} %get-tuple-element.38.refs_0_), channel_id=1, source_target_pairs={{0,2},{1,3},{2,0},{3,1},{4,6},{5,7},{6,4},{7,5},{8,10},{9,11},{10,... | collective-permute-start | bytes 1462280 | tf_op jit(solution)/shard_map/ppermute | solution.py:28
  44.7 22.4 %collective-permute-start.1 = (bf16[136,1792]{1,0:T(8,128)(2,1)}, bf16[136,1792]{1,0:T(8,128)(2,1)}, u32[]{:S(2)}, u32[]{:S(2)}) collective-permute-start(bf16[136,1792]{1,0:T(8,128)(2,1)} %get-tuple-element.39.refs_1_), channel_id=1, source_target_pairs={{0,1},{1,0},{2,3},{3,2},{4,5},{5,4},{6,7},{7,6},{8,9},{9,8},{10,11... | collective-permute-start | bytes 1462280 | tf_op jit(solution)/shard_map/ppermute | solution.py:28
  54.7 20.1 %collective-permute-start.6 = (bf16[136,1792]{1,0:T(8,128)(2,1)}, bf16[136,1792]{1,0:T(8,128)(2,1)}, u32[]{:S(2)}, u32[]{:S(2)}) collective-permute-start(bf16[136,1792]{1,0:T(8,128)(2,1)} %collective-permute-done.refs_3_.refs_2_), channel_id=1, source_target_pairs={{0,2},{1,3},{2,0},{3,1},{4,6},{5,7},{6,4},{7,5},{8,10},{9,11},{10,... | collective-permute-start | bytes 1462280 | tf_op jit(solution)/shard_map/ppermute | solution.py:28
  62.9 42.6 %all-to-all-start.1 = ((bf16[4,136,896]{2,1,0:T(8,128)(2,1)}), bf16[4,136,896]{2,1,0:T(8,128)(2,1)}, u32[]{:S(2)}, u32[]{:S(2)}) async-start(bf16[4,136,896]{2,1,0:T(8,128)(2,1)} %bitcast.50), calls=%async_computation.1 | async-start | bytes 1949696 | tf_op jit(solution)/shard_map/all_to_all | solution.py:35
  77.7 21.4 %collective-permute-start.8 = (bf16[2,136,1792]{2,1,0:T(8,128)(2,1)S(1)}, bf16[2,136,1792]{2,1,0:T(8,128)(2,1)S(1)}, u32[]{:S(2)}, u32[]{:S(2)}) collective-permute-start(bf16[2,136,1792]{2,1,0:T(8,128)(2,1)S(1)} %get-tuple-element.41), channel_id=1, source_target_pairs={{0,1},{1,0},{2,3},{3,2},{4,5},{5,4},{6,7},{7,6},{8,9},{9,8},{10,11... | collective-permute-start | bytes 2924552 | tf_op jit(solution)/shard_map/ppermute | solution.py:28
  78.3 21.1 %collective-permute-start.9 = (bf16[2,136,1792]{2,1,0:T(8,128)(2,1)S(1)}, bf16[2,136,1792]{2,1,0:T(8,128)(2,1)S(1)}, u32[]{:S(2)}, u32[]{:S(2)}) collective-permute-start(bf16[2,136,1792]{2,1,0:T(8,128)(2,1)S(1)} %get-tuple-element.42), channel_id=1, source_target_pairs={{0,2},{1,3},{2,0},{3,1},{4,6},{5,7},{6,4},{7,5},{8,10},{9,11},{10,... | collective-permute-start | bytes 2924552 | tf_op jit(solution)/shard_map/ppermute | solution.py:28
  79.8 22.2 %collective-permute-start.19 = (bf16[128,3584]{1,0:T(8,128)(2,1)S(1)}, bf16[128,3584]{1,0:T(8,128)(2,1)S(1)}, u32[]{:S(2)}, u32[]{:S(2)}) collective-permute-start(bf16[128,3584]{1,0:T(8,128)(2,1)S(1)} %bitcast.57), channel_id=1, source_target_pairs={{0,16},{16,0},{1,17},{17,1},{2,18},{18,2},{3,19},{19,3},{4,20},{20... | collective-permute-start | bytes 2752520 | tf_op jit(solution)/shard_map/ppermute | solution.py:23
  105.5 25.8 %all-to-all-start.3 = ((bf16[4,136,896]{2,1,0:T(8,128)(2,1)}), bf16[4,136,896]{2,1,0:T(8,128)(2,1)}, u32[]{:S(2)}, u32[]{:S(2)}) async-start(bf16[4,136,896]{2,1,0:T(8,128)(2,1)} %bitcast.46), calls=%async_computation.3 | async-start | bytes 1949696 | tf_op jit(solution)/shard_map/all_to_all | solution.py:35
  115.9 23.3 %collective-permute-start.14 = (bf16[136,1792]{1,0:T(8,128)(2,1)}, bf16[136,1792]{1,0:T(8,128)(2,1)}, u32[]{:S(2)}, u32[]{:S(2)}) collective-permute-start(bf16[136,1792]{1,0:T(8,128)(2,1)} %get-tuple-element.47.refs_0_), channel_id=1, source_target_pairs={{0,2},{1,3},{2,0},{3,1},{4,6},{5,7},{6,4},{7,5},{8,10},{9,11},{10,... | collective-permute-start | bytes 1462280 | tf_op jit(solution)/shard_map/ppermute | solution.py:28
  116.4 23.4 %collective-permute-start.13 = (bf16[136,1792]{1,0:T(8,128)(2,1)}, bf16[136,1792]{1,0:T(8,128)(2,1)}, u32[]{:S(2)}, u32[]{:S(2)}) collective-permute-start(bf16[136,1792]{1,0:T(8,128)(2,1)} %get-tuple-element.48.refs_1_), channel_id=1, source_target_pairs={{0,1},{1,0},{2,3},{3,2},{4,5},{5,4},{6,7},{7,6},{8,9},{9,8},{10,11... | collective-permute-start | bytes 1462280 | tf_op jit(solution)/shard_map/ppermute | solution.py:28
  117.0 31.2 %collective-permute-start.10 = (bf16[136,1792]{1,0:T(8,128)(2,1)}, bf16[136,1792]{1,0:T(8,128)(2,1)}, u32[]{:S(2)}, u32[]{:S(2)}) collective-permute-start(bf16[136,1792]{1,0:T(8,128)(2,1)} %copy-done.39), channel_id=1, source_target_pairs={{0,1},{1,0},{2,3},{3,2},{4,5},{5,4},{6,7},{7,6},{8,9},{9,8},{10,11... | collective-permute-start | bytes 1462280 | tf_op jit(solution)/shard_map/ppermute | solution.py:28
  127.3 22.4 %collective-permute-start.16 = (bf16[136,1792]{1,0:T(8,128)(2,1)}, bf16[136,1792]{1,0:T(8,128)(2,1)}, u32[]{:S(2)}, u32[]{:S(2)}) collective-permute-start(bf16[136,1792]{1,0:T(8,128)(2,1)} %collective-permute-done.12.refs_2_), channel_id=1, source_target_pairs={{0,2},{1,3},{2,0},{3,1},{4,6},{5,7},{6,4},{7,5},{8,10},{9,11},{10,... | collective-permute-start | bytes 1462280 | tf_op jit(solution)/shard_map/ppermute | solution.py:28
  128.9 29.8 %collective-permute-start.17 = (bf16[136,1792]{1,0:T(8,128)(2,1)}, bf16[136,1792]{1,0:T(8,128)(2,1)}, u32[]{:S(2)}, u32[]{:S(2)}) collective-permute-start(bf16[136,1792]{1,0:T(8,128)(2,1)} %collective-permute-done.15.refs_5_), channel_id=1, source_target_pairs={{0,1},{1,0},{2,3},{3,2},{4,5},{5,4},{6,7},{7,6},{8,9},{9,8},{10,11... | collective-permute-start | bytes 1462280 | tf_op jit(solution)/shard_map/ppermute | solution.py:28
  139.2 29.9 %collective-permute-start.20 = (bf16[136,1792]{1,0:T(8,128)(2,1)}, bf16[136,1792]{1,0:T(8,128)(2,1)}, u32[]{:S(2)}, u32[]{:S(2)}) collective-permute-start(bf16[136,1792]{1,0:T(8,128)(2,1)} %get-tuple-element.52.refs_0_.refs_8_), channel_id=1, source_target_pairs={{0,1},{1,0},{2,3},{3,2},{4,5},{5,4},{6,7},{7,6},{8,9},{9,8},{10,11... | collective-permute-start | bytes 1462280 | tf_op jit(solution)/shard_map/ppermute | solution.py:28
  139.8 30.8 %collective-permute-start.23 = (bf16[136,1792]{1,0:T(8,128)(2,1)}, bf16[136,1792]{1,0:T(8,128)(2,1)}, u32[]{:S(2)}, u32[]{:S(2)}) collective-permute-start(bf16[136,1792]{1,0:T(8,128)(2,1)} %get-tuple-element.53.refs_1_.refs_9_), channel_id=1, source_target_pairs={{0,2},{1,3},{2,0},{3,1},{4,6},{5,7},{6,4},{7,5},{8,10},{9,11},{10,... | collective-permute-start | bytes 1462280 | tf_op jit(solution)/shard_map/ppermute | solution.py:28
  148.2 29.1 %collective-permute-start.11 = (bf16[136,1792]{1,0:T(8,128)(2,1)}, bf16[136,1792]{1,0:T(8,128)(2,1)S(1)}, u32[]{:S(2)}, u32[]{:S(2)}) collective-permute-start(bf16[136,1792]{1,0:T(8,128)(2,1)} %copy-done.38), channel_id=1, source_target_pairs={{0,2},{1,3},{2,0},{3,1},{4,6},{5,7},{6,4},{7,5},{8,10},{9,11},{10,... | collective-permute-start | bytes 1462280 | tf_op jit(solution)/shard_map/ppermute | solution.py:28
  149.8 36.2 %collective-permute-start.22 = (bf16[136,1792]{1,0:T(8,128)(2,1)}, bf16[136,1792]{1,0:T(8,128)(2,1)}, u32[]{:S(2)}, u32[]{:S(2)}) collective-permute-start(bf16[136,1792]{1,0:T(8,128)(2,1)} %get-tuple-element.52.refs_0_.refs_8_), channel_id=1, source_target_pairs={{0,2},{1,3},{2,0},{3,1},{4,6},{5,7},{6,4},{7,5},{8,10},{9,11},{10,... | collective-permute-start | bytes 1462280 | tf_op jit(solution)/shard_map/ppermute | solution.py:28
  158.7 27.3 %collective-permute-start.21 = (bf16[136,1792]{1,0:T(8,128)(2,1)}, bf16[136,1792]{1,0:T(8,128)(2,1)}, u32[]{:S(2)}, u32[]{:S(2)}) collective-permute-start(bf16[136,1792]{1,0:T(8,128)(2,1)} %get-tuple-element.53.refs_1_.refs_9_), channel_id=1, source_target_pairs={{0,1},{1,0},{2,3},{3,2},{4,5},{5,4},{6,7},{7,6},{8,9},{9,8},{10,11... | collective-permute-start | bytes 1462280 | tf_op jit(solution)/shard_map/ppermute | solution.py:28
  169.1 24.3 %collective-permute-start.26 = (bf16[136,1792]{1,0:T(8,128)(2,1)}, bf16[136,1792]{1,0:T(8,128)(2,1)}, u32[]{:S(2)}, u32[]{:S(2)}) collective-permute-start(bf16[136,1792]{1,0:T(8,128)(2,1)} %collective-permute-done.20.refs_2_.refs_10_), channel_id=1, source_target_pairs={{0,2},{1,3},{2,0},{3,1},{4,6},{5,7},{6,4},{7,5},{8,10},{9,11},{10,... | collective-permute-start | bytes 1462280 | tf_op jit(solution)/shard_map/ppermute | solution.py:28
  170.7 22.7 %collective-permute-start.27 = (bf16[136,1792]{1,0:T(8,128)(2,1)}, bf16[136,1792]{1,0:T(8,128)(2,1)}, u32[]{:S(2)}, u32[]{:S(2)}) collective-permute-start(bf16[136,1792]{1,0:T(8,128)(2,1)} %collective-permute-done.23.refs_5_.refs_13_), channel_id=1, source_target_pairs={{0,1},{1,0},{2,3},{3,2},{4,5},{5,4},{6,7},{7,6},{8,9},{9,8},{10,11... | collective-permute-start | bytes 1462280 | tf_op jit(solution)/shard_map/ppermute | solution.py:28
  181.0 44.3 %all-to-all-start.2 = ((bf16[4,136,896]{2,1,0:T(8,128)(2,1)}), bf16[4,136,896]{2,1,0:T(8,128)(2,1)}, u32[]{:S(2)}, u32[]{:S(2)}) async-start(bf16[4,136,896]{2,1,0:T(8,128)(2,1)} %bitcast.49), calls=%async_computation.2 | async-start | bytes 1949696 | tf_op jit(solution)/shard_map/all_to_all | solution.py:35
  225.3 22.6 %all-to-all-start.4 = ((bf16[4,136,896]{2,1,0:T(8,128)(2,1)}), bf16[4,136,896]{2,1,0:T(8,128)(2,1)}, u32[]{:S(2)}, u32[]{:S(2)}) async-start(bf16[4,136,896]{2,1,0:T(8,128)(2,1)} %bitcast.51), calls=%async_computation.4 | async-start | bytes 1949696 | tf_op jit(solution)/shard_map/all_to_all | solution.py:35
  (58 other events, 450.6 us)

commit v12 on v11

--- a/solution.py
+++ b/solution.py
@@ -445,13 +445,13 @@
     act = a_near_rows((a_mine,) + a_near, up, b_gate)
     a_first, a_ready = a_far_rows(a_far, act, up, down)
     a_first = swap_pair(a_first, experts)
-    b_mine, _ = pack_halves(b_blocks, select, (a_ready,))
+    b_mine, b_packed = pack_halves(b_blocks, select, (a_ready,))
     b_near = spread_halves(b_mine, experts)
     b_far = relay_halves(b_near, experts)
 
     a_second, a_done = a_second_rows(act, down, a_first)
     a_second = swap_pair(a_second, experts)
-    c_send = send_cotangents(b_c, b_gate, b_ids, layout, (a_done,))
+    c_send = send_cotangents(b_c, b_gate, b_ids, layout, (a_done, b_packed))
     c_blocks = across_planes(c_send, layout)
     c_mine, _ = pack_halves(c_blocks, select)
     c_near = spread_halves(c_mine, experts)

time: 256 us -> 257 us (level)
  Pallas kernels: 55.2 us -> 58.7 us
  waiting for transfers between devices: 111 us -> 108 us
    ppermute x28, waiting for transfers between devices: 89.5 us -> 76.9 us  [plane_move(): return lax.ppermute(array, 'expert', [(i, i ^ bit) for i in range(devices)])]
    all_to_all x5, waiting for transfers between devices: 18.6 us -> 27.4 us  [depth_exchange(): lax.all_to_all(blocks, 'expert', split_axis=0, concat_axis=0, tiled=True,...]
    pallas_call x18, Pallas kernels: 55.2 us -> 58.7 us  [on_core(): pl.pallas_call(kernel, out_shape=[jax.ShapeDtypeStruct(shape, kind) for s...]
    unnamed x94 -> x98, local copies, waits for them, and re-layouts: 26.4 us -> 28.1 us
where the time goes in v12:
time: 257 us; the launch traced here: 256 us
  waiting for transfers between devices  108 us (42%)
  Pallas kernels  58.7 us (23%)
  starting transfers between devices  58.7 us (23%)
  local copies, waits for them, and re-layouts  29.1 us (11%)
    ppermute x28, waiting for transfers between devices, plane_move(): return lax.ppermute(array, 'expert', [(i, i ^ bit) for i in range(devices)])  76.9 us
    pallas_call x18, Pallas kernels, on_core(): pl.pallas_call(kernel, out_shape=[jax.ShapeDtypeStruct(shape, kind) for s...  58.7 us
    ppermute x28, starting transfers between devices, plane_move(): return lax.ppermute(array, 'expert', [(i, i ^ bit) for i in range(devices)])  33.5 us
    unnamed x98, local copies, waits for them, and re-layouts  28.1 us
    all_to_all x5, waiting for transfers between devices, depth_exchange(): lax.all_to_all(blocks, 'expert', split_axis=0, concat_axis=0, tiled=True,...  27.4 us
    all_to_all x5, starting transfers between devices, depth_exchange(): lax.all_to_all(blocks, 'expert', split_axis=0, concat_axis=0, tiled=True,...  25 us
  transfers between devices with their start and end apart: 37, of which 19 were waited for; matrix products, arithmetic and copies ran while one was open for 3% of the time, Pallas kernels for 19%

profile of v12, /device:TPU:0, one launch (start us, length us, event | category | flops | bytes accessed | tf_op | source)
XLA Modules:
  0.0 256.1 jit_solution(7764065621798912688)
XLA Ops:
  5.1 6.3 %all-to-all-start = ((bf16[4,136,896]{2,1,0:T(8,128)(2,1)}), bf16[4,136,896]{2,1,0:T(8,128)(2,1)}, u32[]{:S(2)}, u32[]{:S(2)}) async-start(bf16[4,136,896]{2,1,0:T(8,128)(2,1)} %bitcast.3), calls=%async_computation | async-start | bytes 1949696 | tf_op jit(solution)/shard_map/all_to_all | solution.py:35
  14.2 3.9 %copy.17 = bf16[1,256,3584]{1,2,0:T(8,128)(2,1)} copy(bf16[1,256,3584]{2,1,0:T(8,128)(2,1)} %param.16) | data formatting | bytes 3670016 | tf_op args[6]
  18.1 17.6 %all-to-all-done = bf16[4,136,896]{2,1,0:T(8,128)(2,1)} async-done(((bf16[4,136,896]{2,1,0:T(8,128)(2,1)}), bf16[4,136,896]{2,1,0:T(8,128)(2,1)}, u32[]{:S(2)}, u32[]{:S(2)}) %all-to-all-start) | async-done | bytes 974880 | tf_op jit(solution)/shard_map/all_to_all | solution.py:35
  45.8 8.8 %collective-permute-done.refs_3_.refs_2_ = bf16[136,1792]{1,0:T(8,128)(2,1)} collective-permute-done((bf16[136,1792]{1,0:T(8,128)(2,1)}, bf16[136,1792]{1,0:T(8,128)(2,1)}, u32[]{:S(2)}, u32[]{:S(2)}) %collective-permute-start) | collective-permute-done | bytes 487456 | tf_op jit(solution)/shard_map/ppermute | solution.py:28
  62.3 4.3 %all-to-all-start.1 = ((bf16[4,136,896]{2,1,0:T(8,128)(2,1)}), bf16[4,136,896]{2,1,0:T(8,128)(2,1)}, u32[]{:S(2)}, u32[]{:S(2)}) async-start(bf16[4,136,896]{2,1,0:T(8,128)(2,1)} %bitcast.51), calls=%async_computation.1 | async-start | bytes 1949696 | tf_op jit(solution)/shard_map/all_to_all | solution.py:35
  74.8 3.9 %a_far.1 = (bf16[2,136,1792]{2,1,0:T(8,128)(2,1)}, bf16[2,136,1792]{2,1,0:T(8,128)(2,1)}, f32[8,128]{1,0:T(8,128)S(1)}) custom-call(bf16[136,1792]{1,0:T(8,128)(2,1)} %collective-permute-done.6.refs_0_, bf16[136,1792]{1,0:T(8,128)(2,1)} %collective-permute-done.7.refs_1_, bf16[3,136,256]{2,1,0:T(8,128)(2,1)S(1)} %a_near.1.refs_2_.refs_0_, ...), custom_call_target="tpu_custom_call" | custom-call | flops 1000000 | bytes 100000 | tf_op jit(solution)/shard_map/a_far/pallas_call | solution.py:66
  80.8 6.1 %all-to-all-done.1 = bf16[4,136,896]{2,1,0:T(8,128)(2,1)} async-done(((bf16[4,136,896]{2,1,0:T(8,128)(2,1)}), bf16[4,136,896]{2,1,0:T(8,128)(2,1)}, u32[]{:S(2)}, u32[]{:S(2)}) %all-to-all-start.1) | async-done | bytes 974880 | tf_op jit(solution)/shard_map/all_to_all | solution.py:35
  90.8 9.6 %collective-permute-done.8.refs_2_ = bf16[2,136,1792]{2,1,0:T(8,128)(2,1)} collective-permute-done((bf16[2,136,1792]{2,1,0:T(8,128)(2,1)}, bf16[2,136,1792]{2,1,0:T(8,128)(2,1)}, u32[]{:S(2)}, u32[]{:S(2)}) %collective-permute-start.8) | collective-permute-done | bytes 974880 | tf_op jit(solution)/shard_map/ppermute | solution.py:28
  109.1 4.4 %all-to-all-start.3 = ((bf16[4,136,896]{2,1,0:T(8,128)(2,1)}), bf16[4,136,896]{2,1,0:T(8,128)(2,1)}, u32[]{:S(2)}, u32[]{:S(2)}) async-start(bf16[4,136,896]{2,1,0:T(8,128)(2,1)} %bitcast.46), calls=%async_computation.3 | async-start | bytes 1949696 | tf_op jit(solution)/shard_map/all_to_all | solution.py:35
  119.1 8.8 %collective-permute-done.12.refs_2_ = bf16[136,1792]{1,0:T(8,128)(2,1)} collective-permute-done((bf16[136,1792]{1,0:T(8,128)(2,1)}, bf16[136,1792]{1,0:T(8,128)(2,1)}, u32[]{:S(2)}, u32[]{:S(2)}) %collective-permute-start.12) | collective-permute-done | bytes 487456 | tf_op jit(solution)/shard_map/ppermute | solution.py:28
  131.0 3.7 %all-to-all-done.3 = bf16[4,136,896]{2,1,0:T(8,128)(2,1)} async-done(((bf16[4,136,896]{2,1,0:T(8,128)(2,1)}), bf16[4,136,896]{2,1,0:T(8,128)(2,1)}, u32[]{:S(2)}, u32[]{:S(2)}) %all-to-all-start.3) | async-done | bytes 974880 | tf_op jit(solution)/shard_map/all_to_all | solution.py:35
  142.3 6.5 %collective-permute-done.10.refs_4_ = bf16[136,1792]{1,0:T(8,128)(2,1)} collective-permute-done((bf16[136,1792]{1,0:T(8,128)(2,1)}, bf16[136,1792]{1,0:T(8,128)(2,1)}, u32[]{:S(2)}, u32[]{:S(2)}) %collective-permute-start.10) | collective-permute-done | bytes 487456 | tf_op jit(solution)/shard_map/ppermute | solution.py:28
  151.9 7.4 %collective-permute-done.17.refs_7_ = bf16[136,1792]{1,0:T(8,128)(2,1)} collective-permute-done((bf16[136,1792]{1,0:T(8,128)(2,1)}, bf16[136,1792]{1,0:T(8,128)(2,1)}, u32[]{:S(2)}, u32[]{:S(2)}) %collective-permute-start.17) | collective-permute-done | bytes 487456 | tf_op jit(solution)/shard_map/ppermute | solution.py:28
  160.8 9.0 %collective-permute-done.20.refs_2_.refs_10_ = bf16[136,1792]{1,0:T(8,128)(2,1)} collective-permute-done((bf16[136,1792]{1,0:T(8,128)(2,1)}, bf16[136,1792]{1,0:T(8,128)(2,1)}, u32[]{:S(2)}, u32[]{:S(2)}) %collective-permute-start.20) | collective-permute-done | bytes 487456 | tf_op jit(solution)/shard_map/ppermute | solution.py:28
  175.4 4.3 %b_hidden.1 = (f32[4,136,256]{2,1,0:T(8,128)S(1)}, f32[4,136,128]{2,1,0:T(8,128)S(1)}, f32[8,128]{1,0:T(8,128)S(1)}) custom-call(bf16[136,1792]{1,0:T(8,128)(2,1)S(1)} %copy-done.18, bf16[136,1792]{1,0:T(8,128)(2,1)S(1)} %copy-done.21, bf16[136,1792]{1,0:T(8,128)(2,1)} %collective-permute-done.12.refs_2_, bf16[136,1792]{1,0:T(8,128)(2,1)} %collective-permute-done.13.refs_3_, ...), custom_call_target="tpu_custom_call" | custom-call | flops 1000000 | bytes 100000 | tf_op jit(solution)/shard_map/b_hidden/pallas_call | solution.py:66
  179.7 3.3 %a_total.1 = (bf16[544,896]{1,0:T(8,128)(2,1)S(1)}, f32[8,128]{1,0:T(8,128)S(1)}) custom-call(bf16[3,136,256]{2,1,0:T(8,128)(2,1)S(1)} %copy-done.16, bf16[256,3584]{1,0:T(8,128)(2,1)S(1)} %bitcast.40, bf16[2,136,1792]{2,1,0:T(8,128)(2,1)} %collective-permute-done.8.refs_2_, bf16[2,136,1792]{2,1,0:T(8,128)(2,1)} %collective-permute-done.9.refs_3_, ...), custom_call_target="tpu_custom_call" | custom-call | flops 1000000 | bytes 100000 | tf_op jit(solution)/shard_map/a_total/pallas_call | solution.py:66
  184.0 4.8 %all-to-all-start.2 = ((bf16[4,136,896]{2,1,0:T(8,128)(2,1)}), bf16[4,136,896]{2,1,0:T(8,128)(2,1)}, u32[]{:S(2)}, u32[]{:S(2)}) async-start(bf16[4,136,896]{2,1,0:T(8,128)(2,1)} %bitcast.49), calls=%async_computation.2 | async-start | bytes 1949696 | tf_op jit(solution)/shard_map/all_to_all | solution.py:35
  191.3 3.8 %b_near.1 = (bf16[3,136,256]{2,1,0:T(8,128)(2,1)S(1)}, bf16[3,136,256]{2,1,0:T(8,128)(2,1)S(1)}, f32[3,136,128]{2,1,0:T(8,128)S(1)}, bf16[136,1792]{1,0:T(8,128)(2,1)S(1)}, bf16[136,1792]{1,0:T(8,128)(2,1)S(1)}) custom-call(bf16[136,1792]{1,0:T(8,128)(2,1)} %get-tuple-element.54.refs_0_.refs_8_, bf16[136,1792]{1,0:T(8,128)(2,1)} %get-tuple-element.55.refs_1_.refs_9_, ...), custom_call_target="tpu_custom_call" | custom-call | flops 1000000 | bytes 100000 | tf_op jit(solution)/shard_map/b_near/pallas_call | solution.py:66
  201.8 3.8 %collective-permute-done.24.refs_6_.refs_4_ = bf16[136,1792]{1,0:T(8,128)(2,1)S(1)} collective-permute-done((bf16[136,1792]{1,0:T(8,128)(2,1)S(1)}, bf16[136,1792]{1,0:T(8,128)(2,1)S(1)}, u32[]{:S(2)}, u32[]{:S(2)}) %collective-permute-start.24) | collective-permute-done | bytes 487456 | tf_op jit(solution)/shard_map/ppermute | solution.py:28
  205.7 8.7 %collective-permute-done.28.refs_4_ = bf16[136,1792]{1,0:T(8,128)(2,1)S(1)} collective-permute-done((bf16[136,1792]{1,0:T(8,128)(2,1)S(1)}, bf16[136,1792]{1,0:T(8,128)(2,1)S(1)}, u32[]{:S(2)}, u32[]{:S(2)}) %collective-permute-start.28) | collective-permute-done | bytes 487456 | tf_op jit(solution)/shard_map/ppermute | solution.py:28
  217.6 6.8 %collective-permute-done.30.refs_6_ = bf16[136,1792]{1,0:T(8,128)(2,1)S(1)} collective-permute-done((bf16[136,1792]{1,0:T(8,128)(2,1)S(1)}, bf16[136,1792]{1,0:T(8,128)(2,1)S(1)}, u32[]{:S(2)}, u32[]{:S(2)}) %collective-permute-start.30) | collective-permute-done | bytes 487456 | tf_op jit(solution)/shard_map/ppermute | solution.py:28
  228.6 5.2 %all-to-all-start.4 = ((bf16[4,136,896]{2,1,0:T(8,128)(2,1)}), bf16[4,136,896]{2,1,0:T(8,128)(2,1)}, u32[]{:S(2)}, u32[]{:S(2)}) async-start(bf16[4,136,896]{2,1,0:T(8,128)(2,1)} %bitcast.50), calls=%async_computation.4 | async-start | bytes 1949696 | tf_op jit(solution)/shard_map/all_to_all | solution.py:35
  241.7 8.9 %weight_grads.1 = (bf16[3584,256]{1,0:T(8,128)(2,1)}, bf16[256,3584]{1,0:T(8,128)(2,1)}) custom-call(bf16[136,1792]{1,0:T(8,128)(2,1)S(1)} %copy-done.19, bf16[136,1792]{1,0:T(8,128)(2,1)S(1)} %copy-done.22, bf16[136,1792]{1,0:T(8,128)(2,1)} %collective-permute-done.12.refs_2_, bf16[136,1792]{1,0:T(8,128)(2,1)} %collective-permute-done.13.refs_3_, ...), custom_call_target="tpu_custom_call" | custom-call | flops 1000000 | bytes 100000 | tf_op jit(solution)/shard_map/weight_grads/pallas_call | solution.py:66
  250.6 4.6 %backward_out.1 = bf16[128,3584]{1,0:T(8,128)(2,1)} custom-call(bf16[128,3584]{1,0:T(8,128)(2,1)} %collective-permute-done.4.refs_0_, bf16[128,3584]{1,0:T(8,128)(2,1)} %collective-permute-done.19.refs_0_.refs_1_, bf16[544,896]{1,0:T(8,128)(2,1)} %bitcast.24.refs_2_, s32[128,1]{1,0:T(8,128)S(1)} %copy-done.26), custom_call_target="tpu_custom_call" | custom-call | flops 1000000 | bytes 100000 | tf_op jit(solution)/shard_map/backward_out/pallas_call | solution.py:66
  (175 shorter events, 100.3 us)
Async XLA Ops:
  5.1 30.6 %all-to-all-start = ((bf16[4,136,896]{2,1,0:T(8,128)(2,1)}), bf16[4,136,896]{2,1,0:T(8,128)(2,1)}, u32[]{:S(2)}, u32[]{:S(2)}) async-start(bf16[4,136,896]{2,1,0:T(8,128)(2,1)} %bitcast.3), calls=%async_computation | async-start | bytes 1949696 | tf_op jit(solution)/shard_map/all_to_all | solution.py:35
  11.4 46.2 %collective-permute-start.4 = (bf16[128,3584]{1,0:T(8,128)(2,1)}, bf16[128,3584]{1,0:T(8,128)(2,1)}, u32[]{:S(2)}, u32[]{:S(2)}) collective-permute-start(bf16[128,3584]{1,0:T(8,128)(2,1)} %bitcast.10), channel_id=1, source_target_pairs={{0,16},{16,0},{1,17},{17,1},{2,18},{18,2},{3,19},{19,3},{4,20},{20... | collective-permute-start | bytes 2752520 | tf_op jit(solution)/shard_map/ppermute | solution.py:23
  44.7 21.9 %collective-permute-start.2 = (bf16[136,1792]{1,0:T(8,128)(2,1)}, bf16[136,1792]{1,0:T(8,128)(2,1)}, u32[]{:S(2)}, u32[]{:S(2)}) collective-permute-start(bf16[136,1792]{1,0:T(8,128)(2,1)} %get-tuple-element.39.refs_0_), channel_id=1, source_target_pairs={{0,2},{1,3},{2,0},{3,1},{4,6},{5,7},{6,4},{7,5},{8,10},{9,11},{10,... | collective-permute-start | bytes 1462280 | tf_op jit(solution)/shard_map/ppermute | solution.py:28
  45.3 21.3 %collective-permute-start.1 = (bf16[136,1792]{1,0:T(8,128)(2,1)}, bf16[136,1792]{1,0:T(8,128)(2,1)}, u32[]{:S(2)}, u32[]{:S(2)}) collective-permute-start(bf16[136,1792]{1,0:T(8,128)(2,1)} %get-tuple-element.40.refs_1_), channel_id=1, source_target_pairs={{0,1},{1,0},{2,3},{3,2},{4,5},{5,4},{6,7},{7,6},{8,9},{9,8},{10,11... | collective-permute-start | bytes 1462280 | tf_op jit(solution)/shard_map/ppermute | solution.py:28
  54.7 20.1 %collective-permute-start.6 = (bf16[136,1792]{1,0:T(8,128)(2,1)}, bf16[136,1792]{1,0:T(8,128)(2,1)}, u32[]{:S(2)}, u32[]{:S(2)}) collective-permute-start(bf16[136,1792]{1,0:T(8,128)(2,1)} %collective-permute-done.refs_3_.refs_2_), channel_id=1, source_target_pairs={{0,2},{1,3},{2,0},{3,1},{4,6},{5,7},{6,4},{7,5},{8,10},{9,11},{10,... | collective-permute-start | bytes 1462280 | tf_op jit(solution)/shard_map/ppermute | solution.py:28
  62.3 24.5 %all-to-all-start.1 = ((bf16[4,136,896]{2,1,0:T(8,128)(2,1)}), bf16[4,136,896]{2,1,0:T(8,128)(2,1)}, u32[]{:S(2)}, u32[]{:S(2)}) async-start(bf16[4,136,896]{2,1,0:T(8,128)(2,1)} %bitcast.51), calls=%async_computation.1 | async-start | bytes 1949696 | tf_op jit(solution)/shard_map/all_to_all | solution.py:35
  78.7 21.7 %collective-permute-start.8 = (bf16[2,136,1792]{2,1,0:T(8,128)(2,1)}, bf16[2,136,1792]{2,1,0:T(8,128)(2,1)}, u32[]{:S(2)}, u32[]{:S(2)}) collective-permute-start(bf16[2,136,1792]{2,1,0:T(8,128)(2,1)} %get-tuple-element.42), channel_id=1, source_target_pairs={{0,1},{1,0},{2,3},{3,2},{4,5},{5,4},{6,7},{7,6},{8,9},{9,8},{10,11... | collective-permute-start | bytes 2924552 | tf_op jit(solution)/shard_map/ppermute | solution.py:28
  79.3 21.4 %collective-permute-start.9 = (bf16[2,136,1792]{2,1,0:T(8,128)(2,1)}, bf16[2,136,1792]{2,1,0:T(8,128)(2,1)}, u32[]{:S(2)}, u32[]{:S(2)}) collective-permute-start(bf16[2,136,1792]{2,1,0:T(8,128)(2,1)} %get-tuple-element.43), channel_id=1, source_target_pairs={{0,2},{1,3},{2,0},{3,1},{4,6},{5,7},{6,4},{7,5},{8,10},{9,11},{10,... | collective-permute-start | bytes 2924552 | tf_op jit(solution)/shard_map/ppermute | solution.py:28
  80.8 24.3 %collective-permute-start.19 = (bf16[128,3584]{1,0:T(8,128)(2,1)}, bf16[128,3584]{1,0:T(8,128)(2,1)}, u32[]{:S(2)}, u32[]{:S(2)}) collective-permute-start(bf16[128,3584]{1,0:T(8,128)(2,1)} %bitcast.18), channel_id=1, source_target_pairs={{0,16},{16,0},{1,17},{17,1},{2,18},{18,2},{3,19},{19,3},{4,20},{20... | collective-permute-start | bytes 2752520 | tf_op jit(solution)/shard_map/ppermute | solution.py:23
  109.1 25.6 %all-to-all-start.3 = ((bf16[4,136,896]{2,1,0:T(8,128)(2,1)}), bf16[4,136,896]{2,1,0:T(8,128)(2,1)}, u32[]{:S(2)}, u32[]{:S(2)}) async-start(bf16[4,136,896]{2,1,0:T(8,128)(2,1)} %bitcast.46), calls=%async_computation.3 | async-start | bytes 1949696 | tf_op jit(solution)/shard_map/all_to_all | solution.py:35
  116.6 23.3 %collective-permute-start.14 = (bf16[136,1792]{1,0:T(8,128)(2,1)}, bf16[136,1792]{1,0:T(8,128)(2,1)}, u32[]{:S(2)}, u32[]{:S(2)}) collective-permute-start(bf16[136,1792]{1,0:T(8,128)(2,1)} %copy-done.17), channel_id=1, source_target_pairs={{0,2},{1,3},{2,0},{3,1},{4,6},{5,7},{6,4},{7,5},{8,10},{9,11},{10,... | collective-permute-start | bytes 1462280 | tf_op jit(solution)/shard_map/ppermute | solution.py:28
  117.1 23.4 %collective-permute-start.13 = (bf16[136,1792]{1,0:T(8,128)(2,1)}, bf16[136,1792]{1,0:T(8,128)(2,1)}, u32[]{:S(2)}, u32[]{:S(2)}) collective-permute-start(bf16[136,1792]{1,0:T(8,128)(2,1)} %copy-done.20), channel_id=1, source_target_pairs={{0,1},{1,0},{2,3},{3,2},{4,5},{5,4},{6,7},{7,6},{8,9},{9,8},{10,11... | collective-permute-start | bytes 1462280 | tf_op jit(solution)/shard_map/ppermute | solution.py:28
  117.7 31.2 %collective-permute-start.10 = (bf16[136,1792]{1,0:T(8,128)(2,1)}, bf16[136,1792]{1,0:T(8,128)(2,1)}, u32[]{:S(2)}, u32[]{:S(2)}) collective-permute-start(bf16[136,1792]{1,0:T(8,128)(2,1)} %copy-done.42), channel_id=1, source_target_pairs={{0,1},{1,0},{2,3},{3,2},{4,5},{5,4},{6,7},{7,6},{8,9},{9,8},{10,11... | collective-permute-start | bytes 1462280 | tf_op jit(solution)/shard_map/ppermute | solution.py:28
  128.0 22.4 %collective-permute-start.16 = (bf16[136,1792]{1,0:T(8,128)(2,1)}, bf16[136,1792]{1,0:T(8,128)(2,1)}, u32[]{:S(2)}, u32[]{:S(2)}) collective-permute-start(bf16[136,1792]{1,0:T(8,128)(2,1)} %collective-permute-done.12.refs_2_), channel_id=1, source_target_pairs={{0,2},{1,3},{2,0},{3,1},{4,6},{5,7},{6,4},{7,5},{8,10},{9,11},{10,... | collective-permute-start | bytes 1462280 | tf_op jit(solution)/shard_map/ppermute | solution.py:28
  129.5 29.8 %collective-permute-start.17 = (bf16[136,1792]{1,0:T(8,128)(2,1)}, bf16[136,1792]{1,0:T(8,128)(2,1)}, u32[]{:S(2)}, u32[]{:S(2)}) collective-permute-start(bf16[136,1792]{1,0:T(8,128)(2,1)} %collective-permute-done.15.refs_5_), channel_id=1, source_target_pairs={{0,1},{1,0},{2,3},{3,2},{4,5},{5,4},{6,7},{7,6},{8,9},{9,8},{10,11... | collective-permute-start | bytes 1462280 | tf_op jit(solution)/shard_map/ppermute | solution.py:28
  139.9 29.8 %collective-permute-start.20 = (bf16[136,1792]{1,0:T(8,128)(2,1)}, bf16[136,1792]{1,0:T(8,128)(2,1)}, u32[]{:S(2)}, u32[]{:S(2)}) collective-permute-start(bf16[136,1792]{1,0:T(8,128)(2,1)} %get-tuple-element.54.refs_0_.refs_8_), channel_id=1, source_target_pairs={{0,1},{1,0},{2,3},{3,2},{4,5},{5,4},{6,7},{7,6},{8,9},{9,8},{10,11... | collective-permute-start | bytes 1462280 | tf_op jit(solution)/shard_map/ppermute | solution.py:28
  140.5 30.8 %collective-permute-start.23 = (bf16[136,1792]{1,0:T(8,128)(2,1)}, bf16[136,1792]{1,0:T(8,128)(2,1)}, u32[]{:S(2)}, u32[]{:S(2)}) collective-permute-start(bf16[136,1792]{1,0:T(8,128)(2,1)} %get-tuple-element.55.refs_1_.refs_9_), channel_id=1, source_target_pairs={{0,2},{1,3},{2,0},{3,1},{4,6},{5,7},{6,4},{7,5},{8,10},{9,11},{10,... | collective-permute-start | bytes 1462280 | tf_op jit(solution)/shard_map/ppermute | solution.py:28
  148.9 30.8 %collective-permute-start.11 = (bf16[136,1792]{1,0:T(8,128)(2,1)}, bf16[136,1792]{1,0:T(8,128)(2,1)S(1)}, u32[]{:S(2)}, u32[]{:S(2)}) collective-permute-start(bf16[136,1792]{1,0:T(8,128)(2,1)} %copy-done.41), channel_id=1, source_target_pairs={{0,2},{1,3},{2,0},{3,1},{4,6},{5,7},{6,4},{7,5},{8,10},{9,11},{10,... | collective-permute-start | bytes 1462280 | tf_op jit(solution)/shard_map/ppermute | solution.py:28
  150.4 38.4 %collective-permute-start.22 = (bf16[136,1792]{1,0:T(8,128)(2,1)}, bf16[136,1792]{1,0:T(8,128)(2,1)}, u32[]{:S(2)}, u32[]{:S(2)}) collective-permute-start(bf16[136,1792]{1,0:T(8,128)(2,1)} %get-tuple-element.54.refs_0_.refs_8_), channel_id=1, source_target_pairs={{0,2},{1,3},{2,0},{3,1},{4,6},{5,7},{6,4},{7,5},{8,10},{9,11},{10,... | collective-permute-start | bytes 1462280 | tf_op jit(solution)/shard_map/ppermute | solution.py:28
  159.3 29.5 %collective-permute-start.21 = (bf16[136,1792]{1,0:T(8,128)(2,1)}, bf16[136,1792]{1,0:T(8,128)(2,1)}, u32[]{:S(2)}, u32[]{:S(2)}) collective-permute-start(bf16[136,1792]{1,0:T(8,128)(2,1)} %get-tuple-element.55.refs_1_.refs_9_), channel_id=1, source_target_pairs={{0,1},{1,0},{2,3},{3,2},{4,5},{5,4},{6,7},{7,6},{8,9},{9,8},{10,11... | collective-permute-start | bytes 1462280 | tf_op jit(solution)/shard_map/ppermute | solution.py:28
  169.8 26.5 %collective-permute-start.26 = (bf16[136,1792]{1,0:T(8,128)(2,1)}, bf16[136,1792]{1,0:T(8,128)(2,1)}, u32[]{:S(2)}, u32[]{:S(2)}) collective-permute-start(bf16[136,1792]{1,0:T(8,128)(2,1)} %collective-permute-done.20.refs_2_.refs_10_), channel_id=1, source_target_pairs={{0,2},{1,3},{2,0},{3,1},{4,6},{5,7},{6,4},{7,5},{8,10},{9,11},{10,... | collective-permute-start | bytes 1462280 | tf_op jit(solution)/shard_map/ppermute | solution.py:28
  171.3 24.9 %collective-permute-start.27 = (bf16[136,1792]{1,0:T(8,128)(2,1)}, bf16[136,1792]{1,0:T(8,128)(2,1)}, u32[]{:S(2)}, u32[]{:S(2)}) collective-permute-start(bf16[136,1792]{1,0:T(8,128)(2,1)} %collective-permute-done.23.refs_5_.refs_13_), channel_id=1, source_target_pairs={{0,1},{1,0},{2,3},{3,2},{4,5},{5,4},{6,7},{7,6},{8,9},{9,8},{10,11... | collective-permute-start | bytes 1462280 | tf_op jit(solution)/shard_map/ppermute | solution.py:28
  184.0 44.6 %all-to-all-start.2 = ((bf16[4,136,896]{2,1,0:T(8,128)(2,1)}), bf16[4,136,896]{2,1,0:T(8,128)(2,1)}, u32[]{:S(2)}, u32[]{:S(2)}) async-start(bf16[4,136,896]{2,1,0:T(8,128)(2,1)} %bitcast.49), calls=%async_computation.2 | async-start | bytes 1949696 | tf_op jit(solution)/shard_map/all_to_all | solution.py:35
  228.6 21.9 %all-to-all-start.4 = ((bf16[4,136,896]{2,1,0:T(8,128)(2,1)}), bf16[4,136,896]{2,1,0:T(8,128)(2,1)}, u32[]{:S(2)}, u32[]{:S(2)}) async-start(bf16[4,136,896]{2,1,0:T(8,128)(2,1)} %bitcast.50), calls=%async_computation.4 | async-start | bytes 1949696 | tf_op jit(solution)/shard_map/all_to_all | solution.py:35
  (60 other events, 457.0 us)

commit v13 on v11

--- a/solution.py
+++ b/solution.py
@@ -325,7 +325,7 @@
     return (act, hid, term), (by_x, by_y)
 
 
-def b_far_rows(cots, early, near, up, down, line):
+def b_far_rows(cots, early, up, down, line, after):
     half, units, rows = up.shape[1] // 2, up.shape[0], cots[0].shape[0]
 
     def work(ins, outs):
@@ -338,7 +338,7 @@
 
     outs = [((rows, units), BF16)] * 2 + [((rows, half), BF16)] * 2
     args = (*cots, *early, up, down, line)
-    act, hid, by_x, by_y = on_core("b_far", work, outs, *args, after=(near[2],))
+    act, hid, by_x, by_y = on_core("b_far", work, outs, *args, after=after)
     return (act, hid), (by_x, by_y)
 
 
@@ -456,16 +456,16 @@
     c_mine, _ = pack_halves(c_blocks, select)
     c_near = spread_halves(c_mine, experts)
     c_far = relay_halves(c_near, experts)
-    early, b_ready = b_hidden_rows((b_mine,) + b_near + (b_far,), up, col)
-    a_total, a_summed = a_total_rows(act, down, a_first, a_second, place, (b_ready,))
+    early, _ = b_hidden_rows((b_mine,) + b_near + (b_far,), up, col)
+
+    cots = (c_mine,) + c_near
+    near, b_plain = b_near_rows(cots, early, up_turned, down_turned, line, ())
+    a_total, a_summed = a_total_rows(act, down, a_first, a_second, place, (near[2],))
     a_back = across_planes(a_total, layout)
     a_out = forward_out(a_input[0], cols_r, a_back, a_ids, layout)
     a_next = pipe_move(a_out, lambda i, n: i + 1)
-
-    cots = (c_mine,) + c_near
-    near, b_plain = b_near_rows(cots, early, up_turned, down_turned, line, (a_summed,))
     b_plain = swap_pair(b_plain, experts)
-    far, b_relay = b_far_rows(c_far, early, near, up_turned, down_turned, line)
+    far, b_relay = b_far_rows(c_far, early, up_turned, down_turned, line, (near[2], a_summed))
     b_relay = swap_pair(b_relay, experts)
     b_second = b_second_rows(near, up_turned, line, b_relay, b_plain)
     b_second = swap_pair(b_second, experts)

time: 256 us -> 256 us (level)
    ppermute x28, waiting for transfers between devices: 89.5 us -> 92.8 us  [plane_move(): return lax.ppermute(array, 'expert', [(i, i ^ bit) for i in range(devices)])]
    unnamed x94 -> x116, local copies, waits for them, and re-layouts: 26.4 us -> 27.1 us
  transfers between devices with their start and end apart: 37 -> 37, of which waited for: 19 -> 20; matrix products, arithmetic and copies ran while one was open for 3% -> 3% of each run, Pallas kernels for 19% -> 19%
where the time goes in v13:
time: 256 us; the launch traced here: 254 us
  waiting for transfers between devices  113 us (44%)
  starting transfers between devices  56.9 us (22%)
  Pallas kernels  54.5 us (21%)
  local copies, waits for them, and re-layouts  28 us (11%)
    ppermute x28, waiting for transfers between devices, plane_move(): return lax.ppermute(array, 'expert', [(i, i ^ bit) for i in range(devices)])  92.8 us
    pallas_call x18, Pallas kernels, on_core(): pl.pallas_call(kernel, out_shape=[jax.ShapeDtypeStruct(shape, kind) for s...  54.5 us
    ppermute x28, starting transfers between devices, plane_move(): return lax.ppermute(array, 'expert', [(i, i ^ bit) for i in range(devices)])  32.5 us
    unnamed x116, local copies, waits for them, and re-layouts  27.1 us
    all_to_all x5, starting transfers between devices, depth_exchange(): lax.all_to_all(blocks, 'expert', split_axis=0, concat_axis=0, tiled=True,...  24.3 us
    all_to_all x5, waiting for transfers between devices, depth_exchange(): lax.all_to_all(blocks, 'expert', split_axis=0, concat_axis=0, tiled=True,...  19.5 us
  transfers between devices with their start and end apart: 37, of which 20 were waited for; matrix products, arithmetic and copies ran while one was open for 3% of the time, Pallas kernels for 19%

profile of v13, /device:TPU:0, one launch (start us, length us, event | category | flops | bytes accessed | tf_op | source)
XLA Modules:
  0.0 254.5 jit_solution(5424568130058013750)
XLA Ops:
  5.1 6.3 %all-to-all-start = ((bf16[4,136,896]{2,1,0:T(8,128)(2,1)}), bf16[4,136,896]{2,1,0:T(8,128)(2,1)}, u32[]{:S(2)}, u32[]{:S(2)}) async-start(bf16[4,136,896]{2,1,0:T(8,128)(2,1)} %bitcast.3), calls=%async_computation | async-start | bytes 1949696 | tf_op jit(solution)/shard_map/all_to_all | solution.py:35
  14.2 3.9 %copy.17 = bf16[1,256,3584]{1,2,0:T(8,128)(2,1)} copy(bf16[1,256,3584]{2,1,0:T(8,128)(2,1)} %param.16) | data formatting | bytes 3670016 | tf_op args[6]
  18.1 17.6 %all-to-all-done = bf16[4,136,896]{2,1,0:T(8,128)(2,1)} async-done(((bf16[4,136,896]{2,1,0:T(8,128)(2,1)}), bf16[4,136,896]{2,1,0:T(8,128)(2,1)}, u32[]{:S(2)}, u32[]{:S(2)}) %all-to-all-start) | async-done | bytes 974880 | tf_op jit(solution)/shard_map/all_to_all | solution.py:35
  37.2 3.1 %pack.3 = (bf16[136,1792]{1,0:T(8,128)(2,1)}, bf16[136,1792]{1,0:T(8,128)(2,1)}, f32[8,128]{1,0:T(8,128)}) custom-call(bf16[544,896]{1,0:T(8,128)(2,1)} %bitcast.4.refs_0_, bf16[4,136,544]{2,1,0:T(8,128)(2,1)S(1)} %copy-done.8, bf16[256,3584]{1,0:T(8,128)(2,1)S(1)} %bitcast.30, bf16[3584,256]{1,0:T(8,128)(2,1)S(1)} %bitcast.41), custom_call_target="tpu_custom_call" | custom-call | flops 1000000 | bytes 100000 | tf_op jit(solution)/shard_map/pack/pallas_call | solution.py:66
  45.2 9.5 %collective-permute-done.refs_3_.refs_2_ = bf16[136,1792]{1,0:T(8,128)(2,1)} collective-permute-done((bf16[136,1792]{1,0:T(8,128)(2,1)}, bf16[136,1792]{1,0:T(8,128)(2,1)}, u32[]{:S(2)}, u32[]{:S(2)}) %collective-permute-start) | collective-permute-done | bytes 487456 | tf_op jit(solution)/shard_map/ppermute | solution.py:28
  58.2 3.1 %send_normed.1 = (bf16[544,896]{1,0:T(8,128)(2,1)S(1)}, f32[128,128]{1,0:T(8,128)S(1)}) custom-call(bf16[128,3584]{1,0:T(8,128)(2,1)} %collective-permute-done.4.refs_0_, s32[128,1]{1,0:T(8,128)S(1)} %convert_element_type.25.refs_1_.refs_2_.refs_3_, bf16[3584,4]{1,0:T(8,128)(2,1)S(1)} %bitcast.44, bf16[136,1792]{1,0:T(8,128)(2,1)} %collective-permute-done.refs_3_.refs_2_), custom_call_target="tpu_custom_call" | custom-call | flops 1000000 | bytes 100000 | tf_op jit(solution)/shard_map/send_normed/pallas_call | solution.py:66
  62.9 4.2 %all-to-all-start.2 = ((bf16[4,136,896]{2,1,0:T(8,128)(2,1)}), bf16[4,136,896]{2,1,0:T(8,128)(2,1)}, u32[]{:S(2)}, u32[]{:S(2)}) async-start(bf16[4,136,896]{2,1,0:T(8,128)(2,1)} %bitcast.50), calls=%async_computation.2 | async-start | bytes 1949696 | tf_op jit(solution)/shard_map/all_to_all | solution.py:35
  79.8 19.3 %collective-permute-done.8.refs_2_ = bf16[2,136,1792]{2,1,0:T(8,128)(2,1)S(1)} collective-permute-done((bf16[2,136,1792]{2,1,0:T(8,128)(2,1)S(1)}, bf16[2,136,1792]{2,1,0:T(8,128)(2,1)S(1)}, u32[]{:S(2)}, u32[]{:S(2)}) %collective-permute-start.8) | collective-permute-done | bytes 974880 | tf_op jit(solution)/shard_map/ppermute | solution.py:28
  105.5 4.4 %all-to-all-start.1 = ((bf16[4,136,896]{2,1,0:T(8,128)(2,1)}), bf16[4,136,896]{2,1,0:T(8,128)(2,1)}, u32[]{:S(2)}, u32[]{:S(2)}) async-start(bf16[4,136,896]{2,1,0:T(8,128)(2,1)} %bitcast.46), calls=%async_computation.1 | async-start | bytes 1949696 | tf_op jit(solution)/shard_map/all_to_all | solution.py:35
  117.0 10.3 %collective-permute-done.17.refs_2_ = bf16[136,1792]{1,0:T(8,128)(2,1)} collective-permute-done((bf16[136,1792]{1,0:T(8,128)(2,1)}, bf16[136,1792]{1,0:T(8,128)(2,1)}, u32[]{:S(2)}, u32[]{:S(2)}) %collective-permute-start.17) | collective-permute-done | bytes 487456 | tf_op jit(solution)/shard_map/ppermute | solution.py:28
  131.3 3.1 %pack.4 = (bf16[136,1792]{1,0:T(8,128)(2,1)}, bf16[136,1792]{1,0:T(8,128)(2,1)}, f32[8,128]{1,0:T(8,128)}) custom-call(bf16[544,896]{1,0:T(8,128)(2,1)} %bitcast.15.refs_0_, bf16[4,136,544]{2,1,0:T(8,128)(2,1)S(1)} %copy-done.8), custom_call_target="tpu_custom_call" | custom-call | flops 1000000 | bytes 100000 | tf_op jit(solution)/shard_map/pack/pallas_call | solution.py:66
  141.1 8.6 %collective-permute-done.21.refs_6_ = bf16[136,1792]{1,0:T(8,128)(2,1)} collective-permute-done((bf16[136,1792]{1,0:T(8,128)(2,1)}, bf16[136,1792]{1,0:T(8,128)(2,1)}, u32[]{:S(2)}, u32[]{:S(2)}) %collective-permute-start.21) | collective-permute-done | bytes 487456 | tf_op jit(solution)/shard_map/ppermute | solution.py:28
  151.8 6.9 %collective-permute-done.13.refs_2_.refs_10_ = bf16[136,1792]{1,0:T(8,128)(2,1)} collective-permute-done((bf16[136,1792]{1,0:T(8,128)(2,1)}, bf16[136,1792]{1,0:T(8,128)(2,1)}, u32[]{:S(2)}, u32[]{:S(2)}) %collective-permute-start.13) | collective-permute-done | bytes 487456 | tf_op jit(solution)/shard_map/ppermute | solution.py:28
  160.2 8.8 %collective-permute-done.14.refs_3_.refs_11_ = bf16[136,1792]{1,0:T(8,128)(2,1)S(1)} collective-permute-done((bf16[136,1792]{1,0:T(8,128)(2,1)}, bf16[136,1792]{1,0:T(8,128)(2,1)S(1)}, u32[]{:S(2)}, u32[]{:S(2)}) %collective-permute-start.14) | collective-permute-done | bytes 487456 | tf_op jit(solution)/shard_map/ppermute | solution.py:28
  172.6 5.1 %b_hidden.1 = (f32[4,136,256]{2,1,0:T(8,128)S(1)}, f32[4,136,128]{2,1,0:T(8,128)S(1)}, f32[8,128]{1,0:T(8,128)}) custom-call(bf16[136,1792]{1,0:T(8,128)(2,1)} %get-tuple-element.49.refs_0_, bf16[136,1792]{1,0:T(8,128)(2,1)} %get-tuple-element.50.refs_1_, bf16[136,1792]{1,0:T(8,128)(2,1)} %collective-permute-done.17.refs_2_, ...), custom_call_target="tpu_custom_call" | custom-call | flops 1000000 | bytes 100000 | tf_op jit(solution)/shard_map/b_hidden/pallas_call | solution.py:66
  177.7 3.2 %collective-permute-done.15.refs_4_.refs_12_ = bf16[136,1792]{1,0:T(8,128)(2,1)S(1)} collective-permute-done((bf16[136,1792]{1,0:T(8,128)(2,1)}, bf16[136,1792]{1,0:T(8,128)(2,1)S(1)}, u32[]{:S(2)}, u32[]{:S(2)}) %collective-permute-start.15) | collective-permute-done | bytes 487456 | tf_op jit(solution)/shard_map/ppermute | solution.py:28
  181.0 3.7 %b_near.1 = (bf16[3,136,256]{2,1,0:T(8,128)(2,1)S(1)}, bf16[3,136,256]{2,1,0:T(8,128)(2,1)S(1)}, f32[3,136,128]{2,1,0:T(8,128)S(1)}, bf16[136,1792]{1,0:T(8,128)(2,1)S(1)}, bf16[136,1792]{1,0:T(8,128)(2,1)S(1)}) custom-call(bf16[136,1792]{1,0:T(8,128)(2,1)} %get-tuple-element.45.refs_0_.refs_8_, bf16[136,1792]{1,0:T(8,128)(2,1)} %get-tuple-element.46.refs_1_.refs_9_, ...), custom_call_target="tpu_custom_call" | custom-call | flops 1000000 | bytes 100000 | tf_op jit(solution)/shard_map/b_near/pallas_call | solution.py:66
  188.2 4.9 %all-to-all-start.3 = ((bf16[4,136,896]{2,1,0:T(8,128)(2,1)}), bf16[4,136,896]{2,1,0:T(8,128)(2,1)}, u32[]{:S(2)}, u32[]{:S(2)}) async-start(bf16[4,136,896]{2,1,0:T(8,128)(2,1)} %bitcast.49), calls=%async_computation.3 | async-start | bytes 1949696 | tf_op jit(solution)/shard_map/all_to_all | solution.py:35
  204.4 9.6 %collective-permute-done.28.refs_4_ = bf16[136,1792]{1,0:T(8,128)(2,1)S(1)} collective-permute-done((bf16[136,1792]{1,0:T(8,128)(2,1)S(1)}, bf16[136,1792]{1,0:T(8,128)(2,1)S(1)}, u32[]{:S(2)}, u32[]{:S(2)}) %collective-permute-start.28) | collective-permute-done | bytes 487456 | tf_op jit(solution)/shard_map/ppermute | solution.py:28
  217.4 7.3 %collective-permute-done.30.refs_6_ = bf16[136,1792]{1,0:T(8,128)(2,1)S(1)} collective-permute-done((bf16[136,1792]{1,0:T(8,128)(2,1)S(1)}, bf16[136,1792]{1,0:T(8,128)(2,1)S(1)}, u32[]{:S(2)}, u32[]{:S(2)}) %collective-permute-start.30) | collective-permute-done | bytes 487456 | tf_op jit(solution)/shard_map/ppermute | solution.py:28
  228.4 4.4 %all-to-all-start.4 = ((bf16[4,136,896]{2,1,0:T(8,128)(2,1)}), bf16[4,136,896]{2,1,0:T(8,128)(2,1)}, u32[]{:S(2)}, u32[]{:S(2)}) async-start(bf16[4,136,896]{2,1,0:T(8,128)(2,1)} %bitcast.51), calls=%async_computation.4 | async-start | bytes 1949696 | tf_op jit(solution)/shard_map/all_to_all | solution.py:35
  234.0 3.1 %forward_out.1 = bf16[128,3584]{1,0:T(8,128)(2,1)S(1)} custom-call(bf16[128,3584]{1,0:T(8,128)(2,1)S(1)} %bitcast.48, bf16[3584,4]{1,0:T(8,128)(2,1)S(1)} %bitcast.45, bf16[544,896]{1,0:T(8,128)(2,1)} %bitcast.21.refs_2_, s32[128,1]{1,0:T(8,128)S(1)} %copy-done.38), custom_call_target="tpu_custom_call" | custom-call | flops 1000000 | bytes 100000 | tf_op jit(solution)/shard_map/forward_out/pallas_call | solution.py:66
  237.3 8.9 %weight_grads.1 = (bf16[3584,256]{1,0:T(8,128)(2,1)}, bf16[256,3584]{1,0:T(8,128)(2,1)}) custom-call(bf16[136,1792]{1,0:T(8,128)(2,1)} %get-tuple-element.49.refs_0_, bf16[136,1792]{1,0:T(8,128)(2,1)} %get-tuple-element.50.refs_1_, bf16[136,1792]{1,0:T(8,128)(2,1)} %collective-permute-done.17.refs_2_, bf16[136,1792]{1,0:T(8,128)(2,1)} %collective-permute-done.18.refs_3_, ...), custom_call_target="tpu_custom_call" | custom-call | flops 1000000 | bytes 100000 | tf_op jit(solution)/shard_map/weight_grads/pallas_call | solution.py:66
  249.2 4.3 %backward_out.1 = bf16[128,3584]{1,0:T(8,128)(2,1)} custom-call(bf16[128,3584]{1,0:T(8,128)(2,1)} %collective-permute-done.4.refs_0_, bf16[128,3584]{1,0:T(8,128)(2,1)S(1)} %copy-done.19, bf16[544,896]{1,0:T(8,128)(2,1)} %bitcast.24.refs_2_, s32[128,1]{1,0:T(8,128)S(1)} %copy-done.33), custom_call_target="tpu_custom_call" | custom-call | flops 1000000 | bytes 100000 | tf_op jit(solution)/shard_map/backward_out/pallas_call | solution.py:66
  (193 shorter events, 89.6 us)
Async XLA Ops:
  5.1 30.6 %all-to-all-start = ((bf16[4,136,896]{2,1,0:T(8,128)(2,1)}), bf16[4,136,896]{2,1,0:T(8,128)(2,1)}, u32[]{:S(2)}, u32[]{:S(2)}) async-start(bf16[4,136,896]{2,1,0:T(8,128)(2,1)} %bitcast.3), calls=%async_computation | async-start | bytes 1949696 | tf_op jit(solution)/shard_map/all_to_all | solution.py:35
  11.4 46.7 %collective-permute-start.4 = (bf16[128,3584]{1,0:T(8,128)(2,1)}, bf16[128,3584]{1,0:T(8,128)(2,1)}, u32[]{:S(2)}, u32[]{:S(2)}) collective-permute-start(bf16[128,3584]{1,0:T(8,128)(2,1)} %bitcast.10), channel_id=1, source_target_pairs={{0,16},{16,0},{1,17},{17,1},{2,18},{18,2},{3,19},{19,3},{4,20},{20... | collective-permute-start | bytes 2752520 | tf_op jit(solution)/shard_map/ppermute | solution.py:23
  43.5 23.6 %collective-permute-start.1 = (bf16[136,1792]{1,0:T(8,128)(2,1)}, bf16[136,1792]{1,0:T(8,128)(2,1)}, u32[]{:S(2)}, u32[]{:S(2)}) collective-permute-start(bf16[136,1792]{1,0:T(8,128)(2,1)} %get-tuple-element.38.refs_1_), channel_id=1, source_target_pairs={{0,1},{1,0},{2,3},{3,2},{4,5},{5,4},{6,7},{7,6},{8,9},{9,8},{10,11... | collective-permute-start | bytes 1462280 | tf_op jit(solution)/shard_map/ppermute | solution.py:28
  44.7 22.4 %collective-permute-start.2 = (bf16[136,1792]{1,0:T(8,128)(2,1)}, bf16[136,1792]{1,0:T(8,128)(2,1)}, u32[]{:S(2)}, u32[]{:S(2)}) collective-permute-start(bf16[136,1792]{1,0:T(8,128)(2,1)} %get-tuple-element.37.refs_0_), channel_id=1, source_target_pairs={{0,2},{1,3},{2,0},{3,1},{4,6},{5,7},{6,4},{7,5},{8,10},{9,11},{10,... | collective-permute-start | bytes 1462280 | tf_op jit(solution)/shard_map/ppermute | solution.py:28
  54.7 20.1 %collective-permute-start.6 = (bf16[136,1792]{1,0:T(8,128)(2,1)}, bf16[136,1792]{1,0:T(8,128)(2,1)}, u32[]{:S(2)}, u32[]{:S(2)}) collective-permute-start(bf16[136,1792]{1,0:T(8,128)(2,1)} %collective-permute-done.refs_3_.refs_2_), channel_id=1, source_target_pairs={{0,2},{1,3},{2,0},{3,1},{4,6},{5,7},{6,4},{7,5},{8,10},{9,11},{10,... | collective-permute-start | bytes 1462280 | tf_op jit(solution)/shard_map/ppermute | solution.py:28
  62.9 42.6 %all-to-all-start.2 = ((bf16[4,136,896]{2,1,0:T(8,128)(2,1)}), bf16[4,136,896]{2,1,0:T(8,128)(2,1)}, u32[]{:S(2)}, u32[]{:S(2)}) async-start(bf16[4,136,896]{2,1,0:T(8,128)(2,1)} %bitcast.50), calls=%async_computation.2 | async-start | bytes 1949696 | tf_op jit(solution)/shard_map/all_to_all | solution.py:35
  77.7 21.4 %collective-permute-start.8 = (bf16[2,136,1792]{2,1,0:T(8,128)(2,1)S(1)}, bf16[2,136,1792]{2,1,0:T(8,128)(2,1)S(1)}, u32[]{:S(2)}, u32[]{:S(2)}) collective-permute-start(bf16[2,136,1792]{2,1,0:T(8,128)(2,1)S(1)} %get-tuple-element.40), channel_id=1, source_target_pairs={{0,1},{1,0},{2,3},{3,2},{4,5},{5,4},{6,7},{7,6},{8,9},{9,8},{10,11... | collective-permute-start | bytes 2924552 | tf_op jit(solution)/shard_map/ppermute | solution.py:28
  78.3 21.1 %collective-permute-start.9 = (bf16[2,136,1792]{2,1,0:T(8,128)(2,1)S(1)}, bf16[2,136,1792]{2,1,0:T(8,128)(2,1)S(1)}, u32[]{:S(2)}, u32[]{:S(2)}) collective-permute-start(bf16[2,136,1792]{2,1,0:T(8,128)(2,1)S(1)} %get-tuple-element.41), channel_id=1, source_target_pairs={{0,2},{1,3},{2,0},{3,1},{4,6},{5,7},{6,4},{7,5},{8,10},{9,11},{10,... | collective-permute-start | bytes 2924552 | tf_op jit(solution)/shard_map/ppermute | solution.py:28
  79.8 22.1 %collective-permute-start.12 = (bf16[128,3584]{1,0:T(8,128)(2,1)S(1)}, bf16[128,3584]{1,0:T(8,128)(2,1)S(1)}, u32[]{:S(2)}, u32[]{:S(2)}) collective-permute-start(bf16[128,3584]{1,0:T(8,128)(2,1)S(1)} %bitcast.57), channel_id=1, source_target_pairs={{0,16},{16,0},{1,17},{17,1},{2,18},{18,2},{3,19},{19,3},{4,20},{20... | collective-permute-start | bytes 2752520 | tf_op jit(solution)/shard_map/ppermute | solution.py:23
  105.5 25.8 %all-to-all-start.1 = ((bf16[4,136,896]{2,1,0:T(8,128)(2,1)}), bf16[4,136,896]{2,1,0:T(8,128)(2,1)}, u32[]{:S(2)}, u32[]{:S(2)}) async-start(bf16[4,136,896]{2,1,0:T(8,128)(2,1)} %bitcast.46), calls=%async_computation.1 | async-start | bytes 1949696 | tf_op jit(solution)/shard_map/all_to_all | solution.py:35
  115.9 21.9 %collective-permute-start.18 = (bf16[136,1792]{1,0:T(8,128)(2,1)}, bf16[136,1792]{1,0:T(8,128)(2,1)}, u32[]{:S(2)}, u32[]{:S(2)}) collective-permute-start(bf16[136,1792]{1,0:T(8,128)(2,1)} %get-tuple-element.50.refs_1_), channel_id=1, source_target_pairs={{0,1},{1,0},{2,3},{3,2},{4,5},{5,4},{6,7},{7,6},{8,9},{9,8},{10,11... | collective-permute-start | bytes 1462280 | tf_op jit(solution)/shard_map/ppermute | solution.py:28
  116.5 22.7 %collective-permute-start.19 = (bf16[136,1792]{1,0:T(8,128)(2,1)}, bf16[136,1792]{1,0:T(8,128)(2,1)}, u32[]{:S(2)}, u32[]{:S(2)}) collective-permute-start(bf16[136,1792]{1,0:T(8,128)(2,1)} %get-tuple-element.49.refs_0_), channel_id=1, source_target_pairs={{0,2},{1,3},{2,0},{3,1},{4,6},{5,7},{6,4},{7,5},{8,10},{9,11},{10,... | collective-permute-start | bytes 1462280 | tf_op jit(solution)/shard_map/ppermute | solution.py:28
  127.4 22.3 %collective-permute-start.21 = (bf16[136,1792]{1,0:T(8,128)(2,1)}, bf16[136,1792]{1,0:T(8,128)(2,1)}, u32[]{:S(2)}, u32[]{:S(2)}) collective-permute-start(bf16[136,1792]{1,0:T(8,128)(2,1)} %collective-permute-done.17.refs_2_), channel_id=1, source_target_pairs={{0,2},{1,3},{2,0},{3,1},{4,6},{5,7},{6,4},{7,5},{8,10},{9,11},{10,... | collective-permute-start | bytes 1462280 | tf_op jit(solution)/shard_map/ppermute | solution.py:28
  128.9 21.4 %collective-permute-start.22 = (bf16[136,1792]{1,0:T(8,128)(2,1)}, bf16[136,1792]{1,0:T(8,128)(2,1)}, u32[]{:S(2)}, u32[]{:S(2)}) collective-permute-start(bf16[136,1792]{1,0:T(8,128)(2,1)} %collective-permute-done.20.refs_5_), channel_id=1, source_target_pairs={{0,1},{1,0},{2,3},{3,2},{4,5},{5,4},{6,7},{7,6},{8,9},{9,8},{10,11... | collective-permute-start | bytes 1462280 | tf_op jit(solution)/shard_map/ppermute | solution.py:28
  134.4 24.3 %collective-permute-start.13 = (bf16[136,1792]{1,0:T(8,128)(2,1)}, bf16[136,1792]{1,0:T(8,128)(2,1)}, u32[]{:S(2)}, u32[]{:S(2)}) collective-permute-start(bf16[136,1792]{1,0:T(8,128)(2,1)} %get-tuple-element.45.refs_0_.refs_8_), channel_id=1, source_target_pairs={{0,1},{1,0},{2,3},{3,2},{4,5},{5,4},{6,7},{7,6},{8,9},{9,8},{10,11... | collective-permute-start | bytes 1462280 | tf_op jit(solution)/shard_map/ppermute | solution.py:28
  137.8 31.2 %collective-permute-start.14 = (bf16[136,1792]{1,0:T(8,128)(2,1)}, bf16[136,1792]{1,0:T(8,128)(2,1)S(1)}, u32[]{:S(2)}, u32[]{:S(2)}) collective-permute-start(bf16[136,1792]{1,0:T(8,128)(2,1)} %get-tuple-element.46.refs_1_.refs_9_), channel_id=1, source_target_pairs={{0,1},{1,0},{2,3},{3,2},{4,5},{5,4},{6,7},{7,6},{8,9},{9,8},{10,11... | collective-permute-start | bytes 1462280 | tf_op jit(solution)/shard_map/ppermute | solution.py:28
  139.2 31.3 %collective-permute-start.16 = (bf16[136,1792]{1,0:T(8,128)(2,1)}, bf16[136,1792]{1,0:T(8,128)(2,1)}, u32[]{:S(2)}, u32[]{:S(2)}) collective-permute-start(bf16[136,1792]{1,0:T(8,128)(2,1)} %get-tuple-element.46.refs_1_.refs_9_), channel_id=1, source_target_pairs={{0,2},{1,3},{2,0},{3,1},{4,6},{5,7},{6,4},{7,5},{8,10},{9,11},{10,... | collective-permute-start | bytes 1462280 | tf_op jit(solution)/shard_map/ppermute | solution.py:28
  149.7 35.7 %collective-permute-start.10 = (bf16[136,1792]{1,0:T(8,128)(2,1)}, bf16[136,1792]{1,0:T(8,128)(2,1)S(1)}, u32[]{:S(2)}, u32[]{:S(2)}) collective-permute-start(bf16[136,1792]{1,0:T(8,128)(2,1)} %copy-done.48), channel_id=1, source_target_pairs={{0,1},{1,0},{2,3},{3,2},{4,5},{5,4},{6,7},{7,6},{8,9},{9,8},{10,11... | collective-permute-start | bytes 1462280 | tf_op jit(solution)/shard_map/ppermute | solution.py:28
  150.3 35.1 %collective-permute-start.11 = (bf16[136,1792]{1,0:T(8,128)(2,1)}, bf16[136,1792]{1,0:T(8,128)(2,1)S(1)}, u32[]{:S(2)}, u32[]{:S(2)}) collective-permute-start(bf16[136,1792]{1,0:T(8,128)(2,1)} %copy-done.47), channel_id=1, source_target_pairs={{0,2},{1,3},{2,0},{3,1},{4,6},{5,7},{6,4},{7,5},{8,10},{9,11},{10,... | collective-permute-start | bytes 1462280 | tf_op jit(solution)/shard_map/ppermute | solution.py:28
  158.7 22.2 %collective-permute-start.15 = (bf16[136,1792]{1,0:T(8,128)(2,1)}, bf16[136,1792]{1,0:T(8,128)(2,1)S(1)}, u32[]{:S(2)}, u32[]{:S(2)}) collective-permute-start(bf16[136,1792]{1,0:T(8,128)(2,1)} %get-tuple-element.45.refs_0_.refs_8_), channel_id=1, source_target_pairs={{0,2},{1,3},{2,0},{3,1},{4,6},{5,7},{6,4},{7,5},{8,10},{9,11},{10,... | collective-permute-start | bytes 1462280 | tf_op jit(solution)/shard_map/ppermute | solution.py:28
  169.0 26.1 %collective-permute-start.26 = (bf16[136,1792]{1,0:T(8,128)(2,1)}, bf16[136,1792]{1,0:T(8,128)(2,1)}, u32[]{:S(2)}, u32[]{:S(2)}) collective-permute-start(bf16[136,1792]{1,0:T(8,128)(2,1)} %collective-permute-done.13.refs_2_.refs_10_), channel_id=1, source_target_pairs={{0,2},{1,3},{2,0},{3,1},{4,6},{5,7},{6,4},{7,5},{8,10},{9,11},{10,... | collective-permute-start | bytes 1462280 | tf_op jit(solution)/shard_map/ppermute | solution.py:28
  170.6 24.6 %collective-permute-start.27 = (bf16[136,1792]{1,0:T(8,128)(2,1)}, bf16[136,1792]{1,0:T(8,128)(2,1)}, u32[]{:S(2)}, u32[]{:S(2)}) collective-permute-start(bf16[136,1792]{1,0:T(8,128)(2,1)} %collective-permute-done.16.refs_5_.refs_13_), channel_id=1, source_target_pairs={{0,1},{1,0},{2,3},{3,2},{4,5},{5,4},{6,7},{7,6},{8,9},{9,8},{10,11... | collective-permute-start | bytes 1462280 | tf_op jit(solution)/shard_map/ppermute | solution.py:28
  188.2 40.2 %all-to-all-start.3 = ((bf16[4,136,896]{2,1,0:T(8,128)(2,1)}), bf16[4,136,896]{2,1,0:T(8,128)(2,1)}, u32[]{:S(2)}, u32[]{:S(2)}) async-start(bf16[4,136,896]{2,1,0:T(8,128)(2,1)} %bitcast.49), calls=%async_computation.3 | async-start | bytes 1949696 | tf_op jit(solution)/shard_map/all_to_all | solution.py:35
  228.4 19.7 %all-to-all-start.4 = ((bf16[4,136,896]{2,1,0:T(8,128)(2,1)}), bf16[4,136,896]{2,1,0:T(8,128)(2,1)}, u32[]{:S(2)}, u32[]{:S(2)}) async-start(bf16[4,136,896]{2,1,0:T(8,128)(2,1)} %bitcast.51), calls=%async_computation.4 | async-start | bytes 1949696 | tf_op jit(solution)/shard_map/all_to_all | solution.py:35
  (69 other events, 500.8 us)
